TPU v7x, 32 devices: a whole 2x2x4 slice. The times are simulated.
32 devices in a mesh: groups: 2 (over x), seq: 2 (over core), vocab: 8 (over z, y).
Axes of the slice: x: 2, y: 2, z: 4, core: 2. Of those that a mesh axis runs over, the one named last changes fastest.
Arguments:
- teacher_rows: bfloat16 [2048, 8192], P(('groups', 'seq'), 'vocab'), parts along dimension 0, may hold values from -200 to 200
- owner: int32 [2048], P(('groups', 'seq')), parts along dimension 0, may hold values from 0 to 255, as said below
- counts: int32 [4], P(('groups', 'seq')), parts along dimension 0, may hold values from 256 to 512, as said below
- proj_weight: bfloat16 [8192, 3584], P('vocab'), may hold values from -0.0625 to 0.0625
- student_hidden: bfloat16 [1024, 3584], P(('groups', 'seq', 'vocab')), parts along dimension 0, may hold values from -150 to 150
- head_weight: bfloat16 [3584, 19456], P('seq', 'vocab'), may hold values from -0.09375 to 0.09375
- targets: int32 [1024], P(('groups', 'seq')), parts along dimension 0, may hold values from 0 to 19455
Outputs:
- row_loss: float32 [1024], P(('groups', 'seq')), parts along dimension 0
- hidden_grad: bfloat16 [1024, 3584], P(('groups', 'seq', 'vocab')), parts along dimension 0
There are 2 independent parts, one for each index of `groups`. A program takes and returns all parts, laid end to end along the dimension named above; an argument that names none is the same for every part. Nothing has to cross between parts.
Inputs may be any that keep to these rules, and one draw needn't show every extreme that they name: `owner`: in each slab the live teacher tokens' owners never fall, start at 0, end at 255 and give every student token one or two teacher tokens; padded tokens have arbitrary owners. counts[s] is the number of live teacher tokens of slab s; some slab is full.
All inputs are finite; a program needn't handle non-finite values.
Results may differ from a plain program's by a relative error of at most 0.0098.
The roundings to bfloat16 on the way count: a program that leaves them out, or rounds other values in their place, can miss the bound.
Values may be sent and summed in bfloat16 or wider, within the bound.
No kernel may reach another device: no remote copies, remote signals or barrier semaphores. Data moves between devices by JAX's collectives and lax.ppermute only.
A program may use at most 128 MiB of HBM per device.

v0:
```python
import jax
import jax.numpy as jnp
from jax import lax
from jax.sharding import PartitionSpec as P

loss_scale = 64.0


def body(teacher_rows, owner, counts, proj_weight, student_hidden, head_weight, targets):
    teach_rows = teacher_rows.shape[0]
    slab_rows = targets.shape[0]
    vocab_dev = head_weight.shape[1]
    alive = lax.iota(jnp.int32, teach_rows) < counts[0]
    member = (owner[None, :] == lax.iota(jnp.int32, slab_rows)[:, None]) & alive[None, :]
    span_sizes = jnp.sum(member.astype(jnp.float32), axis=1)
    summed = jnp.dot(member.astype(jnp.bfloat16), teacher_rows, preferred_element_type=jnp.float32)
    aligned = (summed / span_sizes[:, None]).astype(jnp.bfloat16)
    partial_proj = jnp.dot(aligned, proj_weight, preferred_element_type=jnp.float32)
    projected = lax.psum(partial_proj, "vocab").astype(jnp.bfloat16)
    hidden_full = lax.all_gather(student_hidden, "vocab", axis=0, tiled=True)
    whole_head = lax.all_gather(head_weight, "seq", axis=0, tiled=True)
    logit_teach = jnp.dot(projected, whole_head, preferred_element_type=jnp.float32)
    logit_stud = jnp.dot(hidden_full, whole_head, preferred_element_type=jnp.float32)
    top_teach, top_stud = lax.pmax(
        (jnp.max(logit_teach, axis=1), jnp.max(logit_stud, axis=1)), "vocab"
    )
    sum_teach, sum_stud = lax.psum(
        (
            jnp.sum(jnp.exp(logit_teach - top_teach[:, None]), axis=1),
            jnp.sum(jnp.exp(logit_stud - top_stud[:, None]), axis=1),
        ),
        "vocab",
    )
    lse_teach = top_teach + jnp.log(sum_teach)
    lse_stud = top_stud + jnp.log(sum_stud)
    log_teach = logit_teach - lse_teach[:, None]
    log_stud = logit_stud - lse_stud[:, None]
    prob_teach = jnp.exp(log_teach)
    prob_stud = jnp.exp(log_stud)
    column = targets - lax.axis_index("vocab") * vocab_dev
    target_hit = lax.iota(jnp.int32, vocab_dev)[None, :] == column[:, None]
    divergence_part = jnp.sum(prob_teach * (log_teach - log_stud), axis=1)
    target_part = jnp.sum(jnp.where(target_hit, logit_stud, 0.0), axis=1)
    divergence, target_logit = lax.psum((divergence_part, target_part), "vocab")
    row_loss = divergence + lse_stud - target_logit
    upstream = (
        loss_scale * (2.0 * prob_stud - prob_teach - target_hit.astype(jnp.float32))
    ).astype(jnp.bfloat16)
    grads = lax.psum_scatter(
        lax.dot_general(
            upstream, whole_head, (((1,), (1,)), ((), ())), preferred_element_type=jnp.float32
        ),
        "vocab",
        scatter_dimension=0,
        tiled=True,
    )
    return (row_loss, grads.astype(jnp.bfloat16))


def solution(mesh):
    return jax.shard_map(
        body,
        mesh=mesh,
        in_specs=(
            P(("groups", "seq"), "vocab"),
            P(("groups", "seq")),
            P(("groups", "seq")),
            P("vocab", None),
            P(("groups", "seq", "vocab"), None),
            P("seq", "vocab"),
            P(("groups", "seq")),
        ),
        out_specs=(P(("groups", "seq")), P(("groups", "seq", "vocab"), None)),
        check_vma=False,
    )
```

profile of v0, /device:TPU:0, one launch (start us, length us, event | category | flops | bytes accessed | tf_op | source)
XLA Modules:
  0.0 345.2 jit_solution(11363454874943186359)
XLA Ops:
  7.2 0.0 copy-start
  7.2 0.0 copy-start.1
  7.2 0.0 all-gather.3.cloned.1.call-start
  7.2 0.7 all-gather.3.cloned.1.call-update
  7.9 0.0 all-gather.5.cloned.1.call-start
  8.0 0.7 all-gather.5.cloned.1.call-update
  8.7 0.0 reduce-scatter.2.cloned.1.call-start
  9.4 0.0 copy-done.1
  9.4 0.2 convert_reduce_fusion
  9.6 0.0 copy-done
  9.6 0.0 copy-start.2
  9.6 7.2 %fusion.9 = f32[256,3584]{1,0:T(8,128)} fusion(bf16[1024,3584]{1,0:T(8,128)(2,1)} %param.10, bf16[512,1024]{1,0:T(8,128)(2,1)S(1)} %copy-done, f32[256]{0:T(256)S(1)} %convert_reduce_fusion, s32[512]{0:T(512)S(1)} %copy-done.1, pred[512]{0:T(512)(128)(4,1)S(1)} %iota_compare_fusion.2), kind=kOutput, calls=%fused_computation.16 | convolution fusion | flops 2148270080 | bytes 12062208 | tf_op jit(solution)/shard_map/dot_general | solution.py:18
  16.8 0.0 copy-done.2
  16.8 159.9 %all-reduce.4 = bf16[256,3584]{1,0:T(8,128)(2,1)} all-reduce(f32[256,3584]{1,0:T(8,128)} %fusion.9), channel_id=1, replica_groups=mesh['groups'=2,'seq'=2,'vocab'=8] {'vocab'}, use_global_device_ids=true, to_apply=%region_1.0 | all-reduce | flops 917504 | bytes 5505024 | tf_op jit(solution)/shard_map/psum | solution.py:19
  176.7 0.0 all-gather.3.cloned.1.call-done
  176.7 9.6 %fusion.21 = (f32[256]{0:T(256)S(1)}, f32[256,2432]{1,0:T(8,128)S(1)}) fusion(bf16[256,3584]{1,0:T(8,128)(2,1)} %all-reduce.4, bf16[3584,2432]{1,0:T(8,128)(2,1)} %all-gather.3.cloned.1.call-done), kind=kOutput, calls=%fused_computation.31 | convolution fusion | flops 4463362048 | bytes 21758976 | tf_op jit(solution)/shard_map/dot_general | solution.py:22
  186.3 0.0 all-gather.5.cloned.1.call-done
  186.3 13.5 %fusion.20 = (f32[256]{0:T(256)}, f32[256,2432]{1,0:T(8,128)}) fusion(bf16[256,3584]{1,0:T(8,128)(2,1)} %all-gather.5.cloned.1.call-done, bf16[3584,2432]{1,0:T(8,128)(2,1)} %all-gather.3.cloned.1.call-done), kind=kOutput, calls=%fused_computation.30 | convolution fusion | flops 4463362048 | bytes 21758976 | tf_op jit(solution)/shard_map/dot_general | solution.py:23
  199.8 20.2 %all-reduce.2 = (f32[256]{0:T(256)S(1)}, f32[256]{0:T(256)S(1)}) all-reduce(f32[256]{0:T(256)} %get-tuple-element.10, f32[256]{0:T(256)S(1)} %get-tuple-element.12), channel_id=1, replica_groups=mesh['groups'=2,'seq'=2,'vocab'=8] {'vocab'}, use_global_device_ids=true, to_apply=%region_7.0 | all-reduce | flops 512 | bytes 4096 | tf_op jit(solution)/shard_map/pmax | solution.py:24
  220.0 3.1 exponential_reduce_fusion
  223.0 18.0 %all-reduce.1 = (f32[256]{0:T(256)}, f32[256]{0:T(256)}) all-reduce(f32[256]{0:T(256)S(1)} %get-tuple-element.14, f32[256]{0:T(256)} %get-tuple-element.15), channel_id=1, replica_groups=mesh['groups'=2,'seq'=2,'vocab'=8] {'vocab'}, use_global_device_ids=true, to_apply=%region_9.0 | all-reduce | flops 512 | bytes 4096 | tf_op jit(solution)/shard_map/psum | solution.py:27
  241.0 0.7 log_add_fusion.1
  241.7 0.7 log_add_fusion
  242.4 14.1 %fusion.3 = f32[256,3584]{1,0:T(8,128)} fusion(bf16[3584,2432]{1,0:T(8,128)(2,1)} %all-gather.3.cloned.1.call-done, f32[256,2432]{1,0:T(8,128)} %get-tuple-element.11, f32[256,2432]{1,0:T(8,128)S(1)} %get-tuple-element.13, s32[256]{0:T(256)S(1)} %broadcast_subtract_fusion, f32[256]{0:T(256)S(1)} %log_add_fusion, f32[256]{0:T(256)S(1)} %log_add_fusion.1), kind=kOutput, calls=%fused_computation.10 | convolution fusion | flops 4468342784 | bytes 26086400 | tf_op jit(solution)/shard_map/dot_general | solution.py:50
  256.5 0.0 reduce-scatter.2.cloned.1.call-update
  256.5 3.3 multiply_reduce_fusion
  259.8 20.0 %all-reduce = (f32[256]{0:T(256)S(1)}, f32[256]{0:T(256)S(1)}) all-reduce(f32[256]{0:T(256)} %get-tuple-element.3, f32[256]{0:T(256)S(1)} %get-tuple-element.2), channel_id=1, replica_groups=mesh['groups'=2,'seq'=2,'vocab'=8] {'vocab'}, use_global_device_ids=true, to_apply=%region_13.14 | all-reduce | flops 512 | bytes 4096 | tf_op jit(solution)/shard_map/psum | solution.py:44
  279.8 0.6 add_subtract_fusion
  280.4 56.5 %reduce-scatter.2.cloned.1.call-done = f32[32,3584]{1,0:T(8,128)} async-done(((f32[256,3584]{1,0:T(8,128)}), f32[32,3584]{1,0:T(8,128)}) %reduce-scatter.2.cloned.1.call-update) | async-done | bytes 458768 | tf_op jit(solution)/shard_map/reduce_scatter | solution.py:49
  336.9 1.7 convert_element_type.24
  (2 shorter events, 0.0 us)
Async XLA Ops:
  7.2 2.4 copy-start
  7.2 2.2 copy-start.1
  7.2 169.5 %all-gather.3.cloned.1.call-start = ((), (), s32[]{:S(2)}) async-start(), calls=%async_computation.1 | async-start | bytes 26148864 | tf_op jit(solution)/shard_map/all_gather | solution.py:21
  7.9 178.4 %all-gather.5.cloned.1.call-start = ((), (), s32[]{:S(2)}) async-start(), calls=%async_computation.2 | async-start | bytes 2064384 | tf_op jit(solution)/shard_map/all_gather | solution.py:20
  8.7 328.2 %reduce-scatter.2.cloned.1.call-start = ((), (), s32[]{:S(2)}) async-start(), calls=%async_computation.3 | async-start | bytes 4128768 | tf_op jit(solution)/shard_map/reduce_scatter | solution.py:49
  9.6 7.2 %copy-start.2 = (s32[256]{0:T(256)S(1)}, s32[256]{0:T(256)}, u32[]{:S(2)}) copy-start(s32[256]{0:T(256)} %param.13) | copy-start | bytes 3076
Sparse Core Ops, SparseCore 0:
  9.6 35.0 all-gather.2
  46.9 75.9 all-gather.4
  256.6 80.2 reduce-scatter.1
where the time goes:
time: 346 us; the launch traced here: 345 us
  blocking collectives  218 us (63%)
  waiting for transfers between devices  58 us (17%)
  matrix products  44.4 us (13%)
  between operations  14.5 us (4%)
  other arithmetic  10.2 us (3%)
    psum x1, blocking collectives, body(): projected = lax.psum(partial_proj, 'vocab').astype(jnp.bfloat16)  160 us
    reduce_scatter x1, waiting for transfers between devices, body(): lax.psum_scatter(lax.dot_general(upstream, whole_head, (((1,), (1,)), (()...  56.5 us
    pmax x1, blocking collectives, body(): lax.pmax((jnp.max(logit_teach, axis=1), jnp.max(logit_stud, axis=1)), 'vo...  20.2 us
    psum x1, blocking collectives, body(): divergence, target_logit = lax.psum((divergence_part, target_part), 'vocab')  20 us
    psum x1, blocking collectives, body(): lax.psum((jnp.sum(jnp.exp(logit_teach - top_teach[:, None]), axis=1), jnp...  18 us
    dot_general x1, matrix products, body(): lax.dot_general(upstream, whole_head, (((1,), (1,)), ((), ())), preferred...  14.1 us
    dot_general x1, matrix products, body(): jnp.dot(hidden_full, whole_head, preferred_element_type=jnp.float32)  13.5 us
    dot_general x1, matrix products, body(): jnp.dot(projected, whole_head, preferred_element_type=jnp.float32)  9.6 us
  transfers between devices with their start and end apart: 3, of which 1 were waited for; matrix products, arithmetic and copies ran while one was open for 6% of the time, Pallas kernels for 0%

commit v1 on v0

v1 whole, which is shorter than its diff:
```python
import functools

import jax
import jax.numpy as jnp
from jax import lax
from jax.experimental import pallas as pl
from jax.experimental.pallas import tpu as pltpu
from jax.sharding import PartitionSpec as P

loss_scale = 64.0
wire = jnp.float16
lanes = 128
vmem_bytes = 18 * 1024 * 1024

in_vmem = pl.BlockSpec(memory_space=pltpu.VMEM)
in_smem = pl.BlockSpec(memory_space=pltpu.SMEM)
in_place = pl.BlockSpec(memory_space=pl.ANY)


def cuts(total, step):
    return [(start, min(step, total - start)) for start in range(0, total, step)]


def project_kernel(count, step, member_ref, teacher_ref, weight_ref, *rest):
    outs, (teacher, weight, sems) = rest[:count], rest[count:]
    blk = outs[0].shape[0]
    parts = cuts(weight.shape[1], step)
    first = pltpu.make_async_copy(teacher_ref, teacher, sems.at[len(parts)])
    first.start()
    copies = []
    for index, (start, size) in enumerate(parts):
        at = pl.ds(start, size)
        copies.append(pltpu.make_async_copy(weight_ref.at[:, at], weight.at[:, at], sems.at[index]))
        copies[-1].start()
    member = member_ref[...]
    sizes = jnp.sum(member.astype(jnp.float32), axis=1, keepdims=True)
    first.wait()
    summed = jnp.dot(member, teacher[...], preferred_element_type=jnp.float32)
    aligned = (summed / sizes).astype(jnp.bfloat16)
    for copy, (start, size) in zip(copies, parts):
        copy.wait()
        product = jnp.dot(aligned, weight[:, start : start + size], preferred_element_type=jnp.float32)
        for piece, out in enumerate(outs):
            out[:, start : start + size] = product[piece * blk : (piece + 1) * blk]


def project(member, teacher_rows, proj_weight, count, step):
    slab_rows, (depth, width) = member.shape[0], proj_weight.shape
    blk = slab_rows // count
    return pl.pallas_call(
        functools.partial(project_kernel, count, step),
        in_specs=[in_vmem, in_place, in_place],
        out_specs=[in_vmem] * count,
        out_shape=[jax.ShapeDtypeStruct((blk, width), jnp.float32)] * count,
        scratch_shapes=[
            pltpu.VMEM(teacher_rows.shape, jnp.bfloat16),
            pltpu.VMEM(proj_weight.shape, jnp.bfloat16),
            pltpu.SemaphoreType.DMA((len(cuts(width, step)) + 1,)),
        ],
        compiler_params=pltpu.CompilerParams(vmem_limit_bytes=vmem_bytes),
        cost_estimate=pl.CostEstimate(
            flops=2 * slab_rows * depth * (width + teacher_rows.shape[0]),
            bytes_accessed=2 * depth * (width + teacher_rows.shape[0]) + 4 * slab_rows * width,
            transcendentals=0,
        ),
    )(member, teacher_rows, proj_weight)


def multiply(core, pieces, heads, logit_ref, step):
    depth, total = heads[0].shape
    highest = None
    for start, size in cuts(total, step):
        part = None
        for half, head_ref in zip((core, 1 - core), heads):
            at = pl.ds(pl.multiple_of(half * depth, lanes), depth)
            rows = [ref[:, at] for ref in pieces]
            rows = jnp.concatenate(rows, axis=0) if len(rows) > 1 else rows[0]
            term = jnp.dot(rows, head_ref[:, start : start + size], preferred_element_type=jnp.float32)
            part = term if part is None else part + term
        logit_ref[:, start : start + size] = part
        for lane in range(0, size, lanes):
            top = part[:, lane : lane + lanes]
            highest = top if highest is None else jnp.maximum(highest, top)
    return highest


def as_columns(first, second, third):
    lane = lax.broadcasted_iota(jnp.int32, (first.shape[0], lanes), 1)
    return jnp.where(lane == 0, first, jnp.where(lane == 1, second, jnp.where(lane == 2, third, 0.0)))


def student_kernel(count, step, chunk, place_ref, *refs):
    pieces, heads = refs[:count], refs[count : count + 2]
    column_ref, logit_ref, scaled_ref, stats_ref, highest, table = refs[count + 2 :]
    highest[...] = multiply(place_ref[1], pieces, heads, logit_ref, step)

    def one(part, carry):
        rows = pl.ds(pl.multiple_of(part * chunk, chunk), chunk)
        logit = logit_ref[rows, :]
        top = jnp.max(highest[rows, :], axis=1, keepdims=True)
        scaled = jnp.exp(logit - top)
        hit = lax.broadcasted_iota(jnp.int32, logit.shape, 1) == column_ref[rows, :]
        picked = jnp.sum(jnp.where(hit, logit, 0.0), axis=1, keepdims=True)
        scaled_ref[rows, :] = scaled
        table[rows, :] = as_columns(top, jnp.sum(scaled, axis=1, keepdims=True), picked)
        return carry

    lax.fori_loop(0, logit_ref.shape[0] // chunk, one, 0)
    stats_ref[...] = table[...].T[0:8]


def teacher_kernel(count, step, chunk, place_ref, *refs):
    pieces, heads = refs[:count], refs[count : count + 2]
    stud_logit_ref, stud_ref, scaled_ref, stats_ref, highest, table = refs[count + 2 :]
    highest[...] = multiply(place_ref[1], pieces, heads, scaled_ref, step)

    def one(part, carry):
        rows = pl.ds(pl.multiple_of(part * chunk, chunk), chunk)
        logit = scaled_ref[rows, :]
        top = jnp.max(highest[rows, :], axis=1, keepdims=True)
        scaled = jnp.exp(logit - top)
        gap = jnp.sum(scaled * (logit - stud_logit_ref[rows, :]), axis=1, keepdims=True)
        scaled_ref[rows, :] = scaled
        table[rows, :] = as_columns(top, jnp.sum(scaled, axis=1, keepdims=True), gap)
        return carry

    lax.fori_loop(0, scaled_ref.shape[0] // chunk, one, 0)
    teach = table[...].T[0:8]
    row = lax.broadcasted_iota(jnp.int32, teach.shape, 0)
    stats_ref[...] = jnp.where(row < 4, teach, pltpu.roll(stud_ref[...], 4, 0))


def head_cost(rows, heads):
    depth, vocab_dev = 2 * heads[0].shape[0], heads[0].shape[1]
    return pl.CostEstimate(
        flops=2 * rows * depth * vocab_dev,
        bytes_accessed=2 * depth * vocab_dev + 12 * rows * vocab_dev,
        transcendentals=rows * vocab_dev,
    )


def student_logits(place, pieces, heads, column, step, chunk):
    rows, vocab_dev = column.shape[0], heads[0].shape[1]
    wide = (rows, vocab_dev)
    return pl.pallas_call(
        functools.partial(student_kernel, len(pieces), step, chunk),
        in_specs=[in_smem] + [in_vmem] * (len(pieces) + 3),
        out_specs=[in_vmem] * 3,
        out_shape=[
            jax.ShapeDtypeStruct(wide, jnp.float32),
            jax.ShapeDtypeStruct(wide, jnp.float32),
            jax.ShapeDtypeStruct((8, rows), jnp.float32),
        ],
        scratch_shapes=[pltpu.VMEM((rows, lanes), jnp.float32)] * 2,
        compiler_params=pltpu.CompilerParams(vmem_limit_bytes=vmem_bytes),
        cost_estimate=head_cost(rows, heads),
    )(place, *pieces, *heads, column)


def teacher_logits(place, pieces, heads, logit_stud, stats_stud, step, chunk):
    rows, vocab_dev = logit_stud.shape
    return pl.pallas_call(
        functools.partial(teacher_kernel, len(pieces), step, chunk),
        in_specs=[in_smem] + [in_vmem] * (len(pieces) + 4),
        out_specs=[in_vmem] * 2,
        out_shape=[
            jax.ShapeDtypeStruct((rows, vocab_dev), jnp.float32),
            jax.ShapeDtypeStruct((8, rows), jnp.float32),
        ],
        scratch_shapes=[pltpu.VMEM((rows, lanes), jnp.float32)] * 2,
        compiler_params=pltpu.CompilerParams(vmem_limit_bytes=vmem_bytes),
        cost_estimate=head_cost(rows, heads),
    )(place, *pieces, *heads, logit_stud, stats_stud)


def swapped(values, distance):
    total = values.shape[1]
    lane = lax.broadcasted_iota(jnp.int32, values.shape, 1)
    return jnp.where(
        (lane & distance) != 0, pltpu.roll(values, distance, 1), pltpu.roll(values, total - distance, 1)
    )


def merged(me, bit, distance, mine, theirs):
    theirs = swapped(theirs, distance)
    upper = ((me >> bit) & 1) == 1
    low, high = jnp.where(upper, theirs, mine), jnp.where(upper, mine, theirs)
    rows = [None] * 8
    for at in (0, 4):
        top = jnp.maximum(low[at : at + 1], high[at : at + 1])
        left, right = jnp.exp(low[at : at + 1] - top), jnp.exp(high[at : at + 1] - top)
        rows[at] = top
        rows[at + 1] = left * low[at + 1 : at + 2] + right * high[at + 1 : at + 2]
        if at == 0:
            rows[2] = left * low[2:3] + right * high[2:3]
    rows[6] = low[6:7] + high[6:7]
    return rows


def merge_kernel(bit, distance, place_ref, mine_ref, theirs_ref, out_ref):
    rows = merged(place_ref[0], bit, distance, mine_ref[...], theirs_ref[...])
    for at, row in enumerate(rows):
        out_ref[at : at + 1, :] = jnp.zeros_like(rows[0]) if row is None else row


def merge(place, bit, distance, mine, theirs):
    return pl.pallas_call(
        functools.partial(merge_kernel, bit, distance),
        in_specs=[in_smem, in_vmem, in_vmem],
        out_specs=in_vmem,
        out_shape=jax.ShapeDtypeStruct(mine.shape, jnp.float32),
    )(place, mine, theirs)


def gradient_kernel(bits, step, chunk, place_ref, *refs):
    count = 1 << bits
    mine_ref, theirs_ref, own_ref, teach_ref, stud_ref, column_ref, *heads, loss_ref = refs[:9]
    outs = refs[9 : count + 9]
    upstream, factors = refs[count + 9 :]
    rows = upstream.shape[0]
    blk = rows // count
    me, core = place_ref[0], place_ref[1]
    last = bits - 1
    top_teach, total_teach, gap, _, top_stud, total_stud, picked, _ = merged(
        me, last, blk << last, mine_ref[...], theirs_ref[...]
    )
    lse_teach = top_teach + jnp.log(total_teach)
    lse_stud = top_stud + jnp.log(total_stud)
    loss = jnp.broadcast_to(gap / total_teach - lse_teach + 2.0 * lse_stud - picked, loss_ref.shape)
    for bit in range(bits):
        loss = jnp.where(((me >> bit) & 1) == 1, swapped(loss, blk << bit), loss)
    loss_ref[...] = loss
    own = own_ref[...]
    scale_teach = -loss_scale * jnp.exp(own[0:1] - lse_teach)
    scale_stud = 2.0 * loss_scale * jnp.exp(own[4:5] - lse_stud)
    line = lax.broadcasted_iota(jnp.int32, (lanes, rows), 0)
    factors[...] = jnp.where(line == 0, scale_teach, scale_stud).T

    def one(part, carry):
        at = pl.ds(pl.multiple_of(part * chunk, chunk), chunk)
        hit = lax.broadcasted_iota(jnp.int32, (chunk, teach_ref.shape[1]), 1) == column_ref[at, :]
        both = teach_ref[at, :] * factors[at, 0:1] + stud_ref[at, :] * factors[at, 1:2]
        upstream[at, :] = jnp.where(hit, both - loss_scale, both).astype(jnp.bfloat16)
        return carry

    lax.fori_loop(0, rows // chunk, one, 0)
    depth = heads[0].shape[0]
    for half, head_ref in zip((core, 1 - core), heads):
        for start, size in cuts(depth, step):
            product = lax.dot_general(
                upstream[...],
                head_ref[start : start + size, :],
                (((1,), (1,)), ((), ())),
                preferred_element_type=jnp.float32,
            )
            at = pl.ds(pl.multiple_of(half * depth + start, lanes), size)
            for piece, out in enumerate(outs):
                out[:, at] = product[piece * blk : (piece + 1) * blk]


def gradient(place, mine, theirs, own, scaled_teach, scaled_stud, column, heads, bits, step, chunk):
    rows, vocab_dev = scaled_teach.shape
    count = 1 << bits
    width = 2 * heads[0].shape[0]
    return pl.pallas_call(
        functools.partial(gradient_kernel, bits, step, chunk),
        in_specs=[in_smem] + [in_vmem] * 8,
        out_specs=[in_vmem] * (count + 1),
        out_shape=[jax.ShapeDtypeStruct((8, rows), jnp.float32)]
        + [jax.ShapeDtypeStruct((rows // count, width), jnp.float32)] * count,
        scratch_shapes=[
            pltpu.VMEM((rows, vocab_dev), jnp.bfloat16),
            pltpu.VMEM((rows, lanes), jnp.float32),
        ],
        compiler_params=pltpu.CompilerParams(vmem_limit_bytes=vmem_bytes),
        cost_estimate=head_cost(rows, heads),
    )(place, mine, theirs, own, scaled_teach, scaled_stud, column, *heads)


def tie(block, *others):
    return lax.optimization_barrier((block, *others))[0]


def make_body(vocab_size):
    bits = vocab_size.bit_length() - 1
    assert vocab_size == 1 << bits

    def swap(block, bit):
        return lax.ppermute(block, "vocab", [(at, at ^ (1 << bit)) for at in range(vocab_size)])

    def lowest(mask):
        return (mask & -mask).bit_length() - 1

    def spread(own, line=None):
        blocks = [own]
        for mask in range(1, vocab_size):
            bit = lowest(mask)
            block = blocks[mask ^ (1 << bit)]
            if line is not None and bit == 0:
                block = tie(block, line[-2])
            blocks.append(swap(block, bit))
            if line is not None and bit == 0:
                line.append(blocks[-1])
        return blocks

    def reduce_blocks(parts):
        terms, line = list(parts), []
        for mask in range(vocab_size - 1, 0, -1):
            bit = lowest(mask)
            block = terms[mask].astype(wire)
            if bit == 0 and len(line) > 1:
                block = tie(block, line[-2])
            block = swap(block, bit)
            if bit == 0:
                line.append(block)
            terms[mask ^ (1 << bit)] = terms[mask ^ (1 << bit)] + block.astype(jnp.float32)
        return terms[0], line

    def body(teacher_rows, owner, counts, proj_weight, student_hidden, head_weight, targets):
        teach_rows = teacher_rows.shape[0]
        slab_rows = targets.shape[0]
        vocab_dev = head_weight.shape[1]
        blk = slab_rows // vocab_size
        chunk = min(slab_rows, 32)
        me = lax.axis_index("vocab")
        place = jnp.stack([me, lax.axis_index("seq")]).astype(jnp.int32)

        def in_order(vec):
            grid = vec.reshape((2,) * bits + (blk,))
            for bit in range(bits):
                grid = jnp.where((me >> bit) & 1 == 1, jnp.flip(grid, bits - 1 - bit), grid)
            return grid.reshape(slab_rows)

        def as_pieces(blocks):
            return blocks if blk % 16 == 0 else [jnp.concatenate(blocks, axis=0)]

        heads = (head_weight, lax.ppermute(head_weight, "seq", [(0, 1), (1, 0)]))

        spot = lax.iota(jnp.int32, slab_rows)
        row_id = ((spot // blk) ^ me) * blk + spot % blk
        alive = lax.iota(jnp.int32, teach_rows) < counts[0]
        member = (owner[None, :] == row_id[:, None]) & alive[None, :]
        parts = project(member.astype(jnp.bfloat16), teacher_rows, proj_weight, vocab_size, 896)
        projected_own, line = reduce_blocks(parts)
        hidden = spread(tie(student_hidden, parts[-1]), line)
        projected = spread(projected_own.astype(jnp.bfloat16))

        column = (in_order(targets) - me * vocab_dev)[:, None]
        logit_stud, scaled_stud, stats_stud = student_logits(
            place, as_pieces(hidden), heads, column, 1280, chunk
        )
        scaled_teach, stats = teacher_logits(
            place, as_pieces(projected), heads, logit_stud, stats_stud, 1280, chunk
        )
        mine = stats
        for bit in range(bits):
            theirs = swap(mine, bit)
            if bit < bits - 1:
                mine = merge(place, bit, blk << bit, mine, theirs)
        loss, *terms = gradient(
            place, mine, theirs, stats, scaled_teach, scaled_stud, column, heads, bits, 896, chunk
        )
        return (loss[0], reduce_blocks(terms)[0].astype(jnp.bfloat16))

    return body


def solution(mesh):
    return jax.shard_map(
        make_body(mesh.shape["vocab"]),
        mesh=mesh,
        in_specs=(
            P(("groups", "seq"), "vocab"),
            P(("groups", "seq")),
            P(("groups", "seq")),
            P("vocab", None),
            P(("groups", "seq", "vocab"), None),
            P("seq", "vocab"),
            P(("groups", "seq")),
        ),
        out_specs=(P(("groups", "seq")), P(("groups", "seq", "vocab"), None)),
        check_vma=False,
    )
```

time: 346 us -> 163 us (0.47)
  blocking collectives: 218 us -> 0 us
  matrix products: 44.4 us -> 0 us
  starting transfers between devices: 0.11 us -> 40.2 us
  Pallas kernels: 0 us -> 39.6 us
  local copies, waits for them, and re-layouts: 0.02 us -> 27.1 us
  between operations: 14.5 us -> 1.59 us
  other arithmetic: 10.2 us -> 2.52 us
  waiting for transfers between devices: 58 us -> 51.7 us
    psum x3 -> x0, blocking collectives: 198 us -> none  [the longest x1 160 us: body(): projected = lax.psum(partial_proj, 'vocab').astype(jnp.bfloat16)]
    reduce_scatter x1 -> x0, waiting for transfers between devices: 56.5 us -> none  [body(): lax.psum_scatter(lax.dot_general(upstream, whole_head, (((1,), (1,)), (()...]
    ppermute x0 -> x32, waiting for transfers between devices: none -> 51.7 us  [the longest x31 51.7 us: swap(): lax.ppermute(block, 'vocab', [(at, at ^ 1 << bit) for at in range(vocab_s...]
    dot_general x4 -> x0, matrix products: 44.4 us -> none  [the longest x1 14.1 us: body(): lax.dot_general(upstream, whole_head, (((1,), (1,)), ((), ())), preferred...]
    ppermute x0 -> x32, starting transfers between devices: none -> 40.2 us  [the longest x31 39.7 us: swap(): lax.ppermute(block, 'vocab', [(at, at ^ 1 << bit) for at in range(vocab_s...]
    pallas_call x0 -> x6, Pallas kernels: none -> 39.6 us  [the longest x1 11.1 us: student_logits(): pl.pallas_call(functools.partial(student_kernel, len(pieces), step, chunk...]
    unnamed x6 -> x52, local copies, waits for them, and re-layouts: 0.02 us -> 26.3 us
    pmax x1 -> x0, blocking collectives: 20.2 us -> none  [body(): lax.pmax((jnp.max(logit_teach, axis=1), jnp.max(logit_stud, axis=1)), 'vo...]
  transfers between devices with their start and end apart: 3 -> 32, of which waited for: 1 -> 17; matrix products, arithmetic and copies ran while one was open for 6% -> 2% of each run, Pallas kernels for 0% -> 9%
where the time goes in v1:
time: 163 us
  waiting for transfers between devices  51.7 us (32%)
  starting transfers between devices  40.2 us (25%)
  Pallas kernels  39.6 us (24%)
  local copies, waits for them, and re-layouts  27.1 us (17%)
  other arithmetic  2.52 us (2%)
    ppermute x31, waiting for transfers between devices, swap(): lax.ppermute(block, 'vocab', [(at, at ^ 1 << bit) for at in range(vocab_s...  51.7 us
    ppermute x31, starting transfers between devices, swap(): lax.ppermute(block, 'vocab', [(at, at ^ 1 << bit) for at in range(vocab_s...  39.7 us
    unnamed x52, local copies, waits for them, and re-layouts  26.3 us
    pallas_call x1, Pallas kernels, student_logits(): pl.pallas_call(functools.partial(student_kernel, len(pieces), step, chunk...  11.1 us
    pallas_call x1, Pallas kernels, teacher_logits(): pl.pallas_call(functools.partial(teacher_kernel, len(pieces), step, chunk...  11.1 us
    pallas_call x1, Pallas kernels, gradient(): pl.pallas_call(functools.partial(gradient_kernel, bits, step, chunk), in_...  10.6 us
    pallas_call x1, Pallas kernels, project(): pl.pallas_call(functools.partial(project_kernel, count, step), in_specs=[...  4.11 us
  transfers between devices with their start and end apart: 32, of which 17 were waited for; matrix products, arithmetic and copies ran while one was open for 2% of the time, Pallas kernels for 9%

profile of v1, /device:TPU:0, one launch (start us, length us, event | category | flops | bytes accessed | tf_op | source)
XLA Modules:
  0.0 162.7 jit_solution(2332638397012352081)
XLA Ops:
  1.9 0.8 and_convert_fusion.member_ref
  2.7 3.1 %copy-done.3 = bf16[1024,3584]{1,0:T(8,128)(2,1)S(1)} copy-done((bf16[1024,3584]{1,0:T(8,128)(2,1)S(1)}, bf16[1024,3584]{1,0:T(8,128)(2,1)}, u32[]{:S(2)}) %copy-start.3) | copy-done | bytes 7340056
  5.8 1.2 copy-done.6
  7.0 4.1 %shard_map.86 = (f32[32,3584]{1,0:T(8,128)S(1)}, f32[32,3584]{1,0:T(8,128)S(1)}, f32[32,3584]{1,0:T(8,128)S(1)}, f32[32,3584]{1,0:T(8,128)S(1)}, f32[32,3584]{1,...) custom-call(bf16[256,512]{1,0:T(8,128)(2,1)S(1)} %and_convert_fusion.member_ref, ...), custom_call_target="tpu_custom_call" | custom-call | flops 2147483648 | bytes 12058624 | tf_op jit(solution)/shard_map/pallas_call | solution.py:50
  11.1 2.6 %collective-permute-start = (f16[32,3584]{1,0:T(8,128)(2,1)S(1)}, f16[32,3584]{1,0:T(8,128)(2,1)S(1)}, u32[]{:S(2)}, u32[]{:S(2)}) collective-permute-start(f16[32,3584]{1,0:T(8,128)(2,1)S(1)} %convert_element_type.94), channel_id=1, source_target_pairs={{0,1},{1,0},{2,3},{3,2},{4,5},{5,4},{6,7},{7,6},{8,9},{9,8},{10,11... | collective-permute-start | bytes 688136 | tf_op jit(solution)/shard_map/ppermute | solution.py:289
  13.8 2.6 %collective-permute-start.18 = (bf16[32,3584]{1,0:T(8,128)(2,1)S(1)}, bf16[32,3584]{1,0:T(8,128)(2,1)S(1)}, u32[]{:S(2)}, u32[]{:S(2)}) collective-permute-start(bf16[32,3584]{1,0:T(8,128)(2,1)S(1)} %copy-done.7), channel_id=1, source_target_pairs={{0,4},{1,5},{2,6},{3,7},{4,0},{5,1},{6,2},{7,3},{8,12},{9,13},{10,... | collective-permute-start | bytes 688136 | tf_op jit(solution)/shard_map/ppermute | solution.py:289
  16.4 1.6 collective-permute-start.16
  18.6 1.4 collective-permute-done
  20.0 2.2 %collective-permute-start.4 = (f16[32,3584]{1,0:T(8,128)(2,1)S(1)}, f16[32,3584]{1,0:T(8,128)(2,1)S(1)}, u32[]{:S(2)}, u32[]{:S(2)}) collective-permute-start(f16[32,3584]{1,0:T(8,128)(2,1)S(1)} %convert_element_type.102), channel_id=1, source_target_pairs={{0,1},{1,0},{2,3},{3,2},{4,5},{5,4},{6,7},{7,6},{8,9},{9,8},{10,11... | collective-permute-start | bytes 688136 | tf_op jit(solution)/shard_map/ppermute | solution.py:289
  22.3 4.3 %collective-permute-done.2 = f16[32,3584]{1,0:T(8,128)(2,1)S(1)} collective-permute-done((f16[32,3584]{1,0:T(8,128)(2,1)S(1)}, f16[32,3584]{1,0:T(8,128)(2,1)S(1)}, u32[]{:S(2)}, u32[]{:S(2)}) %collective-permute-start.2) | collective-permute-done | bytes 229408 | tf_op jit(solution)/shard_map/ppermute | solution.py:289
  26.6 0.6 collective-permute-start.1
  27.1 2.9 %collective-permute-done.4 = f16[32,3584]{1,0:T(8,128)(2,1)S(1)} collective-permute-done((f16[32,3584]{1,0:T(8,128)(2,1)S(1)}, f16[32,3584]{1,0:T(8,128)(2,1)S(1)}, u32[]{:S(2)}, u32[]{:S(2)}) %collective-permute-start.4) | collective-permute-done | bytes 229408 | tf_op jit(solution)/shard_map/ppermute | solution.py:289
  30.1 1.5 collective-permute-start.6
  31.7 0.9 collective-permute-done.1
  32.6 1.4 collective-permute-start.5
  34.0 2.6 %collective-permute-start.3 = (f16[32,3584]{1,0:T(8,128)(2,1)S(1)}, f16[32,3584]{1,0:T(8,128)(2,1)S(1)}, u32[]{:S(2)}, u32[]{:S(2)}) collective-permute-start(f16[32,3584]{1,0:T(8,128)(2,1)S(1)} %add_convert_fusion.6), channel_id=1, source_target_pairs={{0,4},{1,5},{2,6},{3,7},{4,0},{5,1},{6,2},{7,3},{8,12},{9,13},{10,... | collective-permute-start | bytes 688136 | tf_op jit(solution)/shard_map/ppermute | solution.py:289
  37.3 1.5 collective-permute-start.15
  38.8 8.2 %collective-permute-done.5 = f16[32,3584]{1,0:T(8,128)(2,1)S(1)} collective-permute-done((f16[32,3584]{1,0:T(8,128)(2,1)S(1)}, f16[32,3584]{1,0:T(8,128)(2,1)S(1)}, u32[]{:S(2)}, u32[]{:S(2)}) %collective-permute-start.5) | collective-permute-done | bytes 229408 | tf_op jit(solution)/shard_map/ppermute | solution.py:289
  47.1 1.6 %collective-permute-start.17 = (bf16[32,3584]{1,0:T(8,128)(2,1)S(1)}, bf16[32,3584]{1,0:T(8,128)(2,1)S(1)}, u32[]{:S(2)}, u32[]{:S(2)}) collective-permute-start(bf16[32,3584]{1,0:T(8,128)(2,1)S(1)} %collective-permute-done.16.refs_2_), channel_id=1, source_target_pairs={{0,1},{1,0},{2,3},{3,2},{4,5},{5,4},{6,7},{7,6},{8,9},{9,8},{10,11... | collective-permute-start | bytes 688136 | tf_op jit(solution)/shard_map/ppermute | solution.py:289
  49.0 0.7 copy-done.10
  49.7 1.7 %collective-permute-start.8 = (bf16[32,3584]{1,0:T(8,128)(2,1)S(1)}, bf16[32,3584]{1,0:T(8,128)(2,1)}, u32[]{:S(2)}, u32[]{:S(2)}) collective-permute-start(bf16[32,3584]{1,0:T(8,128)(2,1)S(1)} %add_convert_fusion.4.refs_0_), channel_id=1, source_target_pairs={{0,2},{1,3},{2,0},{3,1},{4,6},{5,7},{6,4},{7,5},{8,10},{9,11},{10,... | collective-permute-start | bytes 688136 | tf_op jit(solution)/shard_map/ppermute | solution.py:289
  51.3 2.0 %collective-permute-done.20.refs_6_ = bf16[32,3584]{1,0:T(8,128)(2,1)S(1)} collective-permute-done((bf16[32,3584]{1,0:T(8,128)(2,1)S(1)}, bf16[32,3584]{1,0:T(8,128)(2,1)S(1)}, u32[]{:S(2)}, u32[]{:S(2)}) %collective-permute-start.20) | collective-permute-done | bytes 229408 | tf_op jit(solution)/shard_map/ppermute | solution.py:289
  53.4 2.2 %collective-permute-start.19 = (bf16[32,3584]{1,0:T(8,128)(2,1)S(1)}, bf16[32,3584]{1,0:T(8,128)(2,1)S(1)}, u32[]{:S(2)}, u32[]{:S(2)}) collective-permute-start(bf16[32,3584]{1,0:T(8,128)(2,1)S(1)} %collective-permute-done.18.refs_4_), channel_id=1, source_target_pairs={{0,1},{1,0},{2,3},{3,2},{4,5},{5,4},{6,7},{7,6},{8,9},{9,8},{10,11... | collective-permute-start | bytes 688136 | tf_op jit(solution)/shard_map/ppermute | solution.py:289
  55.6 0.7 copy-done.12
  56.3 1.6 collective-permute-start.21
  57.9 0.7 copy-done.8
  58.8 1.2 collective-permute-done.8.refs_2_
  60.0 1.9 %collective-permute-start.7 = (bf16[32,3584]{1,0:T(8,128)(2,1)S(1)}, bf16[32,3584]{1,0:T(8,128)(2,1)S(1)}, u32[]{:S(2)}, u32[]{:S(2)}) collective-permute-start(bf16[32,3584]{1,0:T(8,128)(2,1)S(1)} %add_convert_fusion.4.refs_0_), channel_id=1, source_target_pairs={{0,1},{1,0},{2,3},{3,2},{4,5},{5,4},{6,7},{7,6},{8,9},{9,8},{10,11... | collective-permute-start | bytes 688136 | tf_op jit(solution)/shard_map/ppermute | solution.py:289
  61.9 0.7 copy-done.14
  62.6 2.2 %collective-permute-start.11 = (bf16[32,3584]{1,0:T(8,128)(2,1)}, bf16[32,3584]{1,0:T(8,128)(2,1)S(1)}, u32[]{:S(2)}, u32[]{:S(2)}) collective-permute-start(bf16[32,3584]{1,0:T(8,128)(2,1)} %collective-permute-done.10.refs_4_), channel_id=1, source_target_pairs={{0,1},{1,0},{2,3},{3,2},{4,5},{5,4},{6,7},{7,6},{8,9},{9,8},{10,11... | collective-permute-start | bytes 688136 | tf_op jit(solution)/shard_map/ppermute | solution.py:289
  64.8 1.9 %collective-permute-done.21.refs_7_ = bf16[32,3584]{1,0:T(8,128)(2,1)S(1)} collective-permute-done((bf16[32,3584]{1,0:T(8,128)(2,1)S(1)}, bf16[32,3584]{1,0:T(8,128)(2,1)S(1)}, u32[]{:S(2)}, u32[]{:S(2)}) %collective-permute-start.21) | collective-permute-done | bytes 229408 | tf_op jit(solution)/shard_map/ppermute | solution.py:289
  66.7 0.7 copy-done.16
  67.4 2.3 %collective-permute-start.9 = (bf16[32,3584]{1,0:T(8,128)(2,1)}, bf16[32,3584]{1,0:T(8,128)(2,1)S(1)}, u32[]{:S(2)}, u32[]{:S(2)}) collective-permute-start(bf16[32,3584]{1,0:T(8,128)(2,1)} %collective-permute-done.8.refs_2_), channel_id=1, source_target_pairs={{0,1},{1,0},{2,3},{3,2},{4,5},{5,4},{6,7},{7,6},{8,9},{9,8},{10,11... | collective-permute-start | bytes 688136 | tf_op jit(solution)/shard_map/ppermute | solution.py:289
  69.8 3.5 %copy-done = bf16[1792,2432]{1,0:T(8,128)(2,1)S(1)} copy-done((bf16[1792,2432]{1,0:T(8,128)(2,1)S(1)}, bf16[1792,2432]{1,0:T(8,128)(2,1)}, u32[]{:S(2)}) %copy-start) | copy-done | bytes 8716312
  73.3 0.9 copy-done.9
  74.2 0.9 copy-done.11
  75.1 0.9 copy-done.13
  76.1 0.9 copy-done.15
  77.0 0.9 copy-done.17
  77.9 11.1 %shard_map.87 = (f32[256,2432]{1,0:T(8,128)S(1)}, f32[256,2432]{1,0:T(8,128)S(1)}, f32[8,256]{1,0:T(8,128)S(1)}) custom-call(s32[2]{0:T(128)S(1)} %pad_add_fusion.place_ref, bf16[32,3584]{1,0:T(8,128)(2,1)S(1)} %copy-done.7, bf16[32,3584]{1,0:T(8,128)(2,1)S(1)} %copy-done.11, bf16[32,3584]{1,0:T(8,128)(2,1)S(1)} %collective-permute-done.16.refs_2_, ...), custom_call_target="tpu_custom_call" | custom-call | flops 4462739456 | bytes 24903680 | tf_op jit(solution)/shard_map/pallas_call | solution.py:145
  89.1 11.1 %shard_map.88 = (f32[256,2432]{1,0:T(8,128)S(1)}, f32[8,256]{1,0:T(8,128)S(1)}) custom-call(s32[2]{0:T(128)S(1)} %pad_add_fusion.place_ref, bf16[32,3584]{1,0:T(8,128)(2,1)S(1)} %add_convert_fusion.4.refs_0_, bf16[32,3584]{1,0:T(8,128)(2,1)S(1)} %collective-permute-done.7.refs_1_, bf16[32,3584]{1,0:T(8,128)(2,1)} %collective-permute-done.8.refs_2_, ...), custom_call_target="tpu_custom_call" | custom-call | flops 4462739456 | bytes 24903680 | tf_op jit(solution)/shard_map/pallas_call | solution.py:162
  100.1 1.4 copy-done.4
  102.1 2.0 %collective-permute-start.22 = (f32[8,256]{1,0:T(8,128)S(1)}, f32[8,256]{1,0:T(8,128)S(1)}, u32[]{:S(2)}, u32[]{:S(2)}) collective-permute-start(f32[8,256]{1,0:T(8,128)S(1)} %get-tuple-element.50.mine_ref.refs_2_), channel_id=1, source_target_pairs={{0,1},{1,0},{2,3},{3,2},{4,5},{5,4},{6,7},{7,6},{8,9},{9,8},{10,11... | collective-permute-start | bytes 24584 | tf_op jit(solution)/shard_map/ppermute | solution.py:289
  104.1 1.7 %collective-permute-done.22.theirs_ref = f32[8,256]{1,0:T(8,128)S(1)} collective-permute-done((f32[8,256]{1,0:T(8,128)S(1)}, f32[8,256]{1,0:T(8,128)S(1)}, u32[]{:S(2)}, u32[]{:S(2)}) %collective-permute-start.22) | collective-permute-done | bytes 8224 | tf_op jit(solution)/shard_map/ppermute | solution.py:289
  105.8 0.6 copy-done.24
  106.3 1.4 shard_map.89.mine_ref
  107.8 3.9 %collective-permute-done.23.theirs_ref = f32[8,256]{1,0:T(8,128)S(1)} collective-permute-done((f32[8,256]{1,0:T(8,128)}, f32[8,256]{1,0:T(8,128)S(1)}, u32[]{:S(2)}, u32[]{:S(2)}) %collective-permute-start.23) | collective-permute-done | bytes 8224 | tf_op jit(solution)/shard_map/ppermute | solution.py:289
  112.2 1.4 shard_map.90.refs_0_
  113.6 4.8 %collective-permute-done.24.refs_1_ = f32[8,256]{1,0:T(8,128)S(1)} collective-permute-done((f32[8,256]{1,0:T(8,128)}, f32[8,256]{1,0:T(8,128)S(1)}, u32[]{:S(2)}, u32[]{:S(2)}) %collective-permute-start.24) | collective-permute-done | bytes 8224 | tf_op jit(solution)/shard_map/ppermute | solution.py:289
  118.4 3.5 %copy-done.2 = bf16[1792,2432]{1,0:T(8,128)(2,1)S(1)} copy-done((bf16[1792,2432]{1,0:T(8,128)(2,1)S(1)}, bf16[1792,2432]{1,0:T(8,128)(2,1)}, u32[]{:S(2)}) %copy-start.2) | copy-done | bytes 8716312
  121.9 1.7 %copy-done.5 = f32[256,2432]{1,0:T(8,128)S(1)} copy-done((f32[256,2432]{1,0:T(8,128)S(1)}, f32[256,2432]{1,0:T(8,128)}, u32[]{:S(2)}) %copy-start.5) | copy-done | bytes 2490392
  123.6 0.7 copy-done.19
  124.3 0.7 copy-done.20
  125.0 0.7 copy-done.22
  125.6 10.6 %shard_map.91 = (f32[8,256]{1,0:T(8,128)S(1)}, f32[32,3584]{1,0:T(8,128)S(1)}, f32[32,3584]{1,0:T(8,128)S(1)}, f32[32,3584]{1,0:T(8,128)S(1)}, f32[32,3584]{1,0:...) custom-call(s32[2]{0:T(128)S(1)} %copy-done.22, ...), custom_call_target="tpu_custom_call" | custom-call | flops 4462739456 | bytes 24903680 | tf_op jit(solution)/shard_map/pallas_call | solution.py:265
  136.2 2.1 %collective-permute-start.27 = (f16[32,3584]{1,0:T(8,128)(2,1)S(1)}, f16[32,3584]{1,0:T(8,128)(2,1)S(1)}, u32[]{:S(2)}, u32[]{:S(2)}) collective-permute-start(f16[32,3584]{1,0:T(8,128)(2,1)S(1)} %convert_element_type.113), channel_id=1, source_target_pairs={{0,1},{1,0},{2,3},{3,2},{4,5},{5,4},{6,7},{7,6},{8,9},{9,8},{10,11... | collective-permute-start | bytes 688136 | tf_op jit(solution)/shard_map/ppermute | solution.py:289
  138.5 3.8 %collective-permute-done.27 = f16[32,3584]{1,0:T(8,128)(2,1)S(1)} collective-permute-done((f16[32,3584]{1,0:T(8,128)(2,1)S(1)}, f16[32,3584]{1,0:T(8,128)(2,1)S(1)}, u32[]{:S(2)}, u32[]{:S(2)}) %collective-permute-start.27) | collective-permute-done | bytes 229408 | tf_op jit(solution)/shard_map/ppermute | solution.py:289
  142.3 2.0 %collective-permute-start.31 = (f16[32,3584]{1,0:T(8,128)(2,1)S(1)}, f16[32,3584]{1,0:T(8,128)(2,1)S(1)}, u32[]{:S(2)}, u32[]{:S(2)}) collective-permute-start(f16[32,3584]{1,0:T(8,128)(2,1)S(1)} %convert_element_type.121), channel_id=1, source_target_pairs={{0,1},{1,0},{2,3},{3,2},{4,5},{5,4},{6,7},{7,6},{8,9},{9,8},{10,11... | collective-permute-start | bytes 688136 | tf_op jit(solution)/shard_map/ppermute | solution.py:289
  144.8 2.0 %collective-permute-start.29 = (f16[32,3584]{1,0:T(8,128)(2,1)S(1)}, f16[32,3584]{1,0:T(8,128)(2,1)S(1)}, u32[]{:S(2)}, u32[]{:S(2)}) collective-permute-start(f16[32,3584]{1,0:T(8,128)(2,1)S(1)} %convert_element_type.117), channel_id=1, source_target_pairs={{0,1},{1,0},{2,3},{3,2},{4,5},{5,4},{6,7},{7,6},{8,9},{9,8},{10,11... | collective-permute-start | bytes 688136 | tf_op jit(solution)/shard_map/ppermute | solution.py:289
  146.9 3.9 %collective-permute-done.29 = f16[32,3584]{1,0:T(8,128)(2,1)S(1)} collective-permute-done((f16[32,3584]{1,0:T(8,128)(2,1)S(1)}, f16[32,3584]{1,0:T(8,128)(2,1)S(1)}, u32[]{:S(2)}, u32[]{:S(2)}) %collective-permute-start.29) | collective-permute-done | bytes 229408 | tf_op jit(solution)/shard_map/ppermute | solution.py:289
  150.9 2.0 %collective-permute-done.26 = f16[32,3584]{1,0:T(8,128)(2,1)S(1)} collective-permute-done((f16[32,3584]{1,0:T(8,128)(2,1)S(1)}, f16[32,3584]{1,0:T(8,128)(2,1)S(1)}, u32[]{:S(2)}, u32[]{:S(2)}) %collective-permute-start.26) | collective-permute-done | bytes 229408 | tf_op jit(solution)/shard_map/ppermute | solution.py:289
  153.7 3.2 %collective-permute-done.30 = f16[32,3584]{1,0:T(8,128)(2,1)S(1)} collective-permute-done((f16[32,3584]{1,0:T(8,128)(2,1)S(1)}, f16[32,3584]{1,0:T(8,128)(2,1)S(1)}, u32[]{:S(2)}, u32[]{:S(2)}) %collective-permute-start.30) | collective-permute-done | bytes 229408 | tf_op jit(solution)/shard_map/ppermute | solution.py:289
  156.9 5.0 %collective-permute-done.28 = f16[32,3584]{1,0:T(8,128)(2,1)S(1)} collective-permute-done((f16[32,3584]{1,0:T(8,128)(2,1)S(1)}, f16[32,3584]{1,0:T(8,128)(2,1)S(1)}, u32[]{:S(2)}, u32[]{:S(2)}) %collective-permute-start.28) | collective-permute-done | bytes 229408 | tf_op jit(solution)/shard_map/ppermute | solution.py:289
  161.9 0.8 add_convert_fusion
  (85 shorter events, 5.4 us)
Async XLA Ops:
  0.6 13.1 %copy-start.7 = (bf16[32,3584]{1,0:T(8,128)(2,1)S(1)}, bf16[32,3584]{1,0:T(8,128)(2,1)}, u32[]{:S(2)}) copy-start(bf16[32,3584]{1,0:T(8,128)(2,1)} %refs_0_) | copy-start | bytes 688132
  0.6 69.1 %collective-permute-start.14 = (bf16[1792,2432]{1,0:T(8,128)(2,1)}, bf16[1792,2432]{1,0:T(8,128)(2,1)}, u32[]{:S(2)}, u32[]{:S(2)}) collective-permute-start(bf16[1792,2432]{1,0:T(8,128)(2,1)} %refs_6_.1), channel_id=1, source_target_pairs={{0,8},{8,0},{1,9},{9,1},{2,10},{10,2},{3,11},{11,3},{4,12},{12,4},... | collective-permute-start | bytes 26148872 | tf_op jit(solution)/shard_map/ppermute | solution.py:337
  1.2 35.5 %copy-start.25 = (s32[256]{0:T(256)S(1)}, s32[256]{0:T(256)}, u32[]{:S(2)}) copy-start(s32[256]{0:T(256)} %param.13) | copy-start | bytes 3076
  2.7 3.1 %copy-start.3 = (bf16[1024,3584]{1,0:T(8,128)(2,1)S(1)}, bf16[1024,3584]{1,0:T(8,128)(2,1)}, u32[]{:S(2)}) copy-start(bf16[1024,3584]{1,0:T(8,128)(2,1)} %weight_ref.1) | copy-start | bytes 22020100
  5.8 1.2 copy-start.6
  11.1 8.9 %collective-permute-start = (f16[32,3584]{1,0:T(8,128)(2,1)S(1)}, f16[32,3584]{1,0:T(8,128)(2,1)S(1)}, u32[]{:S(2)}, u32[]{:S(2)}) collective-permute-start(f16[32,3584]{1,0:T(8,128)(2,1)S(1)} %convert_element_type.94), channel_id=1, source_target_pairs={{0,1},{1,0},{2,3},{3,2},{4,5},{5,4},{6,7},{7,6},{8,9},{9,8},{10,11... | collective-permute-start | bytes 688136 | tf_op jit(solution)/shard_map/ppermute | solution.py:289
  13.8 20.3 %collective-permute-start.18 = (bf16[32,3584]{1,0:T(8,128)(2,1)S(1)}, bf16[32,3584]{1,0:T(8,128)(2,1)S(1)}, u32[]{:S(2)}, u32[]{:S(2)}) collective-permute-start(bf16[32,3584]{1,0:T(8,128)(2,1)S(1)} %copy-done.7), channel_id=1, source_target_pairs={{0,4},{1,5},{2,6},{3,7},{4,0},{5,1},{6,2},{7,3},{8,12},{9,13},{10,... | collective-permute-start | bytes 688136 | tf_op jit(solution)/shard_map/ppermute | solution.py:289
  16.4 20.4 %collective-permute-start.16 = (bf16[32,3584]{1,0:T(8,128)(2,1)S(1)}, bf16[32,3584]{1,0:T(8,128)(2,1)S(1)}, u32[]{:S(2)}, u32[]{:S(2)}) collective-permute-start(bf16[32,3584]{1,0:T(8,128)(2,1)S(1)} %copy-done.7), channel_id=1, source_target_pairs={{0,2},{1,3},{2,0},{3,1},{4,6},{5,7},{6,4},{7,5},{8,10},{9,11},{10,... | collective-permute-start | bytes 688136 | tf_op jit(solution)/shard_map/ppermute | solution.py:289
  18.0 8.6 %collective-permute-start.2 = (f16[32,3584]{1,0:T(8,128)(2,1)S(1)}, f16[32,3584]{1,0:T(8,128)(2,1)S(1)}, u32[]{:S(2)}, u32[]{:S(2)}) collective-permute-start(f16[32,3584]{1,0:T(8,128)(2,1)S(1)} %convert_element_type.98), channel_id=1, source_target_pairs={{0,1},{1,0},{2,3},{3,2},{4,5},{5,4},{6,7},{7,6},{8,9},{9,8},{10,11... | collective-permute-start | bytes 688136 | tf_op jit(solution)/shard_map/ppermute | solution.py:289
  20.0 10.1 %collective-permute-start.4 = (f16[32,3584]{1,0:T(8,128)(2,1)S(1)}, f16[32,3584]{1,0:T(8,128)(2,1)S(1)}, u32[]{:S(2)}, u32[]{:S(2)}) collective-permute-start(f16[32,3584]{1,0:T(8,128)(2,1)S(1)} %convert_element_type.102), channel_id=1, source_target_pairs={{0,1},{1,0},{2,3},{3,2},{4,5},{5,4},{6,7},{7,6},{8,9},{9,8},{10,11... | collective-permute-start | bytes 688136 | tf_op jit(solution)/shard_map/ppermute | solution.py:289
  26.6 6.0 %collective-permute-start.1 = (f16[32,3584]{1,0:T(8,128)(2,1)S(1)}, f16[32,3584]{1,0:T(8,128)(2,1)S(1)}, u32[]{:S(2)}, u32[]{:S(2)}) collective-permute-start(f16[32,3584]{1,0:T(8,128)(2,1)S(1)} %add_convert_fusion.7), channel_id=1, source_target_pairs={{0,2},{1,3},{2,0},{3,1},{4,6},{5,7},{6,4},{7,5},{8,10},{9,11},{10,... | collective-permute-start | bytes 688136 | tf_op jit(solution)/shard_map/ppermute | solution.py:289
  30.1 7.2 %collective-permute-start.6 = (f16[32,3584]{1,0:T(8,128)(2,1)S(1)}, f16[32,3584]{1,0:T(8,128)(2,1)S(1)}, u32[]{:S(2)}, u32[]{:S(2)}) collective-permute-start(f16[32,3584]{1,0:T(8,128)(2,1)S(1)} %convert_element_type.106), channel_id=1, source_target_pairs={{0,1},{1,0},{2,3},{3,2},{4,5},{5,4},{6,7},{7,6},{8,9},{9,8},{10,11... | collective-permute-start | bytes 688136 | tf_op jit(solution)/shard_map/ppermute | solution.py:289
  32.6 14.5 %collective-permute-start.5 = (f16[32,3584]{1,0:T(8,128)(2,1)S(1)}, f16[32,3584]{1,0:T(8,128)(2,1)S(1)}, u32[]{:S(2)}, u32[]{:S(2)}) collective-permute-start(f16[32,3584]{1,0:T(8,128)(2,1)S(1)} %add_convert_fusion.5), channel_id=1, source_target_pairs={{0,2},{1,3},{2,0},{3,1},{4,6},{5,7},{6,4},{7,5},{8,10},{9,11},{10,... | collective-permute-start | bytes 688136 | tf_op jit(solution)/shard_map/ppermute | solution.py:289
  34.0 14.7 %collective-permute-start.3 = (f16[32,3584]{1,0:T(8,128)(2,1)S(1)}, f16[32,3584]{1,0:T(8,128)(2,1)S(1)}, u32[]{:S(2)}, u32[]{:S(2)}) collective-permute-start(f16[32,3584]{1,0:T(8,128)(2,1)S(1)} %add_convert_fusion.6), channel_id=1, source_target_pairs={{0,4},{1,5},{2,6},{3,7},{4,0},{5,1},{6,2},{7,3},{8,12},{9,13},{10,... | collective-permute-start | bytes 688136 | tf_op jit(solution)/shard_map/ppermute | solution.py:289
  36.8 16.6 %collective-permute-start.20 = (bf16[32,3584]{1,0:T(8,128)(2,1)S(1)}, bf16[32,3584]{1,0:T(8,128)(2,1)S(1)}, u32[]{:S(2)}, u32[]{:S(2)}) collective-permute-start(bf16[32,3584]{1,0:T(8,128)(2,1)S(1)} %collective-permute-done.18.refs_4_), channel_id=1, source_target_pairs={{0,2},{1,3},{2,0},{3,1},{4,6},{5,7},{6,4},{7,5},{8,10},{9,11},{10,... | collective-permute-start | bytes 688136 | tf_op jit(solution)/shard_map/ppermute | solution.py:289
  37.3 11.6 %collective-permute-start.15 = (bf16[32,3584]{1,0:T(8,128)(2,1)S(1)}, bf16[32,3584]{1,0:T(8,128)(2,1)S(1)}, u32[]{:S(2)}, u32[]{:S(2)}) collective-permute-start(bf16[32,3584]{1,0:T(8,128)(2,1)S(1)} %copy-done.7), channel_id=1, source_target_pairs={{0,1},{1,0},{2,3},{3,2},{4,5},{5,4},{6,7},{7,6},{8,9},{9,8},{10,11... | collective-permute-start | bytes 688136 | tf_op jit(solution)/shard_map/ppermute | solution.py:289
  47.1 8.5 %collective-permute-start.17 = (bf16[32,3584]{1,0:T(8,128)(2,1)S(1)}, bf16[32,3584]{1,0:T(8,128)(2,1)S(1)}, u32[]{:S(2)}, u32[]{:S(2)}) collective-permute-start(bf16[32,3584]{1,0:T(8,128)(2,1)S(1)} %collective-permute-done.16.refs_2_), channel_id=1, source_target_pairs={{0,1},{1,0},{2,3},{3,2},{4,5},{5,4},{6,7},{7,6},{8,9},{9,8},{10,11... | collective-permute-start | bytes 688136 | tf_op jit(solution)/shard_map/ppermute | solution.py:289
  48.8 9.7 %collective-permute-start.10 = (bf16[32,3584]{1,0:T(8,128)(2,1)S(1)}, bf16[32,3584]{1,0:T(8,128)(2,1)}, u32[]{:S(2)}, u32[]{:S(2)}) collective-permute-start(bf16[32,3584]{1,0:T(8,128)(2,1)S(1)} %add_convert_fusion.4.refs_0_), channel_id=1, source_target_pairs={{0,4},{1,5},{2,6},{3,7},{4,0},{5,1},{6,2},{7,3},{8,12},{9,13},{10,... | collective-permute-start | bytes 688136 | tf_op jit(solution)/shard_map/ppermute | solution.py:289
  49.0 0.7 copy-start.10
  49.7 10.3 %collective-permute-start.8 = (bf16[32,3584]{1,0:T(8,128)(2,1)S(1)}, bf16[32,3584]{1,0:T(8,128)(2,1)}, u32[]{:S(2)}, u32[]{:S(2)}) collective-permute-start(bf16[32,3584]{1,0:T(8,128)(2,1)S(1)} %add_convert_fusion.4.refs_0_), channel_id=1, source_target_pairs={{0,2},{1,3},{2,0},{3,1},{4,6},{5,7},{6,4},{7,5},{8,10},{9,11},{10,... | collective-permute-start | bytes 688136 | tf_op jit(solution)/shard_map/ppermute | solution.py:289
  53.4 8.5 %collective-permute-start.19 = (bf16[32,3584]{1,0:T(8,128)(2,1)S(1)}, bf16[32,3584]{1,0:T(8,128)(2,1)S(1)}, u32[]{:S(2)}, u32[]{:S(2)}) collective-permute-start(bf16[32,3584]{1,0:T(8,128)(2,1)S(1)} %collective-permute-done.18.refs_4_), channel_id=1, source_target_pairs={{0,1},{1,0},{2,3},{3,2},{4,5},{5,4},{6,7},{7,6},{8,9},{9,8},{10,11... | collective-permute-start | bytes 688136 | tf_op jit(solution)/shard_map/ppermute | solution.py:289
  55.6 0.7 copy-start.12
  56.3 10.4 %collective-permute-start.21 = (bf16[32,3584]{1,0:T(8,128)(2,1)S(1)}, bf16[32,3584]{1,0:T(8,128)(2,1)S(1)}, u32[]{:S(2)}, u32[]{:S(2)}) collective-permute-start(bf16[32,3584]{1,0:T(8,128)(2,1)S(1)} %collective-permute-done.20.refs_6_), channel_id=1, source_target_pairs={{0,1},{1,0},{2,3},{3,2},{4,5},{5,4},{6,7},{7,6},{8,9},{9,8},{10,11... | collective-permute-start | bytes 688136 | tf_op jit(solution)/shard_map/ppermute | solution.py:289
  57.9 0.7 copy-start.8
  58.6 11.2 %collective-permute-start.12 = (bf16[32,3584]{1,0:T(8,128)(2,1)}, bf16[32,3584]{1,0:T(8,128)(2,1)}, u32[]{:S(2)}, u32[]{:S(2)}) collective-permute-start(bf16[32,3584]{1,0:T(8,128)(2,1)} %collective-permute-done.10.refs_4_), channel_id=1, source_target_pairs={{0,2},{1,3},{2,0},{3,1},{4,6},{5,7},{6,4},{7,5},{8,10},{9,11},{10,... | collective-permute-start | bytes 688136 | tf_op jit(solution)/shard_map/ppermute | solution.py:289
  60.0 29.0 %collective-permute-start.7 = (bf16[32,3584]{1,0:T(8,128)(2,1)S(1)}, bf16[32,3584]{1,0:T(8,128)(2,1)S(1)}, u32[]{:S(2)}, u32[]{:S(2)}) collective-permute-start(bf16[32,3584]{1,0:T(8,128)(2,1)S(1)} %add_convert_fusion.4.refs_0_), channel_id=1, source_target_pairs={{0,1},{1,0},{2,3},{3,2},{4,5},{5,4},{6,7},{7,6},{8,9},{9,8},{10,11... | collective-permute-start | bytes 688136 | tf_op jit(solution)/shard_map/ppermute | solution.py:289
  61.9 0.7 copy-start.14
  62.6 26.5 %collective-permute-start.11 = (bf16[32,3584]{1,0:T(8,128)(2,1)}, bf16[32,3584]{1,0:T(8,128)(2,1)S(1)}, u32[]{:S(2)}, u32[]{:S(2)}) collective-permute-start(bf16[32,3584]{1,0:T(8,128)(2,1)} %collective-permute-done.10.refs_4_), channel_id=1, source_target_pairs={{0,1},{1,0},{2,3},{3,2},{4,5},{5,4},{6,7},{7,6},{8,9},{9,8},{10,11... | collective-permute-start | bytes 688136 | tf_op jit(solution)/shard_map/ppermute | solution.py:289
  66.7 0.7 copy-start.16
  67.4 21.6 %collective-permute-start.9 = (bf16[32,3584]{1,0:T(8,128)(2,1)}, bf16[32,3584]{1,0:T(8,128)(2,1)S(1)}, u32[]{:S(2)}, u32[]{:S(2)}) collective-permute-start(bf16[32,3584]{1,0:T(8,128)(2,1)} %collective-permute-done.8.refs_2_), channel_id=1, source_target_pairs={{0,1},{1,0},{2,3},{3,2},{4,5},{5,4},{6,7},{7,6},{8,9},{9,8},{10,11... | collective-permute-start | bytes 688136 | tf_op jit(solution)/shard_map/ppermute | solution.py:289
  69.7 19.3 %collective-permute-start.13 = (bf16[32,3584]{1,0:T(8,128)(2,1)}, bf16[32,3584]{1,0:T(8,128)(2,1)S(1)}, u32[]{:S(2)}, u32[]{:S(2)}) collective-permute-start(bf16[32,3584]{1,0:T(8,128)(2,1)} %collective-permute-done.12.refs_6_), channel_id=1, source_target_pairs={{0,1},{1,0},{2,3},{3,2},{4,5},{5,4},{6,7},{7,6},{8,9},{9,8},{10,11... | collective-permute-start | bytes 688136 | tf_op jit(solution)/shard_map/ppermute | solution.py:289
  69.8 3.5 %copy-start = (bf16[1792,2432]{1,0:T(8,128)(2,1)S(1)}, bf16[1792,2432]{1,0:T(8,128)(2,1)}, u32[]{:S(2)}) copy-start(bf16[1792,2432]{1,0:T(8,128)(2,1)} %refs_6_.1) | copy-start | bytes 26148868
  73.3 0.9 copy-start.9
  74.2 0.9 copy-start.11
  75.1 0.9 copy-start.13
  76.1 0.9 copy-start.15
  77.0 0.9 copy-start.17
  77.9 11.1 %copy-start.1 = (bf16[1792,2432]{1,0:T(8,128)(2,1)S(1)}, bf16[1792,2432]{1,0:T(8,128)(2,1)}, u32[]{:S(2)}) copy-start(bf16[1792,2432]{1,0:T(8,128)(2,1)} %refs_6_.1) | copy-start | bytes 26148868
  100.1 1.4 copy-start.4
  101.6 0.5 copy-start.21
  102.1 3.7 %copy-start.18 = (f32[8,256]{1,0:T(8,128)}, f32[8,256]{1,0:T(8,128)S(1)}, u32[]{:S(2)}) copy-start(f32[8,256]{1,0:T(8,128)S(1)} %get-tuple-element.50.mine_ref.refs_2_) | copy-start | bytes 24580
  102.1 3.7 %collective-permute-start.22 = (f32[8,256]{1,0:T(8,128)S(1)}, f32[8,256]{1,0:T(8,128)S(1)}, u32[]{:S(2)}, u32[]{:S(2)}) collective-permute-start(f32[8,256]{1,0:T(8,128)S(1)} %get-tuple-element.50.mine_ref.refs_2_), channel_id=1, source_target_pairs={{0,1},{1,0},{2,3},{3,2},{4,5},{5,4},{6,7},{7,6},{8,9},{9,8},{10,11... | collective-permute-start | bytes 24584 | tf_op jit(solution)/shard_map/ppermute | solution.py:289
  105.7 0.6 copy-start.24
  107.8 3.9 %collective-permute-start.23 = (f32[8,256]{1,0:T(8,128)}, f32[8,256]{1,0:T(8,128)S(1)}, u32[]{:S(2)}, u32[]{:S(2)}) collective-permute-start(f32[8,256]{1,0:T(8,128)} %shard_map.89.mine_ref), channel_id=1, source_target_pairs={{0,2},{1,3},{2,0},{3,1},{4,6},{5,7},{6,4},{7,5},{8,10},{9,11},{10,... | collective-permute-start | bytes 24584 | tf_op jit(solution)/shard_map/ppermute | solution.py:289
  111.6 0.6 copy-start.23
  113.6 4.8 %collective-permute-start.24 = (f32[8,256]{1,0:T(8,128)}, f32[8,256]{1,0:T(8,128)S(1)}, u32[]{:S(2)}, u32[]{:S(2)}) collective-permute-start(f32[8,256]{1,0:T(8,128)} %shard_map.90.refs_0_), channel_id=1, source_target_pairs={{0,4},{1,5},{2,6},{3,7},{4,0},{5,1},{6,2},{7,3},{8,12},{9,13},{10,... | collective-permute-start | bytes 24584 | tf_op jit(solution)/shard_map/ppermute | solution.py:289
  118.4 3.5 %copy-start.2 = (bf16[1792,2432]{1,0:T(8,128)(2,1)S(1)}, bf16[1792,2432]{1,0:T(8,128)(2,1)}, u32[]{:S(2)}) copy-start(bf16[1792,2432]{1,0:T(8,128)(2,1)} %refs_6_.1) | copy-start | bytes 26148868
  121.9 1.7 %copy-start.5 = (f32[256,2432]{1,0:T(8,128)S(1)}, f32[256,2432]{1,0:T(8,128)}, u32[]{:S(2)}) copy-start(f32[256,2432]{1,0:T(8,128)} %copy-done.4) | copy-start | bytes 7471108
  123.6 0.7 copy-start.19
  124.3 0.7 copy-start.20
  124.9 0.7 copy-start.22
  136.2 6.1 %collective-permute-start.27 = (f16[32,3584]{1,0:T(8,128)(2,1)S(1)}, f16[32,3584]{1,0:T(8,128)(2,1)S(1)}, u32[]{:S(2)}, u32[]{:S(2)}) collective-permute-start(f16[32,3584]{1,0:T(8,128)(2,1)S(1)} %convert_element_type.113), channel_id=1, source_target_pairs={{0,1},{1,0},{2,3},{3,2},{4,5},{5,4},{6,7},{7,6},{8,9},{9,8},{10,11... | collective-permute-start | bytes 688136 | tf_op jit(solution)/shard_map/ppermute | solution.py:289
  138.3 6.4 %collective-permute-start.25 = (f16[32,3584]{1,0:T(8,128)(2,1)S(1)}, f16[32,3584]{1,0:T(8,128)(2,1)S(1)}, u32[]{:S(2)}, u32[]{:S(2)}) collective-permute-start(f16[32,3584]{1,0:T(8,128)(2,1)S(1)} %convert_element_type.109), channel_id=1, source_target_pairs={{0,1},{1,0},{2,3},{3,2},{4,5},{5,4},{6,7},{7,6},{8,9},{9,8},{10,11... | collective-permute-start | bytes 688136 | tf_op jit(solution)/shard_map/ppermute | solution.py:289
  142.3 11.4 %collective-permute-start.31 = (f16[32,3584]{1,0:T(8,128)(2,1)S(1)}, f16[32,3584]{1,0:T(8,128)(2,1)S(1)}, u32[]{:S(2)}, u32[]{:S(2)}) collective-permute-start(f16[32,3584]{1,0:T(8,128)(2,1)S(1)} %convert_element_type.121), channel_id=1, source_target_pairs={{0,1},{1,0},{2,3},{3,2},{4,5},{5,4},{6,7},{7,6},{8,9},{9,8},{10,11... | collective-permute-start | bytes 688136 | tf_op jit(solution)/shard_map/ppermute | solution.py:289
  144.8 6.0 %collective-permute-start.29 = (f16[32,3584]{1,0:T(8,128)(2,1)S(1)}, f16[32,3584]{1,0:T(8,128)(2,1)S(1)}, u32[]{:S(2)}, u32[]{:S(2)}) collective-permute-start(f16[32,3584]{1,0:T(8,128)(2,1)S(1)} %convert_element_type.117), channel_id=1, source_target_pairs={{0,1},{1,0},{2,3},{3,2},{4,5},{5,4},{6,7},{7,6},{8,9},{9,8},{10,11... | collective-permute-start | bytes 688136 | tf_op jit(solution)/shard_map/ppermute | solution.py:289
  146.8 6.1 %collective-permute-start.26 = (f16[32,3584]{1,0:T(8,128)(2,1)S(1)}, f16[32,3584]{1,0:T(8,128)(2,1)S(1)}, u32[]{:S(2)}, u32[]{:S(2)}) collective-permute-start(f16[32,3584]{1,0:T(8,128)(2,1)S(1)} %add_convert_fusion.3), channel_id=1, source_target_pairs={{0,2},{1,3},{2,0},{3,1},{4,6},{5,7},{6,4},{7,5},{8,10},{9,11},{10,... | collective-permute-start | bytes 688136 | tf_op jit(solution)/shard_map/ppermute | solution.py:289
  150.8 6.1 %collective-permute-start.30 = (f16[32,3584]{1,0:T(8,128)(2,1)S(1)}, f16[32,3584]{1,0:T(8,128)(2,1)S(1)}, u32[]{:S(2)}, u32[]{:S(2)}) collective-permute-start(f16[32,3584]{1,0:T(8,128)(2,1)S(1)} %add_convert_fusion.1), channel_id=1, source_target_pairs={{0,2},{1,3},{2,0},{3,1},{4,6},{5,7},{6,4},{7,5},{8,10},{9,11},{10,... | collective-permute-start | bytes 688136 | tf_op jit(solution)/shard_map/ppermute | solution.py:289
  153.0 8.9 %collective-permute-start.28 = (f16[32,3584]{1,0:T(8,128)(2,1)S(1)}, f16[32,3584]{1,0:T(8,128)(2,1)S(1)}, u32[]{:S(2)}, u32[]{:S(2)}) collective-permute-start(f16[32,3584]{1,0:T(8,128)(2,1)S(1)} %add_convert_fusion.2), channel_id=1, source_target_pairs={{0,4},{1,5},{2,6},{3,7},{4,0},{5,1},{6,2},{7,3},{8,12},{9,13},{10,... | collective-permute-start | bytes 688136 | tf_op jit(solution)/shard_map/ppermute | solution.py:289

commit v2 on v1

v2 whole, which is shorter than its diff:
```python
import functools

import jax
import jax.numpy as jnp
from jax import lax
from jax.experimental import pallas as pl
from jax.experimental.pallas import tpu as pltpu
from jax.sharding import PartitionSpec as P

loss_scale = 64.0
wire = jnp.float16
lanes = 128
vmem_bytes = 46 * 1024 * 1024
project_bytes = 54 * 1024 * 1024
chunk_columns = 512

in_vmem = pl.BlockSpec(memory_space=pltpu.VMEM)
in_smem = pl.BlockSpec(memory_space=pltpu.SMEM)
in_place = pl.BlockSpec(memory_space=pl.ANY)


def cuts(total, step):
    return [(start, min(step, total - start)) for start in range(0, total, step)]


def project_kernel(count, step, member_ref, teacher_ref, weight_ref, *rest):
    outs, (teacher, weight, sems) = rest[:count], rest[count:]
    blk = outs[0].shape[0]
    parts = cuts(weight.shape[1], step)
    first = pltpu.make_async_copy(teacher_ref, teacher, sems.at[len(parts)])
    first.start()
    copies = []
    for index, (start, size) in enumerate(parts):
        at = pl.ds(start, size)
        copies.append(pltpu.make_async_copy(weight_ref.at[:, at], weight.at[:, at], sems.at[index]))
        copies[-1].start()
    member = member_ref[...]
    sizes = jnp.sum(member.astype(jnp.float32), axis=1, keepdims=True)
    first.wait()
    summed = jnp.dot(member, teacher[...], preferred_element_type=jnp.float32)
    aligned = (summed / sizes).astype(jnp.bfloat16)
    for copy, (start, size) in zip(copies, parts):
        copy.wait()
        product = jnp.dot(aligned, weight[:, start : start + size], preferred_element_type=jnp.float32)
        for piece, out in enumerate(outs):
            out[:, start : start + size] = product[piece * blk : (piece + 1) * blk]


def project(member, teacher_rows, proj_weight, count, step):
    slab_rows, (depth, width) = member.shape[0], proj_weight.shape
    blk = slab_rows // count
    return pl.pallas_call(
        functools.partial(project_kernel, count, step),
        in_specs=[in_vmem, in_place, in_place],
        out_specs=[in_vmem] * count,
        out_shape=[jax.ShapeDtypeStruct((blk, width), jnp.float32)] * count,
        scratch_shapes=[
            pltpu.VMEM(teacher_rows.shape, jnp.bfloat16),
            pltpu.VMEM(proj_weight.shape, jnp.bfloat16),
            pltpu.SemaphoreType.DMA((len(cuts(width, step)) + 1,)),
        ],
        compiler_params=pltpu.CompilerParams(vmem_limit_bytes=project_bytes),
        cost_estimate=pl.CostEstimate(
            flops=2 * slab_rows * depth * (width + teacher_rows.shape[0]),
            bytes_accessed=2 * depth * (width + teacher_rows.shape[0]) + 4 * slab_rows * width,
            transcendentals=0,
        ),
    )(member, teacher_rows, proj_weight)


class Fetch:
    def __init__(self, sems):
        self.sems, self.used = sems, 0

    def start(self, source, target):
        copy = pltpu.make_async_copy(source, target, self.sems.at[self.used])
        copy.start()
        self.used += 1
        return copy


def multiply(pieces, heads, rows, head, logit_ref, highest, fetch, step):
    depth, total = heads[0].shape
    blk = pieces[0].shape[0]
    waits = [fetch.start(piece, rows.at[pl.ds(i * blk, blk)]) for i, piece in enumerate(pieces)]
    first = fetch.used
    for start, size in cuts(total, step):
        for half, source in enumerate(heads):
            at = pl.ds(start, size)
            fetch.start(source.at[:, at], head.at[pl.ds(half * depth, depth), at])
    highest[...] = jnp.full(highest.shape, -jnp.inf, jnp.float32)
    for wait in waits:
        wait.wait()

    def one(index, start, size):
        at = pl.ds(start, size)
        for half, source in enumerate(heads):
            sem = fetch.sems.at[first + 2 * index + half]
            pltpu.make_async_copy(source.at[:, at], head.at[pl.ds(half * depth, depth), at], sem).wait()
        part = jnp.dot(rows[...], head[:, at], preferred_element_type=jnp.float32)
        logit_ref[:, at] = part
        top = part[:, :lanes]
        for lane in range(lanes, size, lanes):
            top = jnp.maximum(top, part[:, lane : lane + lanes])
        highest[...] = jnp.maximum(highest[...], top)

    def body(index, carry):
        one(index, pl.multiple_of(index * step, step), step)
        return carry

    full = total // step
    lax.fori_loop(0, full, body, 0)
    if total % step:
        one(full, full * step, total % step)


def as_columns(first, second, third):
    lane = lax.broadcasted_iota(jnp.int32, (first.shape[0], lanes), 1)
    return jnp.where(lane == 0, first, jnp.where(lane == 1, second, jnp.where(lane == 2, third, 0.0)))


def student_kernel(count, step, chunk, *refs):
    pieces, heads = refs[:count], refs[count : count + 2]
    column_ref, logit_out, scaled_out, stats_ref = refs[count + 2 : count + 6]
    held, head, logit_ref, scaled_ref, highest, table, sems = refs[count + 6 :]
    fetch = Fetch(sems)
    multiply(pieces, heads, held, head, logit_ref, highest, fetch, step)
    first = fetch.start(logit_ref, logit_out)

    def one(part, carry):
        rows = pl.ds(pl.multiple_of(part * chunk, chunk), chunk)
        logit = logit_ref[rows, :]
        top = jnp.max(highest[rows, :], axis=1, keepdims=True)
        scaled = jnp.exp(logit - top)
        hit = lax.broadcasted_iota(jnp.int32, logit.shape, 1) == column_ref[rows, :]
        picked = jnp.sum(jnp.where(hit, logit, 0.0), axis=1, keepdims=True)
        scaled_ref[rows, :] = scaled
        table[rows, :] = as_columns(top, jnp.sum(scaled, axis=1, keepdims=True), picked)
        return carry

    lax.fori_loop(0, logit_ref.shape[0] // chunk, one, 0)
    second = fetch.start(scaled_ref, scaled_out)
    stats_ref[...] = table[...].T[0:8]
    first.wait()
    second.wait()


def teacher_kernel(count, step, chunk, *refs):
    pieces, heads = refs[:count], refs[count : count + 2]
    stud_logit, stud_ref, scaled_ref, stats_ref = refs[count + 2 : count + 6]
    held, head, stud_logit_ref, highest, table, sems = refs[count + 6 :]
    fetch = Fetch(sems)
    multiply(pieces, heads, held, head, scaled_ref, highest, fetch, step)
    copy = fetch.start(stud_logit, stud_logit_ref)
    copy.wait()

    def one(part, carry):
        rows = pl.ds(pl.multiple_of(part * chunk, chunk), chunk)
        logit = scaled_ref[rows, :]
        top = jnp.max(highest[rows, :], axis=1, keepdims=True)
        scaled = jnp.exp(logit - top)
        gap = jnp.sum(scaled * (logit - stud_logit_ref[rows, :]), axis=1, keepdims=True)
        scaled_ref[rows, :] = scaled
        table[rows, :] = as_columns(top, jnp.sum(scaled, axis=1, keepdims=True), gap)
        return carry

    lax.fori_loop(0, scaled_ref.shape[0] // chunk, one, 0)
    teach = table[...].T[0:8]
    row = lax.broadcasted_iota(jnp.int32, teach.shape, 0)
    stats_ref[...] = jnp.where(row < 4, teach, pltpu.roll(stud_ref[...], 4, 0))


def head_cost(rows, heads):
    depth, vocab_dev = 2 * heads[0].shape[0], heads[0].shape[1]
    return pl.CostEstimate(
        flops=2 * rows * depth * vocab_dev,
        bytes_accessed=2 * depth * vocab_dev + 12 * rows * vocab_dev,
        transcendentals=rows * vocab_dev,
    )


def logit_scratch(pieces, heads, wide, extra):
    rows, (depth, vocab_dev) = wide[0], heads[0].shape
    return (
        [pltpu.VMEM((rows, 2 * depth), jnp.bfloat16), pltpu.VMEM((2 * depth, vocab_dev), jnp.bfloat16)]
        + [pltpu.VMEM(wide, jnp.float32)] * extra
        + [pltpu.VMEM((rows, lanes), jnp.float32)] * 2
        + [pltpu.SemaphoreType.DMA((len(pieces) + 2 * len(cuts(vocab_dev, chunk_columns)) + 2,))]
    )


def student_logits(pieces, heads, column, chunk):
    rows, vocab_dev = column.shape[0], heads[0].shape[1]
    wide = (rows, vocab_dev)
    return pl.pallas_call(
        functools.partial(student_kernel, len(pieces), chunk_columns, chunk),
        in_specs=[in_place] * (len(pieces) + 2) + [in_vmem],
        out_specs=[in_place, in_place, in_vmem],
        out_shape=[
            jax.ShapeDtypeStruct(wide, jnp.float32),
            jax.ShapeDtypeStruct(wide, jnp.float32),
            jax.ShapeDtypeStruct((8, rows), jnp.float32),
        ],
        scratch_shapes=logit_scratch(pieces, heads, wide, 2),
        compiler_params=pltpu.CompilerParams(vmem_limit_bytes=vmem_bytes),
        cost_estimate=head_cost(rows, heads),
    )(*pieces, *heads, column)


def teacher_logits(pieces, heads, logit_stud, stats_stud, chunk):
    wide = logit_stud.shape
    return pl.pallas_call(
        functools.partial(teacher_kernel, len(pieces), chunk_columns, chunk),
        in_specs=[in_place] * (len(pieces) + 3) + [in_vmem],
        out_specs=[in_vmem] * 2,
        out_shape=[
            jax.ShapeDtypeStruct(wide, jnp.float32),
            jax.ShapeDtypeStruct((8, wide[0]), jnp.float32),
        ],
        scratch_shapes=logit_scratch(pieces, heads, wide, 1),
        compiler_params=pltpu.CompilerParams(vmem_limit_bytes=vmem_bytes),
        cost_estimate=head_cost(wide[0], heads),
    )(*pieces, *heads, logit_stud, stats_stud)


def swapped(values, distance):
    total = values.shape[1]
    lane = lax.broadcasted_iota(jnp.int32, values.shape, 1)
    return jnp.where(
        (lane & distance) != 0, pltpu.roll(values, distance, 1), pltpu.roll(values, total - distance, 1)
    )


def gradient_kernel(bits, step, fine, chunk, place_ref, *refs):
    count = 1 << bits
    tables, refs = refs[:count], refs[count:]
    teach, stud, column_ref, *heads, loss_ref = refs[:6]
    outs = refs[6 : count + 6]
    entries, teach_ref, stud_ref, head, upstream, factors, sems = refs[count + 6 :]
    rows = upstream.shape[0]
    blk = rows // count
    depth = heads[0].shape[0]
    me = place_ref[0]
    fetch = Fetch(sems)
    waits = [fetch.start(teach, teach_ref), fetch.start(stud, stud_ref)]
    first = fetch.used
    for half, source in enumerate(heads):
        for start, size in cuts(depth, fine):
            fetch.start(source.at[pl.ds(start, size)], head.at[pl.ds(half * depth + start, size)])
    for mask in range(count):
        values = tables[mask][...]
        for bit in range(bits):
            if mask >> bit & 1:
                values = swapped(values, blk << bit)
        entries[me ^ mask] = values
    every = entries[...]
    top_teach = jnp.max(every[:, 0:1], axis=0)
    top_stud = jnp.max(every[:, 4:5], axis=0)
    weight = jnp.exp(every[:, 0:1] - top_teach)
    total_teach = jnp.sum(weight * every[:, 1:2], axis=0)
    total_stud = jnp.sum(jnp.exp(every[:, 4:5] - top_stud) * every[:, 5:6], axis=0)
    lse_teach = top_teach + jnp.log(total_teach)
    lse_stud = top_stud + jnp.log(total_stud)
    gap = jnp.sum(weight * every[:, 2:3], axis=0) / total_teach
    loss = gap - lse_teach + 2.0 * lse_stud - jnp.sum(every[:, 6:7], axis=0)
    loss = jnp.broadcast_to(loss, loss_ref.shape)
    for bit in range(bits):
        loss = jnp.where(((me >> bit) & 1) == 1, swapped(loss, blk << bit), loss)
    loss_ref[...] = loss
    own = tables[0][...]
    scale_teach = -loss_scale * jnp.exp(own[0:1] - lse_teach)
    scale_stud = 2.0 * loss_scale * jnp.exp(own[4:5] - lse_stud)
    line = lax.broadcasted_iota(jnp.int32, (lanes, rows), 0)
    factors[...] = jnp.where(line == 0, scale_teach, scale_stud).T
    for wait in waits:
        wait.wait()

    def one(part, carry):
        at = pl.ds(pl.multiple_of(part * chunk, chunk), chunk)
        hit = lax.broadcasted_iota(jnp.int32, (chunk, teach_ref.shape[1]), 1) == column_ref[at, :]
        both = teach_ref[at, :] * factors[at, 0:1] + stud_ref[at, :] * factors[at, 1:2]
        upstream[at, :] = jnp.where(hit, both - loss_scale, both).astype(jnp.bfloat16)
        return carry

    lax.fori_loop(0, rows // chunk, one, 0)

    def two(index, carry):
        start = pl.multiple_of(index * step, step)
        for part in range(step // fine):
            at = pl.ds(start + part * fine, fine)
            sem = sems.at[first + index * (step // fine) + part]
            pltpu.make_async_copy(head.at[at], head.at[at], sem).wait()
        at = pl.ds(start, step)
        product = lax.dot_general(
            upstream[...], head[at, :], (((1,), (1,)), ((), ())), preferred_element_type=jnp.float32
        )
        for piece, out in enumerate(outs):
            out[:, at] = product[piece * blk : (piece + 1) * blk]
        return carry

    lax.fori_loop(0, 2 * depth // step, two, 0)


def gradient(place, tables, scaled_teach, scaled_stud, column, heads, bits, chunk):
    rows, vocab_dev = scaled_teach.shape
    count = 1 << bits
    depth = heads[0].shape[0]
    fine = 256 if depth % 256 == 0 else depth
    step = 512 if depth % 256 == 0 else depth
    return pl.pallas_call(
        functools.partial(gradient_kernel, bits, step, fine, chunk),
        in_specs=[in_smem] + [in_vmem] * count + [in_place] * 2 + [in_vmem] + [in_place] * 2,
        out_specs=[in_vmem] * (count + 1),
        out_shape=[jax.ShapeDtypeStruct((8, rows), jnp.float32)]
        + [jax.ShapeDtypeStruct((rows // count, 2 * depth), jnp.float32)] * count,
        scratch_shapes=[
            pltpu.VMEM((count, 8, rows), jnp.float32),
            pltpu.VMEM((rows, vocab_dev), jnp.float32),
            pltpu.VMEM((rows, vocab_dev), jnp.float32),
            pltpu.VMEM((2 * depth, vocab_dev), jnp.bfloat16),
            pltpu.VMEM((rows, vocab_dev), jnp.bfloat16),
            pltpu.VMEM((rows, lanes), jnp.float32),
            pltpu.SemaphoreType.DMA((2 + 2 * len(cuts(depth, fine)),)),
        ],
        compiler_params=pltpu.CompilerParams(vmem_limit_bytes=vmem_bytes),
        cost_estimate=head_cost(rows, heads),
    )(place, *tables, scaled_teach, scaled_stud, column, *heads)


def tie(block, *others):
    return lax.optimization_barrier((block, *others))[0]


def make_body(vocab_size):
    bits = vocab_size.bit_length() - 1
    assert vocab_size == 1 << bits

    def swap(block, bit):
        return lax.ppermute(block, "vocab", [(at, at ^ (1 << bit)) for at in range(vocab_size)])

    def lowest(mask):
        return (mask & -mask).bit_length() - 1

    def spread(own, line=None):
        blocks = [own]
        for mask in range(1, vocab_size):
            bit = lowest(mask)
            block = blocks[mask ^ (1 << bit)]
            if line is not None and bit == 0:
                block = tie(block, line[-2])
            blocks.append(swap(block, bit))
            if line is not None and bit == 0:
                line.append(blocks[-1])
        return blocks

    def reduce_blocks(parts):
        terms, line = list(parts), []
        for mask in range(vocab_size - 1, 0, -1):
            bit = lowest(mask)
            block = terms[mask].astype(wire)
            if bit == 0 and len(line) > 1:
                block = tie(block, line[-2])
            block = swap(block, bit)
            if bit == 0:
                line.append(block)
            terms[mask ^ (1 << bit)] = terms[mask ^ (1 << bit)] + block.astype(jnp.float32)
        return terms[0], line

    def body(teacher_rows, owner, counts, proj_weight, student_hidden, head_weight, targets):
        teach_rows = teacher_rows.shape[0]
        slab_rows = targets.shape[0]
        vocab_dev = head_weight.shape[1]
        blk = slab_rows // vocab_size
        chunk = min(slab_rows, 32)
        me = lax.axis_index("vocab")
        core = lax.axis_index("seq")
        place = jnp.stack([me, core]).astype(jnp.int32)

        def in_order(vec):
            grid = vec.reshape((2,) * bits + (blk,))
            for bit in range(bits):
                grid = jnp.where((me >> bit) & 1 == 1, jnp.flip(grid, bits - 1 - bit), grid)
            return grid.reshape(slab_rows)

        def turned(block):
            return jnp.where(core == 1, jnp.roll(block, block.shape[1] // 2, axis=1), block)

        def as_pieces(blocks):
            return blocks if blk % 16 == 0 else [jnp.concatenate(blocks, axis=0)]

        heads = (head_weight, lax.ppermute(head_weight, "seq", [(0, 1), (1, 0)]))

        spot = lax.iota(jnp.int32, slab_rows)
        row_id = ((spot // blk) ^ me) * blk + spot % blk
        alive = lax.iota(jnp.int32, teach_rows) < counts[0]
        member = (owner[None, :] == row_id[:, None]) & alive[None, :]
        parts = project(member.astype(jnp.bfloat16), teacher_rows, proj_weight, vocab_size, 896)
        projected_own, line = reduce_blocks(parts)
        hidden = spread(tie(turned(student_hidden), parts[-1]), line)
        projected = spread(turned(projected_own.astype(jnp.bfloat16)))

        column = (in_order(targets) - me * vocab_dev)[:, None]
        logit_stud, scaled_stud, stats_stud = student_logits(as_pieces(hidden), heads, column, chunk)
        scaled_teach, stats = teacher_logits(as_pieces(projected), heads, logit_stud, stats_stud, chunk)
        tables = [stats] + [
            lax.ppermute(stats, "vocab", [(at, at ^ mask) for at in range(vocab_size)])
            for mask in range(1, vocab_size)
        ]
        loss, *terms = gradient(place, tables, scaled_teach, scaled_stud, column, heads, bits, chunk)
        return (loss[0], turned(reduce_blocks(terms)[0].astype(jnp.bfloat16)))

    return body


def solution(mesh):
    return jax.shard_map(
        make_body(mesh.shape["vocab"]),
        mesh=mesh,
        in_specs=(
            P(("groups", "seq"), "vocab"),
            P(("groups", "seq")),
            P(("groups", "seq")),
            P("vocab", None),
            P(("groups", "seq", "vocab"), None),
            P("seq", "vocab"),
            P(("groups", "seq")),
        ),
        out_specs=(P(("groups", "seq")), P(("groups", "seq", "vocab"), None)),
        check_vma=False,
    )
```

time: 163 us -> 153 us (0.939)
  local copies, waits for them, and re-layouts: 27.1 us -> 2.3 us
  other arithmetic: 2.52 us -> 11.5 us
  starting transfers between devices: 40.2 us -> 44.4 us
  Pallas kernels: 39.6 us -> 42.9 us
  waiting for transfers between devices: 51.7 us -> 50 us
    unnamed x52 -> x6, local copies, waits for them, and re-layouts: 26.3 us -> 1.44 us
    ppermute x0 -> x7, starting transfers between devices: none -> 11.2 us  [body(): lax.ppermute(stats, 'vocab', [(at, at ^ mask) for at in range(vocab_size)])]
    convert_element_type x14, other arithmetic: 0.69 us -> 7.79 us  [reduce_blocks(): block = terms[mask].astype(wire)]
    ppermute x31 -> x28, starting transfers between devices: 39.7 us -> 32.7 us  [swap(): lax.ppermute(block, 'vocab', [(at, at ^ 1 << bit) for at in range(vocab_s...]
    ppermute x31 -> x28, waiting for transfers between devices: 51.7 us -> 48.1 us  [swap(): lax.ppermute(block, 'vocab', [(at, at ^ 1 << bit) for at in range(vocab_s...]
    pallas_call x1, Pallas kernels: 4.11 us -> 7.46 us  [project(): pl.pallas_call(functools.partial(project_kernel, count, step), in_specs=[...]
    ppermute x0 -> x7, waiting for transfers between devices: none -> 1.83 us  [body(): lax.ppermute(stats, 'vocab', [(at, at ^ mask) for at in range(vocab_size)])]
    pallas_call x5 -> x3, Pallas kernels: 35.5 us -> 35.4 us  [the longest x1 12.9 us: student_logits(): pl.pallas_call(functools.partial(student_kernel, len(pieces), chunk_colum...]
  transfers between devices with their start and end apart: 32 -> 36, of which waited for: 17 -> 17; matrix products, arithmetic and copies ran while one was open for 2% -> 8% of each run, Pallas kernels for 9% -> 13%
where the time goes in v2:
time: 153 us
  waiting for transfers between devices  50 us (33%)
  starting transfers between devices  44.4 us (29%)
  Pallas kernels  42.9 us (28%)
  other arithmetic  11.5 us (8%)
  local copies, waits for them, and re-layouts  2.3 us (2%)
    ppermute x28, waiting for transfers between devices, swap(): lax.ppermute(block, 'vocab', [(at, at ^ 1 << bit) for at in range(vocab_s...  48.1 us
    ppermute x28, starting transfers between devices, swap(): lax.ppermute(block, 'vocab', [(at, at ^ 1 << bit) for at in range(vocab_s...  32.7 us
    pallas_call x1, Pallas kernels, student_logits(): pl.pallas_call(functools.partial(student_kernel, len(pieces), chunk_colum...  12.9 us
    pallas_call x1, Pallas kernels, teacher_logits(): pl.pallas_call(functools.partial(teacher_kernel, len(pieces), chunk_colum...  12.4 us
    ppermute x7, starting transfers between devices, body(): lax.ppermute(stats, 'vocab', [(at, at ^ mask) for at in range(vocab_size)])  11.2 us
    pallas_call x1, Pallas kernels, gradient(): pl.pallas_call(functools.partial(gradient_kernel, bits, step, fine, chunk...  10.1 us
    convert_element_type x14, other arithmetic, reduce_blocks(): block = terms[mask].astype(wire)  7.79 us
    pallas_call x1, Pallas kernels, project(): pl.pallas_call(functools.partial(project_kernel, count, step), in_specs=[...  7.46 us
  transfers between devices with their start and end apart: 36, of which 17 were waited for; matrix products, arithmetic and copies ran while one was open for 8% of the time, Pallas kernels for 13%

profile of v2, /device:TPU:0, one launch (start us, length us, event | category | flops | bytes accessed | tf_op | source)
XLA Modules:
  0.0 152.7 jit_solution(12233913844174629505)
XLA Ops:
  0.6 0.5 collective-permute-start.14
  1.8 1.6 %and_convert_fusion.member_ref = bf16[256,512]{1,0:T(8,128)(2,1)} fusion(s32[512]{0:T(512)} %param.8, s32[256]{0:T(256)S(1)} %fusion.3, pred[512]{0:T(512)(128)(4,1)S(1)} %iota_compare_fusion), kind=kLoop, calls=%fused_computation | loop fusion | flops 393216 | bytes 265728 | tf_op jit(solution)/shard_map/convert_element_type | solution.py:397
  3.4 7.5 %shard_map.86 = (f32[32,3584]{1,0:T(8,128)}, f32[32,3584]{1,0:T(8,128)}, f32[32,3584]{1,0:T(8,128)}, f32[32,3584]{1,0:T(8,128)}, f32[32,3584]{1,0:T(8,128)}, /*i...) custom-call(bf16[256,512]{1,0:T(8,128)(2,1)} %and_convert_fusion.member_ref, ...), custom_call_target="tpu_custom_call" | custom-call | flops 2147483648 | bytes 12058624 | tf_op jit(solution)/shard_map/pallas_call | solution.py:52
  10.9 1.0 convert_element_type.94
  11.9 2.6 %collective-permute-start = (f16[32,3584]{1,0:T(8,128)(2,1)S(1)}, f16[32,3584]{1,0:T(8,128)(2,1)S(1)}, u32[]{:S(2)}, u32[]{:S(2)}) collective-permute-start(f16[32,3584]{1,0:T(8,128)(2,1)S(1)} %convert_element_type.94), channel_id=1, source_target_pairs={{0,1},{1,0},{2,3},{3,2},{4,5},{5,4},{6,7},{7,6},{8,9},{9,8},{10,11... | collective-permute-start | bytes 688136 | tf_op jit(solution)/shard_map/ppermute | solution.py:339
  14.6 2.7 %collective-permute-start.18 = (bf16[32,3584]{1,0:T(8,128)(2,1)S(1)}, bf16[32,3584]{1,0:T(8,128)(2,1)S(1)}, u32[]{:S(2)}, u32[]{:S(2)}) collective-permute-start(bf16[32,3584]{1,0:T(8,128)(2,1)S(1)} %maximum_select_fusion.1.refs_0_), channel_id=1, source_target_pairs={{0,4},{1,5},{2,6},{3,7},{4,0},{5,1},{6,2},{7,3},{8,12},{9,13},{10,... | collective-permute-start | bytes 688136 | tf_op jit(solution)/shard_map/ppermute | solution.py:339
  17.3 1.6 %collective-permute-start.16 = (bf16[32,3584]{1,0:T(8,128)(2,1)S(1)}, bf16[32,3584]{1,0:T(8,128)(2,1)S(1)}, u32[]{:S(2)}, u32[]{:S(2)}) collective-permute-start(bf16[32,3584]{1,0:T(8,128)(2,1)S(1)} %maximum_select_fusion.1.refs_0_), channel_id=1, source_target_pairs={{0,2},{1,3},{2,0},{3,1},{4,6},{5,7},{6,4},{7,5},{8,10},{9,11},{10,... | collective-permute-start | bytes 688136 | tf_op jit(solution)/shard_map/ppermute | solution.py:339
  18.9 1.0 convert_element_type.98
  19.9 0.6 collective-permute-start.2
  20.5 1.0 convert_element_type.102
  21.5 1.0 convert_element_type.106
  22.6 1.6 %collective-permute-start.4 = (f16[32,3584]{1,0:T(8,128)(2,1)S(1)}, f16[32,3584]{1,0:T(8,128)(2,1)S(1)}, u32[]{:S(2)}, u32[]{:S(2)}) collective-permute-start(f16[32,3584]{1,0:T(8,128)(2,1)S(1)} %convert_element_type.102), channel_id=1, source_target_pairs={{0,1},{1,0},{2,3},{3,2},{4,5},{5,4},{6,7},{7,6},{8,9},{9,8},{10,11... | collective-permute-start | bytes 688136 | tf_op jit(solution)/shard_map/ppermute | solution.py:339
  24.2 1.1 add_convert_fusion.7
  25.2 3.2 %collective-permute-done.2 = f16[32,3584]{1,0:T(8,128)(2,1)S(1)} collective-permute-done((f16[32,3584]{1,0:T(8,128)(2,1)S(1)}, f16[32,3584]{1,0:T(8,128)(2,1)S(1)}, u32[]{:S(2)}, u32[]{:S(2)}) %collective-permute-start.2) | collective-permute-done | bytes 229408 | tf_op jit(solution)/shard_map/ppermute | solution.py:339
  28.9 3.1 %collective-permute-done.4 = f16[32,3584]{1,0:T(8,128)(2,1)S(1)} collective-permute-done((f16[32,3584]{1,0:T(8,128)(2,1)S(1)}, f16[32,3584]{1,0:T(8,128)(2,1)S(1)}, u32[]{:S(2)}, u32[]{:S(2)}) %collective-permute-start.4) | collective-permute-done | bytes 229408 | tf_op jit(solution)/shard_map/ppermute | solution.py:339
  32.0 0.5 collective-permute-start.6
  32.5 1.1 add_convert_fusion.5
  33.6 0.9 collective-permute-done.1
  34.5 0.6 collective-permute-start.5
  35.1 1.1 add_convert_fusion.6
  36.2 2.7 %collective-permute-start.3 = (f16[32,3584]{1,0:T(8,128)(2,1)S(1)}, f16[32,3584]{1,0:T(8,128)(2,1)S(1)}, u32[]{:S(2)}, u32[]{:S(2)}) collective-permute-start(f16[32,3584]{1,0:T(8,128)(2,1)S(1)} %add_convert_fusion.6), channel_id=1, source_target_pairs={{0,4},{1,5},{2,6},{3,7},{4,0},{5,1},{6,2},{7,3},{8,12},{9,13},{10,... | collective-permute-start | bytes 688136 | tf_op jit(solution)/shard_map/ppermute | solution.py:339
  38.9 0.5 collective-permute-start.20
  39.3 1.1 collective-permute-start.15
  40.4 5.1 %collective-permute-done.5 = f16[32,3584]{1,0:T(8,128)(2,1)S(1)} collective-permute-done((f16[32,3584]{1,0:T(8,128)(2,1)S(1)}, f16[32,3584]{1,0:T(8,128)(2,1)S(1)}, u32[]{:S(2)}, u32[]{:S(2)}) %collective-permute-start.5) | collective-permute-done | bytes 229408 | tf_op jit(solution)/shard_map/ppermute | solution.py:339
  45.6 1.7 %collective-permute-start.17 = (bf16[32,3584]{1,0:T(8,128)(2,1)S(1)}, bf16[32,3584]{1,0:T(8,128)(2,1)S(1)}, u32[]{:S(2)}, u32[]{:S(2)}) collective-permute-start(bf16[32,3584]{1,0:T(8,128)(2,1)S(1)} %collective-permute-done.16.refs_2_), channel_id=1, source_target_pairs={{0,1},{1,0},{2,3},{3,2},{4,5},{5,4},{6,7},{7,6},{8,9},{9,8},{10,11... | collective-permute-start | bytes 688136 | tf_op jit(solution)/shard_map/ppermute | solution.py:339
  47.3 1.2 collective-permute-done.3
  48.5 1.1 add_convert_fusion.4
  49.7 0.7 collective-permute-start.10
  50.6 2.8 %collective-permute-start.8 = (bf16[32,3584]{1,0:T(8,128)(2,1)S(1)}, bf16[32,3584]{1,0:T(8,128)(2,1)S(1)}, u32[]{:S(2)}, u32[]{:S(2)}) collective-permute-start(bf16[32,3584]{1,0:T(8,128)(2,1)S(1)} %maximum_select_fusion.refs_0_), channel_id=1, source_target_pairs={{0,2},{1,3},{2,0},{3,1},{4,6},{5,7},{6,4},{7,5},{8,10},{9,11},{10,... | collective-permute-start | bytes 688136 | tf_op jit(solution)/shard_map/ppermute | solution.py:339
  53.4 1.3 collective-permute-start.19
  54.7 0.8 collective-permute-start.21
  55.4 4.2 %collective-permute-done.10.refs_4_ = bf16[32,3584]{1,0:T(8,128)(2,1)S(1)} collective-permute-done((bf16[32,3584]{1,0:T(8,128)(2,1)S(1)}, bf16[32,3584]{1,0:T(8,128)(2,1)S(1)}, u32[]{:S(2)}, u32[]{:S(2)}) %collective-permute-start.10) | collective-permute-done | bytes 229408 | tf_op jit(solution)/shard_map/ppermute | solution.py:339
  59.6 0.8 collective-permute-start.12
  60.6 0.5 collective-permute-start.7
  61.1 1.6 %collective-permute-start.11 = (bf16[32,3584]{1,0:T(8,128)(2,1)S(1)}, bf16[32,3584]{1,0:T(8,128)(2,1)S(1)}, u32[]{:S(2)}, u32[]{:S(2)}) collective-permute-start(bf16[32,3584]{1,0:T(8,128)(2,1)S(1)} %collective-permute-done.10.refs_4_), channel_id=1, source_target_pairs={{0,1},{1,0},{2,3},{3,2},{4,5},{5,4},{6,7},{7,6},{8,9},{9,8},{10,11... | collective-permute-start | bytes 688136 | tf_op jit(solution)/shard_map/ppermute | solution.py:339
  62.7 2.0 %collective-permute-done.21.refs_7_ = bf16[32,3584]{1,0:T(8,128)(2,1)S(1)} collective-permute-done((bf16[32,3584]{1,0:T(8,128)(2,1)S(1)}, bf16[32,3584]{1,0:T(8,128)(2,1)S(1)}, u32[]{:S(2)}, u32[]{:S(2)}) %collective-permute-start.21) | collective-permute-done | bytes 229408 | tf_op jit(solution)/shard_map/ppermute | solution.py:339
  64.9 0.7 collective-permute-done.12.refs_6_
  65.6 1.0 collective-permute-start.13
  66.7 12.9 %shard_map.87 = (f32[256,2432]{1,0:T(8,128)S(1)}, f32[256,2432]{1,0:T(8,128)S(1)}, f32[8,256]{1,0:T(8,128)S(1)}) custom-call(bf16[32,3584]{1,0:T(8,128)(2,1)S(1)} %maximum_select_fusion.1.refs_0_, bf16[32,3584]{1,0:T(8,128)(2,1)S(1)} %collective-permute-done.15.refs_1_, bf16[32,3584]{1,0:T(8,128)(2,1)S(1)} %collective-permute-done.16.refs_2_, ...), custom_call_target="tpu_custom_call" | custom-call | flops 4462739456 | bytes 24903680 | tf_op jit(solution)/shard_map/pallas_call | solution.py:195
  79.6 1.4 copy-done
  81.1 2.1 %collective-permute-done.13.refs_7_ = bf16[32,3584]{1,0:T(8,128)(2,1)S(1)} collective-permute-done((bf16[32,3584]{1,0:T(8,128)(2,1)S(1)}, bf16[32,3584]{1,0:T(8,128)(2,1)S(1)}, u32[]{:S(2)}, u32[]{:S(2)}) %collective-permute-start.13) | collective-permute-done | bytes 229408 | tf_op jit(solution)/shard_map/ppermute | solution.py:339
  83.2 12.4 %shard_map.88 = (f32[256,2432]{1,0:T(8,128)S(1)}, f32[8,256]{1,0:T(8,128)S(1)}) custom-call(bf16[32,3584]{1,0:T(8,128)(2,1)S(1)} %maximum_select_fusion.refs_0_, bf16[32,3584]{1,0:T(8,128)(2,1)S(1)} %collective-permute-done.7.refs_1_, bf16[32,3584]{1,0:T(8,128)(2,1)S(1)} %collective-permute-done.8.refs_2_, ...), custom_call_target="tpu_custom_call" | custom-call | flops 4462739456 | bytes 24903680 | tf_op jit(solution)/shard_map/pallas_call | solution.py:212
  95.5 2.9 %collective-permute-start.28 = (f32[8,256]{1,0:T(8,128)S(1)}, f32[8,256]{1,0:T(8,128)S(1)}, u32[]{:S(2)}, u32[]{:S(2)}) collective-permute-start(f32[8,256]{1,0:T(8,128)S(1)} %get-tuple-element.50.refs_0_), channel_id=1, source_target_pairs={{0,7},{1,6},{2,5},{3,4},{4,3},{5,2},{6,1},{7,0},{8,15},{9,14},{10,... | collective-permute-start | bytes 24584 | tf_op jit(solution)/shard_map/ppermute | solution.py:406
  98.4 0.7 collective-permute-start.27
  99.1 1.6 %collective-permute-start.26 = (f32[8,256]{1,0:T(8,128)S(1)}, f32[8,256]{1,0:T(8,128)S(1)}, u32[]{:S(2)}, u32[]{:S(2)}) collective-permute-start(f32[8,256]{1,0:T(8,128)S(1)} %get-tuple-element.50.refs_0_), channel_id=1, source_target_pairs={{0,5},{1,4},{2,7},{3,6},{4,1},{5,0},{6,3},{7,2},{8,13},{9,12},{10,... | collective-permute-start | bytes 24584 | tf_op jit(solution)/shard_map/ppermute | solution.py:406
  100.7 2.6 %collective-permute-start.25 = (f32[8,256]{1,0:T(8,128)S(1)}, f32[8,256]{1,0:T(8,128)S(1)}, u32[]{:S(2)}, u32[]{:S(2)}) collective-permute-start(f32[8,256]{1,0:T(8,128)S(1)} %get-tuple-element.50.refs_0_), channel_id=1, source_target_pairs={{0,4},{1,5},{2,6},{3,7},{4,0},{5,1},{6,2},{7,3},{8,12},{9,13},{10,... | collective-permute-start | bytes 24584 | tf_op jit(solution)/shard_map/ppermute | solution.py:406
  103.2 0.5 collective-permute-start.24
  103.7 1.3 collective-permute-start.23
  105.0 1.7 %collective-permute-start.22 = (f32[8,256]{1,0:T(8,128)S(1)}, f32[8,256]{1,0:T(8,128)S(1)}, u32[]{:S(2)}, u32[]{:S(2)}) collective-permute-start(f32[8,256]{1,0:T(8,128)S(1)} %get-tuple-element.50.refs_0_), channel_id=1, source_target_pairs={{0,1},{1,0},{2,3},{3,2},{4,5},{5,4},{6,7},{7,6},{8,9},{9,8},{10,11... | collective-permute-start | bytes 24584 | tf_op jit(solution)/shard_map/ppermute | solution.py:406
  106.8 1.0 collective-permute-done.24.refs_3_
  107.8 0.8 collective-permute-done.22.refs_1_
  108.6 10.1 %shard_map.89 = (f32[8,256]{1,0:T(8,128)S(1)}, f32[32,3584]{1,0:T(8,128)S(1)}, f32[32,3584]{1,0:T(8,128)S(1)}, f32[32,3584]{1,0:T(8,128)S(1)}, f32[32,3584]{1,0:...) custom-call(s32[2]{0:T(128)S(1)} %pad_add_fusion.place_ref, ...), custom_call_target="tpu_custom_call" | custom-call | flops 4462739456 | bytes 24903680 | tf_op jit(solution)/shard_map/pallas_call | solution.py:310
  118.8 1.8 %collective-permute-start.31 = (f16[32,3584]{1,0:T(8,128)(2,1)S(1)}, f16[32,3584]{1,0:T(8,128)(2,1)S(1)}, u32[]{:S(2)}, u32[]{:S(2)}) collective-permute-start(f16[32,3584]{1,0:T(8,128)(2,1)S(1)} %convert_element_type.113), channel_id=1, source_target_pairs={{0,1},{1,0},{2,3},{3,2},{4,5},{5,4},{6,7},{7,6},{8,9},{9,8},{10,11... | collective-permute-start | bytes 688136 | tf_op jit(solution)/shard_map/ppermute | solution.py:339
  121.1 6.4 %collective-permute-done.31 = f16[32,3584]{1,0:T(8,128)(2,1)S(1)} collective-permute-done((f16[32,3584]{1,0:T(8,128)(2,1)S(1)}, f16[32,3584]{1,0:T(8,128)(2,1)S(1)}, u32[]{:S(2)}, u32[]{:S(2)}) %collective-permute-start.31) | collective-permute-done | bytes 229408 | tf_op jit(solution)/shard_map/ppermute | solution.py:339
  127.4 1.7 %collective-permute-start.35 = (f16[32,3584]{1,0:T(8,128)(2,1)S(1)}, f16[32,3584]{1,0:T(8,128)(2,1)S(1)}, u32[]{:S(2)}, u32[]{:S(2)}) collective-permute-start(f16[32,3584]{1,0:T(8,128)(2,1)S(1)} %convert_element_type.121), channel_id=1, source_target_pairs={{0,1},{1,0},{2,3},{3,2},{4,5},{5,4},{6,7},{7,6},{8,9},{9,8},{10,11... | collective-permute-start | bytes 688136 | tf_op jit(solution)/shard_map/ppermute | solution.py:339
  129.2 3.2 %collective-permute-done.29 = f16[32,3584]{1,0:T(8,128)(2,1)S(1)} collective-permute-done((f16[32,3584]{1,0:T(8,128)(2,1)S(1)}, f16[32,3584]{1,0:T(8,128)(2,1)S(1)}, u32[]{:S(2)}, u32[]{:S(2)}) %collective-permute-start.29) | collective-permute-done | bytes 229408 | tf_op jit(solution)/shard_map/ppermute | solution.py:339
  132.3 1.7 %collective-permute-start.33 = (f16[32,3584]{1,0:T(8,128)(2,1)S(1)}, f16[32,3584]{1,0:T(8,128)(2,1)S(1)}, u32[]{:S(2)}, u32[]{:S(2)}) collective-permute-start(f16[32,3584]{1,0:T(8,128)(2,1)S(1)} %convert_element_type.117), channel_id=1, source_target_pairs={{0,1},{1,0},{2,3},{3,2},{4,5},{5,4},{6,7},{7,6},{8,9},{9,8},{10,11... | collective-permute-start | bytes 688136 | tf_op jit(solution)/shard_map/ppermute | solution.py:339
  134.3 4.1 %collective-permute-done.33 = f16[32,3584]{1,0:T(8,128)(2,1)S(1)} collective-permute-done((f16[32,3584]{1,0:T(8,128)(2,1)S(1)}, f16[32,3584]{1,0:T(8,128)(2,1)S(1)}, u32[]{:S(2)}, u32[]{:S(2)}) %collective-permute-start.33) | collective-permute-done | bytes 229408 | tf_op jit(solution)/shard_map/ppermute | solution.py:339
  138.4 0.7 collective-permute-start.34
  139.1 4.1 %collective-permute-done.30 = f16[32,3584]{1,0:T(8,128)(2,1)S(1)} collective-permute-done((f16[32,3584]{1,0:T(8,128)(2,1)S(1)}, f16[32,3584]{1,0:T(8,128)(2,1)S(1)}, u32[]{:S(2)}, u32[]{:S(2)}) %collective-permute-start.30) | collective-permute-done | bytes 229408 | tf_op jit(solution)/shard_map/ppermute | solution.py:339
  143.4 0.6 slice.27
  143.9 1.7 %collective-permute-done.34 = f16[32,3584]{1,0:T(8,128)(2,1)S(1)} collective-permute-done((f16[32,3584]{1,0:T(8,128)(2,1)S(1)}, f16[32,3584]{1,0:T(8,128)(2,1)S(1)}, u32[]{:S(2)}, u32[]{:S(2)}) %collective-permute-start.34) | collective-permute-done | bytes 229408 | tf_op jit(solution)/shard_map/ppermute | solution.py:339
  145.6 6.2 %collective-permute-done.32 = f16[32,3584]{1,0:T(8,128)(2,1)S(1)} collective-permute-done((f16[32,3584]{1,0:T(8,128)(2,1)S(1)}, f16[32,3584]{1,0:T(8,128)(2,1)S(1)}, u32[]{:S(2)}, u32[]{:S(2)}) %collective-permute-start.32) | collective-permute-done | bytes 229408 | tf_op jit(solution)/shard_map/ppermute | solution.py:339
  151.9 0.8 maximum_select_fusion.2
  (51 shorter events, 2.3 us)
Async XLA Ops:
  0.6 13.9 %copy-start.1 = (bf16[32,3584]{1,0:T(8,128)(2,1)S(1)}, bf16[32,3584]{1,0:T(8,128)(2,1)}, u32[]{:S(2)}) copy-start(bf16[32,3584]{1,0:T(8,128)(2,1)} %param.11) | copy-start | bytes 688132
  0.6 66.0 %collective-permute-start.14 = (bf16[1792,2432]{1,0:T(8,128)(2,1)}, bf16[1792,2432]{1,0:T(8,128)(2,1)}, u32[]{:S(2)}, u32[]{:S(2)}) collective-permute-start(bf16[1792,2432]{1,0:T(8,128)(2,1)} %refs_11_.1), channel_id=1, source_target_pairs={{0,8},{8,0},{1,9},{9,1},{2,10},{10,2},{3,11},{11,3},{4,12},{12,4},... | collective-permute-start | bytes 26148872 | tf_op jit(solution)/shard_map/ppermute | solution.py:391
  3.4 47.1 %copy-start.2 = (s32[256]{0:T(256)S(1)}, s32[256]{0:T(256)}, u32[]{:S(2)}) copy-start(s32[256]{0:T(256)} %param.13) | copy-start | bytes 3076
  11.9 10.7 %collective-permute-start = (f16[32,3584]{1,0:T(8,128)(2,1)S(1)}, f16[32,3584]{1,0:T(8,128)(2,1)S(1)}, u32[]{:S(2)}, u32[]{:S(2)}) collective-permute-start(f16[32,3584]{1,0:T(8,128)(2,1)S(1)} %convert_element_type.94), channel_id=1, source_target_pairs={{0,1},{1,0},{2,3},{3,2},{4,5},{5,4},{6,7},{7,6},{8,9},{9,8},{10,11... | collective-permute-start | bytes 688136 | tf_op jit(solution)/shard_map/ppermute | solution.py:339
  14.6 21.6 %collective-permute-start.18 = (bf16[32,3584]{1,0:T(8,128)(2,1)S(1)}, bf16[32,3584]{1,0:T(8,128)(2,1)S(1)}, u32[]{:S(2)}, u32[]{:S(2)}) collective-permute-start(bf16[32,3584]{1,0:T(8,128)(2,1)S(1)} %maximum_select_fusion.1.refs_0_), channel_id=1, source_target_pairs={{0,4},{1,5},{2,6},{3,7},{4,0},{5,1},{6,2},{7,3},{8,12},{9,13},{10,... | collective-permute-start | bytes 688136 | tf_op jit(solution)/shard_map/ppermute | solution.py:339
  17.3 21.6 %collective-permute-start.16 = (bf16[32,3584]{1,0:T(8,128)(2,1)S(1)}, bf16[32,3584]{1,0:T(8,128)(2,1)S(1)}, u32[]{:S(2)}, u32[]{:S(2)}) collective-permute-start(bf16[32,3584]{1,0:T(8,128)(2,1)S(1)} %maximum_select_fusion.1.refs_0_), channel_id=1, source_target_pairs={{0,2},{1,3},{2,0},{3,1},{4,6},{5,7},{6,4},{7,5},{8,10},{9,11},{10,... | collective-permute-start | bytes 688136 | tf_op jit(solution)/shard_map/ppermute | solution.py:339
  19.9 8.6 %collective-permute-start.2 = (f16[32,3584]{1,0:T(8,128)(2,1)S(1)}, f16[32,3584]{1,0:T(8,128)(2,1)S(1)}, u32[]{:S(2)}, u32[]{:S(2)}) collective-permute-start(f16[32,3584]{1,0:T(8,128)(2,1)S(1)} %convert_element_type.98), channel_id=1, source_target_pairs={{0,1},{1,0},{2,3},{3,2},{4,5},{5,4},{6,7},{7,6},{8,9},{9,8},{10,11... | collective-permute-start | bytes 688136 | tf_op jit(solution)/shard_map/ppermute | solution.py:339
  22.6 9.4 %collective-permute-start.4 = (f16[32,3584]{1,0:T(8,128)(2,1)S(1)}, f16[32,3584]{1,0:T(8,128)(2,1)S(1)}, u32[]{:S(2)}, u32[]{:S(2)}) collective-permute-start(f16[32,3584]{1,0:T(8,128)(2,1)S(1)} %convert_element_type.102), channel_id=1, source_target_pairs={{0,1},{1,0},{2,3},{3,2},{4,5},{5,4},{6,7},{7,6},{8,9},{9,8},{10,11... | collective-permute-start | bytes 688136 | tf_op jit(solution)/shard_map/ppermute | solution.py:339
  28.5 6.0 %collective-permute-start.1 = (f16[32,3584]{1,0:T(8,128)(2,1)S(1)}, f16[32,3584]{1,0:T(8,128)(2,1)S(1)}, u32[]{:S(2)}, u32[]{:S(2)}) collective-permute-start(f16[32,3584]{1,0:T(8,128)(2,1)S(1)} %add_convert_fusion.7), channel_id=1, source_target_pairs={{0,2},{1,3},{2,0},{3,1},{4,6},{5,7},{6,4},{7,5},{8,10},{9,11},{10,... | collective-permute-start | bytes 688136 | tf_op jit(solution)/shard_map/ppermute | solution.py:339
  32.0 7.3 %collective-permute-start.6 = (f16[32,3584]{1,0:T(8,128)(2,1)S(1)}, f16[32,3584]{1,0:T(8,128)(2,1)S(1)}, u32[]{:S(2)}, u32[]{:S(2)}) collective-permute-start(f16[32,3584]{1,0:T(8,128)(2,1)S(1)} %convert_element_type.106), channel_id=1, source_target_pairs={{0,1},{1,0},{2,3},{3,2},{4,5},{5,4},{6,7},{7,6},{8,9},{9,8},{10,11... | collective-permute-start | bytes 688136 | tf_op jit(solution)/shard_map/ppermute | solution.py:339
  34.5 11.1 %collective-permute-start.5 = (f16[32,3584]{1,0:T(8,128)(2,1)S(1)}, f16[32,3584]{1,0:T(8,128)(2,1)S(1)}, u32[]{:S(2)}, u32[]{:S(2)}) collective-permute-start(f16[32,3584]{1,0:T(8,128)(2,1)S(1)} %add_convert_fusion.5), channel_id=1, source_target_pairs={{0,2},{1,3},{2,0},{3,1},{4,6},{5,7},{6,4},{7,5},{8,10},{9,11},{10,... | collective-permute-start | bytes 688136 | tf_op jit(solution)/shard_map/ppermute | solution.py:339
  36.2 12.3 %collective-permute-start.3 = (f16[32,3584]{1,0:T(8,128)(2,1)S(1)}, f16[32,3584]{1,0:T(8,128)(2,1)S(1)}, u32[]{:S(2)}, u32[]{:S(2)}) collective-permute-start(f16[32,3584]{1,0:T(8,128)(2,1)S(1)} %add_convert_fusion.6), channel_id=1, source_target_pairs={{0,4},{1,5},{2,6},{3,7},{4,0},{5,1},{6,2},{7,3},{8,12},{9,13},{10,... | collective-permute-start | bytes 688136 | tf_op jit(solution)/shard_map/ppermute | solution.py:339
  38.9 14.5 %collective-permute-start.20 = (bf16[32,3584]{1,0:T(8,128)(2,1)S(1)}, bf16[32,3584]{1,0:T(8,128)(2,1)S(1)}, u32[]{:S(2)}, u32[]{:S(2)}) collective-permute-start(bf16[32,3584]{1,0:T(8,128)(2,1)S(1)} %collective-permute-done.18.refs_4_), channel_id=1, source_target_pairs={{0,2},{1,3},{2,0},{3,1},{4,6},{5,7},{6,4},{7,5},{8,10},{9,11},{10,... | collective-permute-start | bytes 688136 | tf_op jit(solution)/shard_map/ppermute | solution.py:339
  39.3 11.2 %collective-permute-start.15 = (bf16[32,3584]{1,0:T(8,128)(2,1)S(1)}, bf16[32,3584]{1,0:T(8,128)(2,1)S(1)}, u32[]{:S(2)}, u32[]{:S(2)}) collective-permute-start(bf16[32,3584]{1,0:T(8,128)(2,1)S(1)} %maximum_select_fusion.1.refs_0_), channel_id=1, source_target_pairs={{0,1},{1,0},{2,3},{3,2},{4,5},{5,4},{6,7},{7,6},{8,9},{9,8},{10,11... | collective-permute-start | bytes 688136 | tf_op jit(solution)/shard_map/ppermute | solution.py:339
  45.6 9.1 %collective-permute-start.17 = (bf16[32,3584]{1,0:T(8,128)(2,1)S(1)}, bf16[32,3584]{1,0:T(8,128)(2,1)S(1)}, u32[]{:S(2)}, u32[]{:S(2)}) collective-permute-start(bf16[32,3584]{1,0:T(8,128)(2,1)S(1)} %collective-permute-done.16.refs_2_), channel_id=1, source_target_pairs={{0,1},{1,0},{2,3},{3,2},{4,5},{5,4},{6,7},{7,6},{8,9},{9,8},{10,11... | collective-permute-start | bytes 688136 | tf_op jit(solution)/shard_map/ppermute | solution.py:339
  49.7 9.9 %collective-permute-start.10 = (bf16[32,3584]{1,0:T(8,128)(2,1)S(1)}, bf16[32,3584]{1,0:T(8,128)(2,1)S(1)}, u32[]{:S(2)}, u32[]{:S(2)}) collective-permute-start(bf16[32,3584]{1,0:T(8,128)(2,1)S(1)} %maximum_select_fusion.refs_0_), channel_id=1, source_target_pairs={{0,4},{1,5},{2,6},{3,7},{4,0},{5,1},{6,2},{7,3},{8,12},{9,13},{10,... | collective-permute-start | bytes 688136 | tf_op jit(solution)/shard_map/ppermute | solution.py:339
  50.6 10.0 %collective-permute-start.8 = (bf16[32,3584]{1,0:T(8,128)(2,1)S(1)}, bf16[32,3584]{1,0:T(8,128)(2,1)S(1)}, u32[]{:S(2)}, u32[]{:S(2)}) collective-permute-start(bf16[32,3584]{1,0:T(8,128)(2,1)S(1)} %maximum_select_fusion.refs_0_), channel_id=1, source_target_pairs={{0,2},{1,3},{2,0},{3,1},{4,6},{5,7},{6,4},{7,5},{8,10},{9,11},{10,... | collective-permute-start | bytes 688136 | tf_op jit(solution)/shard_map/ppermute | solution.py:339
  53.4 7.7 %collective-permute-start.19 = (bf16[32,3584]{1,0:T(8,128)(2,1)S(1)}, bf16[32,3584]{1,0:T(8,128)(2,1)S(1)}, u32[]{:S(2)}, u32[]{:S(2)}) collective-permute-start(bf16[32,3584]{1,0:T(8,128)(2,1)S(1)} %collective-permute-done.18.refs_4_), channel_id=1, source_target_pairs={{0,1},{1,0},{2,3},{3,2},{4,5},{5,4},{6,7},{7,6},{8,9},{9,8},{10,11... | collective-permute-start | bytes 688136 | tf_op jit(solution)/shard_map/ppermute | solution.py:339
  54.7 9.9 %collective-permute-start.21 = (bf16[32,3584]{1,0:T(8,128)(2,1)S(1)}, bf16[32,3584]{1,0:T(8,128)(2,1)S(1)}, u32[]{:S(2)}, u32[]{:S(2)}) collective-permute-start(bf16[32,3584]{1,0:T(8,128)(2,1)S(1)} %collective-permute-done.20.refs_6_), channel_id=1, source_target_pairs={{0,1},{1,0},{2,3},{3,2},{4,5},{5,4},{6,7},{7,6},{8,9},{9,8},{10,11... | collective-permute-start | bytes 688136 | tf_op jit(solution)/shard_map/ppermute | solution.py:339
  59.6 6.0 %collective-permute-start.12 = (bf16[32,3584]{1,0:T(8,128)(2,1)S(1)}, bf16[32,3584]{1,0:T(8,128)(2,1)S(1)}, u32[]{:S(2)}, u32[]{:S(2)}) collective-permute-start(bf16[32,3584]{1,0:T(8,128)(2,1)S(1)} %collective-permute-done.10.refs_4_), channel_id=1, source_target_pairs={{0,2},{1,3},{2,0},{3,1},{4,6},{5,7},{6,4},{7,5},{8,10},{9,11},{10,... | collective-permute-start | bytes 688136 | tf_op jit(solution)/shard_map/ppermute | solution.py:339
  60.6 20.5 %collective-permute-start.7 = (bf16[32,3584]{1,0:T(8,128)(2,1)S(1)}, bf16[32,3584]{1,0:T(8,128)(2,1)S(1)}, u32[]{:S(2)}, u32[]{:S(2)}) collective-permute-start(bf16[32,3584]{1,0:T(8,128)(2,1)S(1)} %maximum_select_fusion.refs_0_), channel_id=1, source_target_pairs={{0,1},{1,0},{2,3},{3,2},{4,5},{5,4},{6,7},{7,6},{8,9},{9,8},{10,11... | collective-permute-start | bytes 688136 | tf_op jit(solution)/shard_map/ppermute | solution.py:339
  61.1 20.0 %collective-permute-start.11 = (bf16[32,3584]{1,0:T(8,128)(2,1)S(1)}, bf16[32,3584]{1,0:T(8,128)(2,1)S(1)}, u32[]{:S(2)}, u32[]{:S(2)}) collective-permute-start(bf16[32,3584]{1,0:T(8,128)(2,1)S(1)} %collective-permute-done.10.refs_4_), channel_id=1, source_target_pairs={{0,1},{1,0},{2,3},{3,2},{4,5},{5,4},{6,7},{7,6},{8,9},{9,8},{10,11... | collective-permute-start | bytes 688136 | tf_op jit(solution)/shard_map/ppermute | solution.py:339
  64.6 16.4 %collective-permute-start.9 = (bf16[32,3584]{1,0:T(8,128)(2,1)S(1)}, bf16[32,3584]{1,0:T(8,128)(2,1)S(1)}, u32[]{:S(2)}, u32[]{:S(2)}) collective-permute-start(bf16[32,3584]{1,0:T(8,128)(2,1)S(1)} %collective-permute-done.8.refs_2_), channel_id=1, source_target_pairs={{0,1},{1,0},{2,3},{3,2},{4,5},{5,4},{6,7},{7,6},{8,9},{9,8},{10,11... | collective-permute-start | bytes 688136 | tf_op jit(solution)/shard_map/ppermute | solution.py:339
  65.6 17.5 %collective-permute-start.13 = (bf16[32,3584]{1,0:T(8,128)(2,1)S(1)}, bf16[32,3584]{1,0:T(8,128)(2,1)S(1)}, u32[]{:S(2)}, u32[]{:S(2)}) collective-permute-start(bf16[32,3584]{1,0:T(8,128)(2,1)S(1)} %collective-permute-done.12.refs_6_), channel_id=1, source_target_pairs={{0,1},{1,0},{2,3},{3,2},{4,5},{5,4},{6,7},{7,6},{8,9},{9,8},{10,11... | collective-permute-start | bytes 688136 | tf_op jit(solution)/shard_map/ppermute | solution.py:339
  79.6 1.4 copy-start
  95.5 8.2 %collective-permute-start.28 = (f32[8,256]{1,0:T(8,128)S(1)}, f32[8,256]{1,0:T(8,128)S(1)}, u32[]{:S(2)}, u32[]{:S(2)}) collective-permute-start(f32[8,256]{1,0:T(8,128)S(1)} %get-tuple-element.50.refs_0_), channel_id=1, source_target_pairs={{0,7},{1,6},{2,5},{3,4},{4,3},{5,2},{6,1},{7,0},{8,15},{9,14},{10,... | collective-permute-start | bytes 24584 | tf_op jit(solution)/shard_map/ppermute | solution.py:406
  98.4 6.6 %collective-permute-start.27 = (f32[8,256]{1,0:T(8,128)S(1)}, f32[8,256]{1,0:T(8,128)S(1)}, u32[]{:S(2)}, u32[]{:S(2)}) collective-permute-start(f32[8,256]{1,0:T(8,128)S(1)} %get-tuple-element.50.refs_0_), channel_id=1, source_target_pairs={{0,6},{1,7},{2,4},{3,5},{4,2},{5,3},{6,0},{7,1},{8,14},{9,15},{10,... | collective-permute-start | bytes 24584 | tf_op jit(solution)/shard_map/ppermute | solution.py:406
  99.1 7.7 %collective-permute-start.26 = (f32[8,256]{1,0:T(8,128)S(1)}, f32[8,256]{1,0:T(8,128)S(1)}, u32[]{:S(2)}, u32[]{:S(2)}) collective-permute-start(f32[8,256]{1,0:T(8,128)S(1)} %get-tuple-element.50.refs_0_), channel_id=1, source_target_pairs={{0,5},{1,4},{2,7},{3,6},{4,1},{5,0},{6,3},{7,2},{8,13},{9,12},{10,... | collective-permute-start | bytes 24584 | tf_op jit(solution)/shard_map/ppermute | solution.py:406
  100.7 6.1 %collective-permute-start.25 = (f32[8,256]{1,0:T(8,128)S(1)}, f32[8,256]{1,0:T(8,128)S(1)}, u32[]{:S(2)}, u32[]{:S(2)}) collective-permute-start(f32[8,256]{1,0:T(8,128)S(1)} %get-tuple-element.50.refs_0_), channel_id=1, source_target_pairs={{0,4},{1,5},{2,6},{3,7},{4,0},{5,1},{6,2},{7,3},{8,12},{9,13},{10,... | collective-permute-start | bytes 24584 | tf_op jit(solution)/shard_map/ppermute | solution.py:406
  103.2 4.5 %collective-permute-start.24 = (f32[8,256]{1,0:T(8,128)S(1)}, f32[8,256]{1,0:T(8,128)S(1)}, u32[]{:S(2)}, u32[]{:S(2)}) collective-permute-start(f32[8,256]{1,0:T(8,128)S(1)} %get-tuple-element.50.refs_0_), channel_id=1, source_target_pairs={{0,3},{1,2},{2,1},{3,0},{4,7},{5,6},{6,5},{7,4},{8,11},{9,10},{10,... | collective-permute-start | bytes 24584 | tf_op jit(solution)/shard_map/ppermute | solution.py:406
  103.7 4.1 %collective-permute-start.23 = (f32[8,256]{1,0:T(8,128)S(1)}, f32[8,256]{1,0:T(8,128)S(1)}, u32[]{:S(2)}, u32[]{:S(2)}) collective-permute-start(f32[8,256]{1,0:T(8,128)S(1)} %get-tuple-element.50.refs_0_), channel_id=1, source_target_pairs={{0,2},{1,3},{2,0},{3,1},{4,6},{5,7},{6,4},{7,5},{8,10},{9,11},{10,... | collective-permute-start | bytes 24584 | tf_op jit(solution)/shard_map/ppermute | solution.py:406
  105.0 3.7 %collective-permute-start.22 = (f32[8,256]{1,0:T(8,128)S(1)}, f32[8,256]{1,0:T(8,128)S(1)}, u32[]{:S(2)}, u32[]{:S(2)}) collective-permute-start(f32[8,256]{1,0:T(8,128)S(1)} %get-tuple-element.50.refs_0_), channel_id=1, source_target_pairs={{0,1},{1,0},{2,3},{3,2},{4,5},{5,4},{6,7},{7,6},{8,9},{9,8},{10,11... | collective-permute-start | bytes 24584 | tf_op jit(solution)/shard_map/ppermute | solution.py:406
  118.8 8.6 %collective-permute-start.31 = (f16[32,3584]{1,0:T(8,128)(2,1)S(1)}, f16[32,3584]{1,0:T(8,128)(2,1)S(1)}, u32[]{:S(2)}, u32[]{:S(2)}) collective-permute-start(f16[32,3584]{1,0:T(8,128)(2,1)S(1)} %convert_element_type.113), channel_id=1, source_target_pairs={{0,1},{1,0},{2,3},{3,2},{4,5},{5,4},{6,7},{7,6},{8,9},{9,8},{10,11... | collective-permute-start | bytes 688136 | tf_op jit(solution)/shard_map/ppermute | solution.py:339
  120.6 11.7 %collective-permute-start.29 = (f16[32,3584]{1,0:T(8,128)(2,1)S(1)}, f16[32,3584]{1,0:T(8,128)(2,1)S(1)}, u32[]{:S(2)}, u32[]{:S(2)}) collective-permute-start(f16[32,3584]{1,0:T(8,128)(2,1)S(1)} %convert_element_type.109), channel_id=1, source_target_pairs={{0,1},{1,0},{2,3},{3,2},{4,5},{5,4},{6,7},{7,6},{8,9},{9,8},{10,11... | collective-permute-start | bytes 688136 | tf_op jit(solution)/shard_map/ppermute | solution.py:339
  127.4 16.5 %collective-permute-start.35 = (f16[32,3584]{1,0:T(8,128)(2,1)S(1)}, f16[32,3584]{1,0:T(8,128)(2,1)S(1)}, u32[]{:S(2)}, u32[]{:S(2)}) collective-permute-start(f16[32,3584]{1,0:T(8,128)(2,1)S(1)} %convert_element_type.121), channel_id=1, source_target_pairs={{0,1},{1,0},{2,3},{3,2},{4,5},{5,4},{6,7},{7,6},{8,9},{9,8},{10,11... | collective-permute-start | bytes 688136 | tf_op jit(solution)/shard_map/ppermute | solution.py:339
  132.3 6.0 %collective-permute-start.33 = (f16[32,3584]{1,0:T(8,128)(2,1)S(1)}, f16[32,3584]{1,0:T(8,128)(2,1)S(1)}, u32[]{:S(2)}, u32[]{:S(2)}) collective-permute-start(f16[32,3584]{1,0:T(8,128)(2,1)S(1)} %convert_element_type.117), channel_id=1, source_target_pairs={{0,1},{1,0},{2,3},{3,2},{4,5},{5,4},{6,7},{7,6},{8,9},{9,8},{10,11... | collective-permute-start | bytes 688136 | tf_op jit(solution)/shard_map/ppermute | solution.py:339
  134.1 9.0 %collective-permute-start.30 = (f16[32,3584]{1,0:T(8,128)(2,1)S(1)}, f16[32,3584]{1,0:T(8,128)(2,1)S(1)}, u32[]{:S(2)}, u32[]{:S(2)}) collective-permute-start(f16[32,3584]{1,0:T(8,128)(2,1)S(1)} %add_convert_fusion.3), channel_id=1, source_target_pairs={{0,2},{1,3},{2,0},{3,1},{4,6},{5,7},{6,4},{7,5},{8,10},{9,11},{10,... | collective-permute-start | bytes 688136 | tf_op jit(solution)/shard_map/ppermute | solution.py:339
  138.4 7.2 %collective-permute-start.34 = (f16[32,3584]{1,0:T(8,128)(2,1)S(1)}, f16[32,3584]{1,0:T(8,128)(2,1)S(1)}, u32[]{:S(2)}, u32[]{:S(2)}) collective-permute-start(f16[32,3584]{1,0:T(8,128)(2,1)S(1)} %add_convert_fusion.1), channel_id=1, source_target_pairs={{0,2},{1,3},{2,0},{3,1},{4,6},{5,7},{6,4},{7,5},{8,10},{9,11},{10,... | collective-permute-start | bytes 688136 | tf_op jit(solution)/shard_map/ppermute | solution.py:339
  143.3 8.5 %collective-permute-start.32 = (f16[32,3584]{1,0:T(8,128)(2,1)S(1)}, f16[32,3584]{1,0:T(8,128)(2,1)S(1)}, u32[]{:S(2)}, u32[]{:S(2)}) collective-permute-start(f16[32,3584]{1,0:T(8,128)(2,1)S(1)} %add_convert_fusion.2), channel_id=1, source_target_pairs={{0,4},{1,5},{2,6},{3,7},{4,0},{5,1},{6,2},{7,3},{8,12},{9,13},{10,... | collective-permute-start | bytes 688136 | tf_op jit(solution)/shard_map/ppermute | solution.py:339

commit v3 on v2

v3 whole, which is shorter than its diff:
```python
import functools

import jax
import jax.numpy as jnp
from jax import lax
from jax.experimental import pallas as pl
from jax.experimental.pallas import tpu as pltpu
from jax.sharding import PartitionSpec as P

loss_scale = 64.0
wire = jnp.float16
lanes = 128
vmem_bytes = 12 * 1024 * 1024
project_bytes = 52 * 1024 * 1024

in_vmem = pl.BlockSpec(memory_space=pltpu.VMEM)
in_smem = pl.BlockSpec(memory_space=pltpu.SMEM)
in_place = pl.BlockSpec(memory_space=pl.ANY)


def cuts(total, step):
    return [(start, min(step, total - start)) for start in range(0, total, step)]


def project_kernel(count, step, member_ref, teacher_ref, weight_ref, *rest):
    outs, (teacher, weight, aligned, sems) = rest[:count], rest[count:]
    blk = outs[0].shape[0]
    parts = cuts(weight.shape[1], step)
    first = pltpu.make_async_copy(teacher_ref, teacher, sems.at[len(parts)])
    first.start()
    for index, (start, size) in enumerate(parts):
        at = pl.ds(start, size)
        pltpu.make_async_copy(weight_ref.at[:, at], weight.at[:, at], sems.at[index]).start()
    member = member_ref[...]
    sizes = jnp.sum(member.astype(jnp.float32), axis=1, keepdims=True)
    first.wait()
    summed = jnp.dot(member, teacher[...], preferred_element_type=jnp.float32)
    aligned[...] = (summed / sizes).astype(jnp.bfloat16)

    def one(index, carry):
        at = pl.ds(pl.multiple_of(index * step, step), step)
        pltpu.make_async_copy(weight_ref.at[:, at], weight.at[:, at], sems.at[index]).wait()
        product = jnp.dot(aligned[...], weight[:, at], preferred_element_type=jnp.float32)
        for piece, out in enumerate(outs):
            out[:, at] = product[piece * blk : (piece + 1) * blk]
        return carry

    lax.fori_loop(0, len(parts), one, 0)


def project(member, teacher_rows, proj_weight, count, step):
    slab_rows, (depth, width) = member.shape[0], proj_weight.shape
    blk = slab_rows // count
    return pl.pallas_call(
        functools.partial(project_kernel, count, step),
        in_specs=[in_vmem, in_place, in_place],
        out_specs=[in_vmem] * count,
        out_shape=[jax.ShapeDtypeStruct((blk, width), jnp.float32)] * count,
        scratch_shapes=[
            pltpu.VMEM(teacher_rows.shape, jnp.bfloat16),
            pltpu.VMEM(proj_weight.shape, jnp.bfloat16),
            pltpu.VMEM((slab_rows, depth), jnp.bfloat16),
            pltpu.SemaphoreType.DMA((len(cuts(width, step)) + 1,)),
        ],
        compiler_params=pltpu.CompilerParams(vmem_limit_bytes=project_bytes),
        cost_estimate=pl.CostEstimate(
            flops=2 * slab_rows * depth * (width + teacher_rows.shape[0]),
            bytes_accessed=2 * depth * (width + teacher_rows.shape[0]) + 4 * slab_rows * width,
            transcendentals=0,
        ),
    )(member, teacher_rows, proj_weight)


class Fetch:
    def __init__(self, sems):
        self.sems, self.used = sems, 0

    def start(self, source, target):
        copy = pltpu.make_async_copy(source, target, self.sems.at[self.used])
        copy.start()
        self.used += 1
        return copy


def multiply(read_rows, head, logit_ref, highest, step, ready=None):
    total = head.shape[1]
    highest[...] = jnp.full(highest.shape, -jnp.inf, jnp.float32)

    def one(index, start, size):
        at = pl.ds(start, size)
        if ready is not None:
            ready(index, at)
        part = jnp.dot(read_rows(), head[:, at], preferred_element_type=jnp.float32)
        logit_ref[:, at] = part
        top = part[:, :lanes]
        for lane in range(lanes, size, lanes):
            top = jnp.maximum(top, part[:, lane : lane + lanes])
        highest[...] = jnp.maximum(highest[...], top)

    def body(index, carry):
        one(index, pl.multiple_of(index * step, step), step)
        return carry

    full = total // step
    lax.fori_loop(0, full, body, 0)
    if total % step:
        one(full, full * step, total % step)


def as_columns(first, second, third):
    lane = lax.broadcasted_iota(jnp.int32, (first.shape[0], lanes), 1)
    return jnp.where(lane == 0, first, jnp.where(lane == 1, second, jnp.where(lane == 2, third, 0.0)))


def student_kernel(count, step, chunk, *refs):
    pieces, heads = refs[:count], refs[count : count + 2]
    column_ref, logit_ref, scaled_ref, stats_ref, head = refs[count + 2 : count + 7]
    held, highest, table, sems = refs[count + 7 :]
    depth, total = heads[0].shape
    blk = pieces[0].shape[0]
    fetch = Fetch(sems)
    waits = [fetch.start(piece, held.at[pl.ds(i * blk, blk)]) for i, piece in enumerate(pieces)]
    first = fetch.used

    def columns(half, at):
        return heads[half].at[:, at], head.at[pl.ds(half * depth, depth), at]

    for start, size in cuts(total, step):
        for half in range(2):
            fetch.start(*columns(half, pl.ds(start, size)))

    def ready(index, at):
        for half in range(2):
            pltpu.make_async_copy(*columns(half, at), sems.at[first + 2 * index + half]).wait()

    for wait in waits:
        wait.wait()
    multiply(lambda: held[...], head, logit_ref, highest, step, ready)

    def one(part, carry):
        rows = pl.ds(pl.multiple_of(part * chunk, chunk), chunk)
        logit = logit_ref[rows, :]
        top = jnp.max(highest[rows, :], axis=1, keepdims=True)
        scaled = jnp.exp(logit - top)
        hit = lax.broadcasted_iota(jnp.int32, logit.shape, 1) == column_ref[rows, :]
        picked = jnp.sum(jnp.where(hit, logit, 0.0), axis=1, keepdims=True)
        scaled_ref[rows, :] = scaled
        table[rows, :] = as_columns(top, jnp.sum(scaled, axis=1, keepdims=True), picked)
        return carry

    lax.fori_loop(0, logit_ref.shape[0] // chunk, one, 0)
    stats_ref[...] = table[...].T[0:8]


def teacher_kernel(count, step, chunk, *refs):
    pieces = refs[:count]
    head, stud_logit_ref, stud_ref, scaled_ref, stats_ref, highest, table = refs[count:]

    def read_rows():
        return jnp.concatenate([ref[...] for ref in pieces], axis=0) if count > 1 else pieces[0][...]

    multiply(read_rows, head, scaled_ref, highest, step)

    def one(part, carry):
        rows = pl.ds(pl.multiple_of(part * chunk, chunk), chunk)
        logit = scaled_ref[rows, :]
        top = jnp.max(highest[rows, :], axis=1, keepdims=True)
        scaled = jnp.exp(logit - top)
        gap = jnp.sum(scaled * (logit - stud_logit_ref[rows, :]), axis=1, keepdims=True)
        scaled_ref[rows, :] = scaled
        table[rows, :] = as_columns(top, jnp.sum(scaled, axis=1, keepdims=True), gap)
        return carry

    lax.fori_loop(0, scaled_ref.shape[0] // chunk, one, 0)
    teach = table[...].T[0:8]
    row = lax.broadcasted_iota(jnp.int32, teach.shape, 0)
    stats_ref[...] = jnp.where(row < 4, teach, pltpu.roll(stud_ref[...], 4, 0))


def head_cost(rows, head):
    depth, vocab_dev = head.shape
    return pl.CostEstimate(
        flops=2 * rows * depth * vocab_dev,
        bytes_accessed=2 * depth * vocab_dev + 12 * rows * vocab_dev,
        transcendentals=rows * vocab_dev,
    )


def student_logits(pieces, heads, column, step, chunk):
    rows, (depth, vocab_dev) = column.shape[0], heads[0].shape
    wide = (rows, vocab_dev)
    return pl.pallas_call(
        functools.partial(student_kernel, len(pieces), step, chunk),
        in_specs=[in_place] * (len(pieces) + 2) + [in_vmem],
        out_specs=[in_vmem] * 4,
        out_shape=[
            jax.ShapeDtypeStruct(wide, jnp.float32),
            jax.ShapeDtypeStruct(wide, jnp.float32),
            jax.ShapeDtypeStruct((8, rows), jnp.float32),
            jax.ShapeDtypeStruct((2 * depth, vocab_dev), jnp.bfloat16),
        ],
        scratch_shapes=[
            pltpu.VMEM((rows, 2 * depth), jnp.bfloat16),
            pltpu.VMEM((rows, lanes), jnp.float32),
            pltpu.VMEM((rows, lanes), jnp.float32),
            pltpu.SemaphoreType.DMA((len(pieces) + 2 * len(cuts(vocab_dev, step)),)),
        ],
        compiler_params=pltpu.CompilerParams(vmem_limit_bytes=vmem_bytes),
        cost_estimate=head_cost(rows, heads[0]),
    )(*pieces, *heads, column)


def teacher_logits(pieces, head, logit_stud, stats_stud, step, chunk):
    wide = logit_stud.shape
    return pl.pallas_call(
        functools.partial(teacher_kernel, len(pieces), step, chunk),
        in_specs=[in_vmem] * (len(pieces) + 3),
        out_specs=[in_vmem] * 2,
        out_shape=[
            jax.ShapeDtypeStruct(wide, jnp.float32),
            jax.ShapeDtypeStruct((8, wide[0]), jnp.float32),
        ],
        scratch_shapes=[pltpu.VMEM((wide[0], lanes), jnp.float32)] * 2,
        compiler_params=pltpu.CompilerParams(vmem_limit_bytes=vmem_bytes),
        cost_estimate=head_cost(wide[0], head),
    )(*pieces, head, logit_stud, stats_stud)


def swapped(values, distance):
    total = values.shape[1]
    lane = lax.broadcasted_iota(jnp.int32, values.shape, 1)
    return jnp.where(
        (lane & distance) != 0, pltpu.roll(values, distance, 1), pltpu.roll(values, total - distance, 1)
    )


def gradient_kernel(bits, step, chunk, place_ref, *refs):
    count = 1 << bits
    tables, refs = refs[:count], refs[count:]
    teach_ref, stud_ref, column_ref, head, loss_ref = refs[:5]
    outs = refs[5 : count + 5]
    entries, upstream, factors = refs[count + 5 :]
    rows = upstream.shape[0]
    blk = rows // count
    me = place_ref[0]
    for mask in range(count):
        values = tables[mask][...]
        for bit in range(bits):
            if mask >> bit & 1:
                values = swapped(values, blk << bit)
        entries[me ^ mask] = values
    every = entries[...]
    top_teach = jnp.max(every[:, 0:1], axis=0)
    top_stud = jnp.max(every[:, 4:5], axis=0)
    weight = jnp.exp(every[:, 0:1] - top_teach)
    total_teach = jnp.sum(weight * every[:, 1:2], axis=0)
    total_stud = jnp.sum(jnp.exp(every[:, 4:5] - top_stud) * every[:, 5:6], axis=0)
    lse_teach = top_teach + jnp.log(total_teach)
    lse_stud = top_stud + jnp.log(total_stud)
    gap = jnp.sum(weight * every[:, 2:3], axis=0) / total_teach
    loss = gap - lse_teach + 2.0 * lse_stud - jnp.sum(every[:, 6:7], axis=0)
    loss = jnp.broadcast_to(loss, loss_ref.shape)
    for bit in range(bits):
        loss = jnp.where(((me >> bit) & 1) == 1, swapped(loss, blk << bit), loss)
    loss_ref[...] = loss
    own = tables[0][...]
    scale_teach = -loss_scale * jnp.exp(own[0:1] - lse_teach)
    scale_stud = 2.0 * loss_scale * jnp.exp(own[4:5] - lse_stud)
    line = lax.broadcasted_iota(jnp.int32, (lanes, rows), 0)
    factors[...] = jnp.where(line == 0, scale_teach, scale_stud).T

    def one(part, carry):
        at = pl.ds(pl.multiple_of(part * chunk, chunk), chunk)
        hit = lax.broadcasted_iota(jnp.int32, (chunk, teach_ref.shape[1]), 1) == column_ref[at, :]
        both = teach_ref[at, :] * factors[at, 0:1] + stud_ref[at, :] * factors[at, 1:2]
        upstream[at, :] = jnp.where(hit, both - loss_scale, both).astype(jnp.bfloat16)
        return carry

    lax.fori_loop(0, rows // chunk, one, 0)

    def two(index, carry):
        at = pl.ds(pl.multiple_of(index * step, step), step)
        product = lax.dot_general(
            upstream[...], head[at, :], (((1,), (1,)), ((), ())), preferred_element_type=jnp.float32
        )
        for piece, out in enumerate(outs):
            out[:, at] = product[piece * blk : (piece + 1) * blk]
        return carry

    lax.fori_loop(0, head.shape[0] // step, two, 0)


def gradient(place, tables, scaled_teach, scaled_stud, column, head, bits, chunk):
    rows, vocab_dev = scaled_teach.shape
    count, width = 1 << bits, head.shape[0]
    step = 512 if width % 512 == 0 else width
    return pl.pallas_call(
        functools.partial(gradient_kernel, bits, step, chunk),
        in_specs=[in_smem] + [in_vmem] * (count + 4),
        out_specs=[in_vmem] * (count + 1),
        out_shape=[jax.ShapeDtypeStruct((8, rows), jnp.float32)]
        + [jax.ShapeDtypeStruct((rows // count, width), jnp.float32)] * count,
        scratch_shapes=[
            pltpu.VMEM((count, 8, rows), jnp.float32),
            pltpu.VMEM((rows, vocab_dev), jnp.bfloat16),
            pltpu.VMEM((rows, lanes), jnp.float32),
        ],
        compiler_params=pltpu.CompilerParams(vmem_limit_bytes=vmem_bytes),
        cost_estimate=head_cost(rows, head),
    )(place, *tables, scaled_teach, scaled_stud, column, head)


def tie(block, *others):
    return lax.optimization_barrier((block, *others))[0]


def make_body(vocab_size):
    bits = vocab_size.bit_length() - 1
    assert vocab_size == 1 << bits

    def swap(block, bit):
        return lax.ppermute(block, "vocab", [(at, at ^ (1 << bit)) for at in range(vocab_size)])

    def lowest(mask):
        return (mask & -mask).bit_length() - 1

    def spread(own, line):
        blocks = [own]
        for mask in range(1, vocab_size):
            bit = lowest(mask)
            block = blocks[mask ^ (1 << bit)]
            if bit == 0:
                block = tie(block, line[-2])
            blocks.append(swap(block, bit))
            if bit == 0:
                line.append(blocks[-1])
        return blocks

    def reduce_blocks(parts):
        terms, line = list(parts), []
        for mask in range(vocab_size - 1, 0, -1):
            bit = lowest(mask)
            block = terms[mask].astype(wire)
            if bit == 0 and line:
                block = tie(block, line[-1])
            block = swap(block, bit)
            if bit == 0:
                line.append(block)
            terms[mask ^ (1 << bit)] = terms[mask ^ (1 << bit)] + block.astype(jnp.float32)
        return terms[0], line

    def body(teacher_rows, owner, counts, proj_weight, student_hidden, head_weight, targets):
        teach_rows = teacher_rows.shape[0]
        slab_rows = targets.shape[0]
        vocab_dev = head_weight.shape[1]
        blk = slab_rows // vocab_size
        chunk = min(slab_rows, 32)
        me = lax.axis_index("vocab")
        core = lax.axis_index("seq")
        place = jnp.stack([me, core]).astype(jnp.int32)

        def in_order(vec):
            grid = vec.reshape((2,) * bits + (blk,))
            for bit in range(bits):
                grid = jnp.where((me >> bit) & 1 == 1, jnp.flip(grid, bits - 1 - bit), grid)
            return grid.reshape(slab_rows)

        def turned(block):
            return jnp.where(core == 1, jnp.roll(block, block.shape[1] // 2, axis=1), block)

        def as_pieces(blocks):
            return blocks if blk % 16 == 0 else [jnp.concatenate(blocks, axis=0)]

        heads = (head_weight, lax.ppermute(head_weight, "seq", [(0, 1), (1, 0)]))

        spot = lax.iota(jnp.int32, slab_rows)
        row_id = ((spot // blk) ^ me) * blk + spot % blk
        alive = lax.iota(jnp.int32, teach_rows) < counts[0]
        member = (owner[None, :] == row_id[:, None]) & alive[None, :]
        parts = project(member.astype(jnp.bfloat16), teacher_rows, proj_weight, vocab_size, 512 if student_hidden.shape[1] % 512 == 0 else student_hidden.shape[1])
        projected_own, line = reduce_blocks(parts)
        line.append(line[-1])
        hidden = spread(tie(turned(student_hidden), parts[-1]), line)
        projected = spread(turned(projected_own.astype(jnp.bfloat16)), line)

        column = (in_order(targets) - me * vocab_dev)[:, None]
        logit_stud, scaled_stud, stats_stud, head = student_logits(as_pieces(hidden), heads, column, 256, chunk)
        scaled_teach, stats = teacher_logits(as_pieces(projected), head, logit_stud, stats_stud, 512, chunk)
        tables = [stats] + [
            lax.ppermute(stats, "vocab", [(at, at ^ mask) for at in range(vocab_size)])
            for mask in range(1, vocab_size)
        ]
        loss, *terms = gradient(place, tables, scaled_teach, scaled_stud, column, head, bits, chunk)
        return (loss[0], turned(reduce_blocks(terms)[0].astype(jnp.bfloat16)))

    return body


def solution(mesh):
    return jax.shard_map(
        make_body(mesh.shape["vocab"]),
        mesh=mesh,
        in_specs=(
            P(("groups", "seq"), "vocab"),
            P(("groups", "seq")),
            P(("groups", "seq")),
            P("vocab", None),
            P(("groups", "seq", "vocab"), None),
            P("seq", "vocab"),
            P(("groups", "seq")),
        ),
        out_specs=(P(("groups", "seq")), P(("groups", "seq", "vocab"), None)),
        check_vma=False,
    )
```

time: 153 us -> 158 us (1.033)
  waiting for transfers between devices: 50 us -> 74.4 us
  starting transfers between devices: 44.4 us -> 34.3 us
  Pallas kernels: 42.9 us -> 35.7 us
  other arithmetic: 11.5 us -> 7.78 us
  local copies, waits for them, and re-layouts: 2.3 us -> 4.35 us
    ppermute x28, waiting for transfers between devices: 48.1 us -> 70.9 us  [swap(): lax.ppermute(block, 'vocab', [(at, at ^ 1 << bit) for at in range(vocab_s...]
    ppermute x28, starting transfers between devices: 32.7 us -> 22.6 us  [swap(): lax.ppermute(block, 'vocab', [(at, at ^ 1 << bit) for at in range(vocab_s...]
    pallas_call x3, Pallas kernels: 35.4 us -> 29.5 us  [the longest x1 12.5 us: student_logits(): pl.pallas_call(functools.partial(student_kernel, len(pieces), step, chunk...]
    unnamed x6, local copies, waits for them, and re-layouts: 1.44 us -> 3.48 us
    convert_element_type x14, other arithmetic: 7.79 us -> 5.75 us  [reduce_blocks(): block = terms[mask].astype(wire)]
  transfers between devices with their start and end apart: 36 -> 36, of which waited for: 17 -> 24; matrix products, arithmetic and copies ran while one was open for 8% -> 5% of each run, Pallas kernels for 13% -> 12%
where the time goes in v3:
time: 158 us
  waiting for transfers between devices  74.4 us (47%)
  Pallas kernels  35.7 us (23%)
  starting transfers between devices  34.3 us (22%)
  other arithmetic  7.78 us (5%)
  local copies, waits for them, and re-layouts  4.35 us (3%)
    ppermute x28, waiting for transfers between devices, swap(): lax.ppermute(block, 'vocab', [(at, at ^ 1 << bit) for at in range(vocab_s...  70.9 us
    ppermute x28, starting transfers between devices, swap(): lax.ppermute(block, 'vocab', [(at, at ^ 1 << bit) for at in range(vocab_s...  22.6 us
    pallas_call x1, Pallas kernels, student_logits(): pl.pallas_call(functools.partial(student_kernel, len(pieces), step, chunk...  12.5 us
    ppermute x7, starting transfers between devices, body(): lax.ppermute(stats, 'vocab', [(at, at ^ mask) for at in range(vocab_size)])  11.2 us
    pallas_call x1, Pallas kernels, teacher_logits(): pl.pallas_call(functools.partial(teacher_kernel, len(pieces), step, chunk...  8.61 us
    pallas_call x1, Pallas kernels, gradient(): pl.pallas_call(functools.partial(gradient_kernel, bits, step, chunk), in_...  8.37 us
    pallas_call x1, Pallas kernels, project(): pl.pallas_call(functools.partial(project_kernel, count, step), in_specs=[...  6.16 us
    convert_element_type x14, other arithmetic, reduce_blocks(): block = terms[mask].astype(wire)  5.75 us
  transfers between devices with their start and end apart: 36, of which 24 were waited for; matrix products, arithmetic and copies ran while one was open for 5% of the time, Pallas kernels for 12%

profile of v3, /device:TPU:0, one launch (start us, length us, event | category | flops | bytes accessed | tf_op | source)
XLA Modules:
  0.0 158.0 jit_solution(1051896010588663302)
XLA Ops:
  0.6 0.5 collective-permute-start.21
  1.8 0.8 and_convert_fusion.member_ref
  2.7 6.2 %shard_map.86 = (f32[32,3584]{1,0:T(8,128)S(1)}, f32[32,3584]{1,0:T(8,128)S(1)}, f32[32,3584]{1,0:T(8,128)S(1)}, f32[32,3584]{1,0:T(8,128)}, f32[32,3584]{1,0:T(...) custom-call(bf16[256,512]{1,0:T(8,128)(2,1)S(1)} %and_convert_fusion.member_ref, ...), custom_call_target="tpu_custom_call" | custom-call | flops 2147483648 | bytes 12058624 | tf_op jit(solution)/shard_map/pallas_call | solution.py:54
  8.8 1.0 convert_element_type.94
  9.9 2.6 %collective-permute-start = (f16[32,3584]{1,0:T(8,128)(2,1)S(1)}, f16[32,3584]{1,0:T(8,128)(2,1)S(1)}, u32[]{:S(2)}, u32[]{:S(2)}) collective-permute-start(f16[32,3584]{1,0:T(8,128)(2,1)S(1)} %convert_element_type.94), channel_id=1, source_target_pairs={{0,1},{1,0},{2,3},{3,2},{4,5},{5,4},{6,7},{7,6},{8,9},{9,8},{10,11... | collective-permute-start | bytes 688136 | tf_op jit(solution)/shard_map/ppermute | solution.py:322
  12.5 1.0 convert_element_type.98
  13.6 5.1 %collective-permute-done = f16[32,3584]{1,0:T(8,128)(2,1)S(1)} collective-permute-done((f16[32,3584]{1,0:T(8,128)(2,1)S(1)}, f16[32,3584]{1,0:T(8,128)(2,1)S(1)}, u32[]{:S(2)}, u32[]{:S(2)}) %collective-permute-start) | collective-permute-done | bytes 229408 | tf_op jit(solution)/shard_map/ppermute | solution.py:322
  18.8 1.7 %collective-permute-start.2 = (f16[32,3584]{1,0:T(8,128)(2,1)S(1)}, f16[32,3584]{1,0:T(8,128)(2,1)S(1)}, u32[]{:S(2)}, u32[]{:S(2)}) collective-permute-start(f16[32,3584]{1,0:T(8,128)(2,1)S(1)} %convert_element_type.98), channel_id=1, source_target_pairs={{0,1},{1,0},{2,3},{3,2},{4,5},{5,4},{6,7},{7,6},{8,9},{9,8},{10,11... | collective-permute-start | bytes 688136 | tf_op jit(solution)/shard_map/ppermute | solution.py:322
  20.5 1.1 add_convert_fusion.7
  21.6 1.6 %collective-permute-start.1 = (f16[32,3584]{1,0:T(8,128)(2,1)S(1)}, f16[32,3584]{1,0:T(8,128)(2,1)S(1)}, u32[]{:S(2)}, u32[]{:S(2)}) collective-permute-start(f16[32,3584]{1,0:T(8,128)(2,1)S(1)} %add_convert_fusion.7), channel_id=1, source_target_pairs={{0,2},{1,3},{2,0},{3,1},{4,6},{5,7},{6,4},{7,5},{8,10},{9,11},{10,... | collective-permute-start | bytes 688136 | tf_op jit(solution)/shard_map/ppermute | solution.py:322
  23.3 0.5 collective-permute-start.13
  23.8 2.6 %collective-permute-start.7 = (bf16[32,3584]{1,0:T(8,128)(2,1)S(1)}, bf16[32,3584]{1,0:T(8,128)(2,1)S(1)}, u32[]{:S(2)}, u32[]{:S(2)}) collective-permute-start(bf16[32,3584]{1,0:T(8,128)(2,1)S(1)} %maximum_select_fusion.1.refs_0_), channel_id=1, source_target_pairs={{0,4},{1,5},{2,6},{3,7},{4,0},{5,1},{6,2},{7,3},{8,12},{9,13},{10,... | collective-permute-start | bytes 688136 | tf_op jit(solution)/shard_map/ppermute | solution.py:322
  26.4 1.0 convert_element_type.102
  27.5 0.6 collective-permute-start.4
  28.0 7.0 %collective-permute-done.1 = f16[32,3584]{1,0:T(8,128)(2,1)S(1)} collective-permute-done((f16[32,3584]{1,0:T(8,128)(2,1)S(1)}, f16[32,3584]{1,0:T(8,128)(2,1)S(1)}, u32[]{:S(2)}, u32[]{:S(2)}) %collective-permute-start.1) | collective-permute-done | bytes 229408 | tf_op jit(solution)/shard_map/ppermute | solution.py:322
  35.1 1.1 add_convert_fusion.6
  36.2 1.8 %collective-permute-start.3 = (f16[32,3584]{1,0:T(8,128)(2,1)S(1)}, f16[32,3584]{1,0:T(8,128)(2,1)S(1)}, u32[]{:S(2)}, u32[]{:S(2)}) collective-permute-start(f16[32,3584]{1,0:T(8,128)(2,1)S(1)} %add_convert_fusion.6), channel_id=1, source_target_pairs={{0,4},{1,5},{2,6},{3,7},{4,0},{5,1},{6,2},{7,3},{8,12},{9,13},{10,... | collective-permute-start | bytes 688136 | tf_op jit(solution)/shard_map/ppermute | solution.py:322
  38.0 0.5 collective-permute-start.6
  38.5 0.6 collective-permute-done.7.refs_4_
  39.1 3.6 %collective-permute-start.5 = (f16[32,3584]{1,0:T(8,128)(2,1)S(1)}, f16[32,3584]{1,0:T(8,128)(2,1)S(1)}, u32[]{:S(2)}, u32[]{:S(2)}) collective-permute-start(f16[32,3584]{1,0:T(8,128)(2,1)S(1)} %add_convert_fusion.5), channel_id=1, source_target_pairs={{0,2},{1,3},{2,0},{3,1},{4,6},{5,7},{6,4},{7,5},{8,10},{9,11},{10,... | collective-permute-start | bytes 688136 | tf_op jit(solution)/shard_map/ppermute | solution.py:322
  42.7 1.3 collective-permute-done.6
  44.0 4.2 %collective-permute-start.12 = (bf16[32,3584]{1,0:T(8,128)(2,1)S(1)}, bf16[32,3584]{1,0:T(8,128)(2,1)S(1)}, u32[]{:S(2)}, u32[]{:S(2)}) collective-permute-start(bf16[32,3584]{1,0:T(8,128)(2,1)S(1)} %collective-permute-done.7.refs_4_), channel_id=1, source_target_pairs={{0,2},{1,3},{2,0},{3,1},{4,6},{5,7},{6,4},{7,5},{8,10},{9,11},{10,... | collective-permute-start | bytes 688136 | tf_op jit(solution)/shard_map/ppermute | solution.py:322
  48.2 0.5 collective-permute-start.8
  48.7 1.4 collective-permute-done.3
  50.1 0.6 collective-permute-start.14
  50.7 1.8 %collective-permute-done.5 = f16[32,3584]{1,0:T(8,128)(2,1)S(1)} collective-permute-done((f16[32,3584]{1,0:T(8,128)(2,1)S(1)}, f16[32,3584]{1,0:T(8,128)(2,1)S(1)}, u32[]{:S(2)}, u32[]{:S(2)}) %collective-permute-start.5) | collective-permute-done | bytes 229408 | tf_op jit(solution)/shard_map/ppermute | solution.py:322
  52.8 3.4 %collective-permute-done.8.refs_1_ = bf16[32,3584]{1,0:T(8,128)(2,1)S(1)} collective-permute-done((bf16[32,3584]{1,0:T(8,128)(2,1)S(1)}, bf16[32,3584]{1,0:T(8,128)(2,1)S(1)}, u32[]{:S(2)}, u32[]{:S(2)}) %collective-permute-start.8) | collective-permute-done | bytes 229408 | tf_op jit(solution)/shard_map/ppermute | solution.py:322
  56.2 0.2 collective-permute-start.9
  56.4 0.8 collective-permute-done.12.refs_6_
  57.2 4.0 %collective-permute-done.14.refs_3_ = bf16[32,3584]{1,0:T(8,128)(2,1)S(1)} collective-permute-done((bf16[32,3584]{1,0:T(8,128)(2,1)S(1)}, bf16[32,3584]{1,0:T(8,128)(2,1)S(1)}, u32[]{:S(2)}, u32[]{:S(2)}) %collective-permute-start.14) | collective-permute-done | bytes 229408 | tf_op jit(solution)/shard_map/ppermute | solution.py:322
  61.1 0.2 collective-permute-start.15
  61.4 2.3 %collective-permute-done.17.refs_4_ = bf16[32,3584]{1,0:T(8,128)(2,1)S(1)} collective-permute-done((bf16[32,3584]{1,0:T(8,128)(2,1)S(1)}, bf16[32,3584]{1,0:T(8,128)(2,1)S(1)}, u32[]{:S(2)}, u32[]{:S(2)}) %collective-permute-start.17) | collective-permute-done | bytes 229408 | tf_op jit(solution)/shard_map/ppermute | solution.py:322
  63.7 2.3 %collective-permute-done.9.refs_5_ = bf16[32,3584]{1,0:T(8,128)(2,1)S(1)} collective-permute-done((bf16[32,3584]{1,0:T(8,128)(2,1)S(1)}, bf16[32,3584]{1,0:T(8,128)(2,1)S(1)}, u32[]{:S(2)}, u32[]{:S(2)}) %collective-permute-start.9) | collective-permute-done | bytes 229408 | tf_op jit(solution)/shard_map/ppermute | solution.py:322
  66.0 0.2 collective-permute-start.10
  66.3 4.7 %collective-permute-done.15.refs_7_ = bf16[32,3584]{1,0:T(8,128)(2,1)S(1)} collective-permute-done((bf16[32,3584]{1,0:T(8,128)(2,1)S(1)}, bf16[32,3584]{1,0:T(8,128)(2,1)S(1)}, u32[]{:S(2)}, u32[]{:S(2)}) %collective-permute-start.15) | collective-permute-done | bytes 229408 | tf_op jit(solution)/shard_map/ppermute | solution.py:322
  71.0 0.2 collective-permute-start.16
  71.1 4.7 %collective-permute-done.10.refs_1_ = bf16[32,3584]{1,0:T(8,128)(2,1)S(1)} collective-permute-done((bf16[32,3584]{1,0:T(8,128)(2,1)S(1)}, bf16[32,3584]{1,0:T(8,128)(2,1)S(1)}, u32[]{:S(2)}, u32[]{:S(2)}) %collective-permute-start.10) | collective-permute-done | bytes 229408 | tf_op jit(solution)/shard_map/ppermute | solution.py:322
  75.9 0.2 collective-permute-start.18
  76.0 4.7 %collective-permute-done.16.refs_3_ = bf16[32,3584]{1,0:T(8,128)(2,1)S(1)} collective-permute-done((bf16[32,3584]{1,0:T(8,128)(2,1)S(1)}, bf16[32,3584]{1,0:T(8,128)(2,1)S(1)}, u32[]{:S(2)}, u32[]{:S(2)}) %collective-permute-start.16) | collective-permute-done | bytes 229408 | tf_op jit(solution)/shard_map/ppermute | solution.py:322
  80.8 0.2 collective-permute-start.20
  81.0 0.1 sub.26.refs_10_
  81.1 3.5 %copy-done = bf16[1792,2432]{1,0:T(8,128)(2,1)S(1)} copy-done((bf16[1792,2432]{1,0:T(8,128)(2,1)S(1)}, bf16[1792,2432]{1,0:T(8,128)(2,1)}, u32[]{:S(2)}) %copy-start) | copy-done | bytes 8716312
  84.6 12.5 %shard_map.87 = (f32[256,2432]{1,0:T(8,128)S(1)}, f32[256,2432]{1,0:T(8,128)S(1)}, f32[8,256]{1,0:T(8,128)S(1)}, bf16[3584,2432]{1,0:T(8,128)(2,1)S(1)}) custom-call(bf16[32,3584]{1,0:T(8,128)(2,1)S(1)} %maximum_select_fusion.1.refs_0_, bf16[32,3584]{1,0:T(8,128)(2,1)S(1)} %collective-permute-done.8.refs_1_, ...), custom_call_target="tpu_custom_call" | custom-call | flops 2231369728 | bytes 16187392 | tf_op jit(solution)/shard_map/pallas_call | solution.py:192
  97.1 8.6 %shard_map.88 = (f32[256,2432]{1,0:T(8,128)S(1)}, f32[8,256]{1,0:T(8,128)S(1)}) custom-call(bf16[32,3584]{1,0:T(8,128)(2,1)S(1)} %maximum_select_fusion.refs_0_, bf16[32,3584]{1,0:T(8,128)(2,1)S(1)} %collective-permute-done.10.refs_1_, bf16[32,3584]{1,0:T(8,128)(2,1)S(1)} %collective-permute-done.11.refs_2_, ...), custom_call_target="tpu_custom_call" | custom-call | flops 4462739456 | bytes 24903680 | tf_op jit(solution)/shard_map/pallas_call | solution.py:215
  105.8 0.4 collective-permute-start.28
  106.1 4.8 %collective-permute-start.27 = (f32[8,256]{1,0:T(8,128)S(1)}, f32[8,256]{1,0:T(8,128)S(1)}, u32[]{:S(2)}, u32[]{:S(2)}) collective-permute-start(f32[8,256]{1,0:T(8,128)S(1)} %get-tuple-element.63.refs_0_), channel_id=1, source_target_pairs={{0,6},{1,7},{2,4},{3,5},{4,2},{5,3},{6,0},{7,1},{8,14},{9,15},{10,... | collective-permute-start | bytes 24584 | tf_op jit(solution)/shard_map/ppermute | solution.py:390
  110.9 2.5 %collective-permute-start.25 = (f32[8,256]{1,0:T(8,128)S(1)}, f32[8,256]{1,0:T(8,128)S(1)}, u32[]{:S(2)}, u32[]{:S(2)}) collective-permute-start(f32[8,256]{1,0:T(8,128)S(1)} %get-tuple-element.63.refs_0_), channel_id=1, source_target_pairs={{0,4},{1,5},{2,6},{3,7},{4,0},{5,1},{6,2},{7,3},{8,12},{9,13},{10,... | collective-permute-start | bytes 24584 | tf_op jit(solution)/shard_map/ppermute | solution.py:390
  113.5 3.3 %collective-permute-start.23 = (f32[8,256]{1,0:T(8,128)S(1)}, f32[8,256]{1,0:T(8,128)S(1)}, u32[]{:S(2)}, u32[]{:S(2)}) collective-permute-start(f32[8,256]{1,0:T(8,128)S(1)} %get-tuple-element.63.refs_0_), channel_id=1, source_target_pairs={{0,2},{1,3},{2,0},{3,1},{4,6},{5,7},{6,4},{7,5},{8,10},{9,11},{10,... | collective-permute-start | bytes 24584 | tf_op jit(solution)/shard_map/ppermute | solution.py:390
  116.8 0.2 collective-permute-start.22
  117.0 1.0 collective-permute-done.24.refs_3_
  118.0 0.5 collective-permute-done.23.refs_2_
  118.5 1.9 %collective-permute-done.22.refs_1_ = f32[8,256]{1,0:T(8,128)S(1)} collective-permute-done((f32[8,256]{1,0:T(8,128)S(1)}, f32[8,256]{1,0:T(8,128)S(1)}, u32[]{:S(2)}, u32[]{:S(2)}) %collective-permute-start.22) | collective-permute-done | bytes 8224 | tf_op jit(solution)/shard_map/ppermute | solution.py:390
  120.4 8.4 %shard_map.89 = (f32[8,256]{1,0:T(8,128)S(1)}, f32[32,3584]{1,0:T(8,128)S(1)}, f32[32,3584]{1,0:T(8,128)S(1)}, f32[32,3584]{1,0:T(8,128)S(1)}, f32[32,3584]{1,0:...) custom-call(s32[2]{0:T(128)S(1)} %pad_add_fusion.place_ref, ...), custom_call_target="tpu_custom_call" | custom-call | flops 4462739456 | bytes 24903680 | tf_op jit(solution)/shard_map/pallas_call | solution.py:297
  128.8 0.2 collective-permute-start.29
  129.1 6.4 %collective-permute-done.29 = f16[32,3584]{1,0:T(8,128)(2,1)S(1)} collective-permute-done((f16[32,3584]{1,0:T(8,128)(2,1)S(1)}, f16[32,3584]{1,0:T(8,128)(2,1)S(1)}, u32[]{:S(2)}, u32[]{:S(2)}) %collective-permute-start.29) | collective-permute-done | bytes 229408 | tf_op jit(solution)/shard_map/ppermute | solution.py:322
  135.5 0.3 collective-permute-start.30
  135.9 7.3 %collective-permute-done.31 = f16[32,3584]{1,0:T(8,128)(2,1)S(1)} collective-permute-done((f16[32,3584]{1,0:T(8,128)(2,1)S(1)}, f16[32,3584]{1,0:T(8,128)(2,1)S(1)}, u32[]{:S(2)}, u32[]{:S(2)}) %collective-permute-start.31) | collective-permute-done | bytes 229408 | tf_op jit(solution)/shard_map/ppermute | solution.py:322
  143.2 2.9 %collective-permute-done.30 = f16[32,3584]{1,0:T(8,128)(2,1)S(1)} collective-permute-done((f16[32,3584]{1,0:T(8,128)(2,1)S(1)}, f16[32,3584]{1,0:T(8,128)(2,1)S(1)}, u32[]{:S(2)}, u32[]{:S(2)}) %collective-permute-start.30) | collective-permute-done | bytes 229408 | tf_op jit(solution)/shard_map/ppermute | solution.py:322
  146.3 2.9 %collective-permute-done.33 = f16[32,3584]{1,0:T(8,128)(2,1)S(1)} collective-permute-done((f16[32,3584]{1,0:T(8,128)(2,1)S(1)}, f16[32,3584]{1,0:T(8,128)(2,1)S(1)}, u32[]{:S(2)}, u32[]{:S(2)}) %collective-permute-start.33) | collective-permute-done | bytes 229408 | tf_op jit(solution)/shard_map/ppermute | solution.py:322
  149.4 0.6 slice.27
  149.9 4.8 %collective-permute-done.32 = f16[32,3584]{1,0:T(8,128)(2,1)S(1)} collective-permute-done((f16[32,3584]{1,0:T(8,128)(2,1)S(1)}, f16[32,3584]{1,0:T(8,128)(2,1)S(1)}, u32[]{:S(2)}, u32[]{:S(2)}) %collective-permute-start.32) | collective-permute-done | bytes 229408 | tf_op jit(solution)/shard_map/ppermute | solution.py:322
  154.7 0.5 collective-permute-done.35
  155.2 1.8 %collective-permute-done.34 = f16[32,3584]{1,0:T(8,128)(2,1)S(1)} collective-permute-done((f16[32,3584]{1,0:T(8,128)(2,1)S(1)}, f16[32,3584]{1,0:T(8,128)(2,1)S(1)}, u32[]{:S(2)}, u32[]{:S(2)}) %collective-permute-start.34) | collective-permute-done | bytes 229408 | tf_op jit(solution)/shard_map/ppermute | solution.py:322
  157.2 0.8 maximum_select_fusion.2
  (51 shorter events, 1.4 us)
Async XLA Ops:
  0.6 12.9 %copy-start.1 = (bf16[32,3584]{1,0:T(8,128)(2,1)S(1)}, bf16[32,3584]{1,0:T(8,128)(2,1)}, u32[]{:S(2)}) copy-start(bf16[32,3584]{1,0:T(8,128)(2,1)} %param.11) | copy-start | bytes 688132
  0.6 80.5 %collective-permute-start.21 = (bf16[1792,2432]{1,0:T(8,128)(2,1)}, bf16[1792,2432]{1,0:T(8,128)(2,1)}, u32[]{:S(2)}, u32[]{:S(2)}) collective-permute-start(bf16[1792,2432]{1,0:T(8,128)(2,1)} %refs_8_.1), channel_id=1, source_target_pairs={{0,8},{8,0},{1,9},{9,1},{2,10},{10,2},{3,11},{11,3},{4,12},{12,4},... | collective-permute-start | bytes 26148872 | tf_op jit(solution)/shard_map/ppermute | solution.py:374
  2.7 58.6 %copy-start.2 = (s32[256]{0:T(256)S(1)}, s32[256]{0:T(256)}, u32[]{:S(2)}) copy-start(s32[256]{0:T(256)} %param.13) | copy-start | bytes 3076
  9.9 8.9 %collective-permute-start = (f16[32,3584]{1,0:T(8,128)(2,1)S(1)}, f16[32,3584]{1,0:T(8,128)(2,1)S(1)}, u32[]{:S(2)}, u32[]{:S(2)}) collective-permute-start(f16[32,3584]{1,0:T(8,128)(2,1)S(1)} %convert_element_type.94), channel_id=1, source_target_pairs={{0,1},{1,0},{2,3},{3,2},{4,5},{5,4},{6,7},{7,6},{8,9},{9,8},{10,11... | collective-permute-start | bytes 688136 | tf_op jit(solution)/shard_map/ppermute | solution.py:322
  18.8 8.7 %collective-permute-start.2 = (f16[32,3584]{1,0:T(8,128)(2,1)S(1)}, f16[32,3584]{1,0:T(8,128)(2,1)S(1)}, u32[]{:S(2)}, u32[]{:S(2)}) collective-permute-start(f16[32,3584]{1,0:T(8,128)(2,1)S(1)} %convert_element_type.98), channel_id=1, source_target_pairs={{0,1},{1,0},{2,3},{3,2},{4,5},{5,4},{6,7},{7,6},{8,9},{9,8},{10,11... | collective-permute-start | bytes 688136 | tf_op jit(solution)/shard_map/ppermute | solution.py:322
  21.6 13.5 %collective-permute-start.1 = (f16[32,3584]{1,0:T(8,128)(2,1)S(1)}, f16[32,3584]{1,0:T(8,128)(2,1)S(1)}, u32[]{:S(2)}, u32[]{:S(2)}) collective-permute-start(f16[32,3584]{1,0:T(8,128)(2,1)S(1)} %add_convert_fusion.7), channel_id=1, source_target_pairs={{0,2},{1,3},{2,0},{3,1},{4,6},{5,7},{6,4},{7,5},{8,10},{9,11},{10,... | collective-permute-start | bytes 688136 | tf_op jit(solution)/shard_map/ppermute | solution.py:322
  23.3 24.9 %collective-permute-start.13 = (bf16[32,3584]{1,0:T(8,128)(2,1)S(1)}, bf16[32,3584]{1,0:T(8,128)(2,1)S(1)}, u32[]{:S(2)}, u32[]{:S(2)}) collective-permute-start(bf16[32,3584]{1,0:T(8,128)(2,1)S(1)} %maximum_select_fusion.1.refs_0_), channel_id=1, source_target_pairs={{0,2},{1,3},{2,0},{3,1},{4,6},{5,7},{6,4},{7,5},{8,10},{9,11},{10,... | collective-permute-start | bytes 688136 | tf_op jit(solution)/shard_map/ppermute | solution.py:322
  23.8 15.4 %collective-permute-start.7 = (bf16[32,3584]{1,0:T(8,128)(2,1)S(1)}, bf16[32,3584]{1,0:T(8,128)(2,1)S(1)}, u32[]{:S(2)}, u32[]{:S(2)}) collective-permute-start(bf16[32,3584]{1,0:T(8,128)(2,1)S(1)} %maximum_select_fusion.1.refs_0_), channel_id=1, source_target_pairs={{0,4},{1,5},{2,6},{3,7},{4,0},{5,1},{6,2},{7,3},{8,12},{9,13},{10,... | collective-permute-start | bytes 688136 | tf_op jit(solution)/shard_map/ppermute | solution.py:322
  27.5 10.5 %collective-permute-start.4 = (f16[32,3584]{1,0:T(8,128)(2,1)S(1)}, f16[32,3584]{1,0:T(8,128)(2,1)S(1)}, u32[]{:S(2)}, u32[]{:S(2)}) collective-permute-start(f16[32,3584]{1,0:T(8,128)(2,1)S(1)} %convert_element_type.102), channel_id=1, source_target_pairs={{0,1},{1,0},{2,3},{3,2},{4,5},{5,4},{6,7},{7,6},{8,9},{9,8},{10,11... | collective-permute-start | bytes 688136 | tf_op jit(solution)/shard_map/ppermute | solution.py:322
  36.2 13.9 %collective-permute-start.3 = (f16[32,3584]{1,0:T(8,128)(2,1)S(1)}, f16[32,3584]{1,0:T(8,128)(2,1)S(1)}, u32[]{:S(2)}, u32[]{:S(2)}) collective-permute-start(f16[32,3584]{1,0:T(8,128)(2,1)S(1)} %add_convert_fusion.6), channel_id=1, source_target_pairs={{0,4},{1,5},{2,6},{3,7},{4,0},{5,1},{6,2},{7,3},{8,12},{9,13},{10,... | collective-permute-start | bytes 688136 | tf_op jit(solution)/shard_map/ppermute | solution.py:322
  38.0 6.0 %collective-permute-start.6 = (f16[32,3584]{1,0:T(8,128)(2,1)S(1)}, f16[32,3584]{1,0:T(8,128)(2,1)S(1)}, u32[]{:S(2)}, u32[]{:S(2)}) collective-permute-start(f16[32,3584]{1,0:T(8,128)(2,1)S(1)} %convert_element_type.106), channel_id=1, source_target_pairs={{0,1},{1,0},{2,3},{3,2},{4,5},{5,4},{6,7},{7,6},{8,9},{9,8},{10,11... | collective-permute-start | bytes 688136 | tf_op jit(solution)/shard_map/ppermute | solution.py:322
  39.1 13.4 %collective-permute-start.5 = (f16[32,3584]{1,0:T(8,128)(2,1)S(1)}, f16[32,3584]{1,0:T(8,128)(2,1)S(1)}, u32[]{:S(2)}, u32[]{:S(2)}) collective-permute-start(f16[32,3584]{1,0:T(8,128)(2,1)S(1)} %add_convert_fusion.5), channel_id=1, source_target_pairs={{0,2},{1,3},{2,0},{3,1},{4,6},{5,7},{6,4},{7,5},{8,10},{9,11},{10,... | collective-permute-start | bytes 688136 | tf_op jit(solution)/shard_map/ppermute | solution.py:322
  44.0 13.2 %collective-permute-start.12 = (bf16[32,3584]{1,0:T(8,128)(2,1)S(1)}, bf16[32,3584]{1,0:T(8,128)(2,1)S(1)}, u32[]{:S(2)}, u32[]{:S(2)}) collective-permute-start(bf16[32,3584]{1,0:T(8,128)(2,1)S(1)} %collective-permute-done.7.refs_4_), channel_id=1, source_target_pairs={{0,2},{1,3},{2,0},{3,1},{4,6},{5,7},{6,4},{7,5},{8,10},{9,11},{10,... | collective-permute-start | bytes 688136 | tf_op jit(solution)/shard_map/ppermute | solution.py:322
  48.2 8.0 %collective-permute-start.8 = (bf16[32,3584]{1,0:T(8,128)(2,1)S(1)}, bf16[32,3584]{1,0:T(8,128)(2,1)S(1)}, u32[]{:S(2)}, u32[]{:S(2)}) collective-permute-start(bf16[32,3584]{1,0:T(8,128)(2,1)S(1)} %maximum_select_fusion.1.refs_0_), channel_id=1, source_target_pairs={{0,1},{1,0},{2,3},{3,2},{4,5},{5,4},{6,7},{7,6},{8,9},{9,8},{10,11... | collective-permute-start | bytes 688136 | tf_op jit(solution)/shard_map/ppermute | solution.py:322
  50.1 11.0 %collective-permute-start.14 = (bf16[32,3584]{1,0:T(8,128)(2,1)S(1)}, bf16[32,3584]{1,0:T(8,128)(2,1)S(1)}, u32[]{:S(2)}, u32[]{:S(2)}) collective-permute-start(bf16[32,3584]{1,0:T(8,128)(2,1)S(1)} %collective-permute-done.13.refs_2_), channel_id=1, source_target_pairs={{0,1},{1,0},{2,3},{3,2},{4,5},{5,4},{6,7},{7,6},{8,9},{9,8},{10,11... | collective-permute-start | bytes 688136 | tf_op jit(solution)/shard_map/ppermute | solution.py:322
  52.7 11.0 %collective-permute-start.17 = (bf16[32,3584]{1,0:T(8,128)(2,1)S(1)}, bf16[32,3584]{1,0:T(8,128)(2,1)S(1)}, u32[]{:S(2)}, u32[]{:S(2)}) collective-permute-start(bf16[32,3584]{1,0:T(8,128)(2,1)S(1)} %maximum_select_fusion.refs_0_), channel_id=1, source_target_pairs={{0,4},{1,5},{2,6},{3,7},{4,0},{5,1},{6,2},{7,3},{8,12},{9,13},{10,... | collective-permute-start | bytes 688136 | tf_op jit(solution)/shard_map/ppermute | solution.py:322
  56.2 9.8 %collective-permute-start.9 = (bf16[32,3584]{1,0:T(8,128)(2,1)S(1)}, bf16[32,3584]{1,0:T(8,128)(2,1)S(1)}, u32[]{:S(2)}, u32[]{:S(2)}) collective-permute-start(bf16[32,3584]{1,0:T(8,128)(2,1)S(1)} %collective-permute-done.7.refs_4_), channel_id=1, source_target_pairs={{0,1},{1,0},{2,3},{3,2},{4,5},{5,4},{6,7},{7,6},{8,9},{9,8},{10,11... | collective-permute-start | bytes 688136 | tf_op jit(solution)/shard_map/ppermute | solution.py:322
  57.2 9.1 %collective-permute-start.11 = (bf16[32,3584]{1,0:T(8,128)(2,1)S(1)}, bf16[32,3584]{1,0:T(8,128)(2,1)S(1)}, u32[]{:S(2)}, u32[]{:S(2)}) collective-permute-start(bf16[32,3584]{1,0:T(8,128)(2,1)S(1)} %maximum_select_fusion.refs_0_), channel_id=1, source_target_pairs={{0,2},{1,3},{2,0},{3,1},{4,6},{5,7},{6,4},{7,5},{8,10},{9,11},{10,... | collective-permute-start | bytes 688136 | tf_op jit(solution)/shard_map/ppermute | solution.py:322
  61.1 9.8 %collective-permute-start.15 = (bf16[32,3584]{1,0:T(8,128)(2,1)S(1)}, bf16[32,3584]{1,0:T(8,128)(2,1)S(1)}, u32[]{:S(2)}, u32[]{:S(2)}) collective-permute-start(bf16[32,3584]{1,0:T(8,128)(2,1)S(1)} %collective-permute-done.12.refs_6_), channel_id=1, source_target_pairs={{0,1},{1,0},{2,3},{3,2},{4,5},{5,4},{6,7},{7,6},{8,9},{9,8},{10,11... | collective-permute-start | bytes 688136 | tf_op jit(solution)/shard_map/ppermute | solution.py:322
  63.7 12.3 %collective-permute-start.19 = (bf16[32,3584]{1,0:T(8,128)(2,1)S(1)}, bf16[32,3584]{1,0:T(8,128)(2,1)S(1)}, u32[]{:S(2)}, u32[]{:S(2)}) collective-permute-start(bf16[32,3584]{1,0:T(8,128)(2,1)S(1)} %collective-permute-done.17.refs_4_), channel_id=1, source_target_pairs={{0,2},{1,3},{2,0},{3,1},{4,6},{5,7},{6,4},{7,5},{8,10},{9,11},{10,... | collective-permute-start | bytes 688136 | tf_op jit(solution)/shard_map/ppermute | solution.py:322
  66.0 9.8 %collective-permute-start.10 = (bf16[32,3584]{1,0:T(8,128)(2,1)S(1)}, bf16[32,3584]{1,0:T(8,128)(2,1)S(1)}, u32[]{:S(2)}, u32[]{:S(2)}) collective-permute-start(bf16[32,3584]{1,0:T(8,128)(2,1)S(1)} %maximum_select_fusion.refs_0_), channel_id=1, source_target_pairs={{0,1},{1,0},{2,3},{3,2},{4,5},{5,4},{6,7},{7,6},{8,9},{9,8},{10,11... | collective-permute-start | bytes 688136 | tf_op jit(solution)/shard_map/ppermute | solution.py:322
  71.0 9.8 %collective-permute-start.16 = (bf16[32,3584]{1,0:T(8,128)(2,1)S(1)}, bf16[32,3584]{1,0:T(8,128)(2,1)S(1)}, u32[]{:S(2)}, u32[]{:S(2)}) collective-permute-start(bf16[32,3584]{1,0:T(8,128)(2,1)S(1)} %collective-permute-done.11.refs_2_), channel_id=1, source_target_pairs={{0,1},{1,0},{2,3},{3,2},{4,5},{5,4},{6,7},{7,6},{8,9},{9,8},{10,11... | collective-permute-start | bytes 688136 | tf_op jit(solution)/shard_map/ppermute | solution.py:322
  75.9 21.3 %collective-permute-start.18 = (bf16[32,3584]{1,0:T(8,128)(2,1)S(1)}, bf16[32,3584]{1,0:T(8,128)(2,1)}, u32[]{:S(2)}, u32[]{:S(2)}) collective-permute-start(bf16[32,3584]{1,0:T(8,128)(2,1)S(1)} %collective-permute-done.17.refs_4_), channel_id=1, source_target_pairs={{0,1},{1,0},{2,3},{3,2},{4,5},{5,4},{6,7},{7,6},{8,9},{9,8},{10,11... | collective-permute-start | bytes 688136 | tf_op jit(solution)/shard_map/ppermute | solution.py:322
  80.8 16.3 %collective-permute-start.20 = (bf16[32,3584]{1,0:T(8,128)(2,1)S(1)}, bf16[32,3584]{1,0:T(8,128)(2,1)}, u32[]{:S(2)}, u32[]{:S(2)}) collective-permute-start(bf16[32,3584]{1,0:T(8,128)(2,1)S(1)} %collective-permute-done.19.refs_6_), channel_id=1, source_target_pairs={{0,1},{1,0},{2,3},{3,2},{4,5},{5,4},{6,7},{7,6},{8,9},{9,8},{10,11... | collective-permute-start | bytes 688136 | tf_op jit(solution)/shard_map/ppermute | solution.py:322
  81.1 3.5 %copy-start = (bf16[1792,2432]{1,0:T(8,128)(2,1)S(1)}, bf16[1792,2432]{1,0:T(8,128)(2,1)}, u32[]{:S(2)}) copy-start(bf16[1792,2432]{1,0:T(8,128)(2,1)} %refs_8_.1) | copy-start | bytes 26148868
  105.8 7.7 %collective-permute-start.28 = (f32[8,256]{1,0:T(8,128)S(1)}, f32[8,256]{1,0:T(8,128)S(1)}, u32[]{:S(2)}, u32[]{:S(2)}) collective-permute-start(f32[8,256]{1,0:T(8,128)S(1)} %get-tuple-element.63.refs_0_), channel_id=1, source_target_pairs={{0,7},{1,6},{2,5},{3,4},{4,3},{5,2},{6,1},{7,0},{8,15},{9,14},{10,... | collective-permute-start | bytes 24584 | tf_op jit(solution)/shard_map/ppermute | solution.py:390
  106.1 10.6 %collective-permute-start.27 = (f32[8,256]{1,0:T(8,128)S(1)}, f32[8,256]{1,0:T(8,128)S(1)}, u32[]{:S(2)}, u32[]{:S(2)}) collective-permute-start(f32[8,256]{1,0:T(8,128)S(1)} %get-tuple-element.63.refs_0_), channel_id=1, source_target_pairs={{0,6},{1,7},{2,4},{3,5},{4,2},{5,3},{6,0},{7,1},{8,14},{9,15},{10,... | collective-permute-start | bytes 24584 | tf_op jit(solution)/shard_map/ppermute | solution.py:390
  110.9 6.1 %collective-permute-start.26 = (f32[8,256]{1,0:T(8,128)S(1)}, f32[8,256]{1,0:T(8,128)S(1)}, u32[]{:S(2)}, u32[]{:S(2)}) collective-permute-start(f32[8,256]{1,0:T(8,128)S(1)} %get-tuple-element.63.refs_0_), channel_id=1, source_target_pairs={{0,5},{1,4},{2,7},{3,6},{4,1},{5,0},{6,3},{7,2},{8,13},{9,12},{10,... | collective-permute-start | bytes 24584 | tf_op jit(solution)/shard_map/ppermute | solution.py:390
  110.9 6.1 %collective-permute-start.25 = (f32[8,256]{1,0:T(8,128)S(1)}, f32[8,256]{1,0:T(8,128)S(1)}, u32[]{:S(2)}, u32[]{:S(2)}) collective-permute-start(f32[8,256]{1,0:T(8,128)S(1)} %get-tuple-element.63.refs_0_), channel_id=1, source_target_pairs={{0,4},{1,5},{2,6},{3,7},{4,0},{5,1},{6,2},{7,3},{8,12},{9,13},{10,... | collective-permute-start | bytes 24584 | tf_op jit(solution)/shard_map/ppermute | solution.py:390
  113.4 4.5 %collective-permute-start.24 = (f32[8,256]{1,0:T(8,128)S(1)}, f32[8,256]{1,0:T(8,128)S(1)}, u32[]{:S(2)}, u32[]{:S(2)}) collective-permute-start(f32[8,256]{1,0:T(8,128)S(1)} %get-tuple-element.63.refs_0_), channel_id=1, source_target_pairs={{0,3},{1,2},{2,1},{3,0},{4,7},{5,6},{6,5},{7,4},{8,11},{9,10},{10,... | collective-permute-start | bytes 24584 | tf_op jit(solution)/shard_map/ppermute | solution.py:390
  113.5 5.0 %collective-permute-start.23 = (f32[8,256]{1,0:T(8,128)S(1)}, f32[8,256]{1,0:T(8,128)S(1)}, u32[]{:S(2)}, u32[]{:S(2)}) collective-permute-start(f32[8,256]{1,0:T(8,128)S(1)} %get-tuple-element.63.refs_0_), channel_id=1, source_target_pairs={{0,2},{1,3},{2,0},{3,1},{4,6},{5,7},{6,4},{7,5},{8,10},{9,11},{10,... | collective-permute-start | bytes 24584 | tf_op jit(solution)/shard_map/ppermute | solution.py:390
  116.8 3.7 %collective-permute-start.22 = (f32[8,256]{1,0:T(8,128)S(1)}, f32[8,256]{1,0:T(8,128)S(1)}, u32[]{:S(2)}, u32[]{:S(2)}) collective-permute-start(f32[8,256]{1,0:T(8,128)S(1)} %get-tuple-element.63.refs_0_), channel_id=1, source_target_pairs={{0,1},{1,0},{2,3},{3,2},{4,5},{5,4},{6,7},{7,6},{8,9},{9,8},{10,11... | collective-permute-start | bytes 24584 | tf_op jit(solution)/shard_map/ppermute | solution.py:390
  128.8 6.6 %collective-permute-start.29 = (f16[32,3584]{1,0:T(8,128)(2,1)S(1)}, f16[32,3584]{1,0:T(8,128)(2,1)S(1)}, u32[]{:S(2)}, u32[]{:S(2)}) collective-permute-start(f16[32,3584]{1,0:T(8,128)(2,1)S(1)} %convert_element_type.109), channel_id=1, source_target_pairs={{0,1},{1,0},{2,3},{3,2},{4,5},{5,4},{6,7},{7,6},{8,9},{9,8},{10,11... | collective-permute-start | bytes 688136 | tf_op jit(solution)/shard_map/ppermute | solution.py:322
  135.5 7.7 %collective-permute-start.31 = (f16[32,3584]{1,0:T(8,128)(2,1)S(1)}, f16[32,3584]{1,0:T(8,128)(2,1)S(1)}, u32[]{:S(2)}, u32[]{:S(2)}) collective-permute-start(f16[32,3584]{1,0:T(8,128)(2,1)S(1)} %convert_element_type.113), channel_id=1, source_target_pairs={{0,1},{1,0},{2,3},{3,2},{4,5},{5,4},{6,7},{7,6},{8,9},{9,8},{10,11... | collective-permute-start | bytes 688136 | tf_op jit(solution)/shard_map/ppermute | solution.py:322
  135.5 10.6 %collective-permute-start.30 = (f16[32,3584]{1,0:T(8,128)(2,1)S(1)}, f16[32,3584]{1,0:T(8,128)(2,1)S(1)}, u32[]{:S(2)}, u32[]{:S(2)}) collective-permute-start(f16[32,3584]{1,0:T(8,128)(2,1)S(1)} %add_convert_fusion.3), channel_id=1, source_target_pairs={{0,2},{1,3},{2,0},{3,1},{4,6},{5,7},{6,4},{7,5},{8,10},{9,11},{10,... | collective-permute-start | bytes 688136 | tf_op jit(solution)/shard_map/ppermute | solution.py:322
  143.2 6.0 %collective-permute-start.33 = (f16[32,3584]{1,0:T(8,128)(2,1)S(1)}, f16[32,3584]{1,0:T(8,128)(2,1)S(1)}, u32[]{:S(2)}, u32[]{:S(2)}) collective-permute-start(f16[32,3584]{1,0:T(8,128)(2,1)S(1)} %convert_element_type.117), channel_id=1, source_target_pairs={{0,1},{1,0},{2,3},{3,2},{4,5},{5,4},{6,7},{7,6},{8,9},{9,8},{10,11... | collective-permute-start | bytes 688136 | tf_op jit(solution)/shard_map/ppermute | solution.py:322
  146.2 8.5 %collective-permute-start.32 = (f16[32,3584]{1,0:T(8,128)(2,1)S(1)}, f16[32,3584]{1,0:T(8,128)(2,1)S(1)}, u32[]{:S(2)}, u32[]{:S(2)}) collective-permute-start(f16[32,3584]{1,0:T(8,128)(2,1)S(1)} %add_convert_fusion.2), channel_id=1, source_target_pairs={{0,4},{1,5},{2,6},{3,7},{4,0},{5,1},{6,2},{7,3},{8,12},{9,13},{10,... | collective-permute-start | bytes 688136 | tf_op jit(solution)/shard_map/ppermute | solution.py:322
  149.2 6.0 %collective-permute-start.35 = (f16[32,3584]{1,0:T(8,128)(2,1)S(1)}, f16[32,3584]{1,0:T(8,128)(2,1)S(1)}, u32[]{:S(2)}, u32[]{:S(2)}) collective-permute-start(f16[32,3584]{1,0:T(8,128)(2,1)S(1)} %convert_element_type.121), channel_id=1, source_target_pairs={{0,1},{1,0},{2,3},{3,2},{4,5},{5,4},{6,7},{7,6},{8,9},{9,8},{10,11... | collective-permute-start | bytes 688136 | tf_op jit(solution)/shard_map/ppermute | solution.py:322
  149.3 7.8 %collective-permute-start.34 = (f16[32,3584]{1,0:T(8,128)(2,1)S(1)}, f16[32,3584]{1,0:T(8,128)(2,1)S(1)}, u32[]{:S(2)}, u32[]{:S(2)}) collective-permute-start(f16[32,3584]{1,0:T(8,128)(2,1)S(1)} %add_convert_fusion.1), channel_id=1, source_target_pairs={{0,2},{1,3},{2,0},{3,1},{4,6},{5,7},{6,4},{7,5},{8,10},{9,11},{10,... | collective-permute-start | bytes 688136 | tf_op jit(solution)/shard_map/ppermute | solution.py:322

commit v4 on v3

--- a/solution.py
+++ b/solution.py
@@ -11,7 +11,7 @@
 wire = jnp.float16
 lanes = 128
 vmem_bytes = 12 * 1024 * 1024
-project_bytes = 52 * 1024 * 1024
+project_bytes = 50 * 1024 * 1024
 
 in_vmem = pl.BlockSpec(memory_space=pltpu.VMEM)
 in_smem = pl.BlockSpec(memory_space=pltpu.SMEM)
@@ -330,7 +330,7 @@
             bit = lowest(mask)
             block = blocks[mask ^ (1 << bit)]
             if bit == 0:
-                block = tie(block, line[-2])
+                block = tie(block, line[-3])
             blocks.append(swap(block, bit))
             if bit == 0:
                 line.append(blocks[-1])
@@ -341,8 +341,8 @@
         for mask in range(vocab_size - 1, 0, -1):
             bit = lowest(mask)
             block = terms[mask].astype(wire)
-            if bit == 0 and line:
-                block = tie(block, line[-1])
+            if bit == 0 and len(line) > 1:
+                block = tie(block, line[-2])
             block = swap(block, bit)
             if bit == 0:
                 line.append(block)
@@ -379,7 +379,6 @@
         member = (owner[None, :] == row_id[:, None]) & alive[None, :]
         parts = project(member.astype(jnp.bfloat16), teacher_rows, proj_weight, vocab_size, 512 if student_hidden.shape[1] % 512 == 0 else student_hidden.shape[1])
         projected_own, line = reduce_blocks(parts)
-        line.append(line[-1])
         hidden = spread(tie(turned(student_hidden), parts[-1]), line)
         projected = spread(turned(projected_own.astype(jnp.bfloat16)), line)
 

time: 158 us -> 138 us (0.87)
  waiting for transfers between devices: 74.4 us -> 39 us
  starting transfers between devices: 34.3 us -> 55.3 us
  Pallas kernels: 35.7 us -> 32.5 us
  other arithmetic: 7.78 us -> 5.18 us
    ppermute x28, waiting for transfers between devices: 70.9 us -> 37.4 us  [swap(): lax.ppermute(block, 'vocab', [(at, at ^ 1 << bit) for at in range(vocab_s...]
    ppermute x28, starting transfers between devices: 22.6 us -> 43.6 us  [swap(): lax.ppermute(block, 'vocab', [(at, at ^ 1 << bit) for at in range(vocab_s...]
    convert_element_type x14, other arithmetic: 5.75 us -> 2.23 us  [reduce_blocks(): block = terms[mask].astype(wire)]
    ppermute x7, waiting for transfers between devices: 3.4 us -> 1.56 us  [body(): lax.ppermute(stats, 'vocab', [(at, at ^ mask) for at in range(vocab_size)])]
  transfers between devices with their start and end apart: 36 -> 36, of which waited for: 24 -> 17; matrix products, arithmetic and copies ran while one was open for 5% -> 4% of each run, Pallas kernels for 12% -> 12%
where the time goes in v4:
time: 138 us
  starting transfers between devices  55.3 us (40%)
  waiting for transfers between devices  39 us (28%)
  Pallas kernels  32.5 us (24%)
  other arithmetic  5.18 us (4%)
  local copies, waits for them, and re-layouts  4.35 us (3%)
  between operations  1.53 us (1%)
    ppermute x28, starting transfers between devices, swap(): lax.ppermute(block, 'vocab', [(at, at ^ 1 << bit) for at in range(vocab_s...  43.6 us
    ppermute x28, waiting for transfers between devices, swap(): lax.ppermute(block, 'vocab', [(at, at ^ 1 << bit) for at in range(vocab_s...  37.4 us
    pallas_call x1, Pallas kernels, student_logits(): pl.pallas_call(functools.partial(student_kernel, len(pieces), step, chunk...  11.9 us
    ppermute x7, starting transfers between devices, body(): lax.ppermute(stats, 'vocab', [(at, at ^ mask) for at in range(vocab_size)])  11.2 us
    pallas_call x1, Pallas kernels, gradient(): pl.pallas_call(functools.partial(gradient_kernel, bits, step, chunk), in_...  8.33 us
    pallas_call x1, Pallas kernels, teacher_logits(): pl.pallas_call(functools.partial(teacher_kernel, len(pieces), step, chunk...  7.49 us
    pallas_call x1, Pallas kernels, project(): pl.pallas_call(functools.partial(project_kernel, count, step), in_specs=[...  4.83 us
    unnamed x6, local copies, waits for them, and re-layouts  3.48 us
  transfers between devices with their start and end apart: 36, of which 17 were waited for; matrix products, arithmetic and copies ran while one was open for 4% of the time, Pallas kernels for 12%

profile of v4, /device:TPU:0, one launch (start us, length us, event | category | flops | bytes accessed | tf_op | source)
XLA Modules:
  0.0 137.9 jit_solution(2557899287315645590)
XLA Ops:
  0.6 0.5 collective-permute-start.21
  1.8 0.8 and_convert_fusion.member_ref
  2.7 4.8 %shard_map.86 = (f32[32,3584]{1,0:T(8,128)S(1)}, f32[32,3584]{1,0:T(8,128)S(1)}, f32[32,3584]{1,0:T(8,128)S(1)}, f32[32,3584]{1,0:T(8,128)S(1)}, f32[32,3584]{1,...) custom-call(bf16[256,512]{1,0:T(8,128)(2,1)S(1)} %and_convert_fusion.member_ref, ...), custom_call_target="tpu_custom_call" | custom-call | flops 2147483648 | bytes 12058624 | tf_op jit(solution)/shard_map/pallas_call | solution.py:54
  7.5 0.7 convert_element_type.94
  8.2 2.6 %collective-permute-start = (f16[32,3584]{1,0:T(8,128)(2,1)}, f16[32,3584]{1,0:T(8,128)(2,1)}, u32[]{:S(2)}, u32[]{:S(2)}) collective-permute-start(f16[32,3584]{1,0:T(8,128)(2,1)} %convert_element_type.94), channel_id=1, source_target_pairs={{0,1},{1,0},{2,3},{3,2},{4,5},{5,4},{6,7},{7,6},{8,9},{9,8},{10,11... | collective-permute-start | bytes 688136 | tf_op jit(solution)/shard_map/ppermute | solution.py:322
  10.8 1.0 maximum_select_fusion.1.refs_0_
  11.8 2.7 %collective-permute-start.11 = (bf16[32,3584]{1,0:T(8,128)(2,1)S(1)}, bf16[32,3584]{1,0:T(8,128)(2,1)}, u32[]{:S(2)}, u32[]{:S(2)}) collective-permute-start(bf16[32,3584]{1,0:T(8,128)(2,1)S(1)} %maximum_select_fusion.1.refs_0_), channel_id=1, source_target_pairs={{0,4},{1,5},{2,6},{3,7},{4,0},{5,1},{6,2},{7,3},{8,12},{9,13},{10,... | collective-permute-start | bytes 688136 | tf_op jit(solution)/shard_map/ppermute | solution.py:322
  14.5 1.6 %collective-permute-start.7 = (bf16[32,3584]{1,0:T(8,128)(2,1)S(1)}, bf16[32,3584]{1,0:T(8,128)(2,1)}, u32[]{:S(2)}, u32[]{:S(2)}) collective-permute-start(bf16[32,3584]{1,0:T(8,128)(2,1)S(1)} %maximum_select_fusion.1.refs_0_), channel_id=1, source_target_pairs={{0,2},{1,3},{2,0},{3,1},{4,6},{5,7},{6,4},{7,5},{8,10},{9,11},{10,... | collective-permute-start | bytes 688136 | tf_op jit(solution)/shard_map/ppermute | solution.py:322
  16.1 0.6 collective-permute-start.2
  16.7 0.6 collective-permute-done
  17.3 2.2 %collective-permute-start.4 = (f16[32,3584]{1,0:T(8,128)(2,1)S(1)}, f16[32,3584]{1,0:T(8,128)(2,1)S(1)}, u32[]{:S(2)}, u32[]{:S(2)}) collective-permute-start(f16[32,3584]{1,0:T(8,128)(2,1)S(1)} %convert_element_type.102), channel_id=1, source_target_pairs={{0,1},{1,0},{2,3},{3,2},{4,5},{5,4},{6,7},{7,6},{8,9},{9,8},{10,11... | collective-permute-start | bytes 688136 | tf_op jit(solution)/shard_map/ppermute | solution.py:322
  19.5 1.0 add_convert_fusion.7
  20.5 4.2 %collective-permute-done.2 = f16[32,3584]{1,0:T(8,128)(2,1)S(1)} collective-permute-done((f16[32,3584]{1,0:T(8,128)(2,1)S(1)}, f16[32,3584]{1,0:T(8,128)(2,1)S(1)}, u32[]{:S(2)}, u32[]{:S(2)}) %collective-permute-start.2) | collective-permute-done | bytes 229408 | tf_op jit(solution)/shard_map/ppermute | solution.py:322
  24.7 0.4 collective-permute-start.1
  25.1 2.1 %collective-permute-done.4 = f16[32,3584]{1,0:T(8,128)(2,1)S(1)} collective-permute-done((f16[32,3584]{1,0:T(8,128)(2,1)S(1)}, f16[32,3584]{1,0:T(8,128)(2,1)S(1)}, u32[]{:S(2)}, u32[]{:S(2)}) %collective-permute-start.4) | collective-permute-done | bytes 229408 | tf_op jit(solution)/shard_map/ppermute | solution.py:322
  27.3 1.5 %collective-permute-start.6 = (f16[32,3584]{1,0:T(8,128)(2,1)S(1)}, f16[32,3584]{1,0:T(8,128)(2,1)S(1)}, u32[]{:S(2)}, u32[]{:S(2)}) collective-permute-start(f16[32,3584]{1,0:T(8,128)(2,1)S(1)} %convert_element_type.106), channel_id=1, source_target_pairs={{0,1},{1,0},{2,3},{3,2},{4,5},{5,4},{6,7},{7,6},{8,9},{9,8},{10,11... | collective-permute-start | bytes 688136 | tf_op jit(solution)/shard_map/ppermute | solution.py:322
  28.9 1.9 %collective-permute-done.1 = f16[32,3584]{1,0:T(8,128)(2,1)S(1)} collective-permute-done((f16[32,3584]{1,0:T(8,128)(2,1)S(1)}, f16[32,3584]{1,0:T(8,128)(2,1)S(1)}, u32[]{:S(2)}, u32[]{:S(2)}) %collective-permute-start.1) | collective-permute-done | bytes 229408 | tf_op jit(solution)/shard_map/ppermute | solution.py:322
  30.7 0.4 collective-permute-start.5
  31.3 2.7 %collective-permute-start.3 = (f16[32,3584]{1,0:T(8,128)(2,1)S(1)}, f16[32,3584]{1,0:T(8,128)(2,1)S(1)}, u32[]{:S(2)}, u32[]{:S(2)}) collective-permute-start(f16[32,3584]{1,0:T(8,128)(2,1)S(1)} %add_convert_fusion.6), channel_id=1, source_target_pairs={{0,4},{1,5},{2,6},{3,7},{4,0},{5,1},{6,2},{7,3},{8,12},{9,13},{10,... | collective-permute-start | bytes 688136 | tf_op jit(solution)/shard_map/ppermute | solution.py:322
  34.0 1.5 %collective-permute-start.16 = (bf16[32,3584]{1,0:T(8,128)(2,1)S(1)}, bf16[32,3584]{1,0:T(8,128)(2,1)S(1)}, u32[]{:S(2)}, u32[]{:S(2)}) collective-permute-start(bf16[32,3584]{1,0:T(8,128)(2,1)S(1)} %maximum_select_fusion.1.refs_0_), channel_id=1, source_target_pairs={{0,1},{1,0},{2,3},{3,2},{4,5},{5,4},{6,7},{7,6},{8,9},{9,8},{10,11... | collective-permute-start | bytes 688136 | tf_op jit(solution)/shard_map/ppermute | solution.py:322
  35.5 2.1 %collective-permute-start.15 = (bf16[32,3584]{1,0:T(8,128)(2,1)}, bf16[32,3584]{1,0:T(8,128)(2,1)S(1)}, u32[]{:S(2)}, u32[]{:S(2)}) collective-permute-start(bf16[32,3584]{1,0:T(8,128)(2,1)} %collective-permute-done.11.refs_4_), channel_id=1, source_target_pairs={{0,2},{1,3},{2,0},{3,1},{4,6},{5,7},{6,4},{7,5},{8,10},{9,11},{10,... | collective-permute-start | bytes 688136 | tf_op jit(solution)/shard_map/ppermute | solution.py:322
  37.6 4.7 %collective-permute-done.5 = f16[32,3584]{1,0:T(8,128)(2,1)S(1)} collective-permute-done((f16[32,3584]{1,0:T(8,128)(2,1)S(1)}, f16[32,3584]{1,0:T(8,128)(2,1)S(1)}, u32[]{:S(2)}, u32[]{:S(2)}) %collective-permute-start.5) | collective-permute-done | bytes 229408 | tf_op jit(solution)/shard_map/ppermute | solution.py:322
  42.3 1.6 %collective-permute-start.12 = (bf16[32,3584]{1,0:T(8,128)(2,1)}, bf16[32,3584]{1,0:T(8,128)(2,1)S(1)}, u32[]{:S(2)}, u32[]{:S(2)}) collective-permute-start(bf16[32,3584]{1,0:T(8,128)(2,1)} %collective-permute-done.11.refs_4_), channel_id=1, source_target_pairs={{0,1},{1,0},{2,3},{3,2},{4,5},{5,4},{6,7},{7,6},{8,9},{9,8},{10,11... | collective-permute-start | bytes 688136 | tf_op jit(solution)/shard_map/ppermute | solution.py:322
  43.9 0.4 collective-permute-start.8
  44.3 0.1 add_convert_fusion.4
  44.5 2.9 %collective-permute-start.14 = (bf16[32,3584]{1,0:T(8,128)(2,1)S(1)}, bf16[32,3584]{1,0:T(8,128)(2,1)S(1)}, u32[]{:S(2)}, u32[]{:S(2)}) collective-permute-start(bf16[32,3584]{1,0:T(8,128)(2,1)S(1)} %maximum_select_fusion.refs_0_), channel_id=1, source_target_pairs={{0,4},{1,5},{2,6},{3,7},{4,0},{5,1},{6,2},{7,3},{8,12},{9,13},{10,... | collective-permute-start | bytes 688136 | tf_op jit(solution)/shard_map/ppermute | solution.py:322
  47.5 0.5 collective-permute-done.15.refs_6_
  48.0 1.3 collective-permute-start.17
  49.3 4.7 %collective-permute-done.8.refs_3_ = bf16[32,3584]{1,0:T(8,128)(2,1)S(1)} collective-permute-done((bf16[32,3584]{1,0:T(8,128)(2,1)}, bf16[32,3584]{1,0:T(8,128)(2,1)S(1)}, u32[]{:S(2)}, u32[]{:S(2)}) %collective-permute-start.8) | collective-permute-done | bytes 229408 | tf_op jit(solution)/shard_map/ppermute | solution.py:322
  54.1 1.4 %collective-permute-start.10 = (bf16[32,3584]{1,0:T(8,128)(2,1)S(1)}, bf16[32,3584]{1,0:T(8,128)(2,1)S(1)}, u32[]{:S(2)}, u32[]{:S(2)}) collective-permute-start(bf16[32,3584]{1,0:T(8,128)(2,1)S(1)} %maximum_select_fusion.refs_0_), channel_id=1, source_target_pairs={{0,2},{1,3},{2,0},{3,1},{4,6},{5,7},{6,4},{7,5},{8,10},{9,11},{10,... | collective-permute-start | bytes 688136 | tf_op jit(solution)/shard_map/ppermute | solution.py:322
  55.5 1.6 %collective-permute-start.9 = (bf16[32,3584]{1,0:T(8,128)(2,1)S(1)}, bf16[32,3584]{1,0:T(8,128)(2,1)S(1)}, u32[]{:S(2)}, u32[]{:S(2)}) collective-permute-start(bf16[32,3584]{1,0:T(8,128)(2,1)S(1)} %maximum_select_fusion.refs_0_), channel_id=1, source_target_pairs={{0,1},{1,0},{2,3},{3,2},{4,5},{5,4},{6,7},{7,6},{8,9},{9,8},{10,11... | collective-permute-start | bytes 688136 | tf_op jit(solution)/shard_map/ppermute | solution.py:322
  57.1 1.4 %collective-permute-start.19 = (bf16[32,3584]{1,0:T(8,128)(2,1)S(1)}, bf16[32,3584]{1,0:T(8,128)(2,1)S(1)}, u32[]{:S(2)}, u32[]{:S(2)}) collective-permute-start(bf16[32,3584]{1,0:T(8,128)(2,1)S(1)} %collective-permute-done.14.refs_4_), channel_id=1, source_target_pairs={{0,2},{1,3},{2,0},{3,1},{4,6},{5,7},{6,4},{7,5},{8,10},{9,11},{10,... | collective-permute-start | bytes 688136 | tf_op jit(solution)/shard_map/ppermute | solution.py:322
  58.5 1.6 %collective-permute-done.10.refs_2_ = bf16[32,3584]{1,0:T(8,128)(2,1)S(1)} collective-permute-done((bf16[32,3584]{1,0:T(8,128)(2,1)S(1)}, bf16[32,3584]{1,0:T(8,128)(2,1)S(1)}, u32[]{:S(2)}, u32[]{:S(2)}) %collective-permute-start.10) | collective-permute-done | bytes 229408 | tf_op jit(solution)/shard_map/ppermute | solution.py:322
  60.1 2.4 %collective-permute-start.13 = (bf16[32,3584]{1,0:T(8,128)(2,1)S(1)}, bf16[32,3584]{1,0:T(8,128)(2,1)S(1)}, u32[]{:S(2)}, u32[]{:S(2)}) collective-permute-start(bf16[32,3584]{1,0:T(8,128)(2,1)S(1)} %collective-permute-done.10.refs_2_), channel_id=1, source_target_pairs={{0,1},{1,0},{2,3},{3,2},{4,5},{5,4},{6,7},{7,6},{8,9},{9,8},{10,11... | collective-permute-start | bytes 688136 | tf_op jit(solution)/shard_map/ppermute | solution.py:322
  62.5 1.5 %collective-permute-done.9.refs_1_ = bf16[32,3584]{1,0:T(8,128)(2,1)S(1)} collective-permute-done((bf16[32,3584]{1,0:T(8,128)(2,1)S(1)}, bf16[32,3584]{1,0:T(8,128)(2,1)S(1)}, u32[]{:S(2)}, u32[]{:S(2)}) %collective-permute-start.9) | collective-permute-done | bytes 229408 | tf_op jit(solution)/shard_map/ppermute | solution.py:322
  64.0 2.1 %collective-permute-start.20 = (bf16[32,3584]{1,0:T(8,128)(2,1)S(1)}, bf16[32,3584]{1,0:T(8,128)(2,1)S(1)}, u32[]{:S(2)}, u32[]{:S(2)}) collective-permute-start(bf16[32,3584]{1,0:T(8,128)(2,1)S(1)} %collective-permute-done.19.refs_6_), channel_id=1, source_target_pairs={{0,1},{1,0},{2,3},{3,2},{4,5},{5,4},{6,7},{7,6},{8,9},{9,8},{10,11... | collective-permute-start | bytes 688136 | tf_op jit(solution)/shard_map/ppermute | solution.py:322
  66.1 0.1 sub.26.refs_10_
  66.3 3.5 %copy-done = bf16[1792,2432]{1,0:T(8,128)(2,1)S(1)} copy-done((bf16[1792,2432]{1,0:T(8,128)(2,1)S(1)}, bf16[1792,2432]{1,0:T(8,128)(2,1)}, u32[]{:S(2)}) %copy-start) | copy-done | bytes 8716312
  69.8 11.9 %shard_map.87 = (f32[256,2432]{1,0:T(8,128)S(1)}, f32[256,2432]{1,0:T(8,128)S(1)}, f32[8,256]{1,0:T(8,128)S(1)}, bf16[3584,2432]{1,0:T(8,128)(2,1)S(1)}) custom-call(bf16[32,3584]{1,0:T(8,128)(2,1)S(1)} %maximum_select_fusion.1.refs_0_, bf16[32,3584]{1,0:T(8,128)(2,1)S(1)} %collective-permute-done.16.refs_1_, ...), custom_call_target="tpu_custom_call" | custom-call | flops 2231369728 | bytes 16187392 | tf_op jit(solution)/shard_map/pallas_call | solution.py:192
  81.7 7.5 %shard_map.88 = (f32[256,2432]{1,0:T(8,128)S(1)}, f32[8,256]{1,0:T(8,128)S(1)}) custom-call(bf16[32,3584]{1,0:T(8,128)(2,1)S(1)} %maximum_select_fusion.refs_0_, bf16[32,3584]{1,0:T(8,128)(2,1)S(1)} %collective-permute-done.9.refs_1_, bf16[32,3584]{1,0:T(8,128)(2,1)S(1)} %collective-permute-done.10.refs_2_, ...), custom_call_target="tpu_custom_call" | custom-call | flops 4462739456 | bytes 24903680 | tf_op jit(solution)/shard_map/pallas_call | solution.py:215
  89.2 2.3 %collective-permute-start.28 = (f32[8,256]{1,0:T(8,128)S(1)}, f32[8,256]{1,0:T(8,128)S(1)}, u32[]{:S(2)}, u32[]{:S(2)}) collective-permute-start(f32[8,256]{1,0:T(8,128)S(1)} %get-tuple-element.60.refs_0_), channel_id=1, source_target_pairs={{0,7},{1,6},{2,5},{3,4},{4,3},{5,2},{6,1},{7,0},{8,15},{9,14},{10,... | collective-permute-start | bytes 24584 | tf_op jit(solution)/shard_map/ppermute | solution.py:389
  91.5 1.0 collective-permute-start.27
  92.5 2.0 %collective-permute-start.26 = (f32[8,256]{1,0:T(8,128)S(1)}, f32[8,256]{1,0:T(8,128)S(1)}, u32[]{:S(2)}, u32[]{:S(2)}) collective-permute-start(f32[8,256]{1,0:T(8,128)S(1)} %get-tuple-element.60.refs_0_), channel_id=1, source_target_pairs={{0,5},{1,4},{2,7},{3,6},{4,1},{5,0},{6,3},{7,2},{8,13},{9,12},{10,... | collective-permute-start | bytes 24584 | tf_op jit(solution)/shard_map/ppermute | solution.py:389
  94.5 2.3 %collective-permute-start.25 = (f32[8,256]{1,0:T(8,128)S(1)}, f32[8,256]{1,0:T(8,128)S(1)}, u32[]{:S(2)}, u32[]{:S(2)}) collective-permute-start(f32[8,256]{1,0:T(8,128)S(1)} %get-tuple-element.60.refs_0_), channel_id=1, source_target_pairs={{0,4},{1,5},{2,6},{3,7},{4,0},{5,1},{6,2},{7,3},{8,12},{9,13},{10,... | collective-permute-start | bytes 24584 | tf_op jit(solution)/shard_map/ppermute | solution.py:389
  96.9 0.2 collective-permute-start.24
  97.1 1.3 collective-permute-start.23
  98.4 2.0 %collective-permute-start.22 = (f32[8,256]{1,0:T(8,128)S(1)}, f32[8,256]{1,0:T(8,128)S(1)}, u32[]{:S(2)}, u32[]{:S(2)}) collective-permute-start(f32[8,256]{1,0:T(8,128)S(1)} %get-tuple-element.60.refs_0_), channel_id=1, source_target_pairs={{0,1},{1,0},{2,3},{3,2},{4,5},{5,4},{6,7},{7,6},{8,9},{9,8},{10,11... | collective-permute-start | bytes 24584 | tf_op jit(solution)/shard_map/ppermute | solution.py:389
  100.5 1.0 collective-permute-done.24.refs_3_
  101.4 0.6 collective-permute-done.22.refs_1_
  102.0 8.3 %shard_map.89 = (f32[8,256]{1,0:T(8,128)S(1)}, f32[32,3584]{1,0:T(8,128)S(1)}, f32[32,3584]{1,0:T(8,128)S(1)}, f32[32,3584]{1,0:T(8,128)S(1)}, f32[32,3584]{1,0:...) custom-call(s32[2]{0:T(128)S(1)} %pad_add_fusion.place_ref, ...), custom_call_target="tpu_custom_call" | custom-call | flops 4462739456 | bytes 24903680 | tf_op jit(solution)/shard_map/pallas_call | solution.py:297
  110.4 2.1 %collective-permute-start.31 = (f16[32,3584]{1,0:T(8,128)(2,1)S(1)}, f16[32,3584]{1,0:T(8,128)(2,1)S(1)}, u32[]{:S(2)}, u32[]{:S(2)}) collective-permute-start(f16[32,3584]{1,0:T(8,128)(2,1)S(1)} %convert_element_type.113), channel_id=1, source_target_pairs={{0,1},{1,0},{2,3},{3,2},{4,5},{5,4},{6,7},{7,6},{8,9},{9,8},{10,11... | collective-permute-start | bytes 688136 | tf_op jit(solution)/shard_map/ppermute | solution.py:322
  112.6 3.8 %collective-permute-done.31 = f16[32,3584]{1,0:T(8,128)(2,1)S(1)} collective-permute-done((f16[32,3584]{1,0:T(8,128)(2,1)S(1)}, f16[32,3584]{1,0:T(8,128)(2,1)S(1)}, u32[]{:S(2)}, u32[]{:S(2)}) %collective-permute-start.31) | collective-permute-done | bytes 229408 | tf_op jit(solution)/shard_map/ppermute | solution.py:322
  116.5 2.0 %collective-permute-start.35 = (f16[32,3584]{1,0:T(8,128)(2,1)S(1)}, f16[32,3584]{1,0:T(8,128)(2,1)S(1)}, u32[]{:S(2)}, u32[]{:S(2)}) collective-permute-start(f16[32,3584]{1,0:T(8,128)(2,1)S(1)} %convert_element_type.121), channel_id=1, source_target_pairs={{0,1},{1,0},{2,3},{3,2},{4,5},{5,4},{6,7},{7,6},{8,9},{9,8},{10,11... | collective-permute-start | bytes 688136 | tf_op jit(solution)/shard_map/ppermute | solution.py:322
  118.5 0.4 collective-permute-done.29
  118.9 2.0 %collective-permute-start.33 = (f16[32,3584]{1,0:T(8,128)(2,1)S(1)}, f16[32,3584]{1,0:T(8,128)(2,1)S(1)}, u32[]{:S(2)}, u32[]{:S(2)}) collective-permute-start(f16[32,3584]{1,0:T(8,128)(2,1)S(1)} %convert_element_type.117), channel_id=1, source_target_pairs={{0,1},{1,0},{2,3},{3,2},{4,5},{5,4},{6,7},{7,6},{8,9},{9,8},{10,11... | collective-permute-start | bytes 688136 | tf_op jit(solution)/shard_map/ppermute | solution.py:322
  121.0 0.6 collective-permute-start.30
  121.6 3.3 %collective-permute-done.33 = f16[32,3584]{1,0:T(8,128)(2,1)S(1)} collective-permute-done((f16[32,3584]{1,0:T(8,128)(2,1)S(1)}, f16[32,3584]{1,0:T(8,128)(2,1)S(1)}, u32[]{:S(2)}, u32[]{:S(2)}) %collective-permute-start.33) | collective-permute-done | bytes 229408 | tf_op jit(solution)/shard_map/ppermute | solution.py:322
  125.0 1.7 %collective-permute-start.34 = (f16[32,3584]{1,0:T(8,128)(2,1)S(1)}, f16[32,3584]{1,0:T(8,128)(2,1)S(1)}, u32[]{:S(2)}, u32[]{:S(2)}) collective-permute-start(f16[32,3584]{1,0:T(8,128)(2,1)S(1)} %add_convert_fusion.1), channel_id=1, source_target_pairs={{0,2},{1,3},{2,0},{3,1},{4,6},{5,7},{6,4},{7,5},{8,10},{9,11},{10,... | collective-permute-start | bytes 688136 | tf_op jit(solution)/shard_map/ppermute | solution.py:322
  126.7 0.7 collective-permute-done.30
  127.5 1.7 %collective-permute-start.32 = (f16[32,3584]{1,0:T(8,128)(2,1)S(1)}, f16[32,3584]{1,0:T(8,128)(2,1)S(1)}, u32[]{:S(2)}, u32[]{:S(2)}) collective-permute-start(f16[32,3584]{1,0:T(8,128)(2,1)S(1)} %add_convert_fusion.2), channel_id=1, source_target_pairs={{0,4},{1,5},{2,6},{3,7},{4,0},{5,1},{6,2},{7,3},{8,12},{9,13},{10,... | collective-permute-start | bytes 688136 | tf_op jit(solution)/shard_map/ppermute | solution.py:322
  129.2 0.6 slice.27
  129.8 1.3 collective-permute-done.34
  131.1 5.9 %collective-permute-done.32 = f16[32,3584]{1,0:T(8,128)(2,1)S(1)} collective-permute-done((f16[32,3584]{1,0:T(8,128)(2,1)S(1)}, f16[32,3584]{1,0:T(8,128)(2,1)S(1)}, u32[]{:S(2)}, u32[]{:S(2)}) %collective-permute-start.32) | collective-permute-done | bytes 229408 | tf_op jit(solution)/shard_map/ppermute | solution.py:322
  137.1 0.8 maximum_select_fusion.2
  (51 shorter events, 1.1 us)
Async XLA Ops:
  0.6 10.2 %copy-start.1 = (bf16[32,3584]{1,0:T(8,128)(2,1)S(1)}, bf16[32,3584]{1,0:T(8,128)(2,1)}, u32[]{:S(2)}) copy-start(bf16[32,3584]{1,0:T(8,128)(2,1)} %param.11) | copy-start | bytes 688132
  0.6 65.7 %collective-permute-start.21 = (bf16[1792,2432]{1,0:T(8,128)(2,1)}, bf16[1792,2432]{1,0:T(8,128)(2,1)}, u32[]{:S(2)}, u32[]{:S(2)}) collective-permute-start(bf16[1792,2432]{1,0:T(8,128)(2,1)} %refs_8_.1), channel_id=1, source_target_pairs={{0,8},{8,0},{1,9},{9,1},{2,10},{10,2},{3,11},{11,3},{4,12},{12,4},... | collective-permute-start | bytes 26148872 | tf_op jit(solution)/shard_map/ppermute | solution.py:374
  2.7 44.7 %copy-start.2 = (s32[256]{0:T(256)S(1)}, s32[256]{0:T(256)}, u32[]{:S(2)}) copy-start(s32[256]{0:T(256)} %param.13) | copy-start | bytes 3076
  8.2 9.1 %collective-permute-start = (f16[32,3584]{1,0:T(8,128)(2,1)}, f16[32,3584]{1,0:T(8,128)(2,1)}, u32[]{:S(2)}, u32[]{:S(2)}) collective-permute-start(f16[32,3584]{1,0:T(8,128)(2,1)} %convert_element_type.94), channel_id=1, source_target_pairs={{0,1},{1,0},{2,3},{3,2},{4,5},{5,4},{6,7},{7,6},{8,9},{9,8},{10,11... | collective-permute-start | bytes 688136 | tf_op jit(solution)/shard_map/ppermute | solution.py:322
  11.8 19.4 %collective-permute-start.11 = (bf16[32,3584]{1,0:T(8,128)(2,1)S(1)}, bf16[32,3584]{1,0:T(8,128)(2,1)}, u32[]{:S(2)}, u32[]{:S(2)}) collective-permute-start(bf16[32,3584]{1,0:T(8,128)(2,1)S(1)} %maximum_select_fusion.1.refs_0_), channel_id=1, source_target_pairs={{0,4},{1,5},{2,6},{3,7},{4,0},{5,1},{6,2},{7,3},{8,12},{9,13},{10,... | collective-permute-start | bytes 688136 | tf_op jit(solution)/shard_map/ppermute | solution.py:322
  14.5 21.0 %collective-permute-start.7 = (bf16[32,3584]{1,0:T(8,128)(2,1)S(1)}, bf16[32,3584]{1,0:T(8,128)(2,1)}, u32[]{:S(2)}, u32[]{:S(2)}) collective-permute-start(bf16[32,3584]{1,0:T(8,128)(2,1)S(1)} %maximum_select_fusion.1.refs_0_), channel_id=1, source_target_pairs={{0,2},{1,3},{2,0},{3,1},{4,6},{5,7},{6,4},{7,5},{8,10},{9,11},{10,... | collective-permute-start | bytes 688136 | tf_op jit(solution)/shard_map/ppermute | solution.py:322
  16.1 8.6 %collective-permute-start.2 = (f16[32,3584]{1,0:T(8,128)(2,1)S(1)}, f16[32,3584]{1,0:T(8,128)(2,1)S(1)}, u32[]{:S(2)}, u32[]{:S(2)}) collective-permute-start(f16[32,3584]{1,0:T(8,128)(2,1)S(1)} %convert_element_type.98), channel_id=1, source_target_pairs={{0,1},{1,0},{2,3},{3,2},{4,5},{5,4},{6,7},{7,6},{8,9},{9,8},{10,11... | collective-permute-start | bytes 688136 | tf_op jit(solution)/shard_map/ppermute | solution.py:322
  17.3 9.9 %collective-permute-start.4 = (f16[32,3584]{1,0:T(8,128)(2,1)S(1)}, f16[32,3584]{1,0:T(8,128)(2,1)S(1)}, u32[]{:S(2)}, u32[]{:S(2)}) collective-permute-start(f16[32,3584]{1,0:T(8,128)(2,1)S(1)} %convert_element_type.102), channel_id=1, source_target_pairs={{0,1},{1,0},{2,3},{3,2},{4,5},{5,4},{6,7},{7,6},{8,9},{9,8},{10,11... | collective-permute-start | bytes 688136 | tf_op jit(solution)/shard_map/ppermute | solution.py:322
  24.7 6.0 %collective-permute-start.1 = (f16[32,3584]{1,0:T(8,128)(2,1)S(1)}, f16[32,3584]{1,0:T(8,128)(2,1)S(1)}, u32[]{:S(2)}, u32[]{:S(2)}) collective-permute-start(f16[32,3584]{1,0:T(8,128)(2,1)S(1)} %add_convert_fusion.7), channel_id=1, source_target_pairs={{0,2},{1,3},{2,0},{3,1},{4,6},{5,7},{6,4},{7,5},{8,10},{9,11},{10,... | collective-permute-start | bytes 688136 | tf_op jit(solution)/shard_map/ppermute | solution.py:322
  27.3 6.7 %collective-permute-start.6 = (f16[32,3584]{1,0:T(8,128)(2,1)S(1)}, f16[32,3584]{1,0:T(8,128)(2,1)S(1)}, u32[]{:S(2)}, u32[]{:S(2)}) collective-permute-start(f16[32,3584]{1,0:T(8,128)(2,1)S(1)} %convert_element_type.106), channel_id=1, source_target_pairs={{0,1},{1,0},{2,3},{3,2},{4,5},{5,4},{6,7},{7,6},{8,9},{9,8},{10,11... | collective-permute-start | bytes 688136 | tf_op jit(solution)/shard_map/ppermute | solution.py:322
  30.7 11.5 %collective-permute-start.5 = (f16[32,3584]{1,0:T(8,128)(2,1)S(1)}, f16[32,3584]{1,0:T(8,128)(2,1)S(1)}, u32[]{:S(2)}, u32[]{:S(2)}) collective-permute-start(f16[32,3584]{1,0:T(8,128)(2,1)S(1)} %add_convert_fusion.5), channel_id=1, source_target_pairs={{0,2},{1,3},{2,0},{3,1},{4,6},{5,7},{6,4},{7,5},{8,10},{9,11},{10,... | collective-permute-start | bytes 688136 | tf_op jit(solution)/shard_map/ppermute | solution.py:322
  31.3 12.6 %collective-permute-start.3 = (f16[32,3584]{1,0:T(8,128)(2,1)S(1)}, f16[32,3584]{1,0:T(8,128)(2,1)S(1)}, u32[]{:S(2)}, u32[]{:S(2)}) collective-permute-start(f16[32,3584]{1,0:T(8,128)(2,1)S(1)} %add_convert_fusion.6), channel_id=1, source_target_pairs={{0,4},{1,5},{2,6},{3,7},{4,0},{5,1},{6,2},{7,3},{8,12},{9,13},{10,... | collective-permute-start | bytes 688136 | tf_op jit(solution)/shard_map/ppermute | solution.py:322
  34.0 10.5 %collective-permute-start.16 = (bf16[32,3584]{1,0:T(8,128)(2,1)S(1)}, bf16[32,3584]{1,0:T(8,128)(2,1)S(1)}, u32[]{:S(2)}, u32[]{:S(2)}) collective-permute-start(bf16[32,3584]{1,0:T(8,128)(2,1)S(1)} %maximum_select_fusion.1.refs_0_), channel_id=1, source_target_pairs={{0,1},{1,0},{2,3},{3,2},{4,5},{5,4},{6,7},{7,6},{8,9},{9,8},{10,11... | collective-permute-start | bytes 688136 | tf_op jit(solution)/shard_map/ppermute | solution.py:322
  35.5 12.5 %collective-permute-start.15 = (bf16[32,3584]{1,0:T(8,128)(2,1)}, bf16[32,3584]{1,0:T(8,128)(2,1)S(1)}, u32[]{:S(2)}, u32[]{:S(2)}) collective-permute-start(bf16[32,3584]{1,0:T(8,128)(2,1)} %collective-permute-done.11.refs_4_), channel_id=1, source_target_pairs={{0,2},{1,3},{2,0},{3,1},{4,6},{5,7},{6,4},{7,5},{8,10},{9,11},{10,... | collective-permute-start | bytes 688136 | tf_op jit(solution)/shard_map/ppermute | solution.py:322
  42.3 13.2 %collective-permute-start.12 = (bf16[32,3584]{1,0:T(8,128)(2,1)}, bf16[32,3584]{1,0:T(8,128)(2,1)S(1)}, u32[]{:S(2)}, u32[]{:S(2)}) collective-permute-start(bf16[32,3584]{1,0:T(8,128)(2,1)} %collective-permute-done.11.refs_4_), channel_id=1, source_target_pairs={{0,1},{1,0},{2,3},{3,2},{4,5},{5,4},{6,7},{7,6},{8,9},{9,8},{10,11... | collective-permute-start | bytes 688136 | tf_op jit(solution)/shard_map/ppermute | solution.py:322
  43.9 10.2 %collective-permute-start.8 = (bf16[32,3584]{1,0:T(8,128)(2,1)}, bf16[32,3584]{1,0:T(8,128)(2,1)S(1)}, u32[]{:S(2)}, u32[]{:S(2)}) collective-permute-start(bf16[32,3584]{1,0:T(8,128)(2,1)} %collective-permute-done.7.refs_2_), channel_id=1, source_target_pairs={{0,1},{1,0},{2,3},{3,2},{4,5},{5,4},{6,7},{7,6},{8,9},{9,8},{10,11... | collective-permute-start | bytes 688136 | tf_op jit(solution)/shard_map/ppermute | solution.py:322
  44.5 12.6 %collective-permute-start.14 = (bf16[32,3584]{1,0:T(8,128)(2,1)S(1)}, bf16[32,3584]{1,0:T(8,128)(2,1)S(1)}, u32[]{:S(2)}, u32[]{:S(2)}) collective-permute-start(bf16[32,3584]{1,0:T(8,128)(2,1)S(1)} %maximum_select_fusion.refs_0_), channel_id=1, source_target_pairs={{0,4},{1,5},{2,6},{3,7},{4,0},{5,1},{6,2},{7,3},{8,12},{9,13},{10,... | collective-permute-start | bytes 688136 | tf_op jit(solution)/shard_map/ppermute | solution.py:322
  48.0 14.4 %collective-permute-start.17 = (bf16[32,3584]{1,0:T(8,128)(2,1)S(1)}, bf16[32,3584]{1,0:T(8,128)(2,1)S(1)}, u32[]{:S(2)}, u32[]{:S(2)}) collective-permute-start(bf16[32,3584]{1,0:T(8,128)(2,1)S(1)} %collective-permute-done.15.refs_6_), channel_id=1, source_target_pairs={{0,1},{1,0},{2,3},{3,2},{4,5},{5,4},{6,7},{7,6},{8,9},{9,8},{10,11... | collective-permute-start | bytes 688136 | tf_op jit(solution)/shard_map/ppermute | solution.py:322
  54.1 6.0 %collective-permute-start.10 = (bf16[32,3584]{1,0:T(8,128)(2,1)S(1)}, bf16[32,3584]{1,0:T(8,128)(2,1)S(1)}, u32[]{:S(2)}, u32[]{:S(2)}) collective-permute-start(bf16[32,3584]{1,0:T(8,128)(2,1)S(1)} %maximum_select_fusion.refs_0_), channel_id=1, source_target_pairs={{0,2},{1,3},{2,0},{3,1},{4,6},{5,7},{6,4},{7,5},{8,10},{9,11},{10,... | collective-permute-start | bytes 688136 | tf_op jit(solution)/shard_map/ppermute | solution.py:322
  55.5 8.5 %collective-permute-start.9 = (bf16[32,3584]{1,0:T(8,128)(2,1)S(1)}, bf16[32,3584]{1,0:T(8,128)(2,1)S(1)}, u32[]{:S(2)}, u32[]{:S(2)}) collective-permute-start(bf16[32,3584]{1,0:T(8,128)(2,1)S(1)} %maximum_select_fusion.refs_0_), channel_id=1, source_target_pairs={{0,1},{1,0},{2,3},{3,2},{4,5},{5,4},{6,7},{7,6},{8,9},{9,8},{10,11... | collective-permute-start | bytes 688136 | tf_op jit(solution)/shard_map/ppermute | solution.py:322
  57.1 6.9 %collective-permute-start.19 = (bf16[32,3584]{1,0:T(8,128)(2,1)S(1)}, bf16[32,3584]{1,0:T(8,128)(2,1)S(1)}, u32[]{:S(2)}, u32[]{:S(2)}) collective-permute-start(bf16[32,3584]{1,0:T(8,128)(2,1)S(1)} %collective-permute-done.14.refs_4_), channel_id=1, source_target_pairs={{0,2},{1,3},{2,0},{3,1},{4,6},{5,7},{6,4},{7,5},{8,10},{9,11},{10,... | collective-permute-start | bytes 688136 | tf_op jit(solution)/shard_map/ppermute | solution.py:322
  60.1 21.6 %collective-permute-start.13 = (bf16[32,3584]{1,0:T(8,128)(2,1)S(1)}, bf16[32,3584]{1,0:T(8,128)(2,1)S(1)}, u32[]{:S(2)}, u32[]{:S(2)}) collective-permute-start(bf16[32,3584]{1,0:T(8,128)(2,1)S(1)} %collective-permute-done.10.refs_2_), channel_id=1, source_target_pairs={{0,1},{1,0},{2,3},{3,2},{4,5},{5,4},{6,7},{7,6},{8,9},{9,8},{10,11... | collective-permute-start | bytes 688136 | tf_op jit(solution)/shard_map/ppermute | solution.py:322
  62.5 19.2 %collective-permute-start.18 = (bf16[32,3584]{1,0:T(8,128)(2,1)S(1)}, bf16[32,3584]{1,0:T(8,128)(2,1)S(1)}, u32[]{:S(2)}, u32[]{:S(2)}) collective-permute-start(bf16[32,3584]{1,0:T(8,128)(2,1)S(1)} %collective-permute-done.14.refs_4_), channel_id=1, source_target_pairs={{0,1},{1,0},{2,3},{3,2},{4,5},{5,4},{6,7},{7,6},{8,9},{9,8},{10,11... | collective-permute-start | bytes 688136 | tf_op jit(solution)/shard_map/ppermute | solution.py:322
  64.0 17.7 %collective-permute-start.20 = (bf16[32,3584]{1,0:T(8,128)(2,1)S(1)}, bf16[32,3584]{1,0:T(8,128)(2,1)S(1)}, u32[]{:S(2)}, u32[]{:S(2)}) collective-permute-start(bf16[32,3584]{1,0:T(8,128)(2,1)S(1)} %collective-permute-done.19.refs_6_), channel_id=1, source_target_pairs={{0,1},{1,0},{2,3},{3,2},{4,5},{5,4},{6,7},{7,6},{8,9},{9,8},{10,11... | collective-permute-start | bytes 688136 | tf_op jit(solution)/shard_map/ppermute | solution.py:322
  66.3 3.5 %copy-start = (bf16[1792,2432]{1,0:T(8,128)(2,1)S(1)}, bf16[1792,2432]{1,0:T(8,128)(2,1)}, u32[]{:S(2)}) copy-start(bf16[1792,2432]{1,0:T(8,128)(2,1)} %refs_8_.1) | copy-start | bytes 26148868
  89.2 7.9 %collective-permute-start.28 = (f32[8,256]{1,0:T(8,128)S(1)}, f32[8,256]{1,0:T(8,128)S(1)}, u32[]{:S(2)}, u32[]{:S(2)}) collective-permute-start(f32[8,256]{1,0:T(8,128)S(1)} %get-tuple-element.60.refs_0_), channel_id=1, source_target_pairs={{0,7},{1,6},{2,5},{3,4},{4,3},{5,2},{6,1},{7,0},{8,15},{9,14},{10,... | collective-permute-start | bytes 24584 | tf_op jit(solution)/shard_map/ppermute | solution.py:389
  91.5 6.9 %collective-permute-start.27 = (f32[8,256]{1,0:T(8,128)S(1)}, f32[8,256]{1,0:T(8,128)S(1)}, u32[]{:S(2)}, u32[]{:S(2)}) collective-permute-start(f32[8,256]{1,0:T(8,128)S(1)} %get-tuple-element.60.refs_0_), channel_id=1, source_target_pairs={{0,6},{1,7},{2,4},{3,5},{4,2},{5,3},{6,0},{7,1},{8,14},{9,15},{10,... | collective-permute-start | bytes 24584 | tf_op jit(solution)/shard_map/ppermute | solution.py:389
  92.5 8.0 %collective-permute-start.26 = (f32[8,256]{1,0:T(8,128)S(1)}, f32[8,256]{1,0:T(8,128)S(1)}, u32[]{:S(2)}, u32[]{:S(2)}) collective-permute-start(f32[8,256]{1,0:T(8,128)S(1)} %get-tuple-element.60.refs_0_), channel_id=1, source_target_pairs={{0,5},{1,4},{2,7},{3,6},{4,1},{5,0},{6,3},{7,2},{8,13},{9,12},{10,... | collective-permute-start | bytes 24584 | tf_op jit(solution)/shard_map/ppermute | solution.py:389
  94.5 5.9 %collective-permute-start.25 = (f32[8,256]{1,0:T(8,128)S(1)}, f32[8,256]{1,0:T(8,128)S(1)}, u32[]{:S(2)}, u32[]{:S(2)}) collective-permute-start(f32[8,256]{1,0:T(8,128)S(1)} %get-tuple-element.60.refs_0_), channel_id=1, source_target_pairs={{0,4},{1,5},{2,6},{3,7},{4,0},{5,1},{6,2},{7,3},{8,12},{9,13},{10,... | collective-permute-start | bytes 24584 | tf_op jit(solution)/shard_map/ppermute | solution.py:389
  96.9 4.5 %collective-permute-start.24 = (f32[8,256]{1,0:T(8,128)S(1)}, f32[8,256]{1,0:T(8,128)S(1)}, u32[]{:S(2)}, u32[]{:S(2)}) collective-permute-start(f32[8,256]{1,0:T(8,128)S(1)} %get-tuple-element.60.refs_0_), channel_id=1, source_target_pairs={{0,3},{1,2},{2,1},{3,0},{4,7},{5,6},{6,5},{7,4},{8,11},{9,10},{10,... | collective-permute-start | bytes 24584 | tf_op jit(solution)/shard_map/ppermute | solution.py:389
  97.1 4.3 %collective-permute-start.23 = (f32[8,256]{1,0:T(8,128)S(1)}, f32[8,256]{1,0:T(8,128)S(1)}, u32[]{:S(2)}, u32[]{:S(2)}) collective-permute-start(f32[8,256]{1,0:T(8,128)S(1)} %get-tuple-element.60.refs_0_), channel_id=1, source_target_pairs={{0,2},{1,3},{2,0},{3,1},{4,6},{5,7},{6,4},{7,5},{8,10},{9,11},{10,... | collective-permute-start | bytes 24584 | tf_op jit(solution)/shard_map/ppermute | solution.py:389
  98.4 3.7 %collective-permute-start.22 = (f32[8,256]{1,0:T(8,128)S(1)}, f32[8,256]{1,0:T(8,128)S(1)}, u32[]{:S(2)}, u32[]{:S(2)}) collective-permute-start(f32[8,256]{1,0:T(8,128)S(1)} %get-tuple-element.60.refs_0_), channel_id=1, source_target_pairs={{0,1},{1,0},{2,3},{3,2},{4,5},{5,4},{6,7},{7,6},{8,9},{9,8},{10,11... | collective-permute-start | bytes 24584 | tf_op jit(solution)/shard_map/ppermute | solution.py:389
  110.4 6.1 %collective-permute-start.31 = (f16[32,3584]{1,0:T(8,128)(2,1)S(1)}, f16[32,3584]{1,0:T(8,128)(2,1)S(1)}, u32[]{:S(2)}, u32[]{:S(2)}) collective-permute-start(f16[32,3584]{1,0:T(8,128)(2,1)S(1)} %convert_element_type.113), channel_id=1, source_target_pairs={{0,1},{1,0},{2,3},{3,2},{4,5},{5,4},{6,7},{7,6},{8,9},{9,8},{10,11... | collective-permute-start | bytes 688136 | tf_op jit(solution)/shard_map/ppermute | solution.py:322
  112.5 6.4 %collective-permute-start.29 = (f16[32,3584]{1,0:T(8,128)(2,1)S(1)}, f16[32,3584]{1,0:T(8,128)(2,1)S(1)}, u32[]{:S(2)}, u32[]{:S(2)}) collective-permute-start(f16[32,3584]{1,0:T(8,128)(2,1)S(1)} %convert_element_type.109), channel_id=1, source_target_pairs={{0,1},{1,0},{2,3},{3,2},{4,5},{5,4},{6,7},{7,6},{8,9},{9,8},{10,11... | collective-permute-start | bytes 688136 | tf_op jit(solution)/shard_map/ppermute | solution.py:322
  116.5 13.3 %collective-permute-start.35 = (f16[32,3584]{1,0:T(8,128)(2,1)S(1)}, f16[32,3584]{1,0:T(8,128)(2,1)S(1)}, u32[]{:S(2)}, u32[]{:S(2)}) collective-permute-start(f16[32,3584]{1,0:T(8,128)(2,1)S(1)} %convert_element_type.121), channel_id=1, source_target_pairs={{0,1},{1,0},{2,3},{3,2},{4,5},{5,4},{6,7},{7,6},{8,9},{9,8},{10,11... | collective-permute-start | bytes 688136 | tf_op jit(solution)/shard_map/ppermute | solution.py:322
  118.9 6.0 %collective-permute-start.33 = (f16[32,3584]{1,0:T(8,128)(2,1)S(1)}, f16[32,3584]{1,0:T(8,128)(2,1)S(1)}, u32[]{:S(2)}, u32[]{:S(2)}) collective-permute-start(f16[32,3584]{1,0:T(8,128)(2,1)S(1)} %convert_element_type.117), channel_id=1, source_target_pairs={{0,1},{1,0},{2,3},{3,2},{4,5},{5,4},{6,7},{7,6},{8,9},{9,8},{10,11... | collective-permute-start | bytes 688136 | tf_op jit(solution)/shard_map/ppermute | solution.py:322
  121.0 6.4 %collective-permute-start.30 = (f16[32,3584]{1,0:T(8,128)(2,1)S(1)}, f16[32,3584]{1,0:T(8,128)(2,1)S(1)}, u32[]{:S(2)}, u32[]{:S(2)}) collective-permute-start(f16[32,3584]{1,0:T(8,128)(2,1)S(1)} %add_convert_fusion.3), channel_id=1, source_target_pairs={{0,2},{1,3},{2,0},{3,1},{4,6},{5,7},{6,4},{7,5},{8,10},{9,11},{10,... | collective-permute-start | bytes 688136 | tf_op jit(solution)/shard_map/ppermute | solution.py:322
  125.0 6.1 %collective-permute-start.34 = (f16[32,3584]{1,0:T(8,128)(2,1)S(1)}, f16[32,3584]{1,0:T(8,128)(2,1)S(1)}, u32[]{:S(2)}, u32[]{:S(2)}) collective-permute-start(f16[32,3584]{1,0:T(8,128)(2,1)S(1)} %add_convert_fusion.1), channel_id=1, source_target_pairs={{0,2},{1,3},{2,0},{3,1},{4,6},{5,7},{6,4},{7,5},{8,10},{9,11},{10,... | collective-permute-start | bytes 688136 | tf_op jit(solution)/shard_map/ppermute | solution.py:322
  127.5 9.4 %collective-permute-start.32 = (f16[32,3584]{1,0:T(8,128)(2,1)S(1)}, f16[32,3584]{1,0:T(8,128)(2,1)S(1)}, u32[]{:S(2)}, u32[]{:S(2)}) collective-permute-start(f16[32,3584]{1,0:T(8,128)(2,1)S(1)} %add_convert_fusion.2), channel_id=1, source_target_pairs={{0,4},{1,5},{2,6},{3,7},{4,0},{5,1},{6,2},{7,3},{8,12},{9,13},{10,... | collective-permute-start | bytes 688136 | tf_op jit(solution)/shard_map/ppermute | solution.py:322

commit v5 on v4

--- a/solution.py
+++ b/solution.py
@@ -11,6 +11,7 @@
 wire = jnp.float16
 lanes = 128
 vmem_bytes = 12 * 1024 * 1024
+student_bytes = 12 * 1024 * 1024
 project_bytes = 50 * 1024 * 1024
 
 in_vmem = pl.BlockSpec(memory_space=pltpu.VMEM)
@@ -205,7 +206,7 @@
             pltpu.VMEM((rows, lanes), jnp.float32),
             pltpu.SemaphoreType.DMA((len(pieces) + 2 * len(cuts(vocab_dev, step)),)),
         ],
-        compiler_params=pltpu.CompilerParams(vmem_limit_bytes=vmem_bytes),
+        compiler_params=pltpu.CompilerParams(vmem_limit_bytes=student_bytes),
         cost_estimate=head_cost(rows, heads[0]),
     )(*pieces, *heads, column)
 
@@ -324,30 +325,37 @@
     def lowest(mask):
         return (mask & -mask).bit_length() - 1
 
-    def spread(own, line):
-        blocks = [own]
-        for mask in range(1, vocab_size):
-            bit = lowest(mask)
+    def spread(own, mixed):
+        blocks = {0: own}
+        masks = range(1, vocab_size)
+        if not mixed:
+            own_hops = [swap(own, bit) for bit in range(bits - 1)]
+            blocks.update({1 << bit: block for bit, block in enumerate(own_hops)})
+            masks = [mask for mask in masks if mask not in blocks]
+        else:
+            masks = sorted(masks, key=lambda mask: mask & 3 == 3 and mask > 3)
+        for mask in masks:
+            bit = 1 if mixed and mask & 3 == 3 and mask > 3 else lowest(mask)
             block = blocks[mask ^ (1 << bit)]
-            if bit == 0:
-                block = tie(block, line[-3])
-            blocks.append(swap(block, bit))
-            if bit == 0:
-                line.append(blocks[-1])
-        return blocks
-
-    def reduce_blocks(parts):
+            if not mixed and mask ^ (1 << bit) == 1 << (bits - 1):
+                block = tie(block, *own_hops)
+            blocks[mask] = swap(block, bit)
+        return [blocks[mask] for mask in range(vocab_size)]
+
+    def reduce_blocks(parts, gates={}):
         terms, line = list(parts), []
         for mask in range(vocab_size - 1, 0, -1):
             bit = lowest(mask)
             block = terms[mask].astype(wire)
-            if bit == 0 and len(line) > 1:
+            if mask in gates:
+                block = tie(block, gates[mask])
+            elif bit == 0 and len(line) > 1:
                 block = tie(block, line[-2])
             block = swap(block, bit)
             if bit == 0:
                 line.append(block)
             terms[mask ^ (1 << bit)] = terms[mask ^ (1 << bit)] + block.astype(jnp.float32)
-        return terms[0], line
+        return terms[0]
 
     def body(teacher_rows, owner, counts, proj_weight, student_hidden, head_weight, targets):
         teach_rows = teacher_rows.shape[0]
@@ -378,19 +386,21 @@
         alive = lax.iota(jnp.int32, teach_rows) < counts[0]
         member = (owner[None, :] == row_id[:, None]) & alive[None, :]
         parts = project(member.astype(jnp.bfloat16), teacher_rows, proj_weight, vocab_size, 512 if student_hidden.shape[1] % 512 == 0 else student_hidden.shape[1])
-        projected_own, line = reduce_blocks(parts)
-        hidden = spread(tie(turned(student_hidden), parts[-1]), line)
-        projected = spread(turned(projected_own.astype(jnp.bfloat16)), line)
+        hidden = spread(turned(student_hidden), True)
+        gates = dict(zip(range(vocab_size - 1, 0, -2), (hidden[1], hidden[2], hidden[vocab_size // 2])))
+        projected_own = tie(reduce_blocks(parts, gates), *hidden[:-1])
+        projected = spread(turned(projected_own.astype(jnp.bfloat16)), False)
 
         column = (in_order(targets) - me * vocab_dev)[:, None]
         logit_stud, scaled_stud, stats_stud, head = student_logits(as_pieces(hidden), heads, column, 256, chunk)
         scaled_teach, stats = teacher_logits(as_pieces(projected), head, logit_stud, stats_stud, 512, chunk)
-        tables = [stats] + [
-            lax.ppermute(stats, "vocab", [(at, at ^ mask) for at in range(vocab_size)])
-            for mask in range(1, vocab_size)
-        ]
+        tables = [stats]
+        for mask in range(1, vocab_size):
+            far, near = mask & ~3, mask & 3
+            source, hop = (tables[far], near) if near else (stats, far)
+            tables.append(lax.ppermute(source, "vocab", [(at, at ^ hop) for at in range(vocab_size)]))
         loss, *terms = gradient(place, tables, scaled_teach, scaled_stud, column, head, bits, chunk)
-        return (loss[0], turned(reduce_blocks(terms)[0].astype(jnp.bfloat16)))
+        return (loss[0], turned(reduce_blocks(terms).astype(jnp.bfloat16)))
 
     return body
 

time: 138 us -> 147 us (1.065)
  waiting for transfers between devices: 39 us -> 60 us
  starting transfers between devices: 55.3 us -> 42.4 us
  Pallas kernels: 32.5 us -> 34.3 us
  other arithmetic: 5.18 us -> 3.57 us
    ppermute x28, waiting for transfers between devices: 37.4 us -> 58.2 us  [swap(): lax.ppermute(block, 'vocab', [(at, at ^ 1 << bit) for at in range(vocab_s...]
    ppermute x28, starting transfers between devices: 43.6 us -> 31.5 us  [swap(): lax.ppermute(block, 'vocab', [(at, at ^ 1 << bit) for at in range(vocab_s...]
    convert_element_type x14, other arithmetic: 2.23 us -> 0.62 us  [reduce_blocks(): block = terms[mask].astype(wire)]
    unnamed x6 -> x4, local copies, waits for them, and re-layouts: 3.48 us -> 3.48 us
  transfers between devices with their start and end apart: 36 -> 36, of which waited for: 17 -> 22; matrix products, arithmetic and copies ran while one was open for 4% -> 3% of each run, Pallas kernels for 12% -> 12%
where the time goes in v5:
time: 147 us
  waiting for transfers between devices  60 us (41%)
  starting transfers between devices  42.4 us (29%)
  Pallas kernels  34.3 us (23%)
  local copies, waits for them, and re-layouts  5.3 us (4%)
  other arithmetic  3.57 us (2%)
  between operations  1.52 us (1%)
    ppermute x28, waiting for transfers between devices, swap(): lax.ppermute(block, 'vocab', [(at, at ^ 1 << bit) for at in range(vocab_s...  58.2 us
    ppermute x28, starting transfers between devices, swap(): lax.ppermute(block, 'vocab', [(at, at ^ 1 << bit) for at in range(vocab_s...  31.5 us
    pallas_call x1, Pallas kernels, student_logits(): pl.pallas_call(functools.partial(student_kernel, len(pieces), step, chunk...  12.5 us
    ppermute x7, starting transfers between devices, body(): lax.ppermute(source, 'vocab', [(at, at ^ hop) for at in range(vocab_size)])  10.4 us
    pallas_call x1, Pallas kernels, teacher_logits(): pl.pallas_call(functools.partial(teacher_kernel, len(pieces), step, chunk...  8.61 us
    pallas_call x1, Pallas kernels, gradient(): pl.pallas_call(functools.partial(gradient_kernel, bits, step, chunk), in_...  8.37 us
    pallas_call x1, Pallas kernels, project(): pl.pallas_call(functools.partial(project_kernel, count, step), in_specs=[...  4.83 us
    unnamed x4, local copies, waits for them, and re-layouts  3.48 us
  transfers between devices with their start and end apart: 36, of which 22 were waited for; matrix products, arithmetic and copies ran while one was open for 3% of the time, Pallas kernels for 12%

profile of v5, /device:TPU:0, one launch (start us, length us, event | category | flops | bytes accessed | tf_op | source)
XLA Modules:
  0.0 147.2 jit_solution(807826682393116744)
XLA Ops:
  0.6 0.5 collective-permute-start.21
  1.1 1.0 fusion.8
  2.1 1.0 maximum_select_fusion.refs_0_
  3.1 3.7 %collective-permute-start.6 = (bf16[32,3584]{1,0:T(8,128)(2,1)S(1)}, bf16[32,3584]{1,0:T(8,128)(2,1)S(1)}, u32[]{:S(2)}, u32[]{:S(2)}) collective-permute-start(bf16[32,3584]{1,0:T(8,128)(2,1)S(1)} %maximum_select_fusion.refs_0_), channel_id=1, source_target_pairs={{0,4},{1,5},{2,6},{3,7},{4,0},{5,1},{6,2},{7,3},{8,12},{9,13},{10,... | collective-permute-start | bytes 688136 | tf_op jit(solution)/shard_map/ppermute | solution.py:323
  6.8 1.6 %collective-permute-start.3 = (bf16[32,3584]{1,0:T(8,128)(2,1)S(1)}, bf16[32,3584]{1,0:T(8,128)(2,1)S(1)}, u32[]{:S(2)}, u32[]{:S(2)}) collective-permute-start(bf16[32,3584]{1,0:T(8,128)(2,1)S(1)} %maximum_select_fusion.refs_0_), channel_id=1, source_target_pairs={{0,2},{1,3},{2,0},{3,1},{4,6},{5,7},{6,4},{7,5},{8,10},{9,11},{10,... | collective-permute-start | bytes 688136 | tf_op jit(solution)/shard_map/ppermute | solution.py:323
  8.4 1.5 %collective-permute-start = (bf16[32,3584]{1,0:T(8,128)(2,1)S(1)}, bf16[32,3584]{1,0:T(8,128)(2,1)S(1)}, u32[]{:S(2)}, u32[]{:S(2)}) collective-permute-start(bf16[32,3584]{1,0:T(8,128)(2,1)S(1)} %maximum_select_fusion.refs_0_), channel_id=1, source_target_pairs={{0,1},{1,0},{2,3},{3,2},{4,5},{5,4},{6,7},{7,6},{8,9},{9,8},{10,11... | collective-permute-start | bytes 688136 | tf_op jit(solution)/shard_map/ppermute | solution.py:323
  10.6 0.8 and_convert_fusion.member_ref
  11.4 4.8 %shard_map.86 = (f32[32,3584]{1,0:T(8,128)S(1)}, f32[32,3584]{1,0:T(8,128)S(1)}, f32[32,3584]{1,0:T(8,128)S(1)}, f32[32,3584]{1,0:T(8,128)S(1)}, f32[32,3584]{1,...) custom-call(bf16[256,512]{1,0:T(8,128)(2,1)S(1)} %and_convert_fusion.member_ref, ...), custom_call_target="tpu_custom_call" | custom-call | flops 2147483648 | bytes 12058624 | tf_op jit(solution)/shard_map/pallas_call | solution.py:55
  16.3 0.6 collective-permute-start.1
  17.0 0.4 collective-permute-done.3.refs_2_
  17.3 1.6 %collective-permute-start.7 = (f16[32,3584]{1,0:T(8,128)(2,1)S(1)}, f16[32,3584]{1,0:T(8,128)(2,1)S(1)}, u32[]{:S(2)}, u32[]{:S(2)}) collective-permute-start(f16[32,3584]{1,0:T(8,128)(2,1)S(1)} %convert_element_type.102), channel_id=1, source_target_pairs={{0,1},{1,0},{2,3},{3,2},{4,5},{5,4},{6,7},{7,6},{8,9},{9,8},{10,11... | collective-permute-start | bytes 688136 | tf_op jit(solution)/shard_map/ppermute | solution.py:323
  18.9 0.5 collective-permute-start.4
  19.4 5.5 %collective-permute-done.1 = f16[32,3584]{1,0:T(8,128)(2,1)S(1)} collective-permute-done((f16[32,3584]{1,0:T(8,128)(2,1)S(1)}, f16[32,3584]{1,0:T(8,128)(2,1)S(1)}, u32[]{:S(2)}, u32[]{:S(2)}) %collective-permute-start.1) | collective-permute-done | bytes 229408 | tf_op jit(solution)/shard_map/ppermute | solution.py:323
  25.0 0.5 collective-permute-start.2
  25.5 4.3 %collective-permute-done.7 = f16[32,3584]{1,0:T(8,128)(2,1)S(1)} collective-permute-done((f16[32,3584]{1,0:T(8,128)(2,1)S(1)}, f16[32,3584]{1,0:T(8,128)(2,1)S(1)}, u32[]{:S(2)}, u32[]{:S(2)}) %collective-permute-start.7) | collective-permute-done | bytes 229408 | tf_op jit(solution)/shard_map/ppermute | solution.py:323
  29.9 0.5 collective-permute-start.8
  30.4 2.0 %collective-permute-done.4 = f16[32,3584]{1,0:T(8,128)(2,1)S(1)} collective-permute-done((f16[32,3584]{1,0:T(8,128)(2,1)S(1)}, f16[32,3584]{1,0:T(8,128)(2,1)S(1)}, u32[]{:S(2)}, u32[]{:S(2)}) %collective-permute-start.4) | collective-permute-done | bytes 229408 | tf_op jit(solution)/shard_map/ppermute | solution.py:323
  32.4 0.5 collective-permute-start.9
  33.0 0.9 collective-permute-start.5
  33.9 1.4 collective-permute-start.12
  35.3 4.7 %collective-permute-done.8 = f16[32,3584]{1,0:T(8,128)(2,1)S(1)} collective-permute-done((f16[32,3584]{1,0:T(8,128)(2,1)S(1)}, f16[32,3584]{1,0:T(8,128)(2,1)S(1)}, u32[]{:S(2)}, u32[]{:S(2)}) %collective-permute-start.8) | collective-permute-done | bytes 229408 | tf_op jit(solution)/shard_map/ppermute | solution.py:323
  40.0 0.7 collective-permute-done.9
  40.7 1.3 collective-permute-start.10
  42.0 2.0 %collective-permute-done.5 = f16[32,3584]{1,0:T(8,128)(2,1)S(1)} collective-permute-done((f16[32,3584]{1,0:T(8,128)(2,1)S(1)}, f16[32,3584]{1,0:T(8,128)(2,1)S(1)}, u32[]{:S(2)}, u32[]{:S(2)}) %collective-permute-start.5) | collective-permute-done | bytes 229408 | tf_op jit(solution)/shard_map/ppermute | solution.py:323
  44.1 1.7 %collective-permute-done.12.refs_6_ = bf16[32,3584]{1,0:T(8,128)(2,1)S(1)} collective-permute-done((bf16[32,3584]{1,0:T(8,128)(2,1)S(1)}, bf16[32,3584]{1,0:T(8,128)(2,1)S(1)}, u32[]{:S(2)}, u32[]{:S(2)}) %collective-permute-start.12) | collective-permute-done | bytes 229408 | tf_op jit(solution)/shard_map/ppermute | solution.py:323
  46.0 2.5 %collective-permute-done.10.refs_3_ = bf16[32,3584]{1,0:T(8,128)(2,1)S(1)} collective-permute-done((bf16[32,3584]{1,0:T(8,128)(2,1)S(1)}, bf16[32,3584]{1,0:T(8,128)(2,1)S(1)}, u32[]{:S(2)}, u32[]{:S(2)}) %collective-permute-start.10) | collective-permute-done | bytes 229408 | tf_op jit(solution)/shard_map/ppermute | solution.py:323
  48.5 0.3 collective-permute-start.16
  48.8 1.5 collective-permute-start.14
  50.2 1.5 %collective-permute-start.13 = (bf16[32,3584]{1,0:T(8,128)(2,1)S(1)}, bf16[32,3584]{1,0:T(8,128)(2,1)S(1)}, u32[]{:S(2)}, u32[]{:S(2)}) collective-permute-start(bf16[32,3584]{1,0:T(8,128)(2,1)S(1)} %maximum_select_fusion.1.refs_0_), channel_id=1, source_target_pairs={{0,1},{1,0},{2,3},{3,2},{4,5},{5,4},{6,7},{7,6},{8,9},{9,8},{10,11... | collective-permute-start | bytes 688136 | tf_op jit(solution)/shard_map/ppermute | solution.py:323
  51.9 6.0 %collective-permute-done.16.refs_4_ = bf16[32,3584]{1,0:T(8,128)(2,1)S(1)} collective-permute-done((bf16[32,3584]{1,0:T(8,128)(2,1)S(1)}, bf16[32,3584]{1,0:T(8,128)(2,1)S(1)}, u32[]{:S(2)}, u32[]{:S(2)}) %collective-permute-start.16) | collective-permute-done | bytes 229408 | tf_op jit(solution)/shard_map/ppermute | solution.py:323
  57.9 1.3 collective-permute-start.18
  59.2 0.7 collective-permute-start.20
  59.9 0.4 collective-permute-start.17
  60.3 1.6 %collective-permute-start.15 = (bf16[32,3584]{1,0:T(8,128)(2,1)S(1)}, bf16[32,3584]{1,0:T(8,128)(2,1)}, u32[]{:S(2)}, u32[]{:S(2)}) collective-permute-start(bf16[32,3584]{1,0:T(8,128)(2,1)S(1)} %collective-permute-done.14.refs_2_), channel_id=1, source_target_pairs={{0,1},{1,0},{2,3},{3,2},{4,5},{5,4},{6,7},{7,6},{8,9},{9,8},{10,11... | collective-permute-start | bytes 688136 | tf_op jit(solution)/shard_map/ppermute | solution.py:323
  61.9 3.9 %collective-permute-done.18.refs_6_ = bf16[32,3584]{1,0:T(8,128)(2,1)S(1)} collective-permute-done((bf16[32,3584]{1,0:T(8,128)(2,1)S(1)}, bf16[32,3584]{1,0:T(8,128)(2,1)S(1)}, u32[]{:S(2)}, u32[]{:S(2)}) %collective-permute-start.18) | collective-permute-done | bytes 229408 | tf_op jit(solution)/shard_map/ppermute | solution.py:323
  66.0 2.3 %collective-permute-done.20.refs_7_ = bf16[32,3584]{1,0:T(8,128)(2,1)S(1)} collective-permute-done((bf16[32,3584]{1,0:T(8,128)(2,1)S(1)}, bf16[32,3584]{1,0:T(8,128)(2,1)S(1)}, u32[]{:S(2)}, u32[]{:S(2)}) %collective-permute-start.20) | collective-permute-done | bytes 229408 | tf_op jit(solution)/shard_map/ppermute | solution.py:323
  68.3 3.5 %copy-done = bf16[1792,2432]{1,0:T(8,128)(2,1)S(1)} copy-done((bf16[1792,2432]{1,0:T(8,128)(2,1)S(1)}, bf16[1792,2432]{1,0:T(8,128)(2,1)}, u32[]{:S(2)}) %copy-start) | copy-done | bytes 8716312
  71.7 12.5 %shard_map.87 = (f32[256,2432]{1,0:T(8,128)S(1)}, f32[256,2432]{1,0:T(8,128)S(1)}, f32[8,256]{1,0:T(8,128)S(1)}, bf16[3584,2432]{1,0:T(8,128)(2,1)S(1)}) custom-call(bf16[32,3584]{1,0:T(8,128)(2,1)S(1)} %maximum_select_fusion.refs_0_, bf16[32,3584]{1,0:T(8,128)(2,1)S(1)} %collective-permute-done.refs_1_, ...), custom_call_target="tpu_custom_call" | custom-call | flops 2231369728 | bytes 16187392 | tf_op jit(solution)/shard_map/pallas_call | solution.py:193
  84.3 8.6 %shard_map.88 = (f32[256,2432]{1,0:T(8,128)S(1)}, f32[8,256]{1,0:T(8,128)S(1)}) custom-call(bf16[32,3584]{1,0:T(8,128)(2,1)S(1)} %maximum_select_fusion.1.refs_0_, bf16[32,3584]{1,0:T(8,128)(2,1)S(1)} %collective-permute-done.13.refs_1_, bf16[32,3584]{1,0:T(8,128)(2,1)S(1)} %collective-permute-done.14.refs_2_, ...), custom_call_target="tpu_custom_call" | custom-call | flops 4462739456 | bytes 24903680 | tf_op jit(solution)/shard_map/pallas_call | solution.py:216
  92.9 3.4 %collective-permute-start.25 = (f32[8,256]{1,0:T(8,128)S(1)}, f32[8,256]{1,0:T(8,128)S(1)}, u32[]{:S(2)}, u32[]{:S(2)}) collective-permute-start(f32[8,256]{1,0:T(8,128)S(1)} %get-tuple-element.50.refs_0_), channel_id=1, source_target_pairs={{0,4},{1,5},{2,6},{3,7},{4,0},{5,1},{6,2},{7,3},{8,12},{9,13},{10,... | collective-permute-start | bytes 24584 | tf_op jit(solution)/shard_map/ppermute | solution.py:401
  96.3 1.0 collective-permute-start.24
  97.4 0.7 collective-permute-start.23
  98.1 1.8 %collective-permute-start.22 = (f32[8,256]{1,0:T(8,128)S(1)}, f32[8,256]{1,0:T(8,128)S(1)}, u32[]{:S(2)}, u32[]{:S(2)}) collective-permute-start(f32[8,256]{1,0:T(8,128)S(1)} %get-tuple-element.50.refs_0_), channel_id=1, source_target_pairs={{0,1},{1,0},{2,3},{3,2},{4,5},{5,4},{6,7},{7,6},{8,9},{9,8},{10,11... | collective-permute-start | bytes 24584 | tf_op jit(solution)/shard_map/ppermute | solution.py:401
  99.8 1.2 collective-permute-start.28
  101.0 0.6 collective-permute-start.27
  101.6 1.7 %collective-permute-start.26 = (f32[8,256]{1,0:T(8,128)S(1)}, f32[8,256]{1,0:T(8,128)S(1)}, u32[]{:S(2)}, u32[]{:S(2)}) collective-permute-start(f32[8,256]{1,0:T(8,128)S(1)} %collective-permute-done.25.refs_4_), channel_id=1, source_target_pairs={{0,1},{1,0},{2,3},{3,2},{4,5},{5,4},{6,7},{7,6},{8,9},{9,8},{10,11... | collective-permute-start | bytes 24584 | tf_op jit(solution)/shard_map/ppermute | solution.py:401
  103.4 1.0 collective-permute-done.28.refs_7_
  104.7 0.6 collective-permute-done.26.refs_5_
  105.2 8.4 %shard_map.89 = (f32[8,256]{1,0:T(8,128)S(1)}, f32[32,3584]{1,0:T(8,128)S(1)}, f32[32,3584]{1,0:T(8,128)S(1)}, f32[32,3584]{1,0:T(8,128)S(1)}, f32[32,3584]{1,0:...) custom-call(s32[2]{0:T(128)S(1)} %pad_add_fusion.place_ref, ...), custom_call_target="tpu_custom_call" | custom-call | flops 4462739456 | bytes 24903680 | tf_op jit(solution)/shard_map/pallas_call | solution.py:298
  113.6 1.8 %collective-permute-start.31 = (f16[32,3584]{1,0:T(8,128)(2,1)S(1)}, f16[32,3584]{1,0:T(8,128)(2,1)S(1)}, u32[]{:S(2)}, u32[]{:S(2)}) collective-permute-start(f16[32,3584]{1,0:T(8,128)(2,1)S(1)} %convert_element_type.113), channel_id=1, source_target_pairs={{0,1},{1,0},{2,3},{3,2},{4,5},{5,4},{6,7},{7,6},{8,9},{9,8},{10,11... | collective-permute-start | bytes 688136 | tf_op jit(solution)/shard_map/ppermute | solution.py:323
  115.5 0.3 collective-permute-start.29
  115.9 6.4 %collective-permute-done.31 = f16[32,3584]{1,0:T(8,128)(2,1)S(1)} collective-permute-done((f16[32,3584]{1,0:T(8,128)(2,1)S(1)}, f16[32,3584]{1,0:T(8,128)(2,1)S(1)}, u32[]{:S(2)}, u32[]{:S(2)}) %collective-permute-start.31) | collective-permute-done | bytes 229408 | tf_op jit(solution)/shard_map/ppermute | solution.py:323
  122.3 1.7 %collective-permute-start.35 = (f16[32,3584]{1,0:T(8,128)(2,1)S(1)}, f16[32,3584]{1,0:T(8,128)(2,1)S(1)}, u32[]{:S(2)}, u32[]{:S(2)}) collective-permute-start(f16[32,3584]{1,0:T(8,128)(2,1)S(1)} %convert_element_type.121), channel_id=1, source_target_pairs={{0,1},{1,0},{2,3},{3,2},{4,5},{5,4},{6,7},{7,6},{8,9},{9,8},{10,11... | collective-permute-start | bytes 688136 | tf_op jit(solution)/shard_map/ppermute | solution.py:323
  124.0 2.9 %collective-permute-done.29 = f16[32,3584]{1,0:T(8,128)(2,1)S(1)} collective-permute-done((f16[32,3584]{1,0:T(8,128)(2,1)S(1)}, f16[32,3584]{1,0:T(8,128)(2,1)S(1)}, u32[]{:S(2)}, u32[]{:S(2)}) %collective-permute-start.29) | collective-permute-done | bytes 229408 | tf_op jit(solution)/shard_map/ppermute | solution.py:323
  126.9 1.6 %collective-permute-start.33 = (f16[32,3584]{1,0:T(8,128)(2,1)S(1)}, f16[32,3584]{1,0:T(8,128)(2,1)S(1)}, u32[]{:S(2)}, u32[]{:S(2)}) collective-permute-start(f16[32,3584]{1,0:T(8,128)(2,1)S(1)} %convert_element_type.117), channel_id=1, source_target_pairs={{0,1},{1,0},{2,3},{3,2},{4,5},{5,4},{6,7},{7,6},{8,9},{9,8},{10,11... | collective-permute-start | bytes 688136 | tf_op jit(solution)/shard_map/ppermute | solution.py:323
  128.6 1.5 %collective-permute-start.30 = (f16[32,3584]{1,0:T(8,128)(2,1)S(1)}, f16[32,3584]{1,0:T(8,128)(2,1)S(1)}, u32[]{:S(2)}, u32[]{:S(2)}) collective-permute-start(f16[32,3584]{1,0:T(8,128)(2,1)S(1)} %add_convert_fusion.3), channel_id=1, source_target_pairs={{0,2},{1,3},{2,0},{3,1},{4,6},{5,7},{6,4},{7,5},{8,10},{9,11},{10,... | collective-permute-start | bytes 688136 | tf_op jit(solution)/shard_map/ppermute | solution.py:323
  130.1 2.9 %collective-permute-done.33 = f16[32,3584]{1,0:T(8,128)(2,1)S(1)} collective-permute-done((f16[32,3584]{1,0:T(8,128)(2,1)S(1)}, f16[32,3584]{1,0:T(8,128)(2,1)S(1)}, u32[]{:S(2)}, u32[]{:S(2)}) %collective-permute-start.33) | collective-permute-done | bytes 229408 | tf_op jit(solution)/shard_map/ppermute | solution.py:323
  133.0 1.7 %collective-permute-start.34 = (f16[32,3584]{1,0:T(8,128)(2,1)S(1)}, f16[32,3584]{1,0:T(8,128)(2,1)S(1)}, u32[]{:S(2)}, u32[]{:S(2)}) collective-permute-start(f16[32,3584]{1,0:T(8,128)(2,1)S(1)} %add_convert_fusion.1), channel_id=1, source_target_pairs={{0,2},{1,3},{2,0},{3,1},{4,6},{5,7},{6,4},{7,5},{8,10},{9,11},{10,... | collective-permute-start | bytes 688136 | tf_op jit(solution)/shard_map/ppermute | solution.py:323
  134.7 2.1 %collective-permute-done.30 = f16[32,3584]{1,0:T(8,128)(2,1)S(1)} collective-permute-done((f16[32,3584]{1,0:T(8,128)(2,1)S(1)}, f16[32,3584]{1,0:T(8,128)(2,1)S(1)}, u32[]{:S(2)}, u32[]{:S(2)}) %collective-permute-start.30) | collective-permute-done | bytes 229408 | tf_op jit(solution)/shard_map/ppermute | solution.py:323
  136.9 1.1 collective-permute-start.32
  138.0 0.6 slice.27
  138.5 0.9 collective-permute-done.34
  139.4 6.9 %collective-permute-done.32 = f16[32,3584]{1,0:T(8,128)(2,1)S(1)} collective-permute-done((f16[32,3584]{1,0:T(8,128)(2,1)S(1)}, f16[32,3584]{1,0:T(8,128)(2,1)S(1)}, u32[]{:S(2)}, u32[]{:S(2)}) %collective-permute-start.32) | collective-permute-done | bytes 229408 | tf_op jit(solution)/shard_map/ppermute | solution.py:323
  146.4 0.8 maximum_select_fusion.2
  (49 shorter events, 1.7 us)
Async XLA Ops:
  0.6 67.6 %collective-permute-start.21 = (bf16[1792,2432]{1,0:T(8,128)(2,1)}, bf16[1792,2432]{1,0:T(8,128)(2,1)}, u32[]{:S(2)}, u32[]{:S(2)}) collective-permute-start(bf16[1792,2432]{1,0:T(8,128)(2,1)} %refs_8_.1), channel_id=1, source_target_pairs={{0,8},{8,0},{1,9},{9,1},{2,10},{10,2},{3,11},{11,3},{4,12},{12,4},... | collective-permute-start | bytes 26148872 | tf_op jit(solution)/shard_map/ppermute | solution.py:382
  3.1 14.2 %collective-permute-start.6 = (bf16[32,3584]{1,0:T(8,128)(2,1)S(1)}, bf16[32,3584]{1,0:T(8,128)(2,1)S(1)}, u32[]{:S(2)}, u32[]{:S(2)}) collective-permute-start(bf16[32,3584]{1,0:T(8,128)(2,1)S(1)} %maximum_select_fusion.refs_0_), channel_id=1, source_target_pairs={{0,4},{1,5},{2,6},{3,7},{4,0},{5,1},{6,2},{7,3},{8,12},{9,13},{10,... | collective-permute-start | bytes 688136 | tf_op jit(solution)/shard_map/ppermute | solution.py:323
  6.8 10.5 %collective-permute-start.3 = (bf16[32,3584]{1,0:T(8,128)(2,1)S(1)}, bf16[32,3584]{1,0:T(8,128)(2,1)S(1)}, u32[]{:S(2)}, u32[]{:S(2)}) collective-permute-start(bf16[32,3584]{1,0:T(8,128)(2,1)S(1)} %maximum_select_fusion.refs_0_), channel_id=1, source_target_pairs={{0,2},{1,3},{2,0},{3,1},{4,6},{5,7},{6,4},{7,5},{8,10},{9,11},{10,... | collective-permute-start | bytes 688136 | tf_op jit(solution)/shard_map/ppermute | solution.py:323
  8.4 7.9 %collective-permute-start = (bf16[32,3584]{1,0:T(8,128)(2,1)S(1)}, bf16[32,3584]{1,0:T(8,128)(2,1)S(1)}, u32[]{:S(2)}, u32[]{:S(2)}) collective-permute-start(bf16[32,3584]{1,0:T(8,128)(2,1)S(1)} %maximum_select_fusion.refs_0_), channel_id=1, source_target_pairs={{0,1},{1,0},{2,3},{3,2},{4,5},{5,4},{6,7},{7,6},{8,9},{9,8},{10,11... | collective-permute-start | bytes 688136 | tf_op jit(solution)/shard_map/ppermute | solution.py:323
  11.4 40.4 %copy-start.1 = (s32[256]{0:T(256)S(1)}, s32[256]{0:T(256)}, u32[]{:S(2)}) copy-start(s32[256]{0:T(256)} %param.13) | copy-start | bytes 3076
  16.3 8.6 %collective-permute-start.1 = (f16[32,3584]{1,0:T(8,128)(2,1)S(1)}, f16[32,3584]{1,0:T(8,128)(2,1)S(1)}, u32[]{:S(2)}, u32[]{:S(2)}) collective-permute-start(f16[32,3584]{1,0:T(8,128)(2,1)S(1)} %convert_element_type.94), channel_id=1, source_target_pairs={{0,1},{1,0},{2,3},{3,2},{4,5},{5,4},{6,7},{7,6},{8,9},{9,8},{10,11... | collective-permute-start | bytes 688136 | tf_op jit(solution)/shard_map/ppermute | solution.py:323
  17.3 12.5 %collective-permute-start.7 = (f16[32,3584]{1,0:T(8,128)(2,1)S(1)}, f16[32,3584]{1,0:T(8,128)(2,1)S(1)}, u32[]{:S(2)}, u32[]{:S(2)}) collective-permute-start(f16[32,3584]{1,0:T(8,128)(2,1)S(1)} %convert_element_type.102), channel_id=1, source_target_pairs={{0,1},{1,0},{2,3},{3,2},{4,5},{5,4},{6,7},{7,6},{8,9},{9,8},{10,11... | collective-permute-start | bytes 688136 | tf_op jit(solution)/shard_map/ppermute | solution.py:323
  18.9 13.5 %collective-permute-start.4 = (f16[32,3584]{1,0:T(8,128)(2,1)S(1)}, f16[32,3584]{1,0:T(8,128)(2,1)S(1)}, u32[]{:S(2)}, u32[]{:S(2)}) collective-permute-start(f16[32,3584]{1,0:T(8,128)(2,1)S(1)} %convert_element_type.98), channel_id=1, source_target_pairs={{0,1},{1,0},{2,3},{3,2},{4,5},{5,4},{6,7},{7,6},{8,9},{9,8},{10,11... | collective-permute-start | bytes 688136 | tf_op jit(solution)/shard_map/ppermute | solution.py:323
  25.0 8.0 %collective-permute-start.2 = (f16[32,3584]{1,0:T(8,128)(2,1)S(1)}, f16[32,3584]{1,0:T(8,128)(2,1)S(1)}, u32[]{:S(2)}, u32[]{:S(2)}) collective-permute-start(f16[32,3584]{1,0:T(8,128)(2,1)S(1)} %add_convert_fusion.6), channel_id=1, source_target_pairs={{0,2},{1,3},{2,0},{3,1},{4,6},{5,7},{6,4},{7,5},{8,10},{9,11},{10,... | collective-permute-start | bytes 688136 | tf_op jit(solution)/shard_map/ppermute | solution.py:323
  29.9 10.1 %collective-permute-start.8 = (f16[32,3584]{1,0:T(8,128)(2,1)S(1)}, f16[32,3584]{1,0:T(8,128)(2,1)S(1)}, u32[]{:S(2)}, u32[]{:S(2)}) collective-permute-start(f16[32,3584]{1,0:T(8,128)(2,1)S(1)} %add_convert_fusion.4), channel_id=1, source_target_pairs={{0,2},{1,3},{2,0},{3,1},{4,6},{5,7},{6,4},{7,5},{8,10},{9,11},{10,... | collective-permute-start | bytes 688136 | tf_op jit(solution)/shard_map/ppermute | solution.py:323
  32.4 8.3 %collective-permute-start.9 = (f16[32,3584]{1,0:T(8,128)(2,1)S(1)}, f16[32,3584]{1,0:T(8,128)(2,1)S(1)}, u32[]{:S(2)}, u32[]{:S(2)}) collective-permute-start(f16[32,3584]{1,0:T(8,128)(2,1)S(1)} %convert_element_type.106), channel_id=1, source_target_pairs={{0,1},{1,0},{2,3},{3,2},{4,5},{5,4},{6,7},{7,6},{8,9},{9,8},{10,11... | collective-permute-start | bytes 688136 | tf_op jit(solution)/shard_map/ppermute | solution.py:323
  33.0 11.0 %collective-permute-start.5 = (f16[32,3584]{1,0:T(8,128)(2,1)S(1)}, f16[32,3584]{1,0:T(8,128)(2,1)S(1)}, u32[]{:S(2)}, u32[]{:S(2)}) collective-permute-start(f16[32,3584]{1,0:T(8,128)(2,1)S(1)} %add_convert_fusion.5), channel_id=1, source_target_pairs={{0,4},{1,5},{2,6},{3,7},{4,0},{5,1},{6,2},{7,3},{8,12},{9,13},{10,... | collective-permute-start | bytes 688136 | tf_op jit(solution)/shard_map/ppermute | solution.py:323
  33.9 11.9 %collective-permute-start.12 = (bf16[32,3584]{1,0:T(8,128)(2,1)S(1)}, bf16[32,3584]{1,0:T(8,128)(2,1)S(1)}, u32[]{:S(2)}, u32[]{:S(2)}) collective-permute-start(bf16[32,3584]{1,0:T(8,128)(2,1)S(1)} %collective-permute-done.6.refs_4_), channel_id=1, source_target_pairs={{0,2},{1,3},{2,0},{3,1},{4,6},{5,7},{6,4},{7,5},{8,10},{9,11},{10,... | collective-permute-start | bytes 688136 | tf_op jit(solution)/shard_map/ppermute | solution.py:323
  39.9 6.0 %collective-permute-start.11 = (bf16[32,3584]{1,0:T(8,128)(2,1)S(1)}, bf16[32,3584]{1,0:T(8,128)(2,1)S(1)}, u32[]{:S(2)}, u32[]{:S(2)}) collective-permute-start(bf16[32,3584]{1,0:T(8,128)(2,1)S(1)} %collective-permute-done.6.refs_4_), channel_id=1, source_target_pairs={{0,1},{1,0},{2,3},{3,2},{4,5},{5,4},{6,7},{7,6},{8,9},{9,8},{10,11... | collective-permute-start | bytes 688136 | tf_op jit(solution)/shard_map/ppermute | solution.py:323
  40.7 7.7 %collective-permute-start.10 = (bf16[32,3584]{1,0:T(8,128)(2,1)S(1)}, bf16[32,3584]{1,0:T(8,128)(2,1)S(1)}, u32[]{:S(2)}, u32[]{:S(2)}) collective-permute-start(bf16[32,3584]{1,0:T(8,128)(2,1)S(1)} %collective-permute-done.3.refs_2_), channel_id=1, source_target_pairs={{0,1},{1,0},{2,3},{3,2},{4,5},{5,4},{6,7},{7,6},{8,9},{9,8},{10,11... | collective-permute-start | bytes 688136 | tf_op jit(solution)/shard_map/ppermute | solution.py:323
  48.5 9.3 %collective-permute-start.16 = (bf16[32,3584]{1,0:T(8,128)(2,1)S(1)}, bf16[32,3584]{1,0:T(8,128)(2,1)S(1)}, u32[]{:S(2)}, u32[]{:S(2)}) collective-permute-start(bf16[32,3584]{1,0:T(8,128)(2,1)S(1)} %maximum_select_fusion.1.refs_0_), channel_id=1, source_target_pairs={{0,4},{1,5},{2,6},{3,7},{4,0},{5,1},{6,2},{7,3},{8,12},{9,13},{10,... | collective-permute-start | bytes 688136 | tf_op jit(solution)/shard_map/ppermute | solution.py:323
  48.8 9.1 %collective-permute-start.14 = (bf16[32,3584]{1,0:T(8,128)(2,1)S(1)}, bf16[32,3584]{1,0:T(8,128)(2,1)S(1)}, u32[]{:S(2)}, u32[]{:S(2)}) collective-permute-start(bf16[32,3584]{1,0:T(8,128)(2,1)S(1)} %maximum_select_fusion.1.refs_0_), channel_id=1, source_target_pairs={{0,2},{1,3},{2,0},{3,1},{4,6},{5,7},{6,4},{7,5},{8,10},{9,11},{10,... | collective-permute-start | bytes 688136 | tf_op jit(solution)/shard_map/ppermute | solution.py:323
  50.2 7.6 %collective-permute-start.13 = (bf16[32,3584]{1,0:T(8,128)(2,1)S(1)}, bf16[32,3584]{1,0:T(8,128)(2,1)S(1)}, u32[]{:S(2)}, u32[]{:S(2)}) collective-permute-start(bf16[32,3584]{1,0:T(8,128)(2,1)S(1)} %maximum_select_fusion.1.refs_0_), channel_id=1, source_target_pairs={{0,1},{1,0},{2,3},{3,2},{4,5},{5,4},{6,7},{7,6},{8,9},{9,8},{10,11... | collective-permute-start | bytes 688136 | tf_op jit(solution)/shard_map/ppermute | solution.py:323
  57.9 7.9 %collective-permute-start.18 = (bf16[32,3584]{1,0:T(8,128)(2,1)S(1)}, bf16[32,3584]{1,0:T(8,128)(2,1)S(1)}, u32[]{:S(2)}, u32[]{:S(2)}) collective-permute-start(bf16[32,3584]{1,0:T(8,128)(2,1)S(1)} %collective-permute-done.16.refs_4_), channel_id=1, source_target_pairs={{0,2},{1,3},{2,0},{3,1},{4,6},{5,7},{6,4},{7,5},{8,10},{9,11},{10,... | collective-permute-start | bytes 688136 | tf_op jit(solution)/shard_map/ppermute | solution.py:323
  59.2 9.1 %collective-permute-start.20 = (bf16[32,3584]{1,0:T(8,128)(2,1)S(1)}, bf16[32,3584]{1,0:T(8,128)(2,1)S(1)}, u32[]{:S(2)}, u32[]{:S(2)}) collective-permute-start(bf16[32,3584]{1,0:T(8,128)(2,1)S(1)} %collective-permute-done.11.refs_5_), channel_id=1, source_target_pairs={{0,2},{1,3},{2,0},{3,1},{4,6},{5,7},{6,4},{7,5},{8,10},{9,11},{10,... | collective-permute-start | bytes 688136 | tf_op jit(solution)/shard_map/ppermute | solution.py:323
  59.9 24.4 %collective-permute-start.17 = (bf16[32,3584]{1,0:T(8,128)(2,1)S(1)}, bf16[32,3584]{1,0:T(8,128)(2,1)S(1)}, u32[]{:S(2)}, u32[]{:S(2)}) collective-permute-start(bf16[32,3584]{1,0:T(8,128)(2,1)S(1)} %collective-permute-done.16.refs_4_), channel_id=1, source_target_pairs={{0,1},{1,0},{2,3},{3,2},{4,5},{5,4},{6,7},{7,6},{8,9},{9,8},{10,11... | collective-permute-start | bytes 688136 | tf_op jit(solution)/shard_map/ppermute | solution.py:323
  60.3 23.9 %collective-permute-start.15 = (bf16[32,3584]{1,0:T(8,128)(2,1)S(1)}, bf16[32,3584]{1,0:T(8,128)(2,1)}, u32[]{:S(2)}, u32[]{:S(2)}) collective-permute-start(bf16[32,3584]{1,0:T(8,128)(2,1)S(1)} %collective-permute-done.14.refs_2_), channel_id=1, source_target_pairs={{0,1},{1,0},{2,3},{3,2},{4,5},{5,4},{6,7},{7,6},{8,9},{9,8},{10,11... | collective-permute-start | bytes 688136 | tf_op jit(solution)/shard_map/ppermute | solution.py:323
  65.8 18.5 %collective-permute-start.19 = (bf16[32,3584]{1,0:T(8,128)(2,1)S(1)}, bf16[32,3584]{1,0:T(8,128)(2,1)}, u32[]{:S(2)}, u32[]{:S(2)}) collective-permute-start(bf16[32,3584]{1,0:T(8,128)(2,1)S(1)} %collective-permute-done.18.refs_6_), channel_id=1, source_target_pairs={{0,1},{1,0},{2,3},{3,2},{4,5},{5,4},{6,7},{7,6},{8,9},{9,8},{10,11... | collective-permute-start | bytes 688136 | tf_op jit(solution)/shard_map/ppermute | solution.py:323
  68.3 3.5 %copy-start = (bf16[1792,2432]{1,0:T(8,128)(2,1)S(1)}, bf16[1792,2432]{1,0:T(8,128)(2,1)}, u32[]{:S(2)}) copy-start(bf16[1792,2432]{1,0:T(8,128)(2,1)} %refs_8_.1) | copy-start | bytes 26148868
  92.9 6.9 %collective-permute-start.25 = (f32[8,256]{1,0:T(8,128)S(1)}, f32[8,256]{1,0:T(8,128)S(1)}, u32[]{:S(2)}, u32[]{:S(2)}) collective-permute-start(f32[8,256]{1,0:T(8,128)S(1)} %get-tuple-element.50.refs_0_), channel_id=1, source_target_pairs={{0,4},{1,5},{2,6},{3,7},{4,0},{5,1},{6,2},{7,3},{8,12},{9,13},{10,... | collective-permute-start | bytes 24584 | tf_op jit(solution)/shard_map/ppermute | solution.py:401
  96.3 5.2 %collective-permute-start.24 = (f32[8,256]{1,0:T(8,128)S(1)}, f32[8,256]{1,0:T(8,128)S(1)}, u32[]{:S(2)}, u32[]{:S(2)}) collective-permute-start(f32[8,256]{1,0:T(8,128)S(1)} %get-tuple-element.50.refs_0_), channel_id=1, source_target_pairs={{0,3},{1,2},{2,1},{3,0},{4,7},{5,6},{6,5},{7,4},{8,11},{9,10},{10,... | collective-permute-start | bytes 24584 | tf_op jit(solution)/shard_map/ppermute | solution.py:401
  97.4 6.0 %collective-permute-start.23 = (f32[8,256]{1,0:T(8,128)S(1)}, f32[8,256]{1,0:T(8,128)S(1)}, u32[]{:S(2)}, u32[]{:S(2)}) collective-permute-start(f32[8,256]{1,0:T(8,128)S(1)} %get-tuple-element.50.refs_0_), channel_id=1, source_target_pairs={{0,2},{1,3},{2,0},{3,1},{4,6},{5,7},{6,4},{7,5},{8,10},{9,11},{10,... | collective-permute-start | bytes 24584 | tf_op jit(solution)/shard_map/ppermute | solution.py:401
  98.1 5.3 %collective-permute-start.22 = (f32[8,256]{1,0:T(8,128)S(1)}, f32[8,256]{1,0:T(8,128)S(1)}, u32[]{:S(2)}, u32[]{:S(2)}) collective-permute-start(f32[8,256]{1,0:T(8,128)S(1)} %get-tuple-element.50.refs_0_), channel_id=1, source_target_pairs={{0,1},{1,0},{2,3},{3,2},{4,5},{5,4},{6,7},{7,6},{8,9},{9,8},{10,11... | collective-permute-start | bytes 24584 | tf_op jit(solution)/shard_map/ppermute | solution.py:401
  99.8 4.6 %collective-permute-start.28 = (f32[8,256]{1,0:T(8,128)S(1)}, f32[8,256]{1,0:T(8,128)S(1)}, u32[]{:S(2)}, u32[]{:S(2)}) collective-permute-start(f32[8,256]{1,0:T(8,128)S(1)} %collective-permute-done.25.refs_4_), channel_id=1, source_target_pairs={{0,3},{1,2},{2,1},{3,0},{4,7},{5,6},{6,5},{7,4},{8,11},{9,10},{10,... | collective-permute-start | bytes 24584 | tf_op jit(solution)/shard_map/ppermute | solution.py:401
  101.0 3.7 %collective-permute-start.27 = (f32[8,256]{1,0:T(8,128)S(1)}, f32[8,256]{1,0:T(8,128)S(1)}, u32[]{:S(2)}, u32[]{:S(2)}) collective-permute-start(f32[8,256]{1,0:T(8,128)S(1)} %collective-permute-done.25.refs_4_), channel_id=1, source_target_pairs={{0,2},{1,3},{2,0},{3,1},{4,6},{5,7},{6,4},{7,5},{8,10},{9,11},{10,... | collective-permute-start | bytes 24584 | tf_op jit(solution)/shard_map/ppermute | solution.py:401
  101.6 3.7 %collective-permute-start.26 = (f32[8,256]{1,0:T(8,128)S(1)}, f32[8,256]{1,0:T(8,128)S(1)}, u32[]{:S(2)}, u32[]{:S(2)}) collective-permute-start(f32[8,256]{1,0:T(8,128)S(1)} %collective-permute-done.25.refs_4_), channel_id=1, source_target_pairs={{0,1},{1,0},{2,3},{3,2},{4,5},{5,4},{6,7},{7,6},{8,9},{9,8},{10,11... | collective-permute-start | bytes 24584 | tf_op jit(solution)/shard_map/ppermute | solution.py:401
  113.6 8.6 %collective-permute-start.31 = (f16[32,3584]{1,0:T(8,128)(2,1)S(1)}, f16[32,3584]{1,0:T(8,128)(2,1)S(1)}, u32[]{:S(2)}, u32[]{:S(2)}) collective-permute-start(f16[32,3584]{1,0:T(8,128)(2,1)S(1)} %convert_element_type.113), channel_id=1, source_target_pairs={{0,1},{1,0},{2,3},{3,2},{4,5},{5,4},{6,7},{7,6},{8,9},{9,8},{10,11... | collective-permute-start | bytes 688136 | tf_op jit(solution)/shard_map/ppermute | solution.py:323
  115.5 11.5 %collective-permute-start.29 = (f16[32,3584]{1,0:T(8,128)(2,1)S(1)}, f16[32,3584]{1,0:T(8,128)(2,1)S(1)}, u32[]{:S(2)}, u32[]{:S(2)}) collective-permute-start(f16[32,3584]{1,0:T(8,128)(2,1)S(1)} %convert_element_type.109), channel_id=1, source_target_pairs={{0,1},{1,0},{2,3},{3,2},{4,5},{5,4},{6,7},{7,6},{8,9},{9,8},{10,11... | collective-permute-start | bytes 688136 | tf_op jit(solution)/shard_map/ppermute | solution.py:323
  122.3 16.3 %collective-permute-start.35 = (f16[32,3584]{1,0:T(8,128)(2,1)S(1)}, f16[32,3584]{1,0:T(8,128)(2,1)S(1)}, u32[]{:S(2)}, u32[]{:S(2)}) collective-permute-start(f16[32,3584]{1,0:T(8,128)(2,1)S(1)} %convert_element_type.121), channel_id=1, source_target_pairs={{0,1},{1,0},{2,3},{3,2},{4,5},{5,4},{6,7},{7,6},{8,9},{9,8},{10,11... | collective-permute-start | bytes 688136 | tf_op jit(solution)/shard_map/ppermute | solution.py:323
  126.9 6.0 %collective-permute-start.33 = (f16[32,3584]{1,0:T(8,128)(2,1)S(1)}, f16[32,3584]{1,0:T(8,128)(2,1)S(1)}, u32[]{:S(2)}, u32[]{:S(2)}) collective-permute-start(f16[32,3584]{1,0:T(8,128)(2,1)S(1)} %convert_element_type.117), channel_id=1, source_target_pairs={{0,1},{1,0},{2,3},{3,2},{4,5},{5,4},{6,7},{7,6},{8,9},{9,8},{10,11... | collective-permute-start | bytes 688136 | tf_op jit(solution)/shard_map/ppermute | solution.py:323
  128.6 8.2 %collective-permute-start.30 = (f16[32,3584]{1,0:T(8,128)(2,1)S(1)}, f16[32,3584]{1,0:T(8,128)(2,1)S(1)}, u32[]{:S(2)}, u32[]{:S(2)}) collective-permute-start(f16[32,3584]{1,0:T(8,128)(2,1)S(1)} %add_convert_fusion.3), channel_id=1, source_target_pairs={{0,2},{1,3},{2,0},{3,1},{4,6},{5,7},{6,4},{7,5},{8,10},{9,11},{10,... | collective-permute-start | bytes 688136 | tf_op jit(solution)/shard_map/ppermute | solution.py:323
  133.0 6.4 %collective-permute-start.34 = (f16[32,3584]{1,0:T(8,128)(2,1)S(1)}, f16[32,3584]{1,0:T(8,128)(2,1)S(1)}, u32[]{:S(2)}, u32[]{:S(2)}) collective-permute-start(f16[32,3584]{1,0:T(8,128)(2,1)S(1)} %add_convert_fusion.1), channel_id=1, source_target_pairs={{0,2},{1,3},{2,0},{3,1},{4,6},{5,7},{6,4},{7,5},{8,10},{9,11},{10,... | collective-permute-start | bytes 688136 | tf_op jit(solution)/shard_map/ppermute | solution.py:323
  136.9 9.4 %collective-permute-start.32 = (f16[32,3584]{1,0:T(8,128)(2,1)S(1)}, f16[32,3584]{1,0:T(8,128)(2,1)S(1)}, u32[]{:S(2)}, u32[]{:S(2)}) collective-permute-start(f16[32,3584]{1,0:T(8,128)(2,1)S(1)} %add_convert_fusion.2), channel_id=1, source_target_pairs={{0,4},{1,5},{2,6},{3,7},{4,0},{5,1},{6,2},{7,3},{8,12},{9,13},{10,... | collective-permute-start | bytes 688136 | tf_op jit(solution)/shard_map/ppermute | solution.py:323

commit v6 on v5

--- a/solution.py
+++ b/solution.py
@@ -11,8 +11,7 @@
 wire = jnp.float16
 lanes = 128
 vmem_bytes = 12 * 1024 * 1024
-student_bytes = 12 * 1024 * 1024
-project_bytes = 50 * 1024 * 1024
+project_bytes = 47 * 1024 * 1024
 
 in_vmem = pl.BlockSpec(memory_space=pltpu.VMEM)
 in_smem = pl.BlockSpec(memory_space=pltpu.SMEM)
@@ -72,26 +71,14 @@
     )(member, teacher_rows, proj_weight)
 
 
-class Fetch:
-    def __init__(self, sems):
-        self.sems, self.used = sems, 0
-
-    def start(self, source, target):
-        copy = pltpu.make_async_copy(source, target, self.sems.at[self.used])
-        copy.start()
-        self.used += 1
-        return copy
-
-
-def multiply(read_rows, head, logit_ref, highest, step, ready=None):
-    total = head.shape[1]
+def multiply(read_rows, heads, logit_ref, highest, step):
+    depth, total = heads[0].shape
     highest[...] = jnp.full(highest.shape, -jnp.inf, jnp.float32)
 
-    def one(index, start, size):
+    def one(start, size):
         at = pl.ds(start, size)
-        if ready is not None:
-            ready(index, at)
-        part = jnp.dot(read_rows(), head[:, at], preferred_element_type=jnp.float32)
+        part = jnp.dot(read_rows(0, depth), heads[0][:, at], preferred_element_type=jnp.float32)
+        part += jnp.dot(read_rows(depth, 2 * depth), heads[1][:, at], preferred_element_type=jnp.float32)
         logit_ref[:, at] = part
         top = part[:, :lanes]
         for lane in range(lanes, size, lanes):
@@ -99,13 +86,13 @@
         highest[...] = jnp.maximum(highest[...], top)
 
     def body(index, carry):
-        one(index, pl.multiple_of(index * step, step), step)
+        one(pl.multiple_of(index * step, step), step)
         return carry
 
     full = total // step
     lax.fori_loop(0, full, body, 0)
     if total % step:
-        one(full, full * step, total % step)
+        one(full * step, total % step)
 
 
 def as_columns(first, second, third):
@@ -115,28 +102,16 @@
 
 def student_kernel(count, step, chunk, *refs):
     pieces, heads = refs[:count], refs[count : count + 2]
-    column_ref, logit_ref, scaled_ref, stats_ref, head = refs[count + 2 : count + 7]
-    held, highest, table, sems = refs[count + 7 :]
-    depth, total = heads[0].shape
+    column_ref, logit_ref, scaled_ref, stats_ref = refs[count + 2 : count + 6]
+    held, highest, table, sems = refs[count + 6 :]
     blk = pieces[0].shape[0]
-    fetch = Fetch(sems)
-    waits = [fetch.start(piece, held.at[pl.ds(i * blk, blk)]) for i, piece in enumerate(pieces)]
-    first = fetch.used
-
-    def columns(half, at):
-        return heads[half].at[:, at], head.at[pl.ds(half * depth, depth), at]
-
-    for start, size in cuts(total, step):
-        for half in range(2):
-            fetch.start(*columns(half, pl.ds(start, size)))
-
-    def ready(index, at):
-        for half in range(2):
-            pltpu.make_async_copy(*columns(half, at), sems.at[first + 2 * index + half]).wait()
-
-    for wait in waits:
-        wait.wait()
-    multiply(lambda: held[...], head, logit_ref, highest, step, ready)
+    copies = []
+    for i, piece in enumerate(pieces):
+        copies.append(pltpu.make_async_copy(piece, held.at[pl.ds(i * blk, blk)], sems.at[i]))
+        copies[-1].start()
+    for copy in copies:
+        copy.wait()
+    multiply(lambda start, end: held[:, start:end], heads, logit_ref, highest, step)
 
     def one(part, carry):
         rows = pl.ds(pl.multiple_of(part * chunk, chunk), chunk)
@@ -154,13 +129,13 @@
 
 
 def teacher_kernel(count, step, chunk, *refs):
-    pieces = refs[:count]
-    head, stud_logit_ref, stud_ref, scaled_ref, stats_ref, highest, table = refs[count:]
-
-    def read_rows():
-        return jnp.concatenate([ref[...] for ref in pieces], axis=0) if count > 1 else pieces[0][...]
-
-    multiply(read_rows, head, scaled_ref, highest, step)
+    pieces, heads = refs[:count], refs[count : count + 2]
+    stud_logit_ref, stud_ref, scaled_ref, stats_ref, highest, table = refs[count + 2 :]
+
+    def read_rows(start, end):
+        return jnp.concatenate([ref[:, start:end] for ref in pieces], axis=0)
+
+    multiply(read_rows, heads, scaled_ref, highest, step)
 
     def one(part, carry):
         rows = pl.ds(pl.multiple_of(part * chunk, chunk), chunk)
@@ -178,8 +153,8 @@
     stats_ref[...] = jnp.where(row < 4, teach, pltpu.roll(stud_ref[...], 4, 0))
 
 
-def head_cost(rows, head):
-    depth, vocab_dev = head.shape
+def head_cost(rows, heads):
+    depth, vocab_dev = 2 * heads[0].shape[0], heads[0].shape[1]
     return pl.CostEstimate(
         flops=2 * rows * depth * vocab_dev,
         bytes_accessed=2 * depth * vocab_dev + 12 * rows * vocab_dev,
@@ -192,30 +167,29 @@
     wide = (rows, vocab_dev)
     return pl.pallas_call(
         functools.partial(student_kernel, len(pieces), step, chunk),
-        in_specs=[in_place] * (len(pieces) + 2) + [in_vmem],
-        out_specs=[in_vmem] * 4,
+        in_specs=[in_place] * len(pieces) + [in_vmem] * 3,
+        out_specs=[in_vmem] * 3,
         out_shape=[
             jax.ShapeDtypeStruct(wide, jnp.float32),
             jax.ShapeDtypeStruct(wide, jnp.float32),
             jax.ShapeDtypeStruct((8, rows), jnp.float32),
-            jax.ShapeDtypeStruct((2 * depth, vocab_dev), jnp.bfloat16),
         ],
         scratch_shapes=[
             pltpu.VMEM((rows, 2 * depth), jnp.bfloat16),
             pltpu.VMEM((rows, lanes), jnp.float32),
             pltpu.VMEM((rows, lanes), jnp.float32),
-            pltpu.SemaphoreType.DMA((len(pieces) + 2 * len(cuts(vocab_dev, step)),)),
+            pltpu.SemaphoreType.DMA((len(pieces),)),
         ],
-        compiler_params=pltpu.CompilerParams(vmem_limit_bytes=student_bytes),
-        cost_estimate=head_cost(rows, heads[0]),
+        compiler_params=pltpu.CompilerParams(vmem_limit_bytes=vmem_bytes),
+        cost_estimate=head_cost(rows, heads),
     )(*pieces, *heads, column)
 
 
-def teacher_logits(pieces, head, logit_stud, stats_stud, step, chunk):
+def teacher_logits(pieces, heads, logit_stud, stats_stud, step, chunk):
     wide = logit_stud.shape
     return pl.pallas_call(
         functools.partial(teacher_kernel, len(pieces), step, chunk),
-        in_specs=[in_vmem] * (len(pieces) + 3),
+        in_specs=[in_vmem] * (len(pieces) + 4),
         out_specs=[in_vmem] * 2,
         out_shape=[
             jax.ShapeDtypeStruct(wide, jnp.float32),
@@ -223,8 +197,8 @@
         ],
         scratch_shapes=[pltpu.VMEM((wide[0], lanes), jnp.float32)] * 2,
         compiler_params=pltpu.CompilerParams(vmem_limit_bytes=vmem_bytes),
-        cost_estimate=head_cost(wide[0], head),
-    )(*pieces, head, logit_stud, stats_stud)
+        cost_estimate=head_cost(wide[0], heads),
+    )(*pieces, *heads, logit_stud, stats_stud)
 
 
 def swapped(values, distance):
@@ -238,9 +212,9 @@
 def gradient_kernel(bits, step, chunk, place_ref, *refs):
     count = 1 << bits
     tables, refs = refs[:count], refs[count:]
-    teach_ref, stud_ref, column_ref, head, loss_ref = refs[:5]
-    outs = refs[5 : count + 5]
-    entries, upstream, factors = refs[count + 5 :]
+    teach_ref, stud_ref, column_ref, *heads, loss_ref = refs[:6]
+    outs = refs[6 : count + 6]
+    entries, upstream, factors = refs[count + 6 :]
     rows = upstream.shape[0]
     blk = rows // count
     me = place_ref[0]
@@ -279,25 +253,36 @@
 
     lax.fori_loop(0, rows // chunk, one, 0)
 
-    def two(index, carry):
-        at = pl.ds(pl.multiple_of(index * step, step), step)
-        product = lax.dot_general(
-            upstream[...], head[at, :], (((1,), (1,)), ((), ())), preferred_element_type=jnp.float32
-        )
-        for piece, out in enumerate(outs):
-            out[:, at] = product[piece * blk : (piece + 1) * blk]
-        return carry
-
-    lax.fori_loop(0, head.shape[0] // step, two, 0)
-
-
-def gradient(place, tables, scaled_teach, scaled_stud, column, head, bits, chunk):
+    depth = heads[0].shape[0]
+    for half, head in enumerate(heads):
+
+        def two(start, size, half=half, head=head):
+            product = lax.dot_general(
+                upstream[...],
+                head[pl.ds(start, size), :],
+                (((1,), (1,)), ((), ())),
+                preferred_element_type=jnp.float32,
+            )
+            at = pl.ds(pl.multiple_of(half * depth + start, lanes), size)
+            for piece, out in enumerate(outs):
+                out[:, at] = product[piece * blk : (piece + 1) * blk]
+
+        def body(index, carry, two=two):
+            two(pl.multiple_of(index * step, step), step)
+            return carry
+
+        lax.fori_loop(0, depth // step, body, 0)
+        if depth % step:
+            two(depth - depth % step, depth % step)
+
+
+def gradient(place, tables, scaled_teach, scaled_stud, column, heads, bits, chunk):
     rows, vocab_dev = scaled_teach.shape
-    count, width = 1 << bits, head.shape[0]
-    step = 512 if width % 512 == 0 else width
+    count, width = 1 << bits, 2 * heads[0].shape[0]
+    step = 512 if width % 256 == 0 else width // 2
     return pl.pallas_call(
         functools.partial(gradient_kernel, bits, step, chunk),
-        in_specs=[in_smem] + [in_vmem] * (count + 4),
+        in_specs=[in_smem] + [in_vmem] * (count + 5),
         out_specs=[in_vmem] * (count + 1),
         out_shape=[jax.ShapeDtypeStruct((8, rows), jnp.float32)]
         + [jax.ShapeDtypeStruct((rows // count, width), jnp.float32)] * count,
@@ -307,8 +292,8 @@
             pltpu.VMEM((rows, lanes), jnp.float32),
         ],
         compiler_params=pltpu.CompilerParams(vmem_limit_bytes=vmem_bytes),
-        cost_estimate=head_cost(rows, head),
-    )(place, *tables, scaled_teach, scaled_stud, column, head)
+        cost_estimate=head_cost(rows, heads),
+    )(place, *tables, scaled_teach, scaled_stud, column, *heads)
 
 
 def tie(block, *others):
@@ -325,7 +310,7 @@
     def lowest(mask):
         return (mask & -mask).bit_length() - 1
 
-    def spread(own, mixed):
+    def spread(own, mixed, *between):
         blocks = {0: own}
         masks = range(1, vocab_size)
         if not mixed:
@@ -338,7 +323,7 @@
             bit = 1 if mixed and mask & 3 == 3 and mask > 3 else lowest(mask)
             block = blocks[mask ^ (1 << bit)]
             if not mixed and mask ^ (1 << bit) == 1 << (bits - 1):
-                block = tie(block, *own_hops)
+                block = tie(block, *own_hops, *between)
             blocks[mask] = swap(block, bit)
         return [blocks[mask] for mask in range(vocab_size)]
 
@@ -386,20 +371,20 @@
         alive = lax.iota(jnp.int32, teach_rows) < counts[0]
         member = (owner[None, :] == row_id[:, None]) & alive[None, :]
         parts = project(member.astype(jnp.bfloat16), teacher_rows, proj_weight, vocab_size, 512 if student_hidden.shape[1] % 512 == 0 else student_hidden.shape[1])
-        hidden = spread(turned(student_hidden), True)
-        gates = dict(zip(range(vocab_size - 1, 0, -2), (hidden[1], hidden[2], hidden[vocab_size // 2])))
-        projected_own = tie(reduce_blocks(parts, gates), *hidden[:-1])
-        projected = spread(turned(projected_own.astype(jnp.bfloat16)), False)
-
+        hidden = spread(tie(turned(student_hidden), parts[-1]), True)
+        projected_own = tie(reduce_blocks(parts, {3: hidden[1]}), *hidden[:-1])
         column = (in_order(targets) - me * vocab_dev)[:, None]
-        logit_stud, scaled_stud, stats_stud, head = student_logits(as_pieces(hidden), heads, column, 256, chunk)
-        scaled_teach, stats = teacher_logits(as_pieces(projected), head, logit_stud, stats_stud, 512, chunk)
+        logit_stud, scaled_stud, stats_stud = student_logits(as_pieces(hidden), heads, column, 512, chunk)
+        projected = spread(turned(projected_own.astype(jnp.bfloat16)), False, stats_stud)
+        scaled_teach, stats = teacher_logits(
+            as_pieces(projected), heads, logit_stud, stats_stud, 512, chunk
+        )
         tables = [stats]
         for mask in range(1, vocab_size):
             far, near = mask & ~3, mask & 3
             source, hop = (tables[far], near) if near else (stats, far)
             tables.append(lax.ppermute(source, "vocab", [(at, at ^ hop) for at in range(vocab_size)]))
-        loss, *terms = gradient(place, tables, scaled_teach, scaled_stud, column, head, bits, chunk)
+        loss, *terms = gradient(place, tables, scaled_teach, scaled_stud, column, heads, bits, chunk)
         return (loss[0], turned(reduce_blocks(terms).astype(jnp.bfloat16)))
 
     return body

time: 147 us -> 161 us (1.095)
  Pallas kernels: 34.3 us -> 40.1 us
  starting transfers between devices: 42.4 us -> 45.6 us
  other arithmetic: 3.57 us -> 5.91 us
    ppermute x28, starting transfers between devices: 31.5 us -> 38 us  [swap(): lax.ppermute(block, 'vocab', [(at, at ^ 1 << bit) for at in range(vocab_s...]
    ppermute x7, starting transfers between devices: 10.4 us -> 7.09 us  [body(): lax.ppermute(source, 'vocab', [(at, at ^ hop) for at in range(vocab_size)])]
    pallas_call x1, Pallas kernels: 8.37 us -> 11.4 us  [gradient(): pl.pallas_call(functools.partial(gradient_kernel, bits, step, chunk), in_...]
    ppermute x7, waiting for transfers between devices: 1.84 us -> 4.55 us  [body(): lax.ppermute(source, 'vocab', [(at, at ^ hop) for at in range(vocab_size)])]
    pallas_call x1, Pallas kernels: 8.61 us -> 11 us  [teacher_logits(): pl.pallas_call(functools.partial(teacher_kernel, len(pieces), step, chunk...]
    convert_element_type x14, other arithmetic: 0.62 us -> 2.93 us  [reduce_blocks(): block = terms[mask].astype(wire)]
    unnamed x4 -> x10, local copies, waits for them, and re-layouts: 3.48 us -> 4.71 us
  transfers between devices with their start and end apart: 36 -> 36, of which waited for: 22 -> 19; matrix products, arithmetic and copies ran while one was open for 3% -> 4% of each run, Pallas kernels for 12% -> 11%
where the time goes in v6:
time: 161 us; the launch traced here: 160 us
  waiting for transfers between devices  61.4 us (38%)
  starting transfers between devices  45.6 us (28%)
  Pallas kernels  40.1 us (25%)
  other arithmetic  5.91 us (4%)
  local copies, waits for them, and re-layouts  5.57 us (3%)
    ppermute x28, waiting for transfers between devices, swap(): lax.ppermute(block, 'vocab', [(at, at ^ 1 << bit) for at in range(vocab_s...  56.8 us
    ppermute x28, starting transfers between devices, swap(): lax.ppermute(block, 'vocab', [(at, at ^ 1 << bit) for at in range(vocab_s...  38 us
    pallas_call x1, Pallas kernels, student_logits(): pl.pallas_call(functools.partial(student_kernel, len(pieces), step, chunk...  13.3 us
    pallas_call x1, Pallas kernels, gradient(): pl.pallas_call(functools.partial(gradient_kernel, bits, step, chunk), in_...  11.4 us
    pallas_call x1, Pallas kernels, teacher_logits(): pl.pallas_call(functools.partial(teacher_kernel, len(pieces), step, chunk...  11 us
    ppermute x7, starting transfers between devices, body(): lax.ppermute(source, 'vocab', [(at, at ^ hop) for at in range(vocab_size)])  7.09 us
    unnamed x10, local copies, waits for them, and re-layouts  4.71 us
    ppermute x7, waiting for transfers between devices, body(): lax.ppermute(source, 'vocab', [(at, at ^ hop) for at in range(vocab_size)])  4.55 us
  transfers between devices with their start and end apart: 36, of which 19 were waited for; matrix products, arithmetic and copies ran while one was open for 4% of the time, Pallas kernels for 11%

profile of v6, /device:TPU:0, one launch (start us, length us, event | category | flops | bytes accessed | tf_op | source)
XLA Modules:
  0.0 160.2 jit_solution(11016758436322437017)
XLA Ops:
  0.7 0.5 collective-permute-start.18
  1.8 0.8 and_convert_fusion.member_ref
  2.7 1.2 copy-done.2
  3.9 4.4 %shard_map.86 = (f32[32,3584]{1,0:T(8,128)S(1)}, f32[32,3584]{1,0:T(8,128)S(1)}, f32[32,3584]{1,0:T(8,128)S(1)}, f32[32,3584]{1,0:T(8,128)S(1)}, f32[32,3584]{1,...) custom-call(bf16[256,512]{1,0:T(8,128)(2,1)S(1)} %and_convert_fusion.member_ref, ...), custom_call_target="tpu_custom_call" | custom-call | flops 2147483648 | bytes 12058624 | tf_op jit(solution)/shard_map/pallas_call | solution.py:54
  8.4 0.7 convert_element_type.94
  9.1 2.6 %collective-permute-start = (f16[32,3584]{1,0:T(8,128)(2,1)}, f16[32,3584]{1,0:T(8,128)(2,1)}, u32[]{:S(2)}, u32[]{:S(2)}) collective-permute-start(f16[32,3584]{1,0:T(8,128)(2,1)} %convert_element_type.94), channel_id=1, source_target_pairs={{0,1},{1,0},{2,3},{3,2},{4,5},{5,4},{6,7},{7,6},{8,9},{9,8},{10,11... | collective-permute-start | bytes 688136 | tf_op jit(solution)/shard_map/ppermute | solution.py:308
  11.7 1.0 maximum_select_fusion.refs_0_
  12.7 2.7 %collective-permute-start.10 = (bf16[32,3584]{1,0:T(8,128)(2,1)S(1)}, bf16[32,3584]{1,0:T(8,128)(2,1)}, u32[]{:S(2)}, u32[]{:S(2)}) collective-permute-start(bf16[32,3584]{1,0:T(8,128)(2,1)S(1)} %maximum_select_fusion.refs_0_), channel_id=1, source_target_pairs={{0,4},{1,5},{2,6},{3,7},{4,0},{5,1},{6,2},{7,3},{8,12},{9,13},{10,... | collective-permute-start | bytes 688136 | tf_op jit(solution)/shard_map/ppermute | solution.py:308
  15.3 0.5 collective-permute-start.4
  15.8 0.7 convert_element_type.98
  16.6 1.5 collective-permute-start.2
  18.1 0.3 collective-permute-done
  18.4 1.0 add_convert_fusion.6
  19.4 2.1 %collective-permute-start.1 = (f16[32,3584]{1,0:T(8,128)(2,1)S(1)}, f16[32,3584]{1,0:T(8,128)(2,1)S(1)}, u32[]{:S(2)}, u32[]{:S(2)}) collective-permute-start(f16[32,3584]{1,0:T(8,128)(2,1)S(1)} %add_convert_fusion.6), channel_id=1, source_target_pairs={{0,2},{1,3},{2,0},{3,1},{4,6},{5,7},{6,4},{7,5},{8,10},{9,11},{10,... | collective-permute-start | bytes 688136 | tf_op jit(solution)/shard_map/ppermute | solution.py:308
  21.7 6.2 %collective-permute-done.2 = f16[32,3584]{1,0:T(8,128)(2,1)S(1)} collective-permute-done((f16[32,3584]{1,0:T(8,128)(2,1)}, f16[32,3584]{1,0:T(8,128)(2,1)S(1)}, u32[]{:S(2)}, u32[]{:S(2)}) %collective-permute-start.2) | collective-permute-done | bytes 229408 | tf_op jit(solution)/shard_map/ppermute | solution.py:308
  27.9 1.8 %collective-permute-start.8 = (bf16[32,3584]{1,0:T(8,128)(2,1)S(1)}, bf16[32,3584]{1,0:T(8,128)(2,1)S(1)}, u32[]{:S(2)}, u32[]{:S(2)}) collective-permute-start(bf16[32,3584]{1,0:T(8,128)(2,1)S(1)} %maximum_select_fusion.refs_0_), channel_id=1, source_target_pairs={{0,2},{1,3},{2,0},{3,1},{4,6},{5,7},{6,4},{7,5},{8,10},{9,11},{10,... | collective-permute-start | bytes 688136 | tf_op jit(solution)/shard_map/ppermute | solution.py:308
  29.7 1.5 collective-permute-start.7
  31.2 0.5 collective-permute-start.5
  31.8 1.5 collective-permute-start.11
  33.3 0.1 add_convert_fusion.5
  33.4 9.8 %collective-permute-done.5 = f16[32,3584]{1,0:T(8,128)(2,1)S(1)} collective-permute-done((f16[32,3584]{1,0:T(8,128)(2,1)S(1)}, f16[32,3584]{1,0:T(8,128)(2,1)S(1)}, u32[]{:S(2)}, u32[]{:S(2)}) %collective-permute-start.5) | collective-permute-done | bytes 229408 | tf_op jit(solution)/shard_map/ppermute | solution.py:308
  43.2 2.6 %collective-permute-start.3 = (f16[32,3584]{1,0:T(8,128)(2,1)S(1)}, f16[32,3584]{1,0:T(8,128)(2,1)S(1)}, u32[]{:S(2)}, u32[]{:S(2)}) collective-permute-start(f16[32,3584]{1,0:T(8,128)(2,1)S(1)} %add_convert_fusion.5), channel_id=1, source_target_pairs={{0,4},{1,5},{2,6},{3,7},{4,0},{5,1},{6,2},{7,3},{8,12},{9,13},{10,... | collective-permute-start | bytes 688136 | tf_op jit(solution)/shard_map/ppermute | solution.py:308
  45.8 0.5 collective-permute-start.6
  46.4 0.1 sub.26.refs_10_
  46.5 1.6 %collective-permute-start.12 = (bf16[32,3584]{1,0:T(8,128)(2,1)}, bf16[32,3584]{1,0:T(8,128)(2,1)S(1)}, u32[]{:S(2)}, u32[]{:S(2)}) collective-permute-start(bf16[32,3584]{1,0:T(8,128)(2,1)} %collective-permute-done.10.refs_4_), channel_id=1, source_target_pairs={{0,2},{1,3},{2,0},{3,1},{4,6},{5,7},{6,4},{7,5},{8,10},{9,11},{10,... | collective-permute-start | bytes 688136 | tf_op jit(solution)/shard_map/ppermute | solution.py:308
  48.2 1.5 collective-permute-start.9
  49.7 3.6 %collective-permute-done.3 = f16[32,3584]{1,0:T(8,128)(2,1)S(1)} collective-permute-done((f16[32,3584]{1,0:T(8,128)(2,1)S(1)}, f16[32,3584]{1,0:T(8,128)(2,1)S(1)}, u32[]{:S(2)}, u32[]{:S(2)}) %collective-permute-start.3) | collective-permute-done | bytes 229408 | tf_op jit(solution)/shard_map/ppermute | solution.py:308
  53.3 3.5 %collective-permute-done.6 = f16[32,3584]{1,0:T(8,128)(2,1)S(1)} collective-permute-done((f16[32,3584]{1,0:T(8,128)(2,1)S(1)}, f16[32,3584]{1,0:T(8,128)(2,1)S(1)}, u32[]{:S(2)}, u32[]{:S(2)}) %collective-permute-start.6) | collective-permute-done | bytes 229408 | tf_op jit(solution)/shard_map/ppermute | solution.py:308
  56.8 0.1 convert_add_fusion
  56.9 5.0 %collective-permute-done.12.refs_6_ = bf16[32,3584]{1,0:T(8,128)(2,1)S(1)} collective-permute-done((bf16[32,3584]{1,0:T(8,128)(2,1)}, bf16[32,3584]{1,0:T(8,128)(2,1)S(1)}, u32[]{:S(2)}, u32[]{:S(2)}) %collective-permute-start.12) | collective-permute-done | bytes 229408 | tf_op jit(solution)/shard_map/ppermute | solution.py:308
  62.0 2.0 %collective-permute-start.16 = (bf16[32,3584]{1,0:T(8,128)(2,1)S(1)}, bf16[32,3584]{1,0:T(8,128)(2,1)S(1)}, u32[]{:S(2)}, u32[]{:S(2)}) collective-permute-start(bf16[32,3584]{1,0:T(8,128)(2,1)S(1)} %maximum_select_fusion.1.refs_0_), channel_id=1, source_target_pairs={{0,4},{1,5},{2,6},{3,7},{4,0},{5,1},{6,2},{7,3},{8,12},{9,13},{10,... | collective-permute-start | bytes 688136 | tf_op jit(solution)/shard_map/ppermute | solution.py:308
  64.0 2.4 %collective-permute-start.14 = (bf16[32,3584]{1,0:T(8,128)(2,1)S(1)}, bf16[32,3584]{1,0:T(8,128)(2,1)S(1)}, u32[]{:S(2)}, u32[]{:S(2)}) collective-permute-start(bf16[32,3584]{1,0:T(8,128)(2,1)S(1)} %maximum_select_fusion.1.refs_0_), channel_id=1, source_target_pairs={{0,2},{1,3},{2,0},{3,1},{4,6},{5,7},{6,4},{7,5},{8,10},{9,11},{10,... | collective-permute-start | bytes 688136 | tf_op jit(solution)/shard_map/ppermute | solution.py:308
  66.4 1.7 %collective-permute-start.13 = (bf16[32,3584]{1,0:T(8,128)(2,1)S(1)}, bf16[32,3584]{1,0:T(8,128)(2,1)S(1)}, u32[]{:S(2)}, u32[]{:S(2)}) collective-permute-start(bf16[32,3584]{1,0:T(8,128)(2,1)S(1)} %maximum_select_fusion.1.refs_0_), channel_id=1, source_target_pairs={{0,1},{1,0},{2,3},{3,2},{4,5},{5,4},{6,7},{7,6},{8,9},{9,8},{10,11... | collective-permute-start | bytes 688136 | tf_op jit(solution)/shard_map/ppermute | solution.py:308
  68.1 2.5 %collective-permute-done.17.refs_7_ = bf16[32,3584]{1,0:T(8,128)(2,1)S(1)} collective-permute-done((bf16[32,3584]{1,0:T(8,128)(2,1)S(1)}, bf16[32,3584]{1,0:T(8,128)(2,1)S(1)}, u32[]{:S(2)}, u32[]{:S(2)}) %collective-permute-start.17) | collective-permute-done | bytes 229408 | tf_op jit(solution)/shard_map/ppermute | solution.py:308
  70.6 3.5 %copy-done = bf16[1792,2432]{1,0:T(8,128)(2,1)S(1)} copy-done((bf16[1792,2432]{1,0:T(8,128)(2,1)S(1)}, bf16[1792,2432]{1,0:T(8,128)(2,1)}, u32[]{:S(2)}) %copy-start) | copy-done | bytes 8716312
  74.1 13.3 %shard_map.87 = (f32[256,2432]{1,0:T(8,128)S(1)}, f32[256,2432]{1,0:T(8,128)S(1)}, f32[8,256]{1,0:T(8,128)S(1)}) custom-call(bf16[32,3584]{1,0:T(8,128)(2,1)S(1)} %maximum_select_fusion.refs_0_, bf16[32,3584]{1,0:T(8,128)(2,1)} %collective-permute-done.4.refs_1_, bf16[32,3584]{1,0:T(8,128)(2,1)S(1)} %collective-permute-done.8.refs_2_, ...), custom_call_target="tpu_custom_call" | custom-call | flops 4462739456 | bytes 24903680 | tf_op jit(solution)/shard_map/pallas_call | solution.py:168
  87.5 2.4 %collective-permute-start.15 = (bf16[32,3584]{1,0:T(8,128)(2,1)S(1)}, bf16[32,3584]{1,0:T(8,128)(2,1)S(1)}, u32[]{:S(2)}, u32[]{:S(2)}) collective-permute-start(bf16[32,3584]{1,0:T(8,128)(2,1)S(1)} %collective-permute-done.14.refs_2_), channel_id=1, source_target_pairs={{0,1},{1,0},{2,3},{3,2},{4,5},{5,4},{6,7},{7,6},{8,9},{9,8},{10,11... | collective-permute-start | bytes 688136 | tf_op jit(solution)/shard_map/ppermute | solution.py:308
  90.0 3.5 %collective-permute-done.20.refs_6_ = bf16[32,3584]{1,0:T(8,128)(2,1)S(1)} collective-permute-done((bf16[32,3584]{1,0:T(8,128)(2,1)S(1)}, bf16[32,3584]{1,0:T(8,128)(2,1)S(1)}, u32[]{:S(2)}, u32[]{:S(2)}) %collective-permute-start.20) | collective-permute-done | bytes 229408 | tf_op jit(solution)/shard_map/ppermute | solution.py:308
  93.5 2.4 %collective-permute-start.21 = (bf16[32,3584]{1,0:T(8,128)(2,1)S(1)}, bf16[32,3584]{1,0:T(8,128)(2,1)S(1)}, u32[]{:S(2)}, u32[]{:S(2)}) collective-permute-start(bf16[32,3584]{1,0:T(8,128)(2,1)S(1)} %collective-permute-done.20.refs_6_), channel_id=1, source_target_pairs={{0,1},{1,0},{2,3},{3,2},{4,5},{5,4},{6,7},{7,6},{8,9},{9,8},{10,11... | collective-permute-start | bytes 688136 | tf_op jit(solution)/shard_map/ppermute | solution.py:308
  95.9 0.5 collective-permute-done.19.refs_5_
  96.4 3.5 %collective-permute-done.21.refs_7_ = bf16[32,3584]{1,0:T(8,128)(2,1)S(1)} collective-permute-done((bf16[32,3584]{1,0:T(8,128)(2,1)S(1)}, bf16[32,3584]{1,0:T(8,128)(2,1)S(1)}, u32[]{:S(2)}, u32[]{:S(2)}) %collective-permute-start.21) | collective-permute-done | bytes 229408 | tf_op jit(solution)/shard_map/ppermute | solution.py:308
  99.9 11.0 %shard_map.88 = (f32[256,2432]{1,0:T(8,128)S(1)}, f32[8,256]{1,0:T(8,128)S(1)}) custom-call(bf16[32,3584]{1,0:T(8,128)(2,1)S(1)} %maximum_select_fusion.1.refs_0_, bf16[32,3584]{1,0:T(8,128)(2,1)S(1)} %collective-permute-done.13.refs_1_, bf16[32,3584]{1,0:T(8,128)(2,1)S(1)} %collective-permute-done.14.refs_2_, ...), custom_call_target="tpu_custom_call" | custom-call | flops 4462739456 | bytes 24903680 | tf_op jit(solution)/shard_map/pallas_call | solution.py:190
  110.9 2.4 %collective-permute-start.24 = (f32[8,256]{1,0:T(8,128)S(1)}, f32[8,256]{1,0:T(8,128)S(1)}, u32[]{:S(2)}, u32[]{:S(2)}) collective-permute-start(f32[8,256]{1,0:T(8,128)S(1)} %get-tuple-element.46.refs_0_), channel_id=1, source_target_pairs={{0,3},{1,2},{2,1},{3,0},{4,7},{5,6},{6,5},{7,4},{8,11},{9,10},{10,... | collective-permute-start | bytes 24584 | tf_op jit(solution)/shard_map/ppermute | solution.py:386
  113.3 1.1 collective-permute-start.23
  114.5 1.0 collective-permute-done.25.refs_4_
  115.4 2.4 %collective-permute-start.28 = (f32[8,256]{1,0:T(8,128)S(1)}, f32[8,256]{1,0:T(8,128)S(1)}, u32[]{:S(2)}, u32[]{:S(2)}) collective-permute-start(f32[8,256]{1,0:T(8,128)S(1)} %collective-permute-done.25.refs_4_), channel_id=1, source_target_pairs={{0,3},{1,2},{2,1},{3,0},{4,7},{5,6},{6,5},{7,4},{8,11},{9,10},{10,... | collective-permute-start | bytes 24584 | tf_op jit(solution)/shard_map/ppermute | solution.py:386
  117.8 1.1 collective-permute-start.27
  119.0 1.0 collective-permute-done.28.refs_7_
  120.0 1.5 collective-permute-done.27.refs_6_
  121.5 1.1 collective-permute-done.26.refs_5_
  122.6 11.4 %shard_map.89 = (f32[8,256]{1,0:T(8,128)S(1)}, f32[32,3584]{1,0:T(8,128)S(1)}, f32[32,3584]{1,0:T(8,128)S(1)}, f32[32,3584]{1,0:T(8,128)S(1)}, f32[32,3584]{1,0:...) custom-call(s32[2]{0:T(128)S(1)} %pad_add_fusion.place_ref, ...), custom_call_target="tpu_custom_call" | custom-call | flops 4462739456 | bytes 24903680 | tf_op jit(solution)/shard_map/pallas_call | solution.py:283
  134.2 2.1 %collective-permute-start.29 = (f16[32,3584]{1,0:T(8,128)(2,1)S(1)}, f16[32,3584]{1,0:T(8,128)(2,1)S(1)}, u32[]{:S(2)}, u32[]{:S(2)}) collective-permute-start(f16[32,3584]{1,0:T(8,128)(2,1)S(1)} %convert_element_type.109), channel_id=1, source_target_pairs={{0,1},{1,0},{2,3},{3,2},{4,5},{5,4},{6,7},{7,6},{8,9},{9,8},{10,11... | collective-permute-start | bytes 688136 | tf_op jit(solution)/shard_map/ppermute | solution.py:308
  136.3 3.8 %collective-permute-done.31 = f16[32,3584]{1,0:T(8,128)(2,1)S(1)} collective-permute-done((f16[32,3584]{1,0:T(8,128)(2,1)S(1)}, f16[32,3584]{1,0:T(8,128)(2,1)S(1)}, u32[]{:S(2)}, u32[]{:S(2)}) %collective-permute-start.31) | collective-permute-done | bytes 229408 | tf_op jit(solution)/shard_map/ppermute | solution.py:308
  140.2 2.4 %collective-permute-done.29 = f16[32,3584]{1,0:T(8,128)(2,1)S(1)} collective-permute-done((f16[32,3584]{1,0:T(8,128)(2,1)S(1)}, f16[32,3584]{1,0:T(8,128)(2,1)S(1)}, u32[]{:S(2)}, u32[]{:S(2)}) %collective-permute-start.29) | collective-permute-done | bytes 229408 | tf_op jit(solution)/shard_map/ppermute | solution.py:308
  142.7 1.0 collective-permute-start.30
  143.7 5.0 %collective-permute-done.33 = f16[32,3584]{1,0:T(8,128)(2,1)S(1)} collective-permute-done((f16[32,3584]{1,0:T(8,128)(2,1)S(1)}, f16[32,3584]{1,0:T(8,128)(2,1)S(1)}, u32[]{:S(2)}, u32[]{:S(2)}) %collective-permute-start.33) | collective-permute-done | bytes 229408 | tf_op jit(solution)/shard_map/ppermute | solution.py:308
  148.7 1.0 collective-permute-start.34
  149.7 0.1 add_convert_fusion.2
  149.8 1.9 %collective-permute-start.32 = (f16[32,3584]{1,0:T(8,128)(2,1)S(1)}, f16[32,3584]{1,0:T(8,128)(2,1)S(1)}, u32[]{:S(2)}, u32[]{:S(2)}) collective-permute-start(f16[32,3584]{1,0:T(8,128)(2,1)S(1)} %add_convert_fusion.2), channel_id=1, source_target_pairs={{0,4},{1,5},{2,6},{3,7},{4,0},{5,1},{6,2},{7,3},{8,12},{9,13},{10,... | collective-permute-start | bytes 688136 | tf_op jit(solution)/shard_map/ppermute | solution.py:308
  151.7 0.6 slice.27
  152.3 4.3 %collective-permute-done.34 = f16[32,3584]{1,0:T(8,128)(2,1)S(1)} collective-permute-done((f16[32,3584]{1,0:T(8,128)(2,1)S(1)}, f16[32,3584]{1,0:T(8,128)(2,1)S(1)}, u32[]{:S(2)}, u32[]{:S(2)}) %collective-permute-start.34) | collective-permute-done | bytes 229408 | tf_op jit(solution)/shard_map/ppermute | solution.py:308
  156.6 2.6 %collective-permute-done.32 = f16[32,3584]{1,0:T(8,128)(2,1)S(1)} collective-permute-done((f16[32,3584]{1,0:T(8,128)(2,1)S(1)}, f16[32,3584]{1,0:T(8,128)(2,1)S(1)}, u32[]{:S(2)}, u32[]{:S(2)}) %collective-permute-start.32) | collective-permute-done | bytes 229408 | tf_op jit(solution)/shard_map/ppermute | solution.py:308
  159.3 0.1 add_convert_fusion
  159.4 0.8 maximum_select_fusion.2
  (55 shorter events, 1.0 us)
Async XLA Ops:
  0.6 11.0 %copy-start.3 = (bf16[32,3584]{1,0:T(8,128)(2,1)S(1)}, bf16[32,3584]{1,0:T(8,128)(2,1)}, u32[]{:S(2)}) copy-start(bf16[32,3584]{1,0:T(8,128)(2,1)} %param.11) | copy-start | bytes 688132
  0.6 20.8 %copy-start.4 = (s32[256]{0:T(256)S(1)}, s32[256]{0:T(256)}, u32[]{:S(2)}) copy-start(s32[256]{0:T(256)} %param.13) | copy-start | bytes 3076
  0.7 70.0 %collective-permute-start.18 = (bf16[1792,2432]{1,0:T(8,128)(2,1)}, bf16[1792,2432]{1,0:T(8,128)(2,1)}, u32[]{:S(2)}, u32[]{:S(2)}) collective-permute-start(bf16[1792,2432]{1,0:T(8,128)(2,1)} %refs_11_.1), channel_id=1, source_target_pairs={{0,8},{8,0},{1,9},{9,1},{2,10},{10,2},{3,11},{11,3},{4,12},{12,4},... | collective-permute-start | bytes 26148872 | tf_op jit(solution)/shard_map/ppermute | solution.py:367
  2.7 1.2 copy-start.2
  9.1 9.3 %collective-permute-start = (f16[32,3584]{1,0:T(8,128)(2,1)}, f16[32,3584]{1,0:T(8,128)(2,1)}, u32[]{:S(2)}, u32[]{:S(2)}) collective-permute-start(f16[32,3584]{1,0:T(8,128)(2,1)} %convert_element_type.94), channel_id=1, source_target_pairs={{0,1},{1,0},{2,3},{3,2},{4,5},{5,4},{6,7},{7,6},{8,9},{9,8},{10,11... | collective-permute-start | bytes 688136 | tf_op jit(solution)/shard_map/ppermute | solution.py:308
  12.7 18.6 %collective-permute-start.10 = (bf16[32,3584]{1,0:T(8,128)(2,1)S(1)}, bf16[32,3584]{1,0:T(8,128)(2,1)}, u32[]{:S(2)}, u32[]{:S(2)}) collective-permute-start(bf16[32,3584]{1,0:T(8,128)(2,1)S(1)} %maximum_select_fusion.refs_0_), channel_id=1, source_target_pairs={{0,4},{1,5},{2,6},{3,7},{4,0},{5,1},{6,2},{7,3},{8,12},{9,13},{10,... | collective-permute-start | bytes 688136 | tf_op jit(solution)/shard_map/ppermute | solution.py:308
  15.3 14.4 %collective-permute-start.4 = (bf16[32,3584]{1,0:T(8,128)(2,1)S(1)}, bf16[32,3584]{1,0:T(8,128)(2,1)}, u32[]{:S(2)}, u32[]{:S(2)}) collective-permute-start(bf16[32,3584]{1,0:T(8,128)(2,1)S(1)} %maximum_select_fusion.refs_0_), channel_id=1, source_target_pairs={{0,1},{1,0},{2,3},{3,2},{4,5},{5,4},{6,7},{7,6},{8,9},{9,8},{10,11... | collective-permute-start | bytes 688136 | tf_op jit(solution)/shard_map/ppermute | solution.py:308
  16.6 11.4 %collective-permute-start.2 = (f16[32,3584]{1,0:T(8,128)(2,1)}, f16[32,3584]{1,0:T(8,128)(2,1)S(1)}, u32[]{:S(2)}, u32[]{:S(2)}) collective-permute-start(f16[32,3584]{1,0:T(8,128)(2,1)} %convert_element_type.98), channel_id=1, source_target_pairs={{0,1},{1,0},{2,3},{3,2},{4,5},{5,4},{6,7},{7,6},{8,9},{9,8},{10,11... | collective-permute-start | bytes 688136 | tf_op jit(solution)/shard_map/ppermute | solution.py:308
  19.4 12.4 %collective-permute-start.1 = (f16[32,3584]{1,0:T(8,128)(2,1)S(1)}, f16[32,3584]{1,0:T(8,128)(2,1)S(1)}, u32[]{:S(2)}, u32[]{:S(2)}) collective-permute-start(f16[32,3584]{1,0:T(8,128)(2,1)S(1)} %add_convert_fusion.6), channel_id=1, source_target_pairs={{0,2},{1,3},{2,0},{3,1},{4,6},{5,7},{6,4},{7,5},{8,10},{9,11},{10,... | collective-permute-start | bytes 688136 | tf_op jit(solution)/shard_map/ppermute | solution.py:308
  27.9 17.9 %collective-permute-start.8 = (bf16[32,3584]{1,0:T(8,128)(2,1)S(1)}, bf16[32,3584]{1,0:T(8,128)(2,1)S(1)}, u32[]{:S(2)}, u32[]{:S(2)}) collective-permute-start(bf16[32,3584]{1,0:T(8,128)(2,1)S(1)} %maximum_select_fusion.refs_0_), channel_id=1, source_target_pairs={{0,2},{1,3},{2,0},{3,1},{4,6},{5,7},{6,4},{7,5},{8,10},{9,11},{10,... | collective-permute-start | bytes 688136 | tf_op jit(solution)/shard_map/ppermute | solution.py:308
  29.7 16.8 %collective-permute-start.7 = (f16[32,3584]{1,0:T(8,128)(2,1)S(1)}, f16[32,3584]{1,0:T(8,128)(2,1)S(1)}, u32[]{:S(2)}, u32[]{:S(2)}) collective-permute-start(f16[32,3584]{1,0:T(8,128)(2,1)S(1)} %convert_element_type.106), channel_id=1, source_target_pairs={{0,1},{1,0},{2,3},{3,2},{4,5},{5,4},{6,7},{7,6},{8,9},{9,8},{10,11... | collective-permute-start | bytes 688136 | tf_op jit(solution)/shard_map/ppermute | solution.py:308
  31.2 11.9 %collective-permute-start.5 = (f16[32,3584]{1,0:T(8,128)(2,1)S(1)}, f16[32,3584]{1,0:T(8,128)(2,1)S(1)}, u32[]{:S(2)}, u32[]{:S(2)}) collective-permute-start(f16[32,3584]{1,0:T(8,128)(2,1)S(1)} %convert_element_type.102), channel_id=1, source_target_pairs={{0,1},{1,0},{2,3},{3,2},{4,5},{5,4},{6,7},{7,6},{8,9},{9,8},{10,11... | collective-permute-start | bytes 688136 | tf_op jit(solution)/shard_map/ppermute | solution.py:308
  31.8 16.4 %collective-permute-start.11 = (bf16[32,3584]{1,0:T(8,128)(2,1)}, bf16[32,3584]{1,0:T(8,128)(2,1)S(1)}, u32[]{:S(2)}, u32[]{:S(2)}) collective-permute-start(bf16[32,3584]{1,0:T(8,128)(2,1)} %collective-permute-done.10.refs_4_), channel_id=1, source_target_pairs={{0,1},{1,0},{2,3},{3,2},{4,5},{5,4},{6,7},{7,6},{8,9},{9,8},{10,11... | collective-permute-start | bytes 688136 | tf_op jit(solution)/shard_map/ppermute | solution.py:308
  43.2 10.1 %collective-permute-start.3 = (f16[32,3584]{1,0:T(8,128)(2,1)S(1)}, f16[32,3584]{1,0:T(8,128)(2,1)S(1)}, u32[]{:S(2)}, u32[]{:S(2)}) collective-permute-start(f16[32,3584]{1,0:T(8,128)(2,1)S(1)} %add_convert_fusion.5), channel_id=1, source_target_pairs={{0,4},{1,5},{2,6},{3,7},{4,0},{5,1},{6,2},{7,3},{8,12},{9,13},{10,... | collective-permute-start | bytes 688136 | tf_op jit(solution)/shard_map/ppermute | solution.py:308
  45.8 10.9 %collective-permute-start.6 = (f16[32,3584]{1,0:T(8,128)(2,1)S(1)}, f16[32,3584]{1,0:T(8,128)(2,1)S(1)}, u32[]{:S(2)}, u32[]{:S(2)}) collective-permute-start(f16[32,3584]{1,0:T(8,128)(2,1)S(1)} %add_convert_fusion.4), channel_id=1, source_target_pairs={{0,2},{1,3},{2,0},{3,1},{4,6},{5,7},{6,4},{7,5},{8,10},{9,11},{10,... | collective-permute-start | bytes 688136 | tf_op jit(solution)/shard_map/ppermute | solution.py:308
  46.5 15.4 %collective-permute-start.12 = (bf16[32,3584]{1,0:T(8,128)(2,1)}, bf16[32,3584]{1,0:T(8,128)(2,1)S(1)}, u32[]{:S(2)}, u32[]{:S(2)}) collective-permute-start(bf16[32,3584]{1,0:T(8,128)(2,1)} %collective-permute-done.10.refs_4_), channel_id=1, source_target_pairs={{0,2},{1,3},{2,0},{3,1},{4,6},{5,7},{6,4},{7,5},{8,10},{9,11},{10,... | collective-permute-start | bytes 688136 | tf_op jit(solution)/shard_map/ppermute | solution.py:308
  48.2 13.7 %collective-permute-start.9 = (bf16[32,3584]{1,0:T(8,128)(2,1)S(1)}, bf16[32,3584]{1,0:T(8,128)(2,1)S(1)}, u32[]{:S(2)}, u32[]{:S(2)}) collective-permute-start(bf16[32,3584]{1,0:T(8,128)(2,1)S(1)} %collective-permute-done.8.refs_2_), channel_id=1, source_target_pairs={{0,1},{1,0},{2,3},{3,2},{4,5},{5,4},{6,7},{7,6},{8,9},{9,8},{10,11... | collective-permute-start | bytes 688136 | tf_op jit(solution)/shard_map/ppermute | solution.py:308
  53.3 17.4 %collective-permute-start.17 = (bf16[32,3584]{1,0:T(8,128)(2,1)S(1)}, bf16[32,3584]{1,0:T(8,128)(2,1)S(1)}, u32[]{:S(2)}, u32[]{:S(2)}) collective-permute-start(bf16[32,3584]{1,0:T(8,128)(2,1)S(1)} %collective-permute-done.11.refs_5_), channel_id=1, source_target_pairs={{0,2},{1,3},{2,0},{3,1},{4,6},{5,7},{6,4},{7,5},{8,10},{9,11},{10,... | collective-permute-start | bytes 688136 | tf_op jit(solution)/shard_map/ppermute | solution.py:308
  62.0 25.4 %collective-permute-start.16 = (bf16[32,3584]{1,0:T(8,128)(2,1)S(1)}, bf16[32,3584]{1,0:T(8,128)(2,1)S(1)}, u32[]{:S(2)}, u32[]{:S(2)}) collective-permute-start(bf16[32,3584]{1,0:T(8,128)(2,1)S(1)} %maximum_select_fusion.1.refs_0_), channel_id=1, source_target_pairs={{0,4},{1,5},{2,6},{3,7},{4,0},{5,1},{6,2},{7,3},{8,12},{9,13},{10,... | collective-permute-start | bytes 688136 | tf_op jit(solution)/shard_map/ppermute | solution.py:308
  64.0 23.4 %collective-permute-start.14 = (bf16[32,3584]{1,0:T(8,128)(2,1)S(1)}, bf16[32,3584]{1,0:T(8,128)(2,1)S(1)}, u32[]{:S(2)}, u32[]{:S(2)}) collective-permute-start(bf16[32,3584]{1,0:T(8,128)(2,1)S(1)} %maximum_select_fusion.1.refs_0_), channel_id=1, source_target_pairs={{0,2},{1,3},{2,0},{3,1},{4,6},{5,7},{6,4},{7,5},{8,10},{9,11},{10,... | collective-permute-start | bytes 688136 | tf_op jit(solution)/shard_map/ppermute | solution.py:308
  66.4 21.1 %collective-permute-start.13 = (bf16[32,3584]{1,0:T(8,128)(2,1)S(1)}, bf16[32,3584]{1,0:T(8,128)(2,1)S(1)}, u32[]{:S(2)}, u32[]{:S(2)}) collective-permute-start(bf16[32,3584]{1,0:T(8,128)(2,1)S(1)} %maximum_select_fusion.1.refs_0_), channel_id=1, source_target_pairs={{0,1},{1,0},{2,3},{3,2},{4,5},{5,4},{6,7},{7,6},{8,9},{9,8},{10,11... | collective-permute-start | bytes 688136 | tf_op jit(solution)/shard_map/ppermute | solution.py:308
  70.6 3.5 %copy-start = (bf16[1792,2432]{1,0:T(8,128)(2,1)S(1)}, bf16[1792,2432]{1,0:T(8,128)(2,1)}, u32[]{:S(2)}) copy-start(bf16[1792,2432]{1,0:T(8,128)(2,1)} %refs_11_.1) | copy-start | bytes 26148868
  74.1 25.8 %copy-start.1 = (bf16[1792,2432]{1,0:T(8,128)(2,1)S(1)}, bf16[1792,2432]{1,0:T(8,128)(2,1)}, u32[]{:S(2)}) copy-start(bf16[1792,2432]{1,0:T(8,128)(2,1)} %refs_11_.1) | copy-start | bytes 26148868
  87.4 6.1 %collective-permute-start.20 = (bf16[32,3584]{1,0:T(8,128)(2,1)S(1)}, bf16[32,3584]{1,0:T(8,128)(2,1)S(1)}, u32[]{:S(2)}, u32[]{:S(2)}) collective-permute-start(bf16[32,3584]{1,0:T(8,128)(2,1)S(1)} %collective-permute-done.16.refs_4_), channel_id=1, source_target_pairs={{0,2},{1,3},{2,0},{3,1},{4,6},{5,7},{6,4},{7,5},{8,10},{9,11},{10,... | collective-permute-start | bytes 688136 | tf_op jit(solution)/shard_map/ppermute | solution.py:308
  87.5 8.4 %collective-permute-start.15 = (bf16[32,3584]{1,0:T(8,128)(2,1)S(1)}, bf16[32,3584]{1,0:T(8,128)(2,1)S(1)}, u32[]{:S(2)}, u32[]{:S(2)}) collective-permute-start(bf16[32,3584]{1,0:T(8,128)(2,1)S(1)} %collective-permute-done.14.refs_2_), channel_id=1, source_target_pairs={{0,1},{1,0},{2,3},{3,2},{4,5},{5,4},{6,7},{7,6},{8,9},{9,8},{10,11... | collective-permute-start | bytes 688136 | tf_op jit(solution)/shard_map/ppermute | solution.py:308
  89.9 6.5 %collective-permute-start.19 = (bf16[32,3584]{1,0:T(8,128)(2,1)S(1)}, bf16[32,3584]{1,0:T(8,128)(2,1)S(1)}, u32[]{:S(2)}, u32[]{:S(2)}) collective-permute-start(bf16[32,3584]{1,0:T(8,128)(2,1)S(1)} %collective-permute-done.16.refs_4_), channel_id=1, source_target_pairs={{0,1},{1,0},{2,3},{3,2},{4,5},{5,4},{6,7},{7,6},{8,9},{9,8},{10,11... | collective-permute-start | bytes 688136 | tf_op jit(solution)/shard_map/ppermute | solution.py:308
  93.5 6.4 %collective-permute-start.21 = (bf16[32,3584]{1,0:T(8,128)(2,1)S(1)}, bf16[32,3584]{1,0:T(8,128)(2,1)S(1)}, u32[]{:S(2)}, u32[]{:S(2)}) collective-permute-start(bf16[32,3584]{1,0:T(8,128)(2,1)S(1)} %collective-permute-done.20.refs_6_), channel_id=1, source_target_pairs={{0,1},{1,0},{2,3},{3,2},{4,5},{5,4},{6,7},{7,6},{8,9},{9,8},{10,11... | collective-permute-start | bytes 688136 | tf_op jit(solution)/shard_map/ppermute | solution.py:308
  110.8 4.6 %collective-permute-start.25 = (f32[8,256]{1,0:T(8,128)S(1)}, f32[8,256]{1,0:T(8,128)S(1)}, u32[]{:S(2)}, u32[]{:S(2)}) collective-permute-start(f32[8,256]{1,0:T(8,128)S(1)} %get-tuple-element.46.refs_0_), channel_id=1, source_target_pairs={{0,4},{1,5},{2,6},{3,7},{4,0},{5,1},{6,2},{7,3},{8,12},{9,13},{10,... | collective-permute-start | bytes 24584 | tf_op jit(solution)/shard_map/ppermute | solution.py:386
  110.9 8.0 %collective-permute-start.24 = (f32[8,256]{1,0:T(8,128)S(1)}, f32[8,256]{1,0:T(8,128)S(1)}, u32[]{:S(2)}, u32[]{:S(2)}) collective-permute-start(f32[8,256]{1,0:T(8,128)S(1)} %get-tuple-element.46.refs_0_), channel_id=1, source_target_pairs={{0,3},{1,2},{2,1},{3,0},{4,7},{5,6},{6,5},{7,4},{8,11},{9,10},{10,... | collective-permute-start | bytes 24584 | tf_op jit(solution)/shard_map/ppermute | solution.py:386
  113.3 5.7 %collective-permute-start.23 = (f32[8,256]{1,0:T(8,128)S(1)}, f32[8,256]{1,0:T(8,128)S(1)}, u32[]{:S(2)}, u32[]{:S(2)}) collective-permute-start(f32[8,256]{1,0:T(8,128)S(1)} %get-tuple-element.46.refs_0_), channel_id=1, source_target_pairs={{0,2},{1,3},{2,0},{3,1},{4,6},{5,7},{6,4},{7,5},{8,10},{9,11},{10,... | collective-permute-start | bytes 24584 | tf_op jit(solution)/shard_map/ppermute | solution.py:386
  114.5 4.6 %collective-permute-start.22 = (f32[8,256]{1,0:T(8,128)S(1)}, f32[8,256]{1,0:T(8,128)S(1)}, u32[]{:S(2)}, u32[]{:S(2)}) collective-permute-start(f32[8,256]{1,0:T(8,128)S(1)} %get-tuple-element.46.refs_0_), channel_id=1, source_target_pairs={{0,1},{1,0},{2,3},{3,2},{4,5},{5,4},{6,7},{7,6},{8,9},{9,8},{10,11... | collective-permute-start | bytes 24584 | tf_op jit(solution)/shard_map/ppermute | solution.py:386
  115.4 4.5 %collective-permute-start.28 = (f32[8,256]{1,0:T(8,128)S(1)}, f32[8,256]{1,0:T(8,128)S(1)}, u32[]{:S(2)}, u32[]{:S(2)}) collective-permute-start(f32[8,256]{1,0:T(8,128)S(1)} %collective-permute-done.25.refs_4_), channel_id=1, source_target_pairs={{0,3},{1,2},{2,1},{3,0},{4,7},{5,6},{6,5},{7,4},{8,11},{9,10},{10,... | collective-permute-start | bytes 24584 | tf_op jit(solution)/shard_map/ppermute | solution.py:386
  117.8 3.7 %collective-permute-start.27 = (f32[8,256]{1,0:T(8,128)S(1)}, f32[8,256]{1,0:T(8,128)S(1)}, u32[]{:S(2)}, u32[]{:S(2)}) collective-permute-start(f32[8,256]{1,0:T(8,128)S(1)} %collective-permute-done.25.refs_4_), channel_id=1, source_target_pairs={{0,2},{1,3},{2,0},{3,1},{4,6},{5,7},{6,4},{7,5},{8,10},{9,11},{10,... | collective-permute-start | bytes 24584 | tf_op jit(solution)/shard_map/ppermute | solution.py:386
  118.9 3.7 %collective-permute-start.26 = (f32[8,256]{1,0:T(8,128)S(1)}, f32[8,256]{1,0:T(8,128)S(1)}, u32[]{:S(2)}, u32[]{:S(2)}) collective-permute-start(f32[8,256]{1,0:T(8,128)S(1)} %collective-permute-done.25.refs_4_), channel_id=1, source_target_pairs={{0,1},{1,0},{2,3},{3,2},{4,5},{5,4},{6,7},{7,6},{8,9},{9,8},{10,11... | collective-permute-start | bytes 24584 | tf_op jit(solution)/shard_map/ppermute | solution.py:386
  134.1 6.1 %collective-permute-start.31 = (f16[32,3584]{1,0:T(8,128)(2,1)S(1)}, f16[32,3584]{1,0:T(8,128)(2,1)S(1)}, u32[]{:S(2)}, u32[]{:S(2)}) collective-permute-start(f16[32,3584]{1,0:T(8,128)(2,1)S(1)} %convert_element_type.113), channel_id=1, source_target_pairs={{0,1},{1,0},{2,3},{3,2},{4,5},{5,4},{6,7},{7,6},{8,9},{9,8},{10,11... | collective-permute-start | bytes 688136 | tf_op jit(solution)/shard_map/ppermute | solution.py:308
  134.2 8.4 %collective-permute-start.29 = (f16[32,3584]{1,0:T(8,128)(2,1)S(1)}, f16[32,3584]{1,0:T(8,128)(2,1)S(1)}, u32[]{:S(2)}, u32[]{:S(2)}) collective-permute-start(f16[32,3584]{1,0:T(8,128)(2,1)S(1)} %convert_element_type.109), channel_id=1, source_target_pairs={{0,1},{1,0},{2,3},{3,2},{4,5},{5,4},{6,7},{7,6},{8,9},{9,8},{10,11... | collective-permute-start | bytes 688136 | tf_op jit(solution)/shard_map/ppermute | solution.py:308
  140.1 12.1 %collective-permute-start.35 = (f16[32,3584]{1,0:T(8,128)(2,1)S(1)}, f16[32,3584]{1,0:T(8,128)(2,1)S(1)}, u32[]{:S(2)}, u32[]{:S(2)}) collective-permute-start(f16[32,3584]{1,0:T(8,128)(2,1)S(1)} %convert_element_type.121), channel_id=1, source_target_pairs={{0,1},{1,0},{2,3},{3,2},{4,5},{5,4},{6,7},{7,6},{8,9},{9,8},{10,11... | collective-permute-start | bytes 688136 | tf_op jit(solution)/shard_map/ppermute | solution.py:308
  142.6 6.0 %collective-permute-start.33 = (f16[32,3584]{1,0:T(8,128)(2,1)S(1)}, f16[32,3584]{1,0:T(8,128)(2,1)S(1)}, u32[]{:S(2)}, u32[]{:S(2)}) collective-permute-start(f16[32,3584]{1,0:T(8,128)(2,1)S(1)} %convert_element_type.117), channel_id=1, source_target_pairs={{0,1},{1,0},{2,3},{3,2},{4,5},{5,4},{6,7},{7,6},{8,9},{9,8},{10,11... | collective-permute-start | bytes 688136 | tf_op jit(solution)/shard_map/ppermute | solution.py:308
  142.7 7.0 %collective-permute-start.30 = (f16[32,3584]{1,0:T(8,128)(2,1)S(1)}, f16[32,3584]{1,0:T(8,128)(2,1)S(1)}, u32[]{:S(2)}, u32[]{:S(2)}) collective-permute-start(f16[32,3584]{1,0:T(8,128)(2,1)S(1)} %add_convert_fusion.3), channel_id=1, source_target_pairs={{0,2},{1,3},{2,0},{3,1},{4,6},{5,7},{6,4},{7,5},{8,10},{9,11},{10,... | collective-permute-start | bytes 688136 | tf_op jit(solution)/shard_map/ppermute | solution.py:308
  148.7 7.9 %collective-permute-start.34 = (f16[32,3584]{1,0:T(8,128)(2,1)S(1)}, f16[32,3584]{1,0:T(8,128)(2,1)S(1)}, u32[]{:S(2)}, u32[]{:S(2)}) collective-permute-start(f16[32,3584]{1,0:T(8,128)(2,1)S(1)} %add_convert_fusion.1), channel_id=1, source_target_pairs={{0,2},{1,3},{2,0},{3,1},{4,6},{5,7},{6,4},{7,5},{8,10},{9,11},{10,... | collective-permute-start | bytes 688136 | tf_op jit(solution)/shard_map/ppermute | solution.py:308
  149.8 9.5 %collective-permute-start.32 = (f16[32,3584]{1,0:T(8,128)(2,1)S(1)}, f16[32,3584]{1,0:T(8,128)(2,1)S(1)}, u32[]{:S(2)}, u32[]{:S(2)}) collective-permute-start(f16[32,3584]{1,0:T(8,128)(2,1)S(1)} %add_convert_fusion.2), channel_id=1, source_target_pairs={{0,4},{1,5},{2,6},{3,7},{4,0},{5,1},{6,2},{7,3},{8,12},{9,13},{10,... | collective-permute-start | bytes 688136 | tf_op jit(solution)/shard_map/ppermute | solution.py:308

commit v7 on v4

--- a/solution.py
+++ b/solution.py
@@ -11,6 +11,7 @@
 wire = jnp.float16
 lanes = 128
 vmem_bytes = 12 * 1024 * 1024
+logits_bytes = 34 * 1024 * 1024
 project_bytes = 50 * 1024 * 1024
 
 in_vmem = pl.BlockSpec(memory_space=pltpu.VMEM)
@@ -71,27 +72,43 @@
     )(member, teacher_rows, proj_weight)
 
 
-class Fetch:
-    def __init__(self, sems):
-        self.sems, self.used = sems, 0
-
-    def start(self, source, target):
-        copy = pltpu.make_async_copy(source, target, self.sems.at[self.used])
-        copy.start()
-        self.used += 1
-        return copy
-
-
-def multiply(read_rows, head, logit_ref, highest, step, ready=None):
-    total = head.shape[1]
+def as_columns(values):
+    lane = lax.broadcasted_iota(jnp.int32, (values[0].shape[0], lanes), 1)
+    table = jnp.zeros(lane.shape, jnp.float32)
+    for at, value in enumerate(values):
+        if value is not None:
+            table = jnp.where(lane == at, value, table)
+    return table
+
+
+def logits_kernel(count, step, chunk, *refs):
+    pieces, heads = refs[:count], refs[count : count + 2]
+    column_ref, scaled_ref, stats_ref, head = refs[count + 2 : count + 6]
+    held, highest, table, sems = refs[count + 6 :]
+    depth, total = heads[0].shape
+    blk, slab = pieces[0].shape[0], held.shape[0] // 2
+    copies = []
+    for i, piece in enumerate(pieces):
+        copies.append(pltpu.make_async_copy(piece, held.at[pl.ds(i * blk, blk)], sems.at[i]))
+        copies[-1].start()
+
+    def columns(index, half, at):
+        source, target = heads[half].at[:, at], head.at[pl.ds(half * depth, depth), at]
+        return pltpu.make_async_copy(source, target, sems.at[count + 2 * index + half])
+
+    for index, (start, size) in enumerate(cuts(total, step)):
+        for half in range(2):
+            columns(index, half, pl.ds(start, size)).start()
     highest[...] = jnp.full(highest.shape, -jnp.inf, jnp.float32)
+    for copy in copies:
+        copy.wait()
 
     def one(index, start, size):
         at = pl.ds(start, size)
-        if ready is not None:
-            ready(index, at)
-        part = jnp.dot(read_rows(), head[:, at], preferred_element_type=jnp.float32)
-        logit_ref[:, at] = part
+        for half in range(2):
+            columns(index, half, at).wait()
+        part = jnp.dot(held[...], head[:, at], preferred_element_type=jnp.float32)
+        scaled_ref[:, at] = part
         top = part[:, :lanes]
         for lane in range(lanes, size, lanes):
             top = jnp.maximum(top, part[:, lane : lane + lanes])
@@ -106,75 +123,26 @@
     if total % step:
         one(full, full * step, total % step)
 
-
-def as_columns(first, second, third):
-    lane = lax.broadcasted_iota(jnp.int32, (first.shape[0], lanes), 1)
-    return jnp.where(lane == 0, first, jnp.where(lane == 1, second, jnp.where(lane == 2, third, 0.0)))
-
-
-def student_kernel(count, step, chunk, *refs):
-    pieces, heads = refs[:count], refs[count : count + 2]
-    column_ref, logit_ref, scaled_ref, stats_ref, head = refs[count + 2 : count + 7]
-    held, highest, table, sems = refs[count + 7 :]
-    depth, total = heads[0].shape
-    blk = pieces[0].shape[0]
-    fetch = Fetch(sems)
-    waits = [fetch.start(piece, held.at[pl.ds(i * blk, blk)]) for i, piece in enumerate(pieces)]
-    first = fetch.used
-
-    def columns(half, at):
-        return heads[half].at[:, at], head.at[pl.ds(half * depth, depth), at]
-
-    for start, size in cuts(total, step):
-        for half in range(2):
-            fetch.start(*columns(half, pl.ds(start, size)))
-
-    def ready(index, at):
-        for half in range(2):
-            pltpu.make_async_copy(*columns(half, at), sems.at[first + 2 * index + half]).wait()
-
-    for wait in waits:
-        wait.wait()
-    multiply(lambda: held[...], head, logit_ref, highest, step, ready)
-
-    def one(part, carry):
-        rows = pl.ds(pl.multiple_of(part * chunk, chunk), chunk)
-        logit = logit_ref[rows, :]
-        top = jnp.max(highest[rows, :], axis=1, keepdims=True)
-        scaled = jnp.exp(logit - top)
-        hit = lax.broadcasted_iota(jnp.int32, logit.shape, 1) == column_ref[rows, :]
-        picked = jnp.sum(jnp.where(hit, logit, 0.0), axis=1, keepdims=True)
-        scaled_ref[rows, :] = scaled
-        table[rows, :] = as_columns(top, jnp.sum(scaled, axis=1, keepdims=True), picked)
-        return carry
-
-    lax.fori_loop(0, logit_ref.shape[0] // chunk, one, 0)
+    def two(part, carry):
+        start = pl.multiple_of(part * chunk, chunk)
+        own, other = pl.ds(start, chunk), pl.ds(slab + start, chunk)
+        stud, teach = scaled_ref[own, :], scaled_ref[other, :]
+        top_stud = jnp.max(highest[own, :], axis=1, keepdims=True)
+        top_teach = jnp.max(highest[other, :], axis=1, keepdims=True)
+        hit = lax.broadcasted_iota(jnp.int32, stud.shape, 1) == column_ref[own, :]
+        picked = jnp.sum(jnp.where(hit, stud, 0.0), axis=1, keepdims=True)
+        scaled_teach = jnp.exp(teach - top_teach)
+        gap = jnp.sum(scaled_teach * (teach - stud), axis=1, keepdims=True)
+        scaled_stud = jnp.exp(stud - top_stud)
+        scaled_ref[own, :] = scaled_stud
+        scaled_ref[other, :] = scaled_teach
+        sum_teach = jnp.sum(scaled_teach, axis=1, keepdims=True)
+        sum_stud = jnp.sum(scaled_stud, axis=1, keepdims=True)
+        table[own, :] = as_columns([top_teach, sum_teach, gap, None, top_stud, sum_stud, picked])
+        return carry
+
+    lax.fori_loop(0, slab // chunk, two, 0)
     stats_ref[...] = table[...].T[0:8]
-
-
-def teacher_kernel(count, step, chunk, *refs):
-    pieces = refs[:count]
-    head, stud_logit_ref, stud_ref, scaled_ref, stats_ref, highest, table = refs[count:]
-
-    def read_rows():
-        return jnp.concatenate([ref[...] for ref in pieces], axis=0) if count > 1 else pieces[0][...]
-
-    multiply(read_rows, head, scaled_ref, highest, step)
-
-    def one(part, carry):
-        rows = pl.ds(pl.multiple_of(part * chunk, chunk), chunk)
-        logit = scaled_ref[rows, :]
-        top = jnp.max(highest[rows, :], axis=1, keepdims=True)
-        scaled = jnp.exp(logit - top)
-        gap = jnp.sum(scaled * (logit - stud_logit_ref[rows, :]), axis=1, keepdims=True)
-        scaled_ref[rows, :] = scaled
-        table[rows, :] = as_columns(top, jnp.sum(scaled, axis=1, keepdims=True), gap)
-        return carry
-
-    lax.fori_loop(0, scaled_ref.shape[0] // chunk, one, 0)
-    teach = table[...].T[0:8]
-    row = lax.broadcasted_iota(jnp.int32, teach.shape, 0)
-    stats_ref[...] = jnp.where(row < 4, teach, pltpu.roll(stud_ref[...], 4, 0))
 
 
 def head_cost(rows, head):
@@ -186,44 +154,26 @@
     )
 
 
-def student_logits(pieces, heads, column, step, chunk):
-    rows, (depth, vocab_dev) = column.shape[0], heads[0].shape
-    wide = (rows, vocab_dev)
+def logits(pieces, heads, column, step, chunk):
+    slab, (depth, vocab_dev) = column.shape[0], heads[0].shape
     return pl.pallas_call(
-        functools.partial(student_kernel, len(pieces), step, chunk),
+        functools.partial(logits_kernel, len(pieces), step, chunk),
         in_specs=[in_place] * (len(pieces) + 2) + [in_vmem],
-        out_specs=[in_vmem] * 4,
+        out_specs=[in_vmem] * 3,
         out_shape=[
-            jax.ShapeDtypeStruct(wide, jnp.float32),
-            jax.ShapeDtypeStruct(wide, jnp.float32),
-            jax.ShapeDtypeStruct((8, rows), jnp.float32),
+            jax.ShapeDtypeStruct((2 * slab, vocab_dev), jnp.float32),
+            jax.ShapeDtypeStruct((8, slab), jnp.float32),
             jax.ShapeDtypeStruct((2 * depth, vocab_dev), jnp.bfloat16),
         ],
         scratch_shapes=[
-            pltpu.VMEM((rows, 2 * depth), jnp.bfloat16),
-            pltpu.VMEM((rows, lanes), jnp.float32),
-            pltpu.VMEM((rows, lanes), jnp.float32),
+            pltpu.VMEM((2 * slab, 2 * depth), jnp.bfloat16),
+            pltpu.VMEM((2 * slab, lanes), jnp.float32),
+            pltpu.VMEM((slab, lanes), jnp.float32),
             pltpu.SemaphoreType.DMA((len(pieces) + 2 * len(cuts(vocab_dev, step)),)),
         ],
-        compiler_params=pltpu.CompilerParams(vmem_limit_bytes=vmem_bytes),
-        cost_estimate=head_cost(rows, heads[0]),
+        compiler_params=pltpu.CompilerParams(vmem_limit_bytes=logits_bytes),
+        cost_estimate=head_cost(4 * slab, heads[0]),
     )(*pieces, *heads, column)
-
-
-def teacher_logits(pieces, head, logit_stud, stats_stud, step, chunk):
-    wide = logit_stud.shape
-    return pl.pallas_call(
-        functools.partial(teacher_kernel, len(pieces), step, chunk),
-        in_specs=[in_vmem] * (len(pieces) + 3),
-        out_specs=[in_vmem] * 2,
-        out_shape=[
-            jax.ShapeDtypeStruct(wide, jnp.float32),
-            jax.ShapeDtypeStruct((8, wide[0]), jnp.float32),
-        ],
-        scratch_shapes=[pltpu.VMEM((wide[0], lanes), jnp.float32)] * 2,
-        compiler_params=pltpu.CompilerParams(vmem_limit_bytes=vmem_bytes),
-        cost_estimate=head_cost(wide[0], head),
-    )(*pieces, head, logit_stud, stats_stud)
 
 
 def swapped(values, distance):
@@ -237,9 +187,9 @@
 def gradient_kernel(bits, step, chunk, place_ref, *refs):
     count = 1 << bits
     tables, refs = refs[:count], refs[count:]
-    teach_ref, stud_ref, column_ref, head, loss_ref = refs[:5]
-    outs = refs[5 : count + 5]
-    entries, upstream, factors = refs[count + 5 :]
+    scaled_ref, column_ref, head, loss_ref = refs[:4]
+    outs = refs[4 : count + 4]
+    entries, upstream, factors = refs[count + 4 :]
     rows = upstream.shape[0]
     blk = rows // count
     me = place_ref[0]
@@ -270,9 +220,10 @@
     factors[...] = jnp.where(line == 0, scale_teach, scale_stud).T
 
     def one(part, carry):
-        at = pl.ds(pl.multiple_of(part * chunk, chunk), chunk)
-        hit = lax.broadcasted_iota(jnp.int32, (chunk, teach_ref.shape[1]), 1) == column_ref[at, :]
-        both = teach_ref[at, :] * factors[at, 0:1] + stud_ref[at, :] * factors[at, 1:2]
+        start = pl.multiple_of(part * chunk, chunk)
+        at, other = pl.ds(start, chunk), pl.ds(rows + start, chunk)
+        hit = lax.broadcasted_iota(jnp.int32, (chunk, scaled_ref.shape[1]), 1) == column_ref[at, :]
+        both = scaled_ref[other, :] * factors[at, 0:1] + scaled_ref[at, :] * factors[at, 1:2]
         upstream[at, :] = jnp.where(hit, both - loss_scale, both).astype(jnp.bfloat16)
         return carry
 
@@ -290,13 +241,13 @@
     lax.fori_loop(0, head.shape[0] // step, two, 0)
 
 
-def gradient(place, tables, scaled_teach, scaled_stud, column, head, bits, chunk):
-    rows, vocab_dev = scaled_teach.shape
+def gradient(place, tables, scaled, column, head, bits, chunk):
+    rows, vocab_dev = column.shape[0], scaled.shape[1]
     count, width = 1 << bits, head.shape[0]
     step = 512 if width % 512 == 0 else width
     return pl.pallas_call(
         functools.partial(gradient_kernel, bits, step, chunk),
-        in_specs=[in_smem] + [in_vmem] * (count + 4),
+        in_specs=[in_smem] + [in_vmem] * (count + 3),
         out_specs=[in_vmem] * (count + 1),
         out_shape=[jax.ShapeDtypeStruct((8, rows), jnp.float32)]
         + [jax.ShapeDtypeStruct((rows // count, width), jnp.float32)] * count,
@@ -307,7 +258,7 @@
         ],
         compiler_params=pltpu.CompilerParams(vmem_limit_bytes=vmem_bytes),
         cost_estimate=head_cost(rows, head),
-    )(place, *tables, scaled_teach, scaled_stud, column, head)
+    )(place, *tables, scaled, column, head)
 
 
 def tie(block, *others):
@@ -383,13 +334,13 @@
         projected = spread(turned(projected_own.astype(jnp.bfloat16)), line)
 
         column = (in_order(targets) - me * vocab_dev)[:, None]
-        logit_stud, scaled_stud, stats_stud, head = student_logits(as_pieces(hidden), heads, column, 256, chunk)
-        scaled_teach, stats = teacher_logits(as_pieces(projected), head, logit_stud, stats_stud, 512, chunk)
-        tables = [stats] + [
-            lax.ppermute(stats, "vocab", [(at, at ^ mask) for at in range(vocab_size)])
-            for mask in range(1, vocab_size)
-        ]
-        loss, *terms = gradient(place, tables, scaled_teach, scaled_stud, column, head, bits, chunk)
+        scaled, stats, head = logits(as_pieces(hidden) + as_pieces(projected), heads, column, 512, chunk)
+        tables = [stats]
+        for mask in range(1, vocab_size):
+            far, near = mask & ~3, mask & 3
+            source, hop = (tables[far], near) if near else (stats, far)
+            tables.append(lax.ppermute(source, "vocab", [(at, at ^ hop) for at in range(vocab_size)]))
+        loss, *terms = gradient(place, tables, scaled, column, head, bits, chunk)
         return (loss[0], turned(reduce_blocks(terms)[0].astype(jnp.bfloat16)))
 
     return body

time: 138 us -> 163 us (1.18)
  waiting for transfers between devices: 39 us -> 65.6 us
  starting transfers between devices: 55.3 us -> 42.6 us
  local copies, waits for them, and re-layouts: 4.35 us -> 10.3 us
  Pallas kernels: 32.5 us -> 38.4 us
    ppermute x28, waiting for transfers between devices: 37.4 us -> 62.3 us  [swap(): lax.ppermute(block, 'vocab', [(at, at ^ 1 << bit) for at in range(vocab_s...]
    ppermute x28, starting transfers between devices: 43.6 us -> 33.3 us  [swap(): lax.ppermute(block, 'vocab', [(at, at ^ 1 << bit) for at in range(vocab_s...]
    unnamed x6 -> x8, local copies, waits for them, and re-layouts: 3.48 us -> 9.44 us
    pallas_call x2 -> x1, Pallas kernels: 19.4 us -> 25.2 us  [logits(): pl.pallas_call(functools.partial(logits_kernel, len(pieces), step, chunk)...]
    ppermute x7, starting transfers between devices: 11.2 us -> 8.81 us  [body(): lax.ppermute(source, 'vocab', [(at, at ^ hop) for at in range(vocab_size)])]
    ppermute x7, waiting for transfers between devices: 1.56 us -> 3.29 us  [body(): lax.ppermute(source, 'vocab', [(at, at ^ hop) for at in range(vocab_size)])]
  transfers between devices with their start and end apart: 36 -> 36, of which waited for: 17 -> 19; matrix products, arithmetic and copies ran while one was open for 4% -> 2% of each run, Pallas kernels for 12% -> 3%
where the time goes in v7:
time: 163 us; the launch traced here: 162 us
  waiting for transfers between devices  65.6 us (40%)
  starting transfers between devices  42.6 us (26%)
  Pallas kernels  38.4 us (24%)
  local copies, waits for them, and re-layouts  10.3 us (6%)
  other arithmetic  4.03 us (2%)
    ppermute x28, waiting for transfers between devices, swap(): lax.ppermute(block, 'vocab', [(at, at ^ 1 << bit) for at in range(vocab_s...  62.3 us
    ppermute x28, starting transfers between devices, swap(): lax.ppermute(block, 'vocab', [(at, at ^ 1 << bit) for at in range(vocab_s...  33.3 us
    pallas_call x1, Pallas kernels, logits(): pl.pallas_call(functools.partial(logits_kernel, len(pieces), step, chunk)...  25.2 us
    unnamed x8, local copies, waits for them, and re-layouts  9.44 us
    ppermute x7, starting transfers between devices, body(): lax.ppermute(source, 'vocab', [(at, at ^ hop) for at in range(vocab_size)])  8.81 us
    pallas_call x1, Pallas kernels, gradient(): pl.pallas_call(functools.partial(gradient_kernel, bits, step, chunk), in_...  8.36 us
    pallas_call x1, Pallas kernels, project(): pl.pallas_call(functools.partial(project_kernel, count, step), in_specs=[...  4.83 us
    ppermute x7, waiting for transfers between devices, body(): lax.ppermute(source, 'vocab', [(at, at ^ hop) for at in range(vocab_size)])  3.29 us
  transfers between devices with their start and end apart: 36, of which 19 were waited for; matrix products, arithmetic and copies ran while one was open for 2% of the time, Pallas kernels for 3%

profile of v7, /device:TPU:0, one launch (start us, length us, event | category | flops | bytes accessed | tf_op | source)
XLA Modules:
  0.0 162.4 jit_solution(14958757373742271363)
XLA Ops:
  0.6 0.5 collective-permute-start.21
  1.8 0.8 and_convert_fusion.member_ref
  2.7 4.8 %shard_map.86 = (f32[32,3584]{1,0:T(8,128)S(1)}, f32[32,3584]{1,0:T(8,128)S(1)}, f32[32,3584]{1,0:T(8,128)S(1)}, f32[32,3584]{1,0:T(8,128)S(1)}, f32[32,3584]{1,...) custom-call(bf16[256,512]{1,0:T(8,128)(2,1)S(1)} %and_convert_fusion.member_ref, ...), custom_call_target="tpu_custom_call" | custom-call | flops 2147483648 | bytes 12058624 | tf_op jit(solution)/shard_map/pallas_call | solution.py:55
  7.5 0.7 convert_element_type.96
  8.2 2.6 %collective-permute-start.3 = (f16[32,3584]{1,0:T(8,128)(2,1)}, f16[32,3584]{1,0:T(8,128)(2,1)S(1)}, u32[]{:S(2)}, u32[]{:S(2)}) collective-permute-start(f16[32,3584]{1,0:T(8,128)(2,1)} %convert_element_type.96), channel_id=1, source_target_pairs={{0,1},{1,0},{2,3},{3,2},{4,5},{5,4},{6,7},{7,6},{8,9},{9,8},{10,11... | collective-permute-start | bytes 688136 | tf_op jit(solution)/shard_map/ppermute | solution.py:273
  10.8 0.7 convert_element_type.94
  11.5 5.9 %collective-permute-done.3 = f16[32,3584]{1,0:T(8,128)(2,1)S(1)} collective-permute-done((f16[32,3584]{1,0:T(8,128)(2,1)}, f16[32,3584]{1,0:T(8,128)(2,1)S(1)}, u32[]{:S(2)}, u32[]{:S(2)}) %collective-permute-start.3) | collective-permute-done | bytes 229408 | tf_op jit(solution)/shard_map/ppermute | solution.py:273
  17.5 2.1 %collective-permute-start.11 = (f16[32,3584]{1,0:T(8,128)(2,1)S(1)}, f16[32,3584]{1,0:T(8,128)(2,1)S(1)}, u32[]{:S(2)}, u32[]{:S(2)}) collective-permute-start(f16[32,3584]{1,0:T(8,128)(2,1)S(1)} %add_convert_fusion.7), channel_id=1, source_target_pairs={{0,2},{1,3},{2,0},{3,1},{4,6},{5,7},{6,4},{7,5},{8,10},{9,11},{10,... | collective-permute-start | bytes 688136 | tf_op jit(solution)/shard_map/ppermute | solution.py:273
  19.6 2.7 %collective-permute-start.6 = (bf16[32,3584]{1,0:T(8,128)(2,1)S(1)}, bf16[32,3584]{1,0:T(8,128)(2,1)S(1)}, u32[]{:S(2)}, u32[]{:S(2)}) collective-permute-start(bf16[32,3584]{1,0:T(8,128)(2,1)S(1)} %maximum_select_fusion.refs_0_), channel_id=1, source_target_pairs={{0,4},{1,5},{2,6},{3,7},{4,0},{5,1},{6,2},{7,3},{8,12},{9,13},{10,... | collective-permute-start | bytes 688136 | tf_op jit(solution)/shard_map/ppermute | solution.py:273
  22.3 0.4 collective-permute-start.2
  22.8 1.6 collective-permute-start.4
  24.4 6.6 %collective-permute-done.11 = f16[32,3584]{1,0:T(8,128)(2,1)S(1)} collective-permute-done((f16[32,3584]{1,0:T(8,128)(2,1)S(1)}, f16[32,3584]{1,0:T(8,128)(2,1)S(1)}, u32[]{:S(2)}, u32[]{:S(2)}) %collective-permute-start.11) | collective-permute-done | bytes 229408 | tf_op jit(solution)/shard_map/ppermute | solution.py:273
  31.0 2.0 %collective-permute-start.1 = (bf16[32,3584]{1,0:T(8,128)(2,1)S(1)}, bf16[32,3584]{1,0:T(8,128)(2,1)S(1)}, u32[]{:S(2)}, u32[]{:S(2)}) collective-permute-start(bf16[32,3584]{1,0:T(8,128)(2,1)S(1)} %maximum_select_fusion.refs_0_), channel_id=1, source_target_pairs={{0,1},{1,0},{2,3},{3,2},{4,5},{5,4},{6,7},{7,6},{8,9},{9,8},{10,11... | collective-permute-start | bytes 688136 | tf_op jit(solution)/shard_map/ppermute | solution.py:273
  33.0 0.1 add_convert_fusion.6
  33.1 0.1 collective-permute-start.7
  33.2 2.4 %collective-permute-start.9 = (bf16[32,3584]{1,0:T(8,128)(2,1)S(1)}, bf16[32,3584]{1,0:T(8,128)(2,1)S(1)}, u32[]{:S(2)}, u32[]{:S(2)}) collective-permute-start(bf16[32,3584]{1,0:T(8,128)(2,1)S(1)} %collective-permute-done.6.refs_4_), channel_id=1, source_target_pairs={{0,2},{1,3},{2,0},{3,1},{4,6},{5,7},{6,4},{7,5},{8,10},{9,11},{10,... | collective-permute-start | bytes 688136 | tf_op jit(solution)/shard_map/ppermute | solution.py:273
  35.7 0.2 collective-permute-done.2.refs_2_
  35.9 2.0 %collective-permute-start.13 = (f16[32,3584]{1,0:T(8,128)(2,1)S(1)}, f16[32,3584]{1,0:T(8,128)(2,1)S(1)}, u32[]{:S(2)}, u32[]{:S(2)}) collective-permute-start(f16[32,3584]{1,0:T(8,128)(2,1)S(1)} %add_convert_fusion.5), channel_id=1, source_target_pairs={{0,2},{1,3},{2,0},{3,1},{4,6},{5,7},{6,4},{7,5},{8,10},{9,11},{10,... | collective-permute-start | bytes 688136 | tf_op jit(solution)/shard_map/ppermute | solution.py:273
  37.9 6.5 %collective-permute-done.9.refs_6_ = bf16[32,3584]{1,0:T(8,128)(2,1)S(1)} collective-permute-done((bf16[32,3584]{1,0:T(8,128)(2,1)S(1)}, bf16[32,3584]{1,0:T(8,128)(2,1)S(1)}, u32[]{:S(2)}, u32[]{:S(2)}) %collective-permute-start.9) | collective-permute-done | bytes 229408 | tf_op jit(solution)/shard_map/ppermute | solution.py:273
  44.4 2.3 %collective-permute-start.5 = (bf16[32,3584]{1,0:T(8,128)(2,1)S(1)}, bf16[32,3584]{1,0:T(8,128)(2,1)S(1)}, u32[]{:S(2)}, u32[]{:S(2)}) collective-permute-start(bf16[32,3584]{1,0:T(8,128)(2,1)S(1)} %collective-permute-done.2.refs_2_), channel_id=1, source_target_pairs={{0,1},{1,0},{2,3},{3,2},{4,5},{5,4},{6,7},{7,6},{8,9},{9,8},{10,11... | collective-permute-start | bytes 688136 | tf_op jit(solution)/shard_map/ppermute | solution.py:273
  46.9 11.8 %collective-permute-done.12 = f16[32,3584]{1,0:T(8,128)(2,1)S(1)} collective-permute-done((f16[32,3584]{1,0:T(8,128)(2,1)S(1)}, f16[32,3584]{1,0:T(8,128)(2,1)S(1)}, u32[]{:S(2)}, u32[]{:S(2)}) %collective-permute-start.12) | collective-permute-done | bytes 229408 | tf_op jit(solution)/shard_map/ppermute | solution.py:273
  58.7 0.1 add_convert_fusion.4
  59.0 1.4 collective-permute-start.8
  60.4 2.4 %collective-permute-start.15 = (bf16[32,3584]{1,0:T(8,128)(2,1)S(1)}, bf16[32,3584]{1,0:T(8,128)(2,1)S(1)}, u32[]{:S(2)}, u32[]{:S(2)}) collective-permute-start(bf16[32,3584]{1,0:T(8,128)(2,1)S(1)} %maximum_select_fusion.1.refs_8_), channel_id=1, source_target_pairs={{0,2},{1,3},{2,0},{3,1},{4,6},{5,7},{6,4},{7,5},{8,10},{9,11},{10,... | collective-permute-start | bytes 688136 | tf_op jit(solution)/shard_map/ppermute | solution.py:273
  62.8 4.5 %collective-permute-done.17.refs_12_ = bf16[32,3584]{1,0:T(8,128)(2,1)S(1)} collective-permute-done((bf16[32,3584]{1,0:T(8,128)(2,1)S(1)}, bf16[32,3584]{1,0:T(8,128)(2,1)S(1)}, u32[]{:S(2)}, u32[]{:S(2)}) %collective-permute-start.17) | collective-permute-done | bytes 229408 | tf_op jit(solution)/shard_map/ppermute | solution.py:273
  67.5 2.0 %collective-permute-start.18 = (bf16[32,3584]{1,0:T(8,128)(2,1)S(1)}, bf16[32,3584]{1,0:T(8,128)(2,1)S(1)}, u32[]{:S(2)}, u32[]{:S(2)}) collective-permute-start(bf16[32,3584]{1,0:T(8,128)(2,1)S(1)} %collective-permute-done.17.refs_12_), channel_id=1, source_target_pairs={{0,1},{1,0},{2,3},{3,2},{4,5},{5,4},{6,7},{7,6},{8,9},{9,8},{10,11... | collective-permute-start | bytes 688136 | tf_op jit(solution)/shard_map/ppermute | solution.py:273
  69.5 0.6 collective-permute-start.16
  70.2 2.3 %collective-permute-done.14.refs_9_ = bf16[32,3584]{1,0:T(8,128)(2,1)S(1)} collective-permute-done((bf16[32,3584]{1,0:T(8,128)(2,1)S(1)}, bf16[32,3584]{1,0:T(8,128)(2,1)S(1)}, u32[]{:S(2)}, u32[]{:S(2)}) %collective-permute-start.14) | collective-permute-done | bytes 229408 | tf_op jit(solution)/shard_map/ppermute | solution.py:273
  72.4 1.0 collective-permute-done.19.refs_14_
  73.4 1.9 %collective-permute-start.20 = (bf16[32,3584]{1,0:T(8,128)(2,1)S(1)}, bf16[32,3584]{1,0:T(8,128)(2,1)}, u32[]{:S(2)}, u32[]{:S(2)}) collective-permute-start(bf16[32,3584]{1,0:T(8,128)(2,1)S(1)} %collective-permute-done.19.refs_14_), channel_id=1, source_target_pairs={{0,1},{1,0},{2,3},{3,2},{4,5},{5,4},{6,7},{7,6},{8,9},{9,8},{10,11... | collective-permute-start | bytes 688136 | tf_op jit(solution)/shard_map/ppermute | solution.py:273
  75.3 0.1 sub.26.refs_18_.refs_9_
  75.5 0.9 collective-permute-done.18.refs_13_
  76.4 2.6 %collective-permute-done.16.refs_11_ = bf16[32,3584]{1,0:T(8,128)(2,1)} collective-permute-done((bf16[32,3584]{1,0:T(8,128)(2,1)S(1)}, bf16[32,3584]{1,0:T(8,128)(2,1)}, u32[]{:S(2)}, u32[]{:S(2)}) %collective-permute-start.16) | collective-permute-done | bytes 229408 | tf_op jit(solution)/shard_map/ppermute | solution.py:273
  78.9 2.5 %collective-permute-done.20.refs_15_ = bf16[32,3584]{1,0:T(8,128)(2,1)} collective-permute-done((bf16[32,3584]{1,0:T(8,128)(2,1)S(1)}, bf16[32,3584]{1,0:T(8,128)(2,1)}, u32[]{:S(2)}, u32[]{:S(2)}) %collective-permute-start.20) | collective-permute-done | bytes 229408 | tf_op jit(solution)/shard_map/ppermute | solution.py:273
  81.4 3.5 %copy-done.1 = bf16[1792,2432]{1,0:T(8,128)(2,1)S(1)} copy-done((bf16[1792,2432]{1,0:T(8,128)(2,1)S(1)}, bf16[1792,2432]{1,0:T(8,128)(2,1)}, u32[]{:S(2)}) %copy-start.1) | copy-done | bytes 8716312
  84.9 25.2 %shard_map.87 = (f32[512,2432]{1,0:T(8,128)S(1)}, f32[8,256]{1,0:T(8,128)S(1)}, bf16[3584,2432]{1,0:T(8,128)(2,1)}) custom-call(bf16[32,3584]{1,0:T(8,128)(2,1)S(1)} %maximum_select_fusion.refs_0_, bf16[32,3584]{1,0:T(8,128)(2,1)S(1)} %collective-permute-done.1.refs_1_, bf16[32,3584]{1,0:T(8,128)(2,1)S(1)} %collective-permute-done.2.refs_2_, ...), custom_call_target="tpu_custom_call" | custom-call | flops 8925478912 | bytes 38600704 | tf_op jit(solution)/shard_map/pallas_call | solution.py:159
  110.1 1.8 %collective-permute-start.25 = (f32[8,256]{1,0:T(8,128)S(1)}, f32[8,256]{1,0:T(8,128)S(1)}, u32[]{:S(2)}, u32[]{:S(2)}) collective-permute-start(f32[8,256]{1,0:T(8,128)S(1)} %get-tuple-element.54.refs_0_), channel_id=1, source_target_pairs={{0,4},{1,5},{2,6},{3,7},{4,0},{5,1},{6,2},{7,3},{8,12},{9,13},{10,... | collective-permute-start | bytes 24584 | tf_op jit(solution)/shard_map/ppermute | solution.py:342
  111.9 1.5 collective-permute-start.24
  113.4 1.7 %collective-permute-start.23 = (f32[8,256]{1,0:T(8,128)S(1)}, f32[8,256]{1,0:T(8,128)S(1)}, u32[]{:S(2)}, u32[]{:S(2)}) collective-permute-start(f32[8,256]{1,0:T(8,128)S(1)} %get-tuple-element.54.refs_0_), channel_id=1, source_target_pairs={{0,2},{1,3},{2,0},{3,1},{4,6},{5,7},{6,4},{7,5},{8,10},{9,11},{10,... | collective-permute-start | bytes 24584 | tf_op jit(solution)/shard_map/ppermute | solution.py:342
  115.1 0.3 collective-permute-start.22
  115.4 1.8 %collective-permute-start.28 = (f32[8,256]{1,0:T(8,128)S(1)}, f32[8,256]{1,0:T(8,128)S(1)}, u32[]{:S(2)}, u32[]{:S(2)}) collective-permute-start(f32[8,256]{1,0:T(8,128)S(1)} %collective-permute-done.25.refs_4_), channel_id=1, source_target_pairs={{0,3},{1,2},{2,1},{3,0},{4,7},{5,6},{6,5},{7,4},{8,11},{9,10},{10,... | collective-permute-start | bytes 24584 | tf_op jit(solution)/shard_map/ppermute | solution.py:342
  117.2 1.4 collective-permute-start.27
  118.6 0.3 collective-permute-start.26
  119.0 1.0 collective-permute-done.28.refs_7_
  119.9 0.9 collective-permute-done.27.refs_6_
  120.9 1.4 collective-permute-done.26.refs_5_
  122.2 6.0 %copy-done = bf16[3584,2432]{1,0:T(8,128)(2,1)S(1)} copy-done((bf16[3584,2432]{1,0:T(8,128)(2,1)S(1)}, bf16[3584,2432]{1,0:T(8,128)(2,1)}, u32[]{:S(2)}) %copy-start) | copy-done | bytes 17432600
  128.2 8.4 %shard_map.88 = (f32[8,256]{1,0:T(8,128)S(1)}, f32[32,3584]{1,0:T(8,128)S(1)}, f32[32,3584]{1,0:T(8,128)S(1)}, f32[32,3584]{1,0:T(8,128)S(1)}, f32[32,3584]{1,0:...) custom-call(s32[2]{0:T(128)S(1)} %pad_add_fusion.place_ref, ...), custom_call_target="tpu_custom_call" | custom-call | flops 4462739456 | bytes 24903680 | tf_op jit(solution)/shard_map/pallas_call | solution.py:248
  136.6 0.4 collective-permute-start.31
  137.0 1.8 %collective-permute-start.29 = (f16[32,3584]{1,0:T(8,128)(2,1)S(1)}, f16[32,3584]{1,0:T(8,128)(2,1)S(1)}, u32[]{:S(2)}, u32[]{:S(2)}) collective-permute-start(f16[32,3584]{1,0:T(8,128)(2,1)S(1)} %convert_element_type.109), channel_id=1, source_target_pairs={{0,1},{1,0},{2,3},{3,2},{4,5},{5,4},{6,7},{7,6},{8,9},{9,8},{10,11... | collective-permute-start | bytes 688136 | tf_op jit(solution)/shard_map/ppermute | solution.py:273
  138.9 3.8 %collective-permute-done.31 = f16[32,3584]{1,0:T(8,128)(2,1)S(1)} collective-permute-done((f16[32,3584]{1,0:T(8,128)(2,1)S(1)}, f16[32,3584]{1,0:T(8,128)(2,1)S(1)}, u32[]{:S(2)}, u32[]{:S(2)}) %collective-permute-start.31) | collective-permute-done | bytes 229408 | tf_op jit(solution)/shard_map/ppermute | solution.py:273
  142.7 0.3 collective-permute-start.35
  143.0 2.2 %collective-permute-done.29 = f16[32,3584]{1,0:T(8,128)(2,1)S(1)} collective-permute-done((f16[32,3584]{1,0:T(8,128)(2,1)S(1)}, f16[32,3584]{1,0:T(8,128)(2,1)S(1)}, u32[]{:S(2)}, u32[]{:S(2)}) %collective-permute-start.29) | collective-permute-done | bytes 229408 | tf_op jit(solution)/shard_map/ppermute | solution.py:273
  145.1 0.3 collective-permute-start.33
  145.5 1.2 collective-permute-start.30
  146.7 4.5 %collective-permute-done.33 = f16[32,3584]{1,0:T(8,128)(2,1)S(1)} collective-permute-done((f16[32,3584]{1,0:T(8,128)(2,1)S(1)}, f16[32,3584]{1,0:T(8,128)(2,1)S(1)}, u32[]{:S(2)}, u32[]{:S(2)}) %collective-permute-start.33) | collective-permute-done | bytes 229408 | tf_op jit(solution)/shard_map/ppermute | solution.py:273
  151.2 0.7 collective-permute-start.34
  152.0 0.1 add_convert_fusion.2
  152.1 1.9 %collective-permute-start.32 = (f16[32,3584]{1,0:T(8,128)(2,1)S(1)}, f16[32,3584]{1,0:T(8,128)(2,1)S(1)}, u32[]{:S(2)}, u32[]{:S(2)}) collective-permute-start(f16[32,3584]{1,0:T(8,128)(2,1)S(1)} %add_convert_fusion.2), channel_id=1, source_target_pairs={{0,4},{1,5},{2,6},{3,7},{4,0},{5,1},{6,2},{7,3},{8,12},{9,13},{10,... | collective-permute-start | bytes 688136 | tf_op jit(solution)/shard_map/ppermute | solution.py:273
  154.0 0.6 slice.27
  154.6 4.0 %collective-permute-done.34 = f16[32,3584]{1,0:T(8,128)(2,1)S(1)} collective-permute-done((f16[32,3584]{1,0:T(8,128)(2,1)S(1)}, f16[32,3584]{1,0:T(8,128)(2,1)S(1)}, u32[]{:S(2)}, u32[]{:S(2)}) %collective-permute-start.34) | collective-permute-done | bytes 229408 | tf_op jit(solution)/shard_map/ppermute | solution.py:273
  158.6 3.0 %collective-permute-done.32 = f16[32,3584]{1,0:T(8,128)(2,1)S(1)} collective-permute-done((f16[32,3584]{1,0:T(8,128)(2,1)S(1)}, f16[32,3584]{1,0:T(8,128)(2,1)S(1)}, u32[]{:S(2)}, u32[]{:S(2)}) %collective-permute-start.32) | collective-permute-done | bytes 229408 | tf_op jit(solution)/shard_map/ppermute | solution.py:273
  161.6 0.1 add_convert_fusion
  161.7 0.8 maximum_select_fusion.2
  (52 shorter events, 1.0 us)
Async XLA Ops:
  0.6 10.9 %copy-start.2 = (bf16[32,3584]{1,0:T(8,128)(2,1)S(1)}, bf16[32,3584]{1,0:T(8,128)(2,1)}, u32[]{:S(2)}) copy-start(bf16[32,3584]{1,0:T(8,128)(2,1)} %param.11) | copy-start | bytes 688132
  0.6 80.8 %collective-permute-start.21 = (bf16[1792,2432]{1,0:T(8,128)(2,1)}, bf16[1792,2432]{1,0:T(8,128)(2,1)}, u32[]{:S(2)}, u32[]{:S(2)}) collective-permute-start(bf16[1792,2432]{1,0:T(8,128)(2,1)} %refs_16_.1), channel_id=1, source_target_pairs={{0,8},{8,0},{1,9},{9,1},{2,10},{10,2},{3,11},{11,3},{4,12},{12,4},... | collective-permute-start | bytes 26148872 | tf_op jit(solution)/shard_map/ppermute | solution.py:325
  2.7 64.7 %copy-start.3 = (s32[256]{0:T(256)S(1)}, s32[256]{0:T(256)}, u32[]{:S(2)}) copy-start(s32[256]{0:T(256)} %param.13) | copy-start | bytes 3076
  8.2 9.2 %collective-permute-start.3 = (f16[32,3584]{1,0:T(8,128)(2,1)}, f16[32,3584]{1,0:T(8,128)(2,1)S(1)}, u32[]{:S(2)}, u32[]{:S(2)}) collective-permute-start(f16[32,3584]{1,0:T(8,128)(2,1)} %convert_element_type.96), channel_id=1, source_target_pairs={{0,1},{1,0},{2,3},{3,2},{4,5},{5,4},{6,7},{7,6},{8,9},{9,8},{10,11... | collective-permute-start | bytes 688136 | tf_op jit(solution)/shard_map/ppermute | solution.py:273
  11.5 11.3 %collective-permute-start = (f16[32,3584]{1,0:T(8,128)(2,1)}, f16[32,3584]{1,0:T(8,128)(2,1)S(1)}, u32[]{:S(2)}, u32[]{:S(2)}) collective-permute-start(f16[32,3584]{1,0:T(8,128)(2,1)} %convert_element_type.94), channel_id=1, source_target_pairs={{0,1},{1,0},{2,3},{3,2},{4,5},{5,4},{6,7},{7,6},{8,9},{9,8},{10,11... | collective-permute-start | bytes 688136 | tf_op jit(solution)/shard_map/ppermute | solution.py:273
  17.5 13.5 %collective-permute-start.11 = (f16[32,3584]{1,0:T(8,128)(2,1)S(1)}, f16[32,3584]{1,0:T(8,128)(2,1)S(1)}, u32[]{:S(2)}, u32[]{:S(2)}) collective-permute-start(f16[32,3584]{1,0:T(8,128)(2,1)S(1)} %add_convert_fusion.7), channel_id=1, source_target_pairs={{0,2},{1,3},{2,0},{3,1},{4,6},{5,7},{6,4},{7,5},{8,10},{9,11},{10,... | collective-permute-start | bytes 688136 | tf_op jit(solution)/shard_map/ppermute | solution.py:273
  19.6 13.4 %collective-permute-start.6 = (bf16[32,3584]{1,0:T(8,128)(2,1)S(1)}, bf16[32,3584]{1,0:T(8,128)(2,1)S(1)}, u32[]{:S(2)}, u32[]{:S(2)}) collective-permute-start(bf16[32,3584]{1,0:T(8,128)(2,1)S(1)} %maximum_select_fusion.refs_0_), channel_id=1, source_target_pairs={{0,4},{1,5},{2,6},{3,7},{4,0},{5,1},{6,2},{7,3},{8,12},{9,13},{10,... | collective-permute-start | bytes 688136 | tf_op jit(solution)/shard_map/ppermute | solution.py:273
  22.3 13.6 %collective-permute-start.2 = (bf16[32,3584]{1,0:T(8,128)(2,1)S(1)}, bf16[32,3584]{1,0:T(8,128)(2,1)S(1)}, u32[]{:S(2)}, u32[]{:S(2)}) collective-permute-start(bf16[32,3584]{1,0:T(8,128)(2,1)S(1)} %maximum_select_fusion.refs_0_), channel_id=1, source_target_pairs={{0,2},{1,3},{2,0},{3,1},{4,6},{5,7},{6,4},{7,5},{8,10},{9,11},{10,... | collective-permute-start | bytes 688136 | tf_op jit(solution)/shard_map/ppermute | solution.py:273
  22.8 10.4 %collective-permute-start.4 = (f16[32,3584]{1,0:T(8,128)(2,1)S(1)}, f16[32,3584]{1,0:T(8,128)(2,1)S(1)}, u32[]{:S(2)}, u32[]{:S(2)}) collective-permute-start(f16[32,3584]{1,0:T(8,128)(2,1)S(1)} %convert_element_type.95), channel_id=1, source_target_pairs={{0,1},{1,0},{2,3},{3,2},{4,5},{5,4},{6,7},{7,6},{8,9},{9,8},{10,11... | collective-permute-start | bytes 688136 | tf_op jit(solution)/shard_map/ppermute | solution.py:273
  31.0 13.4 %collective-permute-start.1 = (bf16[32,3584]{1,0:T(8,128)(2,1)S(1)}, bf16[32,3584]{1,0:T(8,128)(2,1)S(1)}, u32[]{:S(2)}, u32[]{:S(2)}) collective-permute-start(bf16[32,3584]{1,0:T(8,128)(2,1)S(1)} %maximum_select_fusion.refs_0_), channel_id=1, source_target_pairs={{0,1},{1,0},{2,3},{3,2},{4,5},{5,4},{6,7},{7,6},{8,9},{9,8},{10,11... | collective-permute-start | bytes 688136 | tf_op jit(solution)/shard_map/ppermute | solution.py:273
  33.1 13.7 %collective-permute-start.7 = (f16[32,3584]{1,0:T(8,128)(2,1)S(1)}, f16[32,3584]{1,0:T(8,128)(2,1)S(1)}, u32[]{:S(2)}, u32[]{:S(2)}) collective-permute-start(f16[32,3584]{1,0:T(8,128)(2,1)S(1)} %convert_element_type.97), channel_id=1, source_target_pairs={{0,1},{1,0},{2,3},{3,2},{4,5},{5,4},{6,7},{7,6},{8,9},{9,8},{10,11... | collective-permute-start | bytes 688136 | tf_op jit(solution)/shard_map/ppermute | solution.py:273
  33.2 11.2 %collective-permute-start.9 = (bf16[32,3584]{1,0:T(8,128)(2,1)S(1)}, bf16[32,3584]{1,0:T(8,128)(2,1)S(1)}, u32[]{:S(2)}, u32[]{:S(2)}) collective-permute-start(bf16[32,3584]{1,0:T(8,128)(2,1)S(1)} %collective-permute-done.6.refs_4_), channel_id=1, source_target_pairs={{0,2},{1,3},{2,0},{3,1},{4,6},{5,7},{6,4},{7,5},{8,10},{9,11},{10,... | collective-permute-start | bytes 688136 | tf_op jit(solution)/shard_map/ppermute | solution.py:273
  35.9 11.0 %collective-permute-start.13 = (f16[32,3584]{1,0:T(8,128)(2,1)S(1)}, f16[32,3584]{1,0:T(8,128)(2,1)S(1)}, u32[]{:S(2)}, u32[]{:S(2)}) collective-permute-start(f16[32,3584]{1,0:T(8,128)(2,1)S(1)} %add_convert_fusion.5), channel_id=1, source_target_pairs={{0,2},{1,3},{2,0},{3,1},{4,6},{5,7},{6,4},{7,5},{8,10},{9,11},{10,... | collective-permute-start | bytes 688136 | tf_op jit(solution)/shard_map/ppermute | solution.py:273
  44.4 14.3 %collective-permute-start.12 = (f16[32,3584]{1,0:T(8,128)(2,1)S(1)}, f16[32,3584]{1,0:T(8,128)(2,1)S(1)}, u32[]{:S(2)}, u32[]{:S(2)}) collective-permute-start(f16[32,3584]{1,0:T(8,128)(2,1)S(1)} %add_convert_fusion.6), channel_id=1, source_target_pairs={{0,4},{1,5},{2,6},{3,7},{4,0},{5,1},{6,2},{7,3},{8,12},{9,13},{10,... | collective-permute-start | bytes 688136 | tf_op jit(solution)/shard_map/ppermute | solution.py:273
  44.4 16.0 %collective-permute-start.5 = (bf16[32,3584]{1,0:T(8,128)(2,1)S(1)}, bf16[32,3584]{1,0:T(8,128)(2,1)S(1)}, u32[]{:S(2)}, u32[]{:S(2)}) collective-permute-start(bf16[32,3584]{1,0:T(8,128)(2,1)S(1)} %collective-permute-done.2.refs_2_), channel_id=1, source_target_pairs={{0,1},{1,0},{2,3},{3,2},{4,5},{5,4},{6,7},{7,6},{8,9},{9,8},{10,11... | collective-permute-start | bytes 688136 | tf_op jit(solution)/shard_map/ppermute | solution.py:273
  46.8 16.1 %collective-permute-start.10 = (bf16[32,3584]{1,0:T(8,128)(2,1)S(1)}, bf16[32,3584]{1,0:T(8,128)(2,1)S(1)}, u32[]{:S(2)}, u32[]{:S(2)}) collective-permute-start(bf16[32,3584]{1,0:T(8,128)(2,1)S(1)} %collective-permute-done.9.refs_6_), channel_id=1, source_target_pairs={{0,1},{1,0},{2,3},{3,2},{4,5},{5,4},{6,7},{7,6},{8,9},{9,8},{10,11... | collective-permute-start | bytes 688136 | tf_op jit(solution)/shard_map/ppermute | solution.py:273
  58.9 8.5 %collective-permute-start.17 = (bf16[32,3584]{1,0:T(8,128)(2,1)S(1)}, bf16[32,3584]{1,0:T(8,128)(2,1)S(1)}, u32[]{:S(2)}, u32[]{:S(2)}) collective-permute-start(bf16[32,3584]{1,0:T(8,128)(2,1)S(1)} %maximum_select_fusion.1.refs_8_), channel_id=1, source_target_pairs={{0,4},{1,5},{2,6},{3,7},{4,0},{5,1},{6,2},{7,3},{8,12},{9,13},{10,... | collective-permute-start | bytes 688136 | tf_op jit(solution)/shard_map/ppermute | solution.py:273
  59.0 8.5 %collective-permute-start.8 = (bf16[32,3584]{1,0:T(8,128)(2,1)S(1)}, bf16[32,3584]{1,0:T(8,128)(2,1)S(1)}, u32[]{:S(2)}, u32[]{:S(2)}) collective-permute-start(bf16[32,3584]{1,0:T(8,128)(2,1)S(1)} %collective-permute-done.6.refs_4_), channel_id=1, source_target_pairs={{0,1},{1,0},{2,3},{3,2},{4,5},{5,4},{6,7},{7,6},{8,9},{9,8},{10,11... | collective-permute-start | bytes 688136 | tf_op jit(solution)/shard_map/ppermute | solution.py:273
  60.4 9.1 %collective-permute-start.15 = (bf16[32,3584]{1,0:T(8,128)(2,1)S(1)}, bf16[32,3584]{1,0:T(8,128)(2,1)S(1)}, u32[]{:S(2)}, u32[]{:S(2)}) collective-permute-start(bf16[32,3584]{1,0:T(8,128)(2,1)S(1)} %maximum_select_fusion.1.refs_8_), channel_id=1, source_target_pairs={{0,2},{1,3},{2,0},{3,1},{4,6},{5,7},{6,4},{7,5},{8,10},{9,11},{10,... | collective-permute-start | bytes 688136 | tf_op jit(solution)/shard_map/ppermute | solution.py:273
  62.8 9.6 %collective-permute-start.14 = (bf16[32,3584]{1,0:T(8,128)(2,1)S(1)}, bf16[32,3584]{1,0:T(8,128)(2,1)S(1)}, u32[]{:S(2)}, u32[]{:S(2)}) collective-permute-start(bf16[32,3584]{1,0:T(8,128)(2,1)S(1)} %maximum_select_fusion.1.refs_8_), channel_id=1, source_target_pairs={{0,1},{1,0},{2,3},{3,2},{4,5},{5,4},{6,7},{7,6},{8,9},{9,8},{10,11... | collective-permute-start | bytes 688136 | tf_op jit(solution)/shard_map/ppermute | solution.py:273
  67.4 6.0 %collective-permute-start.19 = (bf16[32,3584]{1,0:T(8,128)(2,1)S(1)}, bf16[32,3584]{1,0:T(8,128)(2,1)S(1)}, u32[]{:S(2)}, u32[]{:S(2)}) collective-permute-start(bf16[32,3584]{1,0:T(8,128)(2,1)S(1)} %collective-permute-done.17.refs_12_), channel_id=1, source_target_pairs={{0,2},{1,3},{2,0},{3,1},{4,6},{5,7},{6,4},{7,5},{8,10},{9,11},{10,... | collective-permute-start | bytes 688136 | tf_op jit(solution)/shard_map/ppermute | solution.py:273
  67.5 8.9 %collective-permute-start.18 = (bf16[32,3584]{1,0:T(8,128)(2,1)S(1)}, bf16[32,3584]{1,0:T(8,128)(2,1)S(1)}, u32[]{:S(2)}, u32[]{:S(2)}) collective-permute-start(bf16[32,3584]{1,0:T(8,128)(2,1)S(1)} %collective-permute-done.17.refs_12_), channel_id=1, source_target_pairs={{0,1},{1,0},{2,3},{3,2},{4,5},{5,4},{6,7},{7,6},{8,9},{9,8},{10,11... | collective-permute-start | bytes 688136 | tf_op jit(solution)/shard_map/ppermute | solution.py:273
  69.5 9.4 %collective-permute-start.16 = (bf16[32,3584]{1,0:T(8,128)(2,1)S(1)}, bf16[32,3584]{1,0:T(8,128)(2,1)}, u32[]{:S(2)}, u32[]{:S(2)}) collective-permute-start(bf16[32,3584]{1,0:T(8,128)(2,1)S(1)} %collective-permute-done.15.refs_10_), channel_id=1, source_target_pairs={{0,1},{1,0},{2,3},{3,2},{4,5},{5,4},{6,7},{7,6},{8,9},{9,8},{10,11... | collective-permute-start | bytes 688136 | tf_op jit(solution)/shard_map/ppermute | solution.py:273
  73.4 8.0 %collective-permute-start.20 = (bf16[32,3584]{1,0:T(8,128)(2,1)S(1)}, bf16[32,3584]{1,0:T(8,128)(2,1)}, u32[]{:S(2)}, u32[]{:S(2)}) collective-permute-start(bf16[32,3584]{1,0:T(8,128)(2,1)S(1)} %collective-permute-done.19.refs_14_), channel_id=1, source_target_pairs={{0,1},{1,0},{2,3},{3,2},{4,5},{5,4},{6,7},{7,6},{8,9},{9,8},{10,11... | collective-permute-start | bytes 688136 | tf_op jit(solution)/shard_map/ppermute | solution.py:273
  81.4 3.5 %copy-start.1 = (bf16[1792,2432]{1,0:T(8,128)(2,1)S(1)}, bf16[1792,2432]{1,0:T(8,128)(2,1)}, u32[]{:S(2)}) copy-start(bf16[1792,2432]{1,0:T(8,128)(2,1)} %refs_16_.1) | copy-start | bytes 26148868
  110.1 5.3 %collective-permute-start.25 = (f32[8,256]{1,0:T(8,128)S(1)}, f32[8,256]{1,0:T(8,128)S(1)}, u32[]{:S(2)}, u32[]{:S(2)}) collective-permute-start(f32[8,256]{1,0:T(8,128)S(1)} %get-tuple-element.54.refs_0_), channel_id=1, source_target_pairs={{0,4},{1,5},{2,6},{3,7},{4,0},{5,1},{6,2},{7,3},{8,12},{9,13},{10,... | collective-permute-start | bytes 24584 | tf_op jit(solution)/shard_map/ppermute | solution.py:342
  111.9 6.7 %collective-permute-start.24 = (f32[8,256]{1,0:T(8,128)S(1)}, f32[8,256]{1,0:T(8,128)S(1)}, u32[]{:S(2)}, u32[]{:S(2)}) collective-permute-start(f32[8,256]{1,0:T(8,128)S(1)} %get-tuple-element.54.refs_0_), channel_id=1, source_target_pairs={{0,3},{1,2},{2,1},{3,0},{4,7},{5,6},{6,5},{7,4},{8,11},{9,10},{10,... | collective-permute-start | bytes 24584 | tf_op jit(solution)/shard_map/ppermute | solution.py:342
  113.4 5.6 %collective-permute-start.23 = (f32[8,256]{1,0:T(8,128)S(1)}, f32[8,256]{1,0:T(8,128)S(1)}, u32[]{:S(2)}, u32[]{:S(2)}) collective-permute-start(f32[8,256]{1,0:T(8,128)S(1)} %get-tuple-element.54.refs_0_), channel_id=1, source_target_pairs={{0,2},{1,3},{2,0},{3,1},{4,6},{5,7},{6,4},{7,5},{8,10},{9,11},{10,... | collective-permute-start | bytes 24584 | tf_op jit(solution)/shard_map/ppermute | solution.py:342
  115.1 3.9 %collective-permute-start.22 = (f32[8,256]{1,0:T(8,128)S(1)}, f32[8,256]{1,0:T(8,128)S(1)}, u32[]{:S(2)}, u32[]{:S(2)}) collective-permute-start(f32[8,256]{1,0:T(8,128)S(1)} %get-tuple-element.54.refs_0_), channel_id=1, source_target_pairs={{0,1},{1,0},{2,3},{3,2},{4,5},{5,4},{6,7},{7,6},{8,9},{9,8},{10,11... | collective-permute-start | bytes 24584 | tf_op jit(solution)/shard_map/ppermute | solution.py:342
  115.4 4.6 %collective-permute-start.28 = (f32[8,256]{1,0:T(8,128)S(1)}, f32[8,256]{1,0:T(8,128)S(1)}, u32[]{:S(2)}, u32[]{:S(2)}) collective-permute-start(f32[8,256]{1,0:T(8,128)S(1)} %collective-permute-done.25.refs_4_), channel_id=1, source_target_pairs={{0,3},{1,2},{2,1},{3,0},{4,7},{5,6},{6,5},{7,4},{8,11},{9,10},{10,... | collective-permute-start | bytes 24584 | tf_op jit(solution)/shard_map/ppermute | solution.py:342
  117.2 3.7 %collective-permute-start.27 = (f32[8,256]{1,0:T(8,128)S(1)}, f32[8,256]{1,0:T(8,128)S(1)}, u32[]{:S(2)}, u32[]{:S(2)}) collective-permute-start(f32[8,256]{1,0:T(8,128)S(1)} %collective-permute-done.25.refs_4_), channel_id=1, source_target_pairs={{0,2},{1,3},{2,0},{3,1},{4,6},{5,7},{6,4},{7,5},{8,10},{9,11},{10,... | collective-permute-start | bytes 24584 | tf_op jit(solution)/shard_map/ppermute | solution.py:342
  118.6 3.7 %collective-permute-start.26 = (f32[8,256]{1,0:T(8,128)S(1)}, f32[8,256]{1,0:T(8,128)S(1)}, u32[]{:S(2)}, u32[]{:S(2)}) collective-permute-start(f32[8,256]{1,0:T(8,128)S(1)} %collective-permute-done.25.refs_4_), channel_id=1, source_target_pairs={{0,1},{1,0},{2,3},{3,2},{4,5},{5,4},{6,7},{7,6},{8,9},{9,8},{10,11... | collective-permute-start | bytes 24584 | tf_op jit(solution)/shard_map/ppermute | solution.py:342
  122.2 6.0 %copy-start = (bf16[3584,2432]{1,0:T(8,128)(2,1)S(1)}, bf16[3584,2432]{1,0:T(8,128)(2,1)}, u32[]{:S(2)}) copy-start(bf16[3584,2432]{1,0:T(8,128)(2,1)} %get-tuple-element.56.refs_10_) | copy-start | bytes 52297732
  136.6 6.1 %collective-permute-start.31 = (f16[32,3584]{1,0:T(8,128)(2,1)S(1)}, f16[32,3584]{1,0:T(8,128)(2,1)S(1)}, u32[]{:S(2)}, u32[]{:S(2)}) collective-permute-start(f16[32,3584]{1,0:T(8,128)(2,1)S(1)} %convert_element_type.113), channel_id=1, source_target_pairs={{0,1},{1,0},{2,3},{3,2},{4,5},{5,4},{6,7},{7,6},{8,9},{9,8},{10,11... | collective-permute-start | bytes 688136 | tf_op jit(solution)/shard_map/ppermute | solution.py:273
  137.0 8.2 %collective-permute-start.29 = (f16[32,3584]{1,0:T(8,128)(2,1)S(1)}, f16[32,3584]{1,0:T(8,128)(2,1)S(1)}, u32[]{:S(2)}, u32[]{:S(2)}) collective-permute-start(f16[32,3584]{1,0:T(8,128)(2,1)S(1)} %convert_element_type.109), channel_id=1, source_target_pairs={{0,1},{1,0},{2,3},{3,2},{4,5},{5,4},{6,7},{7,6},{8,9},{9,8},{10,11... | collective-permute-start | bytes 688136 | tf_op jit(solution)/shard_map/ppermute | solution.py:273
  142.7 11.9 %collective-permute-start.35 = (f16[32,3584]{1,0:T(8,128)(2,1)S(1)}, f16[32,3584]{1,0:T(8,128)(2,1)S(1)}, u32[]{:S(2)}, u32[]{:S(2)}) collective-permute-start(f16[32,3584]{1,0:T(8,128)(2,1)S(1)} %convert_element_type.121), channel_id=1, source_target_pairs={{0,1},{1,0},{2,3},{3,2},{4,5},{5,4},{6,7},{7,6},{8,9},{9,8},{10,11... | collective-permute-start | bytes 688136 | tf_op jit(solution)/shard_map/ppermute | solution.py:273
  145.1 6.0 %collective-permute-start.33 = (f16[32,3584]{1,0:T(8,128)(2,1)S(1)}, f16[32,3584]{1,0:T(8,128)(2,1)S(1)}, u32[]{:S(2)}, u32[]{:S(2)}) collective-permute-start(f16[32,3584]{1,0:T(8,128)(2,1)S(1)} %convert_element_type.117), channel_id=1, source_target_pairs={{0,1},{1,0},{2,3},{3,2},{4,5},{5,4},{6,7},{7,6},{8,9},{9,8},{10,11... | collective-permute-start | bytes 688136 | tf_op jit(solution)/shard_map/ppermute | solution.py:273
  145.5 6.5 %collective-permute-start.30 = (f16[32,3584]{1,0:T(8,128)(2,1)S(1)}, f16[32,3584]{1,0:T(8,128)(2,1)S(1)}, u32[]{:S(2)}, u32[]{:S(2)}) collective-permute-start(f16[32,3584]{1,0:T(8,128)(2,1)S(1)} %add_convert_fusion.3), channel_id=1, source_target_pairs={{0,2},{1,3},{2,0},{3,1},{4,6},{5,7},{6,4},{7,5},{8,10},{9,11},{10,... | collective-permute-start | bytes 688136 | tf_op jit(solution)/shard_map/ppermute | solution.py:273
  151.2 7.4 %collective-permute-start.34 = (f16[32,3584]{1,0:T(8,128)(2,1)S(1)}, f16[32,3584]{1,0:T(8,128)(2,1)S(1)}, u32[]{:S(2)}, u32[]{:S(2)}) collective-permute-start(f16[32,3584]{1,0:T(8,128)(2,1)S(1)} %add_convert_fusion.1), channel_id=1, source_target_pairs={{0,2},{1,3},{2,0},{3,1},{4,6},{5,7},{6,4},{7,5},{8,10},{9,11},{10,... | collective-permute-start | bytes 688136 | tf_op jit(solution)/shard_map/ppermute | solution.py:273
  152.1 9.5 %collective-permute-start.32 = (f16[32,3584]{1,0:T(8,128)(2,1)S(1)}, f16[32,3584]{1,0:T(8,128)(2,1)S(1)}, u32[]{:S(2)}, u32[]{:S(2)}) collective-permute-start(f16[32,3584]{1,0:T(8,128)(2,1)S(1)} %add_convert_fusion.2), channel_id=1, source_target_pairs={{0,4},{1,5},{2,6},{3,7},{4,0},{5,1},{6,2},{7,3},{8,12},{9,13},{10,... | collective-permute-start | bytes 688136 | tf_op jit(solution)/shard_map/ppermute | solution.py:273

commit v8 on v4

--- a/solution.py
+++ b/solution.py
@@ -11,6 +11,7 @@
 wire = jnp.float16
 lanes = 128
 vmem_bytes = 12 * 1024 * 1024
+stage_bytes = 8 * 1024 * 1024
 project_bytes = 50 * 1024 * 1024
 
 in_vmem = pl.BlockSpec(memory_space=pltpu.VMEM)
@@ -71,25 +72,12 @@
     )(member, teacher_rows, proj_weight)
 
 
-class Fetch:
-    def __init__(self, sems):
-        self.sems, self.used = sems, 0
-
-    def start(self, source, target):
-        copy = pltpu.make_async_copy(source, target, self.sems.at[self.used])
-        copy.start()
-        self.used += 1
-        return copy
-
-
-def multiply(read_rows, head, logit_ref, highest, step, ready=None):
+def multiply(read_rows, head, logit_ref, highest, step):
     total = head.shape[1]
     highest[...] = jnp.full(highest.shape, -jnp.inf, jnp.float32)
 
-    def one(index, start, size):
+    def one(start, size):
         at = pl.ds(start, size)
-        if ready is not None:
-            ready(index, at)
         part = jnp.dot(read_rows(), head[:, at], preferred_element_type=jnp.float32)
         logit_ref[:, at] = part
         top = part[:, :lanes]
@@ -98,13 +86,40 @@
         highest[...] = jnp.maximum(highest[...], top)
 
     def body(index, carry):
-        one(index, pl.multiple_of(index * step, step), step)
+        one(pl.multiple_of(index * step, step), step)
         return carry
 
     full = total // step
     lax.fori_loop(0, full, body, 0)
     if total % step:
-        one(full, full * step, total % step)
+        one(full * step, total % step)
+
+
+def stage_kernel(first_ref, second_ref, head, sems):
+    depth = first_ref.shape[0]
+    copies = []
+    for half, source in enumerate((first_ref, second_ref)):
+        for start, size in cuts(depth, 256):
+            target = head.at[pl.ds(half * depth + start, size)]
+            copies.append(
+                pltpu.make_async_copy(source.at[pl.ds(start, size)], target, sems.at[len(copies)])
+            )
+            copies[-1].start()
+    for copy in copies:
+        copy.wait()
+
+
+def stage(heads):
+    depth, vocab_dev = heads[0].shape
+    return pl.pallas_call(
+        stage_kernel,
+        in_specs=[in_place] * 2,
+        out_specs=in_vmem,
+        out_shape=jax.ShapeDtypeStruct((2 * depth, vocab_dev), jnp.bfloat16),
+        scratch_shapes=[pltpu.SemaphoreType.DMA((2 * len(cuts(depth, 256)),))],
+        compiler_params=pltpu.CompilerParams(vmem_limit_bytes=stage_bytes),
+        cost_estimate=pl.CostEstimate(flops=0, bytes_accessed=8 * depth * vocab_dev, transcendentals=0),
+    )(*heads)
 
 
 def as_columns(first, second, third):
@@ -113,29 +128,16 @@
 
 
 def student_kernel(count, step, chunk, *refs):
-    pieces, heads = refs[:count], refs[count : count + 2]
-    column_ref, logit_ref, scaled_ref, stats_ref, head = refs[count + 2 : count + 7]
-    held, highest, table, sems = refs[count + 7 :]
-    depth, total = heads[0].shape
+    pieces = refs[:count]
+    head, column_ref, logit_ref, scaled_ref, stats_ref, held, highest, table, sems = refs[count:]
     blk = pieces[0].shape[0]
-    fetch = Fetch(sems)
-    waits = [fetch.start(piece, held.at[pl.ds(i * blk, blk)]) for i, piece in enumerate(pieces)]
-    first = fetch.used
-
-    def columns(half, at):
-        return heads[half].at[:, at], head.at[pl.ds(half * depth, depth), at]
-
-    for start, size in cuts(total, step):
-        for half in range(2):
-            fetch.start(*columns(half, pl.ds(start, size)))
-
-    def ready(index, at):
-        for half in range(2):
-            pltpu.make_async_copy(*columns(half, at), sems.at[first + 2 * index + half]).wait()
-
-    for wait in waits:
-        wait.wait()
-    multiply(lambda: held[...], head, logit_ref, highest, step, ready)
+    copies = []
+    for i, piece in enumerate(pieces):
+        copies.append(pltpu.make_async_copy(piece, held.at[pl.ds(i * blk, blk)], sems.at[i]))
+        copies[-1].start()
+    for copy in copies:
+        copy.wait()
+    multiply(lambda: held[...], head, logit_ref, highest, step)
 
     def one(part, carry):
         rows = pl.ds(pl.multiple_of(part * chunk, chunk), chunk)
@@ -186,28 +188,27 @@
     )
 
 
-def student_logits(pieces, heads, column, step, chunk):
-    rows, (depth, vocab_dev) = column.shape[0], heads[0].shape
+def student_logits(pieces, head, column, step, chunk):
+    rows, vocab_dev = column.shape[0], head.shape[1]
     wide = (rows, vocab_dev)
     return pl.pallas_call(
         functools.partial(student_kernel, len(pieces), step, chunk),
-        in_specs=[in_place] * (len(pieces) + 2) + [in_vmem],
-        out_specs=[in_vmem] * 4,
+        in_specs=[in_place] * len(pieces) + [in_vmem] * 2,
+        out_specs=[in_vmem] * 3,
         out_shape=[
             jax.ShapeDtypeStruct(wide, jnp.float32),
             jax.ShapeDtypeStruct(wide, jnp.float32),
             jax.ShapeDtypeStruct((8, rows), jnp.float32),
-            jax.ShapeDtypeStruct((2 * depth, vocab_dev), jnp.bfloat16),
         ],
         scratch_shapes=[
-            pltpu.VMEM((rows, 2 * depth), jnp.bfloat16),
+            pltpu.VMEM((rows, head.shape[0]), jnp.bfloat16),
             pltpu.VMEM((rows, lanes), jnp.float32),
             pltpu.VMEM((rows, lanes), jnp.float32),
-            pltpu.SemaphoreType.DMA((len(pieces) + 2 * len(cuts(vocab_dev, step)),)),
+            pltpu.SemaphoreType.DMA((len(pieces),)),
         ],
         compiler_params=pltpu.CompilerParams(vmem_limit_bytes=vmem_bytes),
-        cost_estimate=head_cost(rows, heads[0]),
-    )(*pieces, *heads, column)
+        cost_estimate=head_cost(rows, head),
+    )(*pieces, head, column)
 
 
 def teacher_logits(pieces, head, logit_stud, stats_stud, step, chunk):
@@ -336,13 +337,15 @@
                 line.append(blocks[-1])
         return blocks
 
-    def reduce_blocks(parts):
+    def reduce_blocks(parts, beside=None):
         terms, line = list(parts), []
         for mask in range(vocab_size - 1, 0, -1):
             bit = lowest(mask)
             block = terms[mask].astype(wire)
             if bit == 0 and len(line) > 1:
                 block = tie(block, line[-2])
+                if beside is not None and len(line) == 2:
+                    block = tie(block, beside(line[0]))
             block = swap(block, bit)
             if bit == 0:
                 line.append(block)
@@ -371,24 +374,32 @@
         def as_pieces(blocks):
             return blocks if blk % 16 == 0 else [jnp.concatenate(blocks, axis=0)]
 
-        heads = (head_weight, lax.ppermute(head_weight, "seq", [(0, 1), (1, 0)]))
+        other_half = lax.ppermute(head_weight, "seq", [(0, 1), (1, 0)])
 
         spot = lax.iota(jnp.int32, slab_rows)
         row_id = ((spot // blk) ^ me) * blk + spot % blk
         alive = lax.iota(jnp.int32, teach_rows) < counts[0]
         member = (owner[None, :] == row_id[:, None]) & alive[None, :]
         parts = project(member.astype(jnp.bfloat16), teacher_rows, proj_weight, vocab_size, 512 if student_hidden.shape[1] % 512 == 0 else student_hidden.shape[1])
-        projected_own, line = reduce_blocks(parts)
+        staged = []
+
+        def stage_after(block):
+            staged.append(stage((head_weight, tie(other_half, block))))
+            return staged[0]
+
+        projected_own, line = reduce_blocks(parts, stage_after)
+        head = staged[0]
         hidden = spread(tie(turned(student_hidden), parts[-1]), line)
         projected = spread(turned(projected_own.astype(jnp.bfloat16)), line)
 
         column = (in_order(targets) - me * vocab_dev)[:, None]
-        logit_stud, scaled_stud, stats_stud, head = student_logits(as_pieces(hidden), heads, column, 256, chunk)
+        logit_stud, scaled_stud, stats_stud = student_logits(as_pieces(hidden), head, column, 512, chunk)
         scaled_teach, stats = teacher_logits(as_pieces(projected), head, logit_stud, stats_stud, 512, chunk)
-        tables = [stats] + [
-            lax.ppermute(stats, "vocab", [(at, at ^ mask) for at in range(vocab_size)])
-            for mask in range(1, vocab_size)
-        ]
+        tables = [stats]
+        for mask in range(1, vocab_size):
+            far, near = mask & ~3, mask & 3
+            source, hop = (tables[far], near) if near else (stats, far)
+            tables.append(lax.ppermute(source, "vocab", [(at, at ^ hop) for at in range(vocab_size)]))
         loss, *terms = gradient(place, tables, scaled_teach, scaled_stud, column, head, bits, chunk)
         return (loss[0], turned(reduce_blocks(terms)[0].astype(jnp.bfloat16)))
 

time: 138 us -> 154 us (1.12)
  starting transfers between devices: 55.3 us -> 37.2 us
  waiting for transfers between devices: 39 us -> 57 us
  local copies, waits for them, and re-layouts: 4.35 us -> 16.3 us
  Pallas kernels: 32.5 us -> 36.7 us
    ppermute x28, waiting for transfers between devices: 37.4 us -> 53.4 us  [swap(): lax.ppermute(block, 'vocab', [(at, at ^ 1 << bit) for at in range(vocab_s...]
    ppermute x28, starting transfers between devices: 43.6 us -> 27.9 us  [swap(): lax.ppermute(block, 'vocab', [(at, at ^ 1 << bit) for at in range(vocab_s...]
    unnamed x6 -> x10, local copies, waits for them, and re-layouts: 3.48 us -> 15.5 us
    pallas_call x0 -> x1, Pallas kernels: none -> 5.9 us  [stage(): pl.pallas_call(stage_kernel, in_specs=[in_place] * 2, out_specs=in_vmem,...]
    ppermute x8, starting transfers between devices: 11.7 us -> 9.27 us  [the longest x7 8.76 us: body(): lax.ppermute(source, 'vocab', [(at, at ^ hop) for at in range(vocab_size)])]
    ppermute x8, waiting for transfers between devices: 1.57 us -> 3.59 us  [the longest x7 3.59 us: body(): lax.ppermute(source, 'vocab', [(at, at ^ hop) for at in range(vocab_size)])]
    pallas_call x1, Pallas kernels: 11.9 us -> 10.1 us  [student_logits(): pl.pallas_call(functools.partial(student_kernel, len(pieces), step, chunk...]
  transfers between devices with their start and end apart: 36 -> 36, of which waited for: 17 -> 17; matrix products, arithmetic and copies ran while one was open for 4% -> 3% of each run, Pallas kernels for 12% -> 14%
where the time goes in v8:
time: 154 us
  waiting for transfers between devices  57 us (37%)
  starting transfers between devices  37.2 us (24%)
  Pallas kernels  36.7 us (24%)
  local copies, waits for them, and re-layouts  16.3 us (11%)
  other arithmetic  4.94 us (3%)
  between operations  1.57 us (1%)
    ppermute x28, waiting for transfers between devices, swap(): lax.ppermute(block, 'vocab', [(at, at ^ 1 << bit) for at in range(vocab_s...  53.4 us
    ppermute x28, starting transfers between devices, swap(): lax.ppermute(block, 'vocab', [(at, at ^ 1 << bit) for at in range(vocab_s...  27.9 us
    unnamed x10, local copies, waits for them, and re-layouts  15.5 us
    pallas_call x1, Pallas kernels, student_logits(): pl.pallas_call(functools.partial(student_kernel, len(pieces), step, chunk...  10.1 us
    ppermute x7, starting transfers between devices, body(): lax.ppermute(source, 'vocab', [(at, at ^ hop) for at in range(vocab_size)])  8.76 us
    pallas_call x1, Pallas kernels, gradient(): pl.pallas_call(functools.partial(gradient_kernel, bits, step, chunk), in_...  8.34 us
    pallas_call x1, Pallas kernels, teacher_logits(): pl.pallas_call(functools.partial(teacher_kernel, len(pieces), step, chunk...  7.53 us
    pallas_call x1, Pallas kernels, stage(): pl.pallas_call(stage_kernel, in_specs=[in_place] * 2, out_specs=in_vmem,...  5.9 us
  transfers between devices with their start and end apart: 36, of which 17 were waited for; matrix products, arithmetic and copies ran while one was open for 3% of the time, Pallas kernels for 14%

profile of v8, /device:TPU:0, one launch (start us, length us, event | category | flops | bytes accessed | tf_op | source)
XLA Modules:
  0.0 153.7 jit_solution(17728498780286836149)
XLA Ops:
  0.6 0.5 collective-permute-start.4
  1.8 0.8 and_convert_fusion.member_ref
  2.7 4.8 %shard_map.86 = (f32[32,3584]{1,0:T(8,128)S(1)}, f32[32,3584]{1,0:T(8,128)S(1)}, f32[32,3584]{1,0:T(8,128)S(1)}, f32[32,3584]{1,0:T(8,128)S(1)}, f32[32,3584]{1,...) custom-call(bf16[256,512]{1,0:T(8,128)(2,1)S(1)} %and_convert_fusion.member_ref, ...), custom_call_target="tpu_custom_call" | custom-call | flops 2147483648 | bytes 12058624 | tf_op jit(solution)/shard_map/pallas_call | solution.py:55
  7.5 0.7 convert_element_type.98
  8.2 2.6 %collective-permute-start.2 = (f16[32,3584]{1,0:T(8,128)(2,1)}, f16[32,3584]{1,0:T(8,128)(2,1)}, u32[]{:S(2)}, u32[]{:S(2)}) collective-permute-start(f16[32,3584]{1,0:T(8,128)(2,1)} %convert_element_type.98), channel_id=1, source_target_pairs={{0,1},{1,0},{2,3},{3,2},{4,5},{5,4},{6,7},{7,6},{8,9},{9,8},{10,11... | collective-permute-start | bytes 688136 | tf_op jit(solution)/shard_map/ppermute | solution.py:323
  10.8 0.7 convert_element_type.94
  11.5 10.6 %collective-permute-done = f16[32,3584]{1,0:T(8,128)(2,1)S(1)} collective-permute-done((f16[32,3584]{1,0:T(8,128)(2,1)}, f16[32,3584]{1,0:T(8,128)(2,1)S(1)}, u32[]{:S(2)}, u32[]{:S(2)}) %collective-permute-start) | collective-permute-done | bytes 229408 | tf_op jit(solution)/shard_map/ppermute | solution.py:323
  22.2 1.9 %collective-permute-start.1 = (f16[32,3584]{1,0:T(8,128)(2,1)S(1)}, f16[32,3584]{1,0:T(8,128)(2,1)S(1)}, u32[]{:S(2)}, u32[]{:S(2)}) collective-permute-start(f16[32,3584]{1,0:T(8,128)(2,1)S(1)} %add_convert_fusion.7), channel_id=1, source_target_pairs={{0,2},{1,3},{2,0},{3,1},{4,6},{5,7},{6,4},{7,5},{8,10},{9,11},{10,... | collective-permute-start | bytes 688136 | tf_op jit(solution)/shard_map/ppermute | solution.py:323
  24.1 0.3 collective-permute-start.8
  24.4 2.8 %collective-permute-start.12 = (bf16[32,3584]{1,0:T(8,128)(2,1)S(1)}, bf16[32,3584]{1,0:T(8,128)(2,1)S(1)}, u32[]{:S(2)}, u32[]{:S(2)}) collective-permute-start(bf16[32,3584]{1,0:T(8,128)(2,1)S(1)} %maximum_select_fusion.1.refs_0_), channel_id=1, source_target_pairs={{0,4},{1,5},{2,6},{3,7},{4,0},{5,1},{6,2},{7,3},{8,12},{9,13},{10,... | collective-permute-start | bytes 688136 | tf_op jit(solution)/shard_map/ppermute | solution.py:323
  27.3 1.6 %collective-permute-start.7 = (f16[32,3584]{1,0:T(8,128)(2,1)S(1)}, f16[32,3584]{1,0:T(8,128)(2,1)S(1)}, u32[]{:S(2)}, u32[]{:S(2)}) collective-permute-start(f16[32,3584]{1,0:T(8,128)(2,1)S(1)} %convert_element_type.106), channel_id=1, source_target_pairs={{0,1},{1,0},{2,3},{3,2},{4,5},{5,4},{6,7},{7,6},{8,9},{9,8},{10,11... | collective-permute-start | bytes 688136 | tf_op jit(solution)/shard_map/ppermute | solution.py:323
  28.9 3.5 %copy-done.2 = bf16[1792,2432]{1,0:T(8,128)(2,1)S(1)} copy-done((bf16[1792,2432]{1,0:T(8,128)(2,1)S(1)}, bf16[1792,2432]{1,0:T(8,128)(2,1)}, u32[]{:S(2)}) %copy-start.2) | copy-done | bytes 8716312
  32.4 5.9 %shard_map.87.refs_8_.refs_11_ = bf16[3584,2432]{1,0:T(8,128)(2,1)S(1)} custom-call(bf16[1792,2432]{1,0:T(8,128)(2,1)S(1)} %copy-done.2, bf16[1792,2432]{1,0:T(8,128)(2,1)} %collective-permute-done.4.second_ref), custom_call_target="tpu_custom_call" | custom-call | bytes 34865152 | tf_op jit(solution)/shard_map/pallas_call | solution.py:114
  38.3 6.0 %copy-done = bf16[3584,2432]{1,0:T(8,128)(2,1)} copy-done((bf16[3584,2432]{1,0:T(8,128)(2,1)}, bf16[3584,2432]{1,0:T(8,128)(2,1)S(1)}, u32[]{:S(2)}) %copy-start) | copy-done | bytes 17432600
  44.3 0.5 collective-permute-start.5
  44.8 1.0 add_convert_fusion.6
  45.8 0.2 collective-permute-start.3
  46.0 4.4 %collective-permute-done.5 = f16[32,3584]{1,0:T(8,128)(2,1)S(1)} collective-permute-done((f16[32,3584]{1,0:T(8,128)(2,1)S(1)}, f16[32,3584]{1,0:T(8,128)(2,1)S(1)}, u32[]{:S(2)}, u32[]{:S(2)}) %collective-permute-start.5) | collective-permute-done | bytes 229408 | tf_op jit(solution)/shard_map/ppermute | solution.py:323
  50.4 1.6 %collective-permute-start.6 = (f16[32,3584]{1,0:T(8,128)(2,1)S(1)}, f16[32,3584]{1,0:T(8,128)(2,1)S(1)}, u32[]{:S(2)}, u32[]{:S(2)}) collective-permute-start(f16[32,3584]{1,0:T(8,128)(2,1)S(1)} %add_convert_fusion.5), channel_id=1, source_target_pairs={{0,2},{1,3},{2,0},{3,1},{4,6},{5,7},{6,4},{7,5},{8,10},{9,11},{10,... | collective-permute-start | bytes 688136 | tf_op jit(solution)/shard_map/ppermute | solution.py:323
  52.1 0.5 collective-permute-start.17
  52.6 0.4 collective-permute-start.16
  53.0 1.5 collective-permute-start.9
  54.6 3.0 %collective-permute-done.3 = f16[32,3584]{1,0:T(8,128)(2,1)S(1)} collective-permute-done((f16[32,3584]{1,0:T(8,128)(2,1)S(1)}, f16[32,3584]{1,0:T(8,128)(2,1)S(1)}, u32[]{:S(2)}, u32[]{:S(2)}) %collective-permute-start.3) | collective-permute-done | bytes 229408 | tf_op jit(solution)/shard_map/ppermute | solution.py:323
  57.6 5.5 %collective-permute-done.6 = f16[32,3584]{1,0:T(8,128)(2,1)S(1)} collective-permute-done((f16[32,3584]{1,0:T(8,128)(2,1)S(1)}, f16[32,3584]{1,0:T(8,128)(2,1)S(1)}, u32[]{:S(2)}, u32[]{:S(2)}) %collective-permute-start.6) | collective-permute-done | bytes 229408 | tf_op jit(solution)/shard_map/ppermute | solution.py:323
  63.5 0.3 collective-permute-start.13
  63.8 2.7 %collective-permute-done.16.refs_6_ = bf16[32,3584]{1,0:T(8,128)(2,1)S(1)} collective-permute-done((bf16[32,3584]{1,0:T(8,128)(2,1)S(1)}, bf16[32,3584]{1,0:T(8,128)(2,1)S(1)}, u32[]{:S(2)}, u32[]{:S(2)}) %collective-permute-start.16) | collective-permute-done | bytes 229408 | tf_op jit(solution)/shard_map/ppermute | solution.py:323
  66.5 0.5 collective-permute-start.18
  67.1 0.5 collective-permute-start.11
  67.5 1.0 collective-permute-start.10
  68.6 3.5 %collective-permute-done.15.refs_4_ = bf16[32,3584]{1,0:T(8,128)(2,1)S(1)} collective-permute-done((bf16[32,3584]{1,0:T(8,128)(2,1)S(1)}, bf16[32,3584]{1,0:T(8,128)(2,1)S(1)}, u32[]{:S(2)}, u32[]{:S(2)}) %collective-permute-start.15) | collective-permute-done | bytes 229408 | tf_op jit(solution)/shard_map/ppermute | solution.py:323
  72.1 0.1 sub.26.refs_9_.refs_10_
  72.3 4.4 %collective-permute-done.11.refs_2_ = bf16[32,3584]{1,0:T(8,128)(2,1)S(1)} collective-permute-done((bf16[32,3584]{1,0:T(8,128)(2,1)S(1)}, bf16[32,3584]{1,0:T(8,128)(2,1)S(1)}, u32[]{:S(2)}, u32[]{:S(2)}) %collective-permute-start.11) | collective-permute-done | bytes 229408 | tf_op jit(solution)/shard_map/ppermute | solution.py:323
  76.7 0.8 collective-permute-start.14
  77.5 1.2 collective-permute-start.19
  78.7 3.2 %collective-permute-done.10.refs_1_ = bf16[32,3584]{1,0:T(8,128)(2,1)S(1)} collective-permute-done((bf16[32,3584]{1,0:T(8,128)(2,1)S(1)}, bf16[32,3584]{1,0:T(8,128)(2,1)S(1)}, u32[]{:S(2)}, u32[]{:S(2)}) %collective-permute-start.10) | collective-permute-done | bytes 229408 | tf_op jit(solution)/shard_map/ppermute | solution.py:323
  81.9 0.2 collective-permute-start.21
  82.1 6.0 %copy-done.1 = bf16[3584,2432]{1,0:T(8,128)(2,1)S(1)} copy-done((bf16[3584,2432]{1,0:T(8,128)(2,1)S(1)}, bf16[3584,2432]{1,0:T(8,128)(2,1)}, u32[]{:S(2)}) %copy-start.1) | copy-done | bytes 17432600
  88.1 10.1 %shard_map.88 = (f32[256,2432]{1,0:T(8,128)S(1)}, f32[256,2432]{1,0:T(8,128)S(1)}, f32[8,256]{1,0:T(8,128)S(1)}) custom-call(bf16[32,3584]{1,0:T(8,128)(2,1)S(1)} %maximum_select_fusion.1.refs_0_, bf16[32,3584]{1,0:T(8,128)(2,1)S(1)} %collective-permute-done.17.refs_1_, bf16[32,3584]{1,0:T(8,128)(2,1)S(1)} %collective-permute-done.8.refs_2_, ...), custom_call_target="tpu_custom_call" | custom-call | flops 4462739456 | bytes 24903680 | tf_op jit(solution)/shard_map/pallas_call | solution.py:194
  98.3 7.5 %shard_map.89 = (f32[256,2432]{1,0:T(8,128)S(1)}, f32[8,256]{1,0:T(8,128)S(1)}) custom-call(bf16[32,3584]{1,0:T(8,128)(2,1)S(1)} %maximum_select_fusion.refs_0_, bf16[32,3584]{1,0:T(8,128)(2,1)S(1)} %collective-permute-done.10.refs_1_, bf16[32,3584]{1,0:T(8,128)(2,1)S(1)} %collective-permute-done.11.refs_2_, ...), custom_call_target="tpu_custom_call" | custom-call | flops 4462739456 | bytes 24903680 | tf_op jit(solution)/shard_map/pallas_call | solution.py:216
  105.8 1.8 %collective-permute-start.25 = (f32[8,256]{1,0:T(8,128)S(1)}, f32[8,256]{1,0:T(8,128)S(1)}, u32[]{:S(2)}, u32[]{:S(2)}) collective-permute-start(f32[8,256]{1,0:T(8,128)S(1)} %get-tuple-element.62.refs_0_), channel_id=1, source_target_pairs={{0,4},{1,5},{2,6},{3,7},{4,0},{5,1},{6,2},{7,3},{8,12},{9,13},{10,... | collective-permute-start | bytes 24584 | tf_op jit(solution)/shard_map/ppermute | solution.py:402
  107.6 0.1 collective-permute-start.22
  107.7 2.5 %collective-permute-start.23 = (f32[8,256]{1,0:T(8,128)S(1)}, f32[8,256]{1,0:T(8,128)S(1)}, u32[]{:S(2)}, u32[]{:S(2)}) collective-permute-start(f32[8,256]{1,0:T(8,128)S(1)} %get-tuple-element.62.refs_0_), channel_id=1, source_target_pairs={{0,2},{1,3},{2,0},{3,1},{4,6},{5,7},{6,4},{7,5},{8,10},{9,11},{10,... | collective-permute-start | bytes 24584 | tf_op jit(solution)/shard_map/ppermute | solution.py:402
  110.2 0.9 collective-permute-start.24
  111.1 1.1 collective-permute-start.26
  112.2 1.5 collective-permute-start.27
  113.7 0.9 collective-permute-start.28
  114.6 0.2 collective-permute-done.24.refs_3_
  114.8 1.0 collective-permute-done.27.refs_6_
  115.8 2.4 %collective-permute-done.28.refs_7_ = f32[8,256]{1,0:T(8,128)S(1)} collective-permute-done((f32[8,256]{1,0:T(8,128)S(1)}, f32[8,256]{1,0:T(8,128)S(1)}, u32[]{:S(2)}, u32[]{:S(2)}) %collective-permute-start.28) | collective-permute-done | bytes 8224 | tf_op jit(solution)/shard_map/ppermute | solution.py:402
  118.2 8.3 %shard_map.90 = (f32[8,256]{1,0:T(8,128)S(1)}, f32[32,3584]{1,0:T(8,128)S(1)}, f32[32,3584]{1,0:T(8,128)S(1)}, f32[32,3584]{1,0:T(8,128)S(1)}, f32[32,3584]{1,0:...) custom-call(s32[2]{0:T(128)S(1)} %pad_add_fusion.place_ref, ...), custom_call_target="tpu_custom_call" | custom-call | flops 4462739456 | bytes 24903680 | tf_op jit(solution)/shard_map/pallas_call | solution.py:298
  126.7 2.1 %collective-permute-start.29 = (f16[32,3584]{1,0:T(8,128)(2,1)S(1)}, f16[32,3584]{1,0:T(8,128)(2,1)S(1)}, u32[]{:S(2)}, u32[]{:S(2)}) collective-permute-start(f16[32,3584]{1,0:T(8,128)(2,1)S(1)} %convert_element_type.109), channel_id=1, source_target_pairs={{0,1},{1,0},{2,3},{3,2},{4,5},{5,4},{6,7},{7,6},{8,9},{9,8},{10,11... | collective-permute-start | bytes 688136 | tf_op jit(solution)/shard_map/ppermute | solution.py:323
  128.8 4.3 %collective-permute-done.31 = f16[32,3584]{1,0:T(8,128)(2,1)S(1)} collective-permute-done((f16[32,3584]{1,0:T(8,128)(2,1)S(1)}, f16[32,3584]{1,0:T(8,128)(2,1)S(1)}, u32[]{:S(2)}, u32[]{:S(2)}) %collective-permute-start.31) | collective-permute-done | bytes 229408 | tf_op jit(solution)/shard_map/ppermute | solution.py:323
  133.2 1.2 collective-permute-start.35
  134.3 1.3 collective-permute-done.29
  135.6 1.2 collective-permute-start.33
  136.9 1.8 %collective-permute-start.30 = (f16[32,3584]{1,0:T(8,128)(2,1)S(1)}, f16[32,3584]{1,0:T(8,128)(2,1)S(1)}, u32[]{:S(2)}, u32[]{:S(2)}) collective-permute-start(f16[32,3584]{1,0:T(8,128)(2,1)S(1)} %add_convert_fusion.3), channel_id=1, source_target_pairs={{0,2},{1,3},{2,0},{3,1},{4,6},{5,7},{6,4},{7,5},{8,10},{9,11},{10,... | collective-permute-start | bytes 688136 | tf_op jit(solution)/shard_map/ppermute | solution.py:323
  138.7 3.0 %collective-permute-done.33 = f16[32,3584]{1,0:T(8,128)(2,1)S(1)} collective-permute-done((f16[32,3584]{1,0:T(8,128)(2,1)S(1)}, f16[32,3584]{1,0:T(8,128)(2,1)S(1)}, u32[]{:S(2)}, u32[]{:S(2)}) %collective-permute-start.33) | collective-permute-done | bytes 229408 | tf_op jit(solution)/shard_map/ppermute | solution.py:323
  141.7 1.2 collective-permute-start.34
  142.9 0.4 collective-permute-done.30
  143.4 1.8 %collective-permute-start.32 = (f16[32,3584]{1,0:T(8,128)(2,1)S(1)}, f16[32,3584]{1,0:T(8,128)(2,1)S(1)}, u32[]{:S(2)}, u32[]{:S(2)}) collective-permute-start(f16[32,3584]{1,0:T(8,128)(2,1)S(1)} %add_convert_fusion.2), channel_id=1, source_target_pairs={{0,4},{1,5},{2,6},{3,7},{4,0},{5,1},{6,2},{7,3},{8,12},{9,13},{10,... | collective-permute-start | bytes 688136 | tf_op jit(solution)/shard_map/ppermute | solution.py:323
  145.2 0.6 slice.27
  145.8 2.0 %collective-permute-done.34 = f16[32,3584]{1,0:T(8,128)(2,1)S(1)} collective-permute-done((f16[32,3584]{1,0:T(8,128)(2,1)S(1)}, f16[32,3584]{1,0:T(8,128)(2,1)S(1)}, u32[]{:S(2)}, u32[]{:S(2)}) %collective-permute-start.34) | collective-permute-done | bytes 229408 | tf_op jit(solution)/shard_map/ppermute | solution.py:323
  147.8 5.1 %collective-permute-done.32 = f16[32,3584]{1,0:T(8,128)(2,1)S(1)} collective-permute-done((f16[32,3584]{1,0:T(8,128)(2,1)S(1)}, f16[32,3584]{1,0:T(8,128)(2,1)S(1)}, u32[]{:S(2)}, u32[]{:S(2)}) %collective-permute-start.32) | collective-permute-done | bytes 229408 | tf_op jit(solution)/shard_map/ppermute | solution.py:323
  153.0 0.8 maximum_select_fusion.2
  (56 shorter events, 1.3 us)
Async XLA Ops:
  0.6 10.9 %copy-start.3 = (bf16[32,3584]{1,0:T(8,128)(2,1)S(1)}, bf16[32,3584]{1,0:T(8,128)(2,1)}, u32[]{:S(2)}) copy-start(bf16[32,3584]{1,0:T(8,128)(2,1)} %param.11) | copy-start | bytes 688132
  0.6 28.3 %collective-permute-start.4 = (bf16[1792,2432]{1,0:T(8,128)(2,1)}, bf16[1792,2432]{1,0:T(8,128)(2,1)}, u32[]{:S(2)}, u32[]{:S(2)}) collective-permute-start(bf16[1792,2432]{1,0:T(8,128)(2,1)} %first_ref.1), channel_id=1, source_target_pairs={{0,8},{8,0},{1,9},{9,1},{2,10},{10,2},{3,11},{11,3},{4,12},{12,4},... | collective-permute-start | bytes 26148872 | tf_op jit(solution)/shard_map/ppermute | solution.py:377
  8.2 19.1 %collective-permute-start.2 = (f16[32,3584]{1,0:T(8,128)(2,1)}, f16[32,3584]{1,0:T(8,128)(2,1)}, u32[]{:S(2)}, u32[]{:S(2)}) collective-permute-start(f16[32,3584]{1,0:T(8,128)(2,1)} %convert_element_type.98), channel_id=1, source_target_pairs={{0,1},{1,0},{2,3},{3,2},{4,5},{5,4},{6,7},{7,6},{8,9},{9,8},{10,11... | collective-permute-start | bytes 688136 | tf_op jit(solution)/shard_map/ppermute | solution.py:323
  11.5 10.6 %collective-permute-start = (f16[32,3584]{1,0:T(8,128)(2,1)}, f16[32,3584]{1,0:T(8,128)(2,1)S(1)}, u32[]{:S(2)}, u32[]{:S(2)}) collective-permute-start(f16[32,3584]{1,0:T(8,128)(2,1)} %convert_element_type.94), channel_id=1, source_target_pairs={{0,1},{1,0},{2,3},{3,2},{4,5},{5,4},{6,7},{7,6},{8,9},{9,8},{10,11... | collective-permute-start | bytes 688136 | tf_op jit(solution)/shard_map/ppermute | solution.py:323
  22.2 22.6 %collective-permute-start.1 = (f16[32,3584]{1,0:T(8,128)(2,1)S(1)}, f16[32,3584]{1,0:T(8,128)(2,1)S(1)}, u32[]{:S(2)}, u32[]{:S(2)}) collective-permute-start(f16[32,3584]{1,0:T(8,128)(2,1)S(1)} %add_convert_fusion.7), channel_id=1, source_target_pairs={{0,2},{1,3},{2,0},{3,1},{4,6},{5,7},{6,4},{7,5},{8,10},{9,11},{10,... | collective-permute-start | bytes 688136 | tf_op jit(solution)/shard_map/ppermute | solution.py:323
  24.1 28.0 %collective-permute-start.8 = (bf16[32,3584]{1,0:T(8,128)(2,1)S(1)}, bf16[32,3584]{1,0:T(8,128)(2,1)S(1)}, u32[]{:S(2)}, u32[]{:S(2)}) collective-permute-start(bf16[32,3584]{1,0:T(8,128)(2,1)S(1)} %maximum_select_fusion.1.refs_0_), channel_id=1, source_target_pairs={{0,2},{1,3},{2,0},{3,1},{4,6},{5,7},{6,4},{7,5},{8,10},{9,11},{10,... | collective-permute-start | bytes 688136 | tf_op jit(solution)/shard_map/ppermute | solution.py:323
  24.4 28.2 %collective-permute-start.12 = (bf16[32,3584]{1,0:T(8,128)(2,1)S(1)}, bf16[32,3584]{1,0:T(8,128)(2,1)S(1)}, u32[]{:S(2)}, u32[]{:S(2)}) collective-permute-start(bf16[32,3584]{1,0:T(8,128)(2,1)S(1)} %maximum_select_fusion.1.refs_0_), channel_id=1, source_target_pairs={{0,4},{1,5},{2,6},{3,7},{4,0},{5,1},{6,2},{7,3},{8,12},{9,13},{10,... | collective-permute-start | bytes 688136 | tf_op jit(solution)/shard_map/ppermute | solution.py:323
  27.3 36.1 %copy-start.4 = (s32[256]{0:T(256)S(1)}, s32[256]{0:T(256)}, u32[]{:S(2)}) copy-start(s32[256]{0:T(256)} %param.13) | copy-start | bytes 3076
  27.3 25.7 %collective-permute-start.7 = (f16[32,3584]{1,0:T(8,128)(2,1)S(1)}, f16[32,3584]{1,0:T(8,128)(2,1)S(1)}, u32[]{:S(2)}, u32[]{:S(2)}) collective-permute-start(f16[32,3584]{1,0:T(8,128)(2,1)S(1)} %convert_element_type.106), channel_id=1, source_target_pairs={{0,1},{1,0},{2,3},{3,2},{4,5},{5,4},{6,7},{7,6},{8,9},{9,8},{10,11... | collective-permute-start | bytes 688136 | tf_op jit(solution)/shard_map/ppermute | solution.py:323
  28.9 3.5 %copy-start.2 = (bf16[1792,2432]{1,0:T(8,128)(2,1)S(1)}, bf16[1792,2432]{1,0:T(8,128)(2,1)}, u32[]{:S(2)}) copy-start(bf16[1792,2432]{1,0:T(8,128)(2,1)} %first_ref.1) | copy-start | bytes 26148868
  38.3 6.0 %copy-start = (bf16[3584,2432]{1,0:T(8,128)(2,1)}, bf16[3584,2432]{1,0:T(8,128)(2,1)S(1)}, u32[]{:S(2)}) copy-start(bf16[3584,2432]{1,0:T(8,128)(2,1)S(1)} %shard_map.87.refs_8_.refs_11_) | copy-start | bytes 52297732
  44.3 6.1 %collective-permute-start.5 = (f16[32,3584]{1,0:T(8,128)(2,1)S(1)}, f16[32,3584]{1,0:T(8,128)(2,1)S(1)}, u32[]{:S(2)}, u32[]{:S(2)}) collective-permute-start(f16[32,3584]{1,0:T(8,128)(2,1)S(1)} %convert_element_type.102), channel_id=1, source_target_pairs={{0,1},{1,0},{2,3},{3,2},{4,5},{5,4},{6,7},{7,6},{8,9},{9,8},{10,11... | collective-permute-start | bytes 688136 | tf_op jit(solution)/shard_map/ppermute | solution.py:323
  45.8 11.7 %collective-permute-start.3 = (f16[32,3584]{1,0:T(8,128)(2,1)S(1)}, f16[32,3584]{1,0:T(8,128)(2,1)S(1)}, u32[]{:S(2)}, u32[]{:S(2)}) collective-permute-start(f16[32,3584]{1,0:T(8,128)(2,1)S(1)} %add_convert_fusion.6), channel_id=1, source_target_pairs={{0,4},{1,5},{2,6},{3,7},{4,0},{5,1},{6,2},{7,3},{8,12},{9,13},{10,... | collective-permute-start | bytes 688136 | tf_op jit(solution)/shard_map/ppermute | solution.py:323
  50.4 12.7 %collective-permute-start.6 = (f16[32,3584]{1,0:T(8,128)(2,1)S(1)}, f16[32,3584]{1,0:T(8,128)(2,1)S(1)}, u32[]{:S(2)}, u32[]{:S(2)}) collective-permute-start(f16[32,3584]{1,0:T(8,128)(2,1)S(1)} %add_convert_fusion.5), channel_id=1, source_target_pairs={{0,2},{1,3},{2,0},{3,1},{4,6},{5,7},{6,4},{7,5},{8,10},{9,11},{10,... | collective-permute-start | bytes 688136 | tf_op jit(solution)/shard_map/ppermute | solution.py:323
  52.1 14.5 %collective-permute-start.17 = (bf16[32,3584]{1,0:T(8,128)(2,1)S(1)}, bf16[32,3584]{1,0:T(8,128)(2,1)S(1)}, u32[]{:S(2)}, u32[]{:S(2)}) collective-permute-start(bf16[32,3584]{1,0:T(8,128)(2,1)S(1)} %maximum_select_fusion.1.refs_0_), channel_id=1, source_target_pairs={{0,1},{1,0},{2,3},{3,2},{4,5},{5,4},{6,7},{7,6},{8,9},{9,8},{10,11... | collective-permute-start | bytes 688136 | tf_op jit(solution)/shard_map/ppermute | solution.py:323
  52.6 14.0 %collective-permute-start.16 = (bf16[32,3584]{1,0:T(8,128)(2,1)S(1)}, bf16[32,3584]{1,0:T(8,128)(2,1)S(1)}, u32[]{:S(2)}, u32[]{:S(2)}) collective-permute-start(bf16[32,3584]{1,0:T(8,128)(2,1)S(1)} %collective-permute-done.12.refs_4_), channel_id=1, source_target_pairs={{0,2},{1,3},{2,0},{3,1},{4,6},{5,7},{6,4},{7,5},{8,10},{9,11},{10,... | collective-permute-start | bytes 688136 | tf_op jit(solution)/shard_map/ppermute | solution.py:323
  53.0 14.5 %collective-permute-start.9 = (bf16[32,3584]{1,0:T(8,128)(2,1)S(1)}, bf16[32,3584]{1,0:T(8,128)(2,1)S(1)}, u32[]{:S(2)}, u32[]{:S(2)}) collective-permute-start(bf16[32,3584]{1,0:T(8,128)(2,1)S(1)} %collective-permute-done.8.refs_2_), channel_id=1, source_target_pairs={{0,1},{1,0},{2,3},{3,2},{4,5},{5,4},{6,7},{7,6},{8,9},{9,8},{10,11... | collective-permute-start | bytes 688136 | tf_op jit(solution)/shard_map/ppermute | solution.py:323
  63.3 8.8 %collective-permute-start.15 = (bf16[32,3584]{1,0:T(8,128)(2,1)S(1)}, bf16[32,3584]{1,0:T(8,128)(2,1)S(1)}, u32[]{:S(2)}, u32[]{:S(2)}) collective-permute-start(bf16[32,3584]{1,0:T(8,128)(2,1)S(1)} %maximum_select_fusion.refs_0_), channel_id=1, source_target_pairs={{0,4},{1,5},{2,6},{3,7},{4,0},{5,1},{6,2},{7,3},{8,12},{9,13},{10,... | collective-permute-start | bytes 688136 | tf_op jit(solution)/shard_map/ppermute | solution.py:323
  63.5 8.7 %collective-permute-start.13 = (bf16[32,3584]{1,0:T(8,128)(2,1)S(1)}, bf16[32,3584]{1,0:T(8,128)(2,1)S(1)}, u32[]{:S(2)}, u32[]{:S(2)}) collective-permute-start(bf16[32,3584]{1,0:T(8,128)(2,1)S(1)} %collective-permute-done.12.refs_4_), channel_id=1, source_target_pairs={{0,1},{1,0},{2,3},{3,2},{4,5},{5,4},{6,7},{7,6},{8,9},{9,8},{10,11... | collective-permute-start | bytes 688136 | tf_op jit(solution)/shard_map/ppermute | solution.py:323
  66.5 10.9 %collective-permute-start.18 = (bf16[32,3584]{1,0:T(8,128)(2,1)S(1)}, bf16[32,3584]{1,0:T(8,128)(2,1)S(1)}, u32[]{:S(2)}, u32[]{:S(2)}) collective-permute-start(bf16[32,3584]{1,0:T(8,128)(2,1)S(1)} %collective-permute-done.16.refs_6_), channel_id=1, source_target_pairs={{0,1},{1,0},{2,3},{3,2},{4,5},{5,4},{6,7},{7,6},{8,9},{9,8},{10,11... | collective-permute-start | bytes 688136 | tf_op jit(solution)/shard_map/ppermute | solution.py:323
  67.1 9.6 %collective-permute-start.11 = (bf16[32,3584]{1,0:T(8,128)(2,1)S(1)}, bf16[32,3584]{1,0:T(8,128)(2,1)S(1)}, u32[]{:S(2)}, u32[]{:S(2)}) collective-permute-start(bf16[32,3584]{1,0:T(8,128)(2,1)S(1)} %maximum_select_fusion.refs_0_), channel_id=1, source_target_pairs={{0,2},{1,3},{2,0},{3,1},{4,6},{5,7},{6,4},{7,5},{8,10},{9,11},{10,... | collective-permute-start | bytes 688136 | tf_op jit(solution)/shard_map/ppermute | solution.py:323
  67.5 14.4 %collective-permute-start.10 = (bf16[32,3584]{1,0:T(8,128)(2,1)S(1)}, bf16[32,3584]{1,0:T(8,128)(2,1)S(1)}, u32[]{:S(2)}, u32[]{:S(2)}) collective-permute-start(bf16[32,3584]{1,0:T(8,128)(2,1)S(1)} %maximum_select_fusion.refs_0_), channel_id=1, source_target_pairs={{0,1},{1,0},{2,3},{3,2},{4,5},{5,4},{6,7},{7,6},{8,9},{9,8},{10,11... | collective-permute-start | bytes 688136 | tf_op jit(solution)/shard_map/ppermute | solution.py:323
  72.1 9.8 %collective-permute-start.20 = (bf16[32,3584]{1,0:T(8,128)(2,1)S(1)}, bf16[32,3584]{1,0:T(8,128)(2,1)S(1)}, u32[]{:S(2)}, u32[]{:S(2)}) collective-permute-start(bf16[32,3584]{1,0:T(8,128)(2,1)S(1)} %collective-permute-done.15.refs_4_), channel_id=1, source_target_pairs={{0,2},{1,3},{2,0},{3,1},{4,6},{5,7},{6,4},{7,5},{8,10},{9,11},{10,... | collective-permute-start | bytes 688136 | tf_op jit(solution)/shard_map/ppermute | solution.py:323
  76.7 21.6 %collective-permute-start.14 = (bf16[32,3584]{1,0:T(8,128)(2,1)S(1)}, bf16[32,3584]{1,0:T(8,128)(2,1)S(1)}, u32[]{:S(2)}, u32[]{:S(2)}) collective-permute-start(bf16[32,3584]{1,0:T(8,128)(2,1)S(1)} %collective-permute-done.11.refs_2_), channel_id=1, source_target_pairs={{0,1},{1,0},{2,3},{3,2},{4,5},{5,4},{6,7},{7,6},{8,9},{9,8},{10,11... | collective-permute-start | bytes 688136 | tf_op jit(solution)/shard_map/ppermute | solution.py:323
  77.5 20.8 %collective-permute-start.19 = (bf16[32,3584]{1,0:T(8,128)(2,1)S(1)}, bf16[32,3584]{1,0:T(8,128)(2,1)S(1)}, u32[]{:S(2)}, u32[]{:S(2)}) collective-permute-start(bf16[32,3584]{1,0:T(8,128)(2,1)S(1)} %collective-permute-done.15.refs_4_), channel_id=1, source_target_pairs={{0,1},{1,0},{2,3},{3,2},{4,5},{5,4},{6,7},{7,6},{8,9},{9,8},{10,11... | collective-permute-start | bytes 688136 | tf_op jit(solution)/shard_map/ppermute | solution.py:323
  81.9 16.4 %collective-permute-start.21 = (bf16[32,3584]{1,0:T(8,128)(2,1)S(1)}, bf16[32,3584]{1,0:T(8,128)(2,1)S(1)}, u32[]{:S(2)}, u32[]{:S(2)}) collective-permute-start(bf16[32,3584]{1,0:T(8,128)(2,1)S(1)} %collective-permute-done.20.refs_6_), channel_id=1, source_target_pairs={{0,1},{1,0},{2,3},{3,2},{4,5},{5,4},{6,7},{7,6},{8,9},{9,8},{10,11... | collective-permute-start | bytes 688136 | tf_op jit(solution)/shard_map/ppermute | solution.py:323
  82.1 6.0 %copy-start.1 = (bf16[3584,2432]{1,0:T(8,128)(2,1)S(1)}, bf16[3584,2432]{1,0:T(8,128)(2,1)}, u32[]{:S(2)}) copy-start(bf16[3584,2432]{1,0:T(8,128)(2,1)} %copy-done) | copy-start | bytes 52297732
  105.8 5.3 %collective-permute-start.25 = (f32[8,256]{1,0:T(8,128)S(1)}, f32[8,256]{1,0:T(8,128)S(1)}, u32[]{:S(2)}, u32[]{:S(2)}) collective-permute-start(f32[8,256]{1,0:T(8,128)S(1)} %get-tuple-element.62.refs_0_), channel_id=1, source_target_pairs={{0,4},{1,5},{2,6},{3,7},{4,0},{5,1},{6,2},{7,3},{8,12},{9,13},{10,... | collective-permute-start | bytes 24584 | tf_op jit(solution)/shard_map/ppermute | solution.py:402
  107.6 6.1 %collective-permute-start.22 = (f32[8,256]{1,0:T(8,128)S(1)}, f32[8,256]{1,0:T(8,128)S(1)}, u32[]{:S(2)}, u32[]{:S(2)}) collective-permute-start(f32[8,256]{1,0:T(8,128)S(1)} %get-tuple-element.62.refs_0_), channel_id=1, source_target_pairs={{0,1},{1,0},{2,3},{3,2},{4,5},{5,4},{6,7},{7,6},{8,9},{9,8},{10,11... | collective-permute-start | bytes 24584 | tf_op jit(solution)/shard_map/ppermute | solution.py:402
  107.7 6.9 %collective-permute-start.23 = (f32[8,256]{1,0:T(8,128)S(1)}, f32[8,256]{1,0:T(8,128)S(1)}, u32[]{:S(2)}, u32[]{:S(2)}) collective-permute-start(f32[8,256]{1,0:T(8,128)S(1)} %get-tuple-element.62.refs_0_), channel_id=1, source_target_pairs={{0,2},{1,3},{2,0},{3,1},{4,6},{5,7},{6,4},{7,5},{8,10},{9,11},{10,... | collective-permute-start | bytes 24584 | tf_op jit(solution)/shard_map/ppermute | solution.py:402
  110.2 4.6 %collective-permute-start.24 = (f32[8,256]{1,0:T(8,128)S(1)}, f32[8,256]{1,0:T(8,128)S(1)}, u32[]{:S(2)}, u32[]{:S(2)}) collective-permute-start(f32[8,256]{1,0:T(8,128)S(1)} %get-tuple-element.62.refs_0_), channel_id=1, source_target_pairs={{0,3},{1,2},{2,1},{3,0},{4,7},{5,6},{6,5},{7,4},{8,11},{9,10},{10,... | collective-permute-start | bytes 24584 | tf_op jit(solution)/shard_map/ppermute | solution.py:402
  111.1 3.7 %collective-permute-start.26 = (f32[8,256]{1,0:T(8,128)S(1)}, f32[8,256]{1,0:T(8,128)S(1)}, u32[]{:S(2)}, u32[]{:S(2)}) collective-permute-start(f32[8,256]{1,0:T(8,128)S(1)} %collective-permute-done.25.refs_4_), channel_id=1, source_target_pairs={{0,1},{1,0},{2,3},{3,2},{4,5},{5,4},{6,7},{7,6},{8,9},{9,8},{10,11... | collective-permute-start | bytes 24584 | tf_op jit(solution)/shard_map/ppermute | solution.py:402
  112.2 3.7 %collective-permute-start.27 = (f32[8,256]{1,0:T(8,128)S(1)}, f32[8,256]{1,0:T(8,128)S(1)}, u32[]{:S(2)}, u32[]{:S(2)}) collective-permute-start(f32[8,256]{1,0:T(8,128)S(1)} %collective-permute-done.25.refs_4_), channel_id=1, source_target_pairs={{0,2},{1,3},{2,0},{3,1},{4,6},{5,7},{6,4},{7,5},{8,10},{9,11},{10,... | collective-permute-start | bytes 24584 | tf_op jit(solution)/shard_map/ppermute | solution.py:402
  113.7 4.6 %collective-permute-start.28 = (f32[8,256]{1,0:T(8,128)S(1)}, f32[8,256]{1,0:T(8,128)S(1)}, u32[]{:S(2)}, u32[]{:S(2)}) collective-permute-start(f32[8,256]{1,0:T(8,128)S(1)} %collective-permute-done.25.refs_4_), channel_id=1, source_target_pairs={{0,3},{1,2},{2,1},{3,0},{4,7},{5,6},{6,5},{7,4},{8,11},{9,10},{10,... | collective-permute-start | bytes 24584 | tf_op jit(solution)/shard_map/ppermute | solution.py:402
  126.6 6.6 %collective-permute-start.31 = (f16[32,3584]{1,0:T(8,128)(2,1)S(1)}, f16[32,3584]{1,0:T(8,128)(2,1)S(1)}, u32[]{:S(2)}, u32[]{:S(2)}) collective-permute-start(f16[32,3584]{1,0:T(8,128)(2,1)S(1)} %convert_element_type.113), channel_id=1, source_target_pairs={{0,1},{1,0},{2,3},{3,2},{4,5},{5,4},{6,7},{7,6},{8,9},{9,8},{10,11... | collective-permute-start | bytes 688136 | tf_op jit(solution)/shard_map/ppermute | solution.py:323
  126.7 8.9 %collective-permute-start.29 = (f16[32,3584]{1,0:T(8,128)(2,1)S(1)}, f16[32,3584]{1,0:T(8,128)(2,1)S(1)}, u32[]{:S(2)}, u32[]{:S(2)}) collective-permute-start(f16[32,3584]{1,0:T(8,128)(2,1)S(1)} %convert_element_type.109), channel_id=1, source_target_pairs={{0,1},{1,0},{2,3},{3,2},{4,5},{5,4},{6,7},{7,6},{8,9},{9,8},{10,11... | collective-permute-start | bytes 688136 | tf_op jit(solution)/shard_map/ppermute | solution.py:323
  133.2 12.6 %collective-permute-start.35 = (f16[32,3584]{1,0:T(8,128)(2,1)S(1)}, f16[32,3584]{1,0:T(8,128)(2,1)S(1)}, u32[]{:S(2)}, u32[]{:S(2)}) collective-permute-start(f16[32,3584]{1,0:T(8,128)(2,1)S(1)} %convert_element_type.121), channel_id=1, source_target_pairs={{0,1},{1,0},{2,3},{3,2},{4,5},{5,4},{6,7},{7,6},{8,9},{9,8},{10,11... | collective-permute-start | bytes 688136 | tf_op jit(solution)/shard_map/ppermute | solution.py:323
  135.6 6.0 %collective-permute-start.33 = (f16[32,3584]{1,0:T(8,128)(2,1)S(1)}, f16[32,3584]{1,0:T(8,128)(2,1)S(1)}, u32[]{:S(2)}, u32[]{:S(2)}) collective-permute-start(f16[32,3584]{1,0:T(8,128)(2,1)S(1)} %convert_element_type.117), channel_id=1, source_target_pairs={{0,1},{1,0},{2,3},{3,2},{4,5},{5,4},{6,7},{7,6},{8,9},{9,8},{10,11... | collective-permute-start | bytes 688136 | tf_op jit(solution)/shard_map/ppermute | solution.py:323
  136.9 6.4 %collective-permute-start.30 = (f16[32,3584]{1,0:T(8,128)(2,1)S(1)}, f16[32,3584]{1,0:T(8,128)(2,1)S(1)}, u32[]{:S(2)}, u32[]{:S(2)}) collective-permute-start(f16[32,3584]{1,0:T(8,128)(2,1)S(1)} %add_convert_fusion.3), channel_id=1, source_target_pairs={{0,2},{1,3},{2,0},{3,1},{4,6},{5,7},{6,4},{7,5},{8,10},{9,11},{10,... | collective-permute-start | bytes 688136 | tf_op jit(solution)/shard_map/ppermute | solution.py:323
  141.7 6.1 %collective-permute-start.34 = (f16[32,3584]{1,0:T(8,128)(2,1)S(1)}, f16[32,3584]{1,0:T(8,128)(2,1)S(1)}, u32[]{:S(2)}, u32[]{:S(2)}) collective-permute-start(f16[32,3584]{1,0:T(8,128)(2,1)S(1)} %add_convert_fusion.1), channel_id=1, source_target_pairs={{0,2},{1,3},{2,0},{3,1},{4,6},{5,7},{6,4},{7,5},{8,10},{9,11},{10,... | collective-permute-start | bytes 688136 | tf_op jit(solution)/shard_map/ppermute | solution.py:323
  143.4 9.4 %collective-permute-start.32 = (f16[32,3584]{1,0:T(8,128)(2,1)S(1)}, f16[32,3584]{1,0:T(8,128)(2,1)S(1)}, u32[]{:S(2)}, u32[]{:S(2)}) collective-permute-start(f16[32,3584]{1,0:T(8,128)(2,1)S(1)} %add_convert_fusion.2), channel_id=1, source_target_pairs={{0,4},{1,5},{2,6},{3,7},{4,0},{5,1},{6,2},{7,3},{8,12},{9,13},{10,... | collective-permute-start | bytes 688136 | tf_op jit(solution)/shard_map/ppermute | solution.py:323

commit v9 on v4

--- a/solution.py
+++ b/solution.py
@@ -314,12 +314,24 @@
     return lax.optimization_barrier((block, *others))[0]
 
 
-def make_body(vocab_size):
+def flipped(mask):
+    return (mask & ~3) | ((mask & 1) << 1) | ((mask >> 1) & 1)
+
+
+def make_body(vocab_size, cores):
     bits = vocab_size.bit_length() - 1
     assert vocab_size == 1 << bits
 
+    def trade(block, mask):
+        pairs = [
+            (core * vocab_size + at, core * vocab_size + (at ^ (flipped(mask) if core % 2 else mask)))
+            for core in range(cores)
+            for at in range(vocab_size)
+        ]
+        return lax.ppermute(block, ("seq", "vocab"), pairs)
+
     def swap(block, bit):
-        return lax.ppermute(block, "vocab", [(at, at ^ (1 << bit)) for at in range(vocab_size)])
+        return trade(block, 1 << bit)
 
     def lowest(mask):
         return (mask & -mask).bit_length() - 1
@@ -357,12 +369,18 @@
         chunk = min(slab_rows, 32)
         me = lax.axis_index("vocab")
         core = lax.axis_index("seq")
-        place = jnp.stack([me, core]).astype(jnp.int32)
+        odd = core % 2 == 1
+        spin = jnp.where(odd, flipped(me), me)
+        place = jnp.stack([spin, core]).astype(jnp.int32)
+
+        def by_core(vec):
+            grid = vec.reshape(-1, 2, 2, blk)
+            return jnp.where(odd, jnp.swapaxes(grid, 1, 2), grid).reshape(slab_rows)
 
         def in_order(vec):
-            grid = vec.reshape((2,) * bits + (blk,))
+            grid = by_core(vec).reshape((2,) * bits + (blk,))
             for bit in range(bits):
-                grid = jnp.where((me >> bit) & 1 == 1, jnp.flip(grid, bits - 1 - bit), grid)
+                grid = jnp.where((spin >> bit) & 1 == 1, jnp.flip(grid, bits - 1 - bit), grid)
             return grid.reshape(slab_rows)
 
         def turned(block):
@@ -374,7 +392,7 @@
         heads = (head_weight, lax.ppermute(head_weight, "seq", [(0, 1), (1, 0)]))
 
         spot = lax.iota(jnp.int32, slab_rows)
-        row_id = ((spot // blk) ^ me) * blk + spot % blk
+        row_id = (jnp.where(odd, flipped(spot // blk), spot // blk) ^ me) * blk + spot % blk
         alive = lax.iota(jnp.int32, teach_rows) < counts[0]
         member = (owner[None, :] == row_id[:, None]) & alive[None, :]
         parts = project(member.astype(jnp.bfloat16), teacher_rows, proj_weight, vocab_size, 512 if student_hidden.shape[1] % 512 == 0 else student_hidden.shape[1])
@@ -385,19 +403,19 @@
         column = (in_order(targets) - me * vocab_dev)[:, None]
         logit_stud, scaled_stud, stats_stud, head = student_logits(as_pieces(hidden), heads, column, 256, chunk)
         scaled_teach, stats = teacher_logits(as_pieces(projected), head, logit_stud, stats_stud, 512, chunk)
-        tables = [stats] + [
-            lax.ppermute(stats, "vocab", [(at, at ^ mask) for at in range(vocab_size)])
-            for mask in range(1, vocab_size)
-        ]
+        tables = [stats]
+        for mask in range(1, vocab_size):
+            far, near = mask & ~3, mask & 3
+            tables.append(trade(tables[far], near) if near else trade(stats, far))
         loss, *terms = gradient(place, tables, scaled_teach, scaled_stud, column, head, bits, chunk)
-        return (loss[0], turned(reduce_blocks(terms)[0].astype(jnp.bfloat16)))
+        return (by_core(loss[0]), turned(reduce_blocks(terms)[0].astype(jnp.bfloat16)))
 
     return body
 
 
 def solution(mesh):
     return jax.shard_map(
-        make_body(mesh.shape["vocab"]),
+        make_body(mesh.shape["vocab"], mesh.shape["seq"]),
         mesh=mesh,
         in_specs=(
             P(("groups", "seq"), "vocab"),

time: 138 us -> 142 us (1.029)
  waiting for transfers between devices: 39 us -> 52.7 us
  starting transfers between devices: 55.3 us -> 45.5 us
    ppermute x35, waiting for transfers between devices: 39 us -> 52.7 us  [trade(): return lax.ppermute(block, ('seq', 'vocab'), pairs)]
    ppermute x35, starting transfers between devices: 54.8 us -> 45 us  [trade(): return lax.ppermute(block, ('seq', 'vocab'), pairs)]
where the time goes in v9:
time: 142 us
  waiting for transfers between devices  52.7 us (37%)
  starting transfers between devices  45.5 us (32%)
  Pallas kernels  32.5 us (23%)
  other arithmetic  5.2 us (4%)
  local copies, waits for them, and re-layouts  4.54 us (3%)
  between operations  1.58 us (1%)
    ppermute x35, waiting for transfers between devices, trade(): return lax.ppermute(block, ('seq', 'vocab'), pairs)  52.7 us
    ppermute x35, starting transfers between devices, trade(): return lax.ppermute(block, ('seq', 'vocab'), pairs)  45 us
    pallas_call x1, Pallas kernels, student_logits(): pl.pallas_call(functools.partial(student_kernel, len(pieces), step, chunk...  11.9 us
    pallas_call x1, Pallas kernels, gradient(): pl.pallas_call(functools.partial(gradient_kernel, bits, step, chunk), in_...  8.33 us
    pallas_call x1, Pallas kernels, teacher_logits(): pl.pallas_call(functools.partial(teacher_kernel, len(pieces), step, chunk...  7.49 us
    pallas_call x1, Pallas kernels, project(): pl.pallas_call(functools.partial(project_kernel, count, step), in_specs=[...  4.83 us
    unnamed x6, local copies, waits for them, and re-layouts  3.48 us
  transfers between devices with their start and end apart: 36, of which 17 were waited for; matrix products, arithmetic and copies ran while one was open for 4% of the time, Pallas kernels for 12%

profile of v9, /device:TPU:0, one launch (start us, length us, event | category | flops | bytes accessed | tf_op | source)
XLA Modules:
  0.0 142.0 jit_solution(1975517423693092964)
XLA Ops:
  0.6 0.5 collective-permute-start.21
  1.8 0.8 and_convert_fusion.member_ref
  2.7 4.8 %shard_map.86 = (f32[32,3584]{1,0:T(8,128)S(1)}, f32[32,3584]{1,0:T(8,128)S(1)}, f32[32,3584]{1,0:T(8,128)S(1)}, f32[32,3584]{1,0:T(8,128)S(1)}, f32[32,3584]{1,...) custom-call(bf16[256,512]{1,0:T(8,128)(2,1)S(1)} %and_convert_fusion.member_ref, ...), custom_call_target="tpu_custom_call" | custom-call | flops 2147483648 | bytes 12058624 | tf_op jit(solution)/shard_map/pallas_call | solution.py:54
  7.5 0.7 convert_element_type.94
  8.2 2.6 %collective-permute-start = (f16[32,3584]{1,0:T(8,128)(2,1)}, f16[32,3584]{1,0:T(8,128)(2,1)}, u32[]{:S(2)}, u32[]{:S(2)}) collective-permute-start(f16[32,3584]{1,0:T(8,128)(2,1)} %convert_element_type.94), channel_id=1, source_target_pairs={{0,1},{1,0},{2,3},{3,2},{4,5},{5,4},{6,7},{7,6},{8,10},{9,11},{10,... | collective-permute-start | bytes 688136 | tf_op jit(solution)/shard_map/ppermute | solution.py:331
  10.8 1.0 maximum_select_fusion.1.refs_0_
  11.8 2.6 %collective-permute-start.11 = (bf16[32,3584]{1,0:T(8,128)(2,1)S(1)}, bf16[32,3584]{1,0:T(8,128)(2,1)}, u32[]{:S(2)}, u32[]{:S(2)}) collective-permute-start(bf16[32,3584]{1,0:T(8,128)(2,1)S(1)} %maximum_select_fusion.1.refs_0_), channel_id=1, source_target_pairs={{0,4},{1,5},{2,6},{3,7},{4,0},{5,1},{6,2},{7,3},{8,12},{9,13},{10,... | collective-permute-start | bytes 688136 | tf_op jit(solution)/shard_map/ppermute | solution.py:331
  14.5 1.6 %collective-permute-start.7 = (bf16[32,3584]{1,0:T(8,128)(2,1)S(1)}, bf16[32,3584]{1,0:T(8,128)(2,1)}, u32[]{:S(2)}, u32[]{:S(2)}) collective-permute-start(bf16[32,3584]{1,0:T(8,128)(2,1)S(1)} %maximum_select_fusion.1.refs_0_), channel_id=1, source_target_pairs={{0,2},{1,3},{2,0},{3,1},{4,6},{5,7},{6,4},{7,5},{8,9},{9,8},{10,11... | collective-permute-start | bytes 688136 | tf_op jit(solution)/shard_map/ppermute | solution.py:331
  16.1 0.6 collective-permute-start.2
  16.7 1.6 %collective-permute-start.4 = (f16[32,3584]{1,0:T(8,128)(2,1)S(1)}, f16[32,3584]{1,0:T(8,128)(2,1)S(1)}, u32[]{:S(2)}, u32[]{:S(2)}) collective-permute-start(f16[32,3584]{1,0:T(8,128)(2,1)S(1)} %convert_element_type.102), channel_id=1, source_target_pairs={{0,1},{1,0},{2,3},{3,2},{4,5},{5,4},{6,7},{7,6},{8,10},{9,11},{10,... | collective-permute-start | bytes 688136 | tf_op jit(solution)/shard_map/ppermute | solution.py:331
  18.3 1.0 add_convert_fusion.7
  19.3 2.9 %collective-permute-done.2 = f16[32,3584]{1,0:T(8,128)(2,1)S(1)} collective-permute-done((f16[32,3584]{1,0:T(8,128)(2,1)S(1)}, f16[32,3584]{1,0:T(8,128)(2,1)S(1)}, u32[]{:S(2)}, u32[]{:S(2)}) %collective-permute-start.2) | collective-permute-done | bytes 229408 | tf_op jit(solution)/shard_map/ppermute | solution.py:331
  22.2 0.4 collective-permute-start.1
  22.6 2.0 %collective-permute-done.4 = f16[32,3584]{1,0:T(8,128)(2,1)S(1)} collective-permute-done((f16[32,3584]{1,0:T(8,128)(2,1)S(1)}, f16[32,3584]{1,0:T(8,128)(2,1)S(1)}, u32[]{:S(2)}, u32[]{:S(2)}) %collective-permute-start.4) | collective-permute-done | bytes 229408 | tf_op jit(solution)/shard_map/ppermute | solution.py:331
  24.6 0.5 collective-permute-start.6
  25.2 4.6 %collective-permute-done.1 = f16[32,3584]{1,0:T(8,128)(2,1)S(1)} collective-permute-done((f16[32,3584]{1,0:T(8,128)(2,1)S(1)}, f16[32,3584]{1,0:T(8,128)(2,1)S(1)}, u32[]{:S(2)}, u32[]{:S(2)}) %collective-permute-start.1) | collective-permute-done | bytes 229408 | tf_op jit(solution)/shard_map/ppermute | solution.py:331
  29.8 1.6 %collective-permute-start.5 = (f16[32,3584]{1,0:T(8,128)(2,1)S(1)}, f16[32,3584]{1,0:T(8,128)(2,1)S(1)}, u32[]{:S(2)}, u32[]{:S(2)}) collective-permute-start(f16[32,3584]{1,0:T(8,128)(2,1)S(1)} %add_convert_fusion.5), channel_id=1, source_target_pairs={{0,2},{1,3},{2,0},{3,1},{4,6},{5,7},{6,4},{7,5},{8,9},{9,8},{10,11... | collective-permute-start | bytes 688136 | tf_op jit(solution)/shard_map/ppermute | solution.py:331
  31.4 0.1 add_convert_fusion.6
  31.5 2.2 %collective-permute-start.3 = (f16[32,3584]{1,0:T(8,128)(2,1)S(1)}, f16[32,3584]{1,0:T(8,128)(2,1)S(1)}, u32[]{:S(2)}, u32[]{:S(2)}) collective-permute-start(f16[32,3584]{1,0:T(8,128)(2,1)S(1)} %add_convert_fusion.6), channel_id=1, source_target_pairs={{0,4},{1,5},{2,6},{3,7},{4,0},{5,1},{6,2},{7,3},{8,12},{9,13},{10,... | collective-permute-start | bytes 688136 | tf_op jit(solution)/shard_map/ppermute | solution.py:331
  33.7 0.8 collective-permute-start.16
  34.5 1.0 collective-permute-start.15
  35.5 4.3 %collective-permute-done.5 = f16[32,3584]{1,0:T(8,128)(2,1)S(1)} collective-permute-done((f16[32,3584]{1,0:T(8,128)(2,1)S(1)}, f16[32,3584]{1,0:T(8,128)(2,1)S(1)}, u32[]{:S(2)}, u32[]{:S(2)}) %collective-permute-start.5) | collective-permute-done | bytes 229408 | tf_op jit(solution)/shard_map/ppermute | solution.py:331
  39.8 2.9 %collective-permute-start.12 = (bf16[32,3584]{1,0:T(8,128)(2,1)}, bf16[32,3584]{1,0:T(8,128)(2,1)S(1)}, u32[]{:S(2)}, u32[]{:S(2)}) collective-permute-start(bf16[32,3584]{1,0:T(8,128)(2,1)} %collective-permute-done.11.refs_4_), channel_id=1, source_target_pairs={{0,1},{1,0},{2,3},{3,2},{4,5},{5,4},{6,7},{7,6},{8,10},{9,11},{10,... | collective-permute-start | bytes 688136 | tf_op jit(solution)/shard_map/ppermute | solution.py:331
  42.7 2.3 %collective-permute-done.3 = f16[32,3584]{1,0:T(8,128)(2,1)S(1)} collective-permute-done((f16[32,3584]{1,0:T(8,128)(2,1)S(1)}, f16[32,3584]{1,0:T(8,128)(2,1)S(1)}, u32[]{:S(2)}, u32[]{:S(2)}) %collective-permute-start.3) | collective-permute-done | bytes 229408 | tf_op jit(solution)/shard_map/ppermute | solution.py:331
  45.0 2.1 %collective-permute-start.8 = (bf16[32,3584]{1,0:T(8,128)(2,1)}, bf16[32,3584]{1,0:T(8,128)(2,1)S(1)}, u32[]{:S(2)}, u32[]{:S(2)}) collective-permute-start(bf16[32,3584]{1,0:T(8,128)(2,1)} %collective-permute-done.7.refs_2_), channel_id=1, source_target_pairs={{0,1},{1,0},{2,3},{3,2},{4,5},{5,4},{6,7},{7,6},{8,10},{9,11},{10,... | collective-permute-start | bytes 688136 | tf_op jit(solution)/shard_map/ppermute | solution.py:331
  47.1 0.1 add_convert_fusion.4
  47.5 0.1 collective-permute-start.17
  47.6 3.7 %collective-permute-done.8.refs_3_ = bf16[32,3584]{1,0:T(8,128)(2,1)S(1)} collective-permute-done((bf16[32,3584]{1,0:T(8,128)(2,1)}, bf16[32,3584]{1,0:T(8,128)(2,1)S(1)}, u32[]{:S(2)}, u32[]{:S(2)}) %collective-permute-start.8) | collective-permute-done | bytes 229408 | tf_op jit(solution)/shard_map/ppermute | solution.py:331
  51.3 0.6 collective-permute-start.10
  51.9 1.5 %collective-permute-start.9 = (bf16[32,3584]{1,0:T(8,128)(2,1)S(1)}, bf16[32,3584]{1,0:T(8,128)(2,1)S(1)}, u32[]{:S(2)}, u32[]{:S(2)}) collective-permute-start(bf16[32,3584]{1,0:T(8,128)(2,1)S(1)} %maximum_select_fusion.refs_0_), channel_id=1, source_target_pairs={{0,1},{1,0},{2,3},{3,2},{4,5},{5,4},{6,7},{7,6},{8,10},{9,11},{10,... | collective-permute-start | bytes 688136 | tf_op jit(solution)/shard_map/ppermute | solution.py:331
  53.4 3.9 %collective-permute-done.14.refs_4_ = bf16[32,3584]{1,0:T(8,128)(2,1)S(1)} collective-permute-done((bf16[32,3584]{1,0:T(8,128)(2,1)S(1)}, bf16[32,3584]{1,0:T(8,128)(2,1)S(1)}, u32[]{:S(2)}, u32[]{:S(2)}) %collective-permute-start.14) | collective-permute-done | bytes 229408 | tf_op jit(solution)/shard_map/ppermute | solution.py:331
  57.3 1.3 collective-permute-start.19
  58.6 3.2 %collective-permute-done.10.refs_2_ = bf16[32,3584]{1,0:T(8,128)(2,1)S(1)} collective-permute-done((bf16[32,3584]{1,0:T(8,128)(2,1)S(1)}, bf16[32,3584]{1,0:T(8,128)(2,1)S(1)}, u32[]{:S(2)}, u32[]{:S(2)}) %collective-permute-start.10) | collective-permute-done | bytes 229408 | tf_op jit(solution)/shard_map/ppermute | solution.py:331
  61.8 2.4 %collective-permute-start.13 = (bf16[32,3584]{1,0:T(8,128)(2,1)S(1)}, bf16[32,3584]{1,0:T(8,128)(2,1)S(1)}, u32[]{:S(2)}, u32[]{:S(2)}) collective-permute-start(bf16[32,3584]{1,0:T(8,128)(2,1)S(1)} %collective-permute-done.10.refs_2_), channel_id=1, source_target_pairs={{0,1},{1,0},{2,3},{3,2},{4,5},{5,4},{6,7},{7,6},{8,10},{9,11},{10,... | collective-permute-start | bytes 688136 | tf_op jit(solution)/shard_map/ppermute | solution.py:331
  64.2 2.5 %collective-permute-done.19.refs_6_ = bf16[32,3584]{1,0:T(8,128)(2,1)S(1)} collective-permute-done((bf16[32,3584]{1,0:T(8,128)(2,1)S(1)}, bf16[32,3584]{1,0:T(8,128)(2,1)S(1)}, u32[]{:S(2)}, u32[]{:S(2)}) %collective-permute-start.19) | collective-permute-done | bytes 229408 | tf_op jit(solution)/shard_map/ppermute | solution.py:331
  66.7 2.4 %collective-permute-start.20 = (bf16[32,3584]{1,0:T(8,128)(2,1)S(1)}, bf16[32,3584]{1,0:T(8,128)(2,1)S(1)}, u32[]{:S(2)}, u32[]{:S(2)}) collective-permute-start(bf16[32,3584]{1,0:T(8,128)(2,1)S(1)} %collective-permute-done.19.refs_6_), channel_id=1, source_target_pairs={{0,1},{1,0},{2,3},{3,2},{4,5},{5,4},{6,7},{7,6},{8,10},{9,11},{10,... | collective-permute-start | bytes 688136 | tf_op jit(solution)/shard_map/ppermute | solution.py:331
  69.1 0.1 sub.30.refs_10_
  69.3 3.5 %copy-done = bf16[1792,2432]{1,0:T(8,128)(2,1)S(1)} copy-done((bf16[1792,2432]{1,0:T(8,128)(2,1)S(1)}, bf16[1792,2432]{1,0:T(8,128)(2,1)}, u32[]{:S(2)}) %copy-start) | copy-done | bytes 8716312
  72.7 11.9 %shard_map.87 = (f32[256,2432]{1,0:T(8,128)S(1)}, f32[256,2432]{1,0:T(8,128)S(1)}, f32[8,256]{1,0:T(8,128)S(1)}, bf16[3584,2432]{1,0:T(8,128)(2,1)S(1)}) custom-call(bf16[32,3584]{1,0:T(8,128)(2,1)S(1)} %maximum_select_fusion.1.refs_0_, bf16[32,3584]{1,0:T(8,128)(2,1)S(1)} %collective-permute-done.16.refs_1_, ...), custom_call_target="tpu_custom_call" | custom-call | flops 2231369728 | bytes 16187392 | tf_op jit(solution)/shard_map/pallas_call | solution.py:192
  84.7 7.5 %shard_map.88 = (f32[256,2432]{1,0:T(8,128)S(1)}, f32[8,256]{1,0:T(8,128)S(1)}) custom-call(bf16[32,3584]{1,0:T(8,128)(2,1)S(1)} %maximum_select_fusion.refs_0_, bf16[32,3584]{1,0:T(8,128)(2,1)S(1)} %collective-permute-done.9.refs_1_, bf16[32,3584]{1,0:T(8,128)(2,1)S(1)} %collective-permute-done.10.refs_2_, ...), custom_call_target="tpu_custom_call" | custom-call | flops 4462739456 | bytes 24903680 | tf_op jit(solution)/shard_map/pallas_call | solution.py:215
  92.2 3.4 %collective-permute-start.24 = (f32[8,256]{1,0:T(8,128)S(1)}, f32[8,256]{1,0:T(8,128)S(1)}, u32[]{:S(2)}, u32[]{:S(2)}) collective-permute-start(f32[8,256]{1,0:T(8,128)S(1)} %get-tuple-element.60.refs_0_), channel_id=1, source_target_pairs={{0,3},{1,2},{2,1},{3,0},{4,7},{5,6},{6,5},{7,4},{8,11},{9,10},{10,... | collective-permute-start | bytes 24584 | tf_op jit(solution)/shard_map/ppermute | solution.py:331
  95.6 0.6 collective-permute-start.22
  96.1 0.6 collective-permute-done.25.refs_4_
  96.7 2.3 %collective-permute-start.28 = (f32[8,256]{1,0:T(8,128)S(1)}, f32[8,256]{1,0:T(8,128)S(1)}, u32[]{:S(2)}, u32[]{:S(2)}) collective-permute-start(f32[8,256]{1,0:T(8,128)S(1)} %collective-permute-done.25.refs_4_), channel_id=1, source_target_pairs={{0,3},{1,2},{2,1},{3,0},{4,7},{5,6},{6,5},{7,4},{8,11},{9,10},{10,... | collective-permute-start | bytes 24584 | tf_op jit(solution)/shard_map/ppermute | solution.py:331
  99.1 1.2 collective-permute-start.26
  100.3 1.0 collective-permute-done.28.refs_7_
  101.3 1.4 %collective-permute-done.27.refs_6_ = f32[8,256]{1,0:T(8,128)S(1)} collective-permute-done((f32[8,256]{1,0:T(8,128)S(1)}, f32[8,256]{1,0:T(8,128)S(1)}, u32[]{:S(2)}, u32[]{:S(2)}) %collective-permute-start.27) | collective-permute-done | bytes 8224 | tf_op jit(solution)/shard_map/ppermute | solution.py:331
  102.7 8.3 %shard_map.89 = (f32[8,256]{1,0:T(8,128)S(1)}, f32[32,3584]{1,0:T(8,128)S(1)}, f32[32,3584]{1,0:T(8,128)S(1)}, f32[32,3584]{1,0:T(8,128)S(1)}, f32[32,3584]{1,0:...) custom-call(s32[2]{0:T(128)S(1)} %pad_add_fusion.place_ref, ...), custom_call_target="tpu_custom_call" | custom-call | flops 4462739456 | bytes 24903680 | tf_op jit(solution)/shard_map/pallas_call | solution.py:297
  111.1 1.2 collective-permute-start.31
  112.4 0.9 collective-permute-start.29
  113.3 3.8 %collective-permute-done.31 = f16[32,3584]{1,0:T(8,128)(2,1)S(1)} collective-permute-done((f16[32,3584]{1,0:T(8,128)(2,1)S(1)}, f16[32,3584]{1,0:T(8,128)(2,1)S(1)}, u32[]{:S(2)}, u32[]{:S(2)}) %collective-permute-start.31) | collective-permute-done | bytes 229408 | tf_op jit(solution)/shard_map/ppermute | solution.py:331
  117.2 1.2 collective-permute-start.35
  118.3 1.3 collective-permute-done.29
  119.6 1.2 collective-permute-start.33
  120.9 1.6 %collective-permute-start.30 = (f16[32,3584]{1,0:T(8,128)(2,1)S(1)}, f16[32,3584]{1,0:T(8,128)(2,1)S(1)}, u32[]{:S(2)}, u32[]{:S(2)}) collective-permute-start(f16[32,3584]{1,0:T(8,128)(2,1)S(1)} %add_convert_fusion.3), channel_id=1, source_target_pairs={{0,2},{1,3},{2,0},{3,1},{4,6},{5,7},{6,4},{7,5},{8,9},{9,8},{10,11... | collective-permute-start | bytes 688136 | tf_op jit(solution)/shard_map/ppermute | solution.py:331
  122.5 7.6 %collective-permute-done.33 = f16[32,3584]{1,0:T(8,128)(2,1)S(1)} collective-permute-done((f16[32,3584]{1,0:T(8,128)(2,1)S(1)}, f16[32,3584]{1,0:T(8,128)(2,1)S(1)}, u32[]{:S(2)}, u32[]{:S(2)}) %collective-permute-start.33) | collective-permute-done | bytes 229408 | tf_op jit(solution)/shard_map/ppermute | solution.py:331
  130.2 1.4 %collective-permute-start.34 = (f16[32,3584]{1,0:T(8,128)(2,1)S(1)}, f16[32,3584]{1,0:T(8,128)(2,1)S(1)}, u32[]{:S(2)}, u32[]{:S(2)}) collective-permute-start(f16[32,3584]{1,0:T(8,128)(2,1)S(1)} %add_convert_fusion.1), channel_id=1, source_target_pairs={{0,2},{1,3},{2,0},{3,1},{4,6},{5,7},{6,4},{7,5},{8,9},{9,8},{10,11... | collective-permute-start | bytes 688136 | tf_op jit(solution)/shard_map/ppermute | solution.py:331
  131.6 0.1 add_convert_fusion.2
  131.7 1.1 collective-permute-start.32
  132.9 0.6 reshape.60
  133.6 2.7 %collective-permute-done.34 = f16[32,3584]{1,0:T(8,128)(2,1)S(1)} collective-permute-done((f16[32,3584]{1,0:T(8,128)(2,1)S(1)}, f16[32,3584]{1,0:T(8,128)(2,1)S(1)}, u32[]{:S(2)}, u32[]{:S(2)}) %collective-permute-start.34) | collective-permute-done | bytes 229408 | tf_op jit(solution)/shard_map/ppermute | solution.py:331
  136.3 4.9 %collective-permute-done.32 = f16[32,3584]{1,0:T(8,128)(2,1)S(1)} collective-permute-done((f16[32,3584]{1,0:T(8,128)(2,1)S(1)}, f16[32,3584]{1,0:T(8,128)(2,1)S(1)}, u32[]{:S(2)}, u32[]{:S(2)}) %collective-permute-start.32) | collective-permute-done | bytes 229408 | tf_op jit(solution)/shard_map/ppermute | solution.py:331
  141.2 0.1 add_convert_fusion
  141.3 0.8 maximum_select_fusion.2
  (55 shorter events, 1.0 us)
Async XLA Ops:
  0.6 10.2 %copy-start.1 = (bf16[32,3584]{1,0:T(8,128)(2,1)S(1)}, bf16[32,3584]{1,0:T(8,128)(2,1)}, u32[]{:S(2)}) copy-start(bf16[32,3584]{1,0:T(8,128)(2,1)} %param.11) | copy-start | bytes 688132
  0.6 68.6 %collective-permute-start.21 = (bf16[1792,2432]{1,0:T(8,128)(2,1)}, bf16[1792,2432]{1,0:T(8,128)(2,1)}, u32[]{:S(2)}, u32[]{:S(2)}) collective-permute-start(bf16[1792,2432]{1,0:T(8,128)(2,1)} %refs_8_.1), channel_id=1, source_target_pairs={{0,8},{8,0},{1,9},{9,1},{2,10},{10,2},{3,11},{11,3},{4,12},{12,4},... | collective-permute-start | bytes 26148872 | tf_op jit(solution)/shard_map/ppermute | solution.py:392
  2.7 44.7 %copy-start.2 = (s32[256]{0:T(256)S(1)}, s32[256]{0:T(256)}, u32[]{:S(2)}) copy-start(s32[256]{0:T(256)} %param.13) | copy-start | bytes 3076
  8.2 8.5 %collective-permute-start = (f16[32,3584]{1,0:T(8,128)(2,1)}, f16[32,3584]{1,0:T(8,128)(2,1)}, u32[]{:S(2)}, u32[]{:S(2)}) collective-permute-start(f16[32,3584]{1,0:T(8,128)(2,1)} %convert_element_type.94), channel_id=1, source_target_pairs={{0,1},{1,0},{2,3},{3,2},{4,5},{5,4},{6,7},{7,6},{8,10},{9,11},{10,... | collective-permute-start | bytes 688136 | tf_op jit(solution)/shard_map/ppermute | solution.py:331
  11.8 19.6 %collective-permute-start.11 = (bf16[32,3584]{1,0:T(8,128)(2,1)S(1)}, bf16[32,3584]{1,0:T(8,128)(2,1)}, u32[]{:S(2)}, u32[]{:S(2)}) collective-permute-start(bf16[32,3584]{1,0:T(8,128)(2,1)S(1)} %maximum_select_fusion.1.refs_0_), channel_id=1, source_target_pairs={{0,4},{1,5},{2,6},{3,7},{4,0},{5,1},{6,2},{7,3},{8,12},{9,13},{10,... | collective-permute-start | bytes 688136 | tf_op jit(solution)/shard_map/ppermute | solution.py:331
  14.5 20.0 %collective-permute-start.7 = (bf16[32,3584]{1,0:T(8,128)(2,1)S(1)}, bf16[32,3584]{1,0:T(8,128)(2,1)}, u32[]{:S(2)}, u32[]{:S(2)}) collective-permute-start(bf16[32,3584]{1,0:T(8,128)(2,1)S(1)} %maximum_select_fusion.1.refs_0_), channel_id=1, source_target_pairs={{0,2},{1,3},{2,0},{3,1},{4,6},{5,7},{6,4},{7,5},{8,9},{9,8},{10,11... | collective-permute-start | bytes 688136 | tf_op jit(solution)/shard_map/ppermute | solution.py:331
  16.1 6.1 %collective-permute-start.2 = (f16[32,3584]{1,0:T(8,128)(2,1)S(1)}, f16[32,3584]{1,0:T(8,128)(2,1)S(1)}, u32[]{:S(2)}, u32[]{:S(2)}) collective-permute-start(f16[32,3584]{1,0:T(8,128)(2,1)S(1)} %convert_element_type.98), channel_id=1, source_target_pairs={{0,1},{1,0},{2,3},{3,2},{4,5},{5,4},{6,7},{7,6},{8,10},{9,11},{10,... | collective-permute-start | bytes 688136 | tf_op jit(solution)/shard_map/ppermute | solution.py:331
  16.7 7.9 %collective-permute-start.4 = (f16[32,3584]{1,0:T(8,128)(2,1)S(1)}, f16[32,3584]{1,0:T(8,128)(2,1)S(1)}, u32[]{:S(2)}, u32[]{:S(2)}) collective-permute-start(f16[32,3584]{1,0:T(8,128)(2,1)S(1)} %convert_element_type.102), channel_id=1, source_target_pairs={{0,1},{1,0},{2,3},{3,2},{4,5},{5,4},{6,7},{7,6},{8,10},{9,11},{10,... | collective-permute-start | bytes 688136 | tf_op jit(solution)/shard_map/ppermute | solution.py:331
  22.2 7.6 %collective-permute-start.1 = (f16[32,3584]{1,0:T(8,128)(2,1)S(1)}, f16[32,3584]{1,0:T(8,128)(2,1)S(1)}, u32[]{:S(2)}, u32[]{:S(2)}) collective-permute-start(f16[32,3584]{1,0:T(8,128)(2,1)S(1)} %add_convert_fusion.7), channel_id=1, source_target_pairs={{0,2},{1,3},{2,0},{3,1},{4,6},{5,7},{6,4},{7,5},{8,9},{9,8},{10,11... | collective-permute-start | bytes 688136 | tf_op jit(solution)/shard_map/ppermute | solution.py:331
  24.6 9.0 %collective-permute-start.6 = (f16[32,3584]{1,0:T(8,128)(2,1)S(1)}, f16[32,3584]{1,0:T(8,128)(2,1)S(1)}, u32[]{:S(2)}, u32[]{:S(2)}) collective-permute-start(f16[32,3584]{1,0:T(8,128)(2,1)S(1)} %convert_element_type.106), channel_id=1, source_target_pairs={{0,1},{1,0},{2,3},{3,2},{4,5},{5,4},{6,7},{7,6},{8,10},{9,11},{10,... | collective-permute-start | bytes 688136 | tf_op jit(solution)/shard_map/ppermute | solution.py:331
  29.8 10.0 %collective-permute-start.5 = (f16[32,3584]{1,0:T(8,128)(2,1)S(1)}, f16[32,3584]{1,0:T(8,128)(2,1)S(1)}, u32[]{:S(2)}, u32[]{:S(2)}) collective-permute-start(f16[32,3584]{1,0:T(8,128)(2,1)S(1)} %add_convert_fusion.5), channel_id=1, source_target_pairs={{0,2},{1,3},{2,0},{3,1},{4,6},{5,7},{6,4},{7,5},{8,9},{9,8},{10,11... | collective-permute-start | bytes 688136 | tf_op jit(solution)/shard_map/ppermute | solution.py:331
  31.5 13.5 %collective-permute-start.3 = (f16[32,3584]{1,0:T(8,128)(2,1)S(1)}, f16[32,3584]{1,0:T(8,128)(2,1)S(1)}, u32[]{:S(2)}, u32[]{:S(2)}) collective-permute-start(f16[32,3584]{1,0:T(8,128)(2,1)S(1)} %add_convert_fusion.6), channel_id=1, source_target_pairs={{0,4},{1,5},{2,6},{3,7},{4,0},{5,1},{6,2},{7,3},{8,12},{9,13},{10,... | collective-permute-start | bytes 688136 | tf_op jit(solution)/shard_map/ppermute | solution.py:331
  33.7 13.6 %collective-permute-start.16 = (bf16[32,3584]{1,0:T(8,128)(2,1)S(1)}, bf16[32,3584]{1,0:T(8,128)(2,1)S(1)}, u32[]{:S(2)}, u32[]{:S(2)}) collective-permute-start(bf16[32,3584]{1,0:T(8,128)(2,1)S(1)} %maximum_select_fusion.1.refs_0_), channel_id=1, source_target_pairs={{0,1},{1,0},{2,3},{3,2},{4,5},{5,4},{6,7},{7,6},{8,10},{9,11},{10,... | collective-permute-start | bytes 688136 | tf_op jit(solution)/shard_map/ppermute | solution.py:331
  34.5 13.0 %collective-permute-start.15 = (bf16[32,3584]{1,0:T(8,128)(2,1)}, bf16[32,3584]{1,0:T(8,128)(2,1)S(1)}, u32[]{:S(2)}, u32[]{:S(2)}) collective-permute-start(bf16[32,3584]{1,0:T(8,128)(2,1)} %collective-permute-done.11.refs_4_), channel_id=1, source_target_pairs={{0,2},{1,3},{2,0},{3,1},{4,6},{5,7},{6,4},{7,5},{8,9},{9,8},{10,11... | collective-permute-start | bytes 688136 | tf_op jit(solution)/shard_map/ppermute | solution.py:331
  39.8 12.1 %collective-permute-start.12 = (bf16[32,3584]{1,0:T(8,128)(2,1)}, bf16[32,3584]{1,0:T(8,128)(2,1)S(1)}, u32[]{:S(2)}, u32[]{:S(2)}) collective-permute-start(bf16[32,3584]{1,0:T(8,128)(2,1)} %collective-permute-done.11.refs_4_), channel_id=1, source_target_pairs={{0,1},{1,0},{2,3},{3,2},{4,5},{5,4},{6,7},{7,6},{8,10},{9,11},{10,... | collective-permute-start | bytes 688136 | tf_op jit(solution)/shard_map/ppermute | solution.py:331
  45.0 6.3 %collective-permute-start.8 = (bf16[32,3584]{1,0:T(8,128)(2,1)}, bf16[32,3584]{1,0:T(8,128)(2,1)S(1)}, u32[]{:S(2)}, u32[]{:S(2)}) collective-permute-start(bf16[32,3584]{1,0:T(8,128)(2,1)} %collective-permute-done.7.refs_2_), channel_id=1, source_target_pairs={{0,1},{1,0},{2,3},{3,2},{4,5},{5,4},{6,7},{7,6},{8,10},{9,11},{10,... | collective-permute-start | bytes 688136 | tf_op jit(solution)/shard_map/ppermute | solution.py:331
  47.3 10.0 %collective-permute-start.14 = (bf16[32,3584]{1,0:T(8,128)(2,1)S(1)}, bf16[32,3584]{1,0:T(8,128)(2,1)S(1)}, u32[]{:S(2)}, u32[]{:S(2)}) collective-permute-start(bf16[32,3584]{1,0:T(8,128)(2,1)S(1)} %maximum_select_fusion.refs_0_), channel_id=1, source_target_pairs={{0,4},{1,5},{2,6},{3,7},{4,0},{5,1},{6,2},{7,3},{8,12},{9,13},{10,... | collective-permute-start | bytes 688136 | tf_op jit(solution)/shard_map/ppermute | solution.py:331
  47.5 16.7 %collective-permute-start.17 = (bf16[32,3584]{1,0:T(8,128)(2,1)S(1)}, bf16[32,3584]{1,0:T(8,128)(2,1)S(1)}, u32[]{:S(2)}, u32[]{:S(2)}) collective-permute-start(bf16[32,3584]{1,0:T(8,128)(2,1)S(1)} %collective-permute-done.15.refs_6_), channel_id=1, source_target_pairs={{0,1},{1,0},{2,3},{3,2},{4,5},{5,4},{6,7},{7,6},{8,10},{9,11},{10,... | collective-permute-start | bytes 688136 | tf_op jit(solution)/shard_map/ppermute | solution.py:331
  51.3 10.5 %collective-permute-start.10 = (bf16[32,3584]{1,0:T(8,128)(2,1)S(1)}, bf16[32,3584]{1,0:T(8,128)(2,1)S(1)}, u32[]{:S(2)}, u32[]{:S(2)}) collective-permute-start(bf16[32,3584]{1,0:T(8,128)(2,1)S(1)} %maximum_select_fusion.refs_0_), channel_id=1, source_target_pairs={{0,2},{1,3},{2,0},{3,1},{4,6},{5,7},{6,4},{7,5},{8,9},{9,8},{10,11... | collective-permute-start | bytes 688136 | tf_op jit(solution)/shard_map/ppermute | solution.py:331
  51.9 12.3 %collective-permute-start.9 = (bf16[32,3584]{1,0:T(8,128)(2,1)S(1)}, bf16[32,3584]{1,0:T(8,128)(2,1)S(1)}, u32[]{:S(2)}, u32[]{:S(2)}) collective-permute-start(bf16[32,3584]{1,0:T(8,128)(2,1)S(1)} %maximum_select_fusion.refs_0_), channel_id=1, source_target_pairs={{0,1},{1,0},{2,3},{3,2},{4,5},{5,4},{6,7},{7,6},{8,10},{9,11},{10,... | collective-permute-start | bytes 688136 | tf_op jit(solution)/shard_map/ppermute | solution.py:331
  57.3 9.4 %collective-permute-start.19 = (bf16[32,3584]{1,0:T(8,128)(2,1)S(1)}, bf16[32,3584]{1,0:T(8,128)(2,1)S(1)}, u32[]{:S(2)}, u32[]{:S(2)}) collective-permute-start(bf16[32,3584]{1,0:T(8,128)(2,1)S(1)} %collective-permute-done.14.refs_4_), channel_id=1, source_target_pairs={{0,2},{1,3},{2,0},{3,1},{4,6},{5,7},{6,4},{7,5},{8,9},{9,8},{10,11... | collective-permute-start | bytes 688136 | tf_op jit(solution)/shard_map/ppermute | solution.py:331
  61.8 22.8 %collective-permute-start.13 = (bf16[32,3584]{1,0:T(8,128)(2,1)S(1)}, bf16[32,3584]{1,0:T(8,128)(2,1)S(1)}, u32[]{:S(2)}, u32[]{:S(2)}) collective-permute-start(bf16[32,3584]{1,0:T(8,128)(2,1)S(1)} %collective-permute-done.10.refs_2_), channel_id=1, source_target_pairs={{0,1},{1,0},{2,3},{3,2},{4,5},{5,4},{6,7},{7,6},{8,10},{9,11},{10,... | collective-permute-start | bytes 688136 | tf_op jit(solution)/shard_map/ppermute | solution.py:331
  64.2 20.5 %collective-permute-start.18 = (bf16[32,3584]{1,0:T(8,128)(2,1)S(1)}, bf16[32,3584]{1,0:T(8,128)(2,1)S(1)}, u32[]{:S(2)}, u32[]{:S(2)}) collective-permute-start(bf16[32,3584]{1,0:T(8,128)(2,1)S(1)} %collective-permute-done.14.refs_4_), channel_id=1, source_target_pairs={{0,1},{1,0},{2,3},{3,2},{4,5},{5,4},{6,7},{7,6},{8,10},{9,11},{10,... | collective-permute-start | bytes 688136 | tf_op jit(solution)/shard_map/ppermute | solution.py:331
  66.7 17.9 %collective-permute-start.20 = (bf16[32,3584]{1,0:T(8,128)(2,1)S(1)}, bf16[32,3584]{1,0:T(8,128)(2,1)S(1)}, u32[]{:S(2)}, u32[]{:S(2)}) collective-permute-start(bf16[32,3584]{1,0:T(8,128)(2,1)S(1)} %collective-permute-done.19.refs_6_), channel_id=1, source_target_pairs={{0,1},{1,0},{2,3},{3,2},{4,5},{5,4},{6,7},{7,6},{8,10},{9,11},{10,... | collective-permute-start | bytes 688136 | tf_op jit(solution)/shard_map/ppermute | solution.py:331
  69.3 3.5 %copy-start = (bf16[1792,2432]{1,0:T(8,128)(2,1)S(1)}, bf16[1792,2432]{1,0:T(8,128)(2,1)}, u32[]{:S(2)}) copy-start(bf16[1792,2432]{1,0:T(8,128)(2,1)} %refs_8_.1) | copy-start | bytes 26148868
  92.2 4.6 %collective-permute-start.25 = (f32[8,256]{1,0:T(8,128)S(1)}, f32[8,256]{1,0:T(8,128)S(1)}, u32[]{:S(2)}, u32[]{:S(2)}) collective-permute-start(f32[8,256]{1,0:T(8,128)S(1)} %get-tuple-element.60.refs_0_), channel_id=1, source_target_pairs={{0,4},{1,5},{2,6},{3,7},{4,0},{5,1},{6,2},{7,3},{8,12},{9,13},{10,... | collective-permute-start | bytes 24584 | tf_op jit(solution)/shard_map/ppermute | solution.py:331
  92.2 6.9 %collective-permute-start.24 = (f32[8,256]{1,0:T(8,128)S(1)}, f32[8,256]{1,0:T(8,128)S(1)}, u32[]{:S(2)}, u32[]{:S(2)}) collective-permute-start(f32[8,256]{1,0:T(8,128)S(1)} %get-tuple-element.60.refs_0_), channel_id=1, source_target_pairs={{0,3},{1,2},{2,1},{3,0},{4,7},{5,6},{6,5},{7,4},{8,11},{9,10},{10,... | collective-permute-start | bytes 24584 | tf_op jit(solution)/shard_map/ppermute | solution.py:331
  95.6 4.7 %collective-permute-start.23 = (f32[8,256]{1,0:T(8,128)S(1)}, f32[8,256]{1,0:T(8,128)S(1)}, u32[]{:S(2)}, u32[]{:S(2)}) collective-permute-start(f32[8,256]{1,0:T(8,128)S(1)} %get-tuple-element.60.refs_0_), channel_id=1, source_target_pairs={{0,2},{1,3},{2,0},{3,1},{4,6},{5,7},{6,4},{7,5},{8,9},{9,8},{10,11... | collective-permute-start | bytes 24584 | tf_op jit(solution)/shard_map/ppermute | solution.py:331
  95.6 4.7 %collective-permute-start.22 = (f32[8,256]{1,0:T(8,128)S(1)}, f32[8,256]{1,0:T(8,128)S(1)}, u32[]{:S(2)}, u32[]{:S(2)}) collective-permute-start(f32[8,256]{1,0:T(8,128)S(1)} %get-tuple-element.60.refs_0_), channel_id=1, source_target_pairs={{0,1},{1,0},{2,3},{3,2},{4,5},{5,4},{6,7},{7,6},{8,10},{9,11},{10,... | collective-permute-start | bytes 24584 | tf_op jit(solution)/shard_map/ppermute | solution.py:331
  96.7 4.5 %collective-permute-start.28 = (f32[8,256]{1,0:T(8,128)S(1)}, f32[8,256]{1,0:T(8,128)S(1)}, u32[]{:S(2)}, u32[]{:S(2)}) collective-permute-start(f32[8,256]{1,0:T(8,128)S(1)} %collective-permute-done.25.refs_4_), channel_id=1, source_target_pairs={{0,3},{1,2},{2,1},{3,0},{4,7},{5,6},{6,5},{7,4},{8,11},{9,10},{10,... | collective-permute-start | bytes 24584 | tf_op jit(solution)/shard_map/ppermute | solution.py:331
  99.1 3.7 %collective-permute-start.27 = (f32[8,256]{1,0:T(8,128)S(1)}, f32[8,256]{1,0:T(8,128)S(1)}, u32[]{:S(2)}, u32[]{:S(2)}) collective-permute-start(f32[8,256]{1,0:T(8,128)S(1)} %collective-permute-done.25.refs_4_), channel_id=1, source_target_pairs={{0,2},{1,3},{2,0},{3,1},{4,6},{5,7},{6,4},{7,5},{8,9},{9,8},{10,11... | collective-permute-start | bytes 24584 | tf_op jit(solution)/shard_map/ppermute | solution.py:331
  99.1 3.7 %collective-permute-start.26 = (f32[8,256]{1,0:T(8,128)S(1)}, f32[8,256]{1,0:T(8,128)S(1)}, u32[]{:S(2)}, u32[]{:S(2)}) collective-permute-start(f32[8,256]{1,0:T(8,128)S(1)} %collective-permute-done.25.refs_4_), channel_id=1, source_target_pairs={{0,1},{1,0},{2,3},{3,2},{4,5},{5,4},{6,7},{7,6},{8,10},{9,11},{10,... | collective-permute-start | bytes 24584 | tf_op jit(solution)/shard_map/ppermute | solution.py:331
  111.1 6.1 %collective-permute-start.31 = (f16[32,3584]{1,0:T(8,128)(2,1)S(1)}, f16[32,3584]{1,0:T(8,128)(2,1)S(1)}, u32[]{:S(2)}, u32[]{:S(2)}) collective-permute-start(f16[32,3584]{1,0:T(8,128)(2,1)S(1)} %convert_element_type.113), channel_id=1, source_target_pairs={{0,1},{1,0},{2,3},{3,2},{4,5},{5,4},{6,7},{7,6},{8,10},{9,11},{10,... | collective-permute-start | bytes 688136 | tf_op jit(solution)/shard_map/ppermute | solution.py:331
  112.4 7.3 %collective-permute-start.29 = (f16[32,3584]{1,0:T(8,128)(2,1)S(1)}, f16[32,3584]{1,0:T(8,128)(2,1)S(1)}, u32[]{:S(2)}, u32[]{:S(2)}) collective-permute-start(f16[32,3584]{1,0:T(8,128)(2,1)S(1)} %convert_element_type.109), channel_id=1, source_target_pairs={{0,1},{1,0},{2,3},{3,2},{4,5},{5,4},{6,7},{7,6},{8,10},{9,11},{10,... | collective-permute-start | bytes 688136 | tf_op jit(solution)/shard_map/ppermute | solution.py:331
  117.2 16.4 %collective-permute-start.35 = (f16[32,3584]{1,0:T(8,128)(2,1)S(1)}, f16[32,3584]{1,0:T(8,128)(2,1)S(1)}, u32[]{:S(2)}, u32[]{:S(2)}) collective-permute-start(f16[32,3584]{1,0:T(8,128)(2,1)S(1)} %convert_element_type.121), channel_id=1, source_target_pairs={{0,1},{1,0},{2,3},{3,2},{4,5},{5,4},{6,7},{7,6},{8,10},{9,11},{10,... | collective-permute-start | bytes 688136 | tf_op jit(solution)/shard_map/ppermute | solution.py:331
  119.6 10.5 %collective-permute-start.33 = (f16[32,3584]{1,0:T(8,128)(2,1)S(1)}, f16[32,3584]{1,0:T(8,128)(2,1)S(1)}, u32[]{:S(2)}, u32[]{:S(2)}) collective-permute-start(f16[32,3584]{1,0:T(8,128)(2,1)S(1)} %convert_element_type.117), channel_id=1, source_target_pairs={{0,1},{1,0},{2,3},{3,2},{4,5},{5,4},{6,7},{7,6},{8,10},{9,11},{10,... | collective-permute-start | bytes 688136 | tf_op jit(solution)/shard_map/ppermute | solution.py:331
  120.9 10.8 %collective-permute-start.30 = (f16[32,3584]{1,0:T(8,128)(2,1)S(1)}, f16[32,3584]{1,0:T(8,128)(2,1)S(1)}, u32[]{:S(2)}, u32[]{:S(2)}) collective-permute-start(f16[32,3584]{1,0:T(8,128)(2,1)S(1)} %add_convert_fusion.3), channel_id=1, source_target_pairs={{0,2},{1,3},{2,0},{3,1},{4,6},{5,7},{6,4},{7,5},{8,9},{9,8},{10,11... | collective-permute-start | bytes 688136 | tf_op jit(solution)/shard_map/ppermute | solution.py:331
  130.2 6.1 %collective-permute-start.34 = (f16[32,3584]{1,0:T(8,128)(2,1)S(1)}, f16[32,3584]{1,0:T(8,128)(2,1)S(1)}, u32[]{:S(2)}, u32[]{:S(2)}) collective-permute-start(f16[32,3584]{1,0:T(8,128)(2,1)S(1)} %add_convert_fusion.1), channel_id=1, source_target_pairs={{0,2},{1,3},{2,0},{3,1},{4,6},{5,7},{6,4},{7,5},{8,9},{9,8},{10,11... | collective-permute-start | bytes 688136 | tf_op jit(solution)/shard_map/ppermute | solution.py:331
  131.7 9.4 %collective-permute-start.32 = (f16[32,3584]{1,0:T(8,128)(2,1)S(1)}, f16[32,3584]{1,0:T(8,128)(2,1)S(1)}, u32[]{:S(2)}, u32[]{:S(2)}) collective-permute-start(f16[32,3584]{1,0:T(8,128)(2,1)S(1)} %add_convert_fusion.2), channel_id=1, source_target_pairs={{0,4},{1,5},{2,6},{3,7},{4,0},{5,1},{6,2},{7,3},{8,12},{9,13},{10,... | collective-permute-start | bytes 688136 | tf_op jit(solution)/shard_map/ppermute | solution.py:331

commit v10 on v4

--- a/solution.py
+++ b/solution.py
@@ -293,7 +293,7 @@
 def gradient(place, tables, scaled_teach, scaled_stud, column, head, bits, chunk):
     rows, vocab_dev = scaled_teach.shape
     count, width = 1 << bits, head.shape[0]
-    step = 512 if width % 512 == 0 else width
+    step = 896 if width % 896 == 0 else width
     return pl.pallas_call(
         functools.partial(gradient_kernel, bits, step, chunk),
         in_specs=[in_smem] + [in_vmem] * (count + 4),
@@ -318,16 +318,19 @@
     bits = vocab_size.bit_length() - 1
     assert vocab_size == 1 << bits
 
+    def trade(block, mask):
+        return lax.ppermute(block, "vocab", [(at, at ^ mask) for at in range(vocab_size)])
+
     def swap(block, bit):
-        return lax.ppermute(block, "vocab", [(at, at ^ (1 << bit)) for at in range(vocab_size)])
+        return trade(block, 1 << bit)
 
     def lowest(mask):
         return (mask & -mask).bit_length() - 1
 
-    def spread(own, line):
+    def spread(own, line, around):
         blocks = [own]
         for mask in range(1, vocab_size):
-            bit = lowest(mask)
+            bit = 1 if around and mask & 3 == 3 and mask > 3 else lowest(mask)
             block = blocks[mask ^ (1 << bit)]
             if bit == 0:
                 block = tie(block, line[-3])
@@ -379,16 +382,16 @@
         member = (owner[None, :] == row_id[:, None]) & alive[None, :]
         parts = project(member.astype(jnp.bfloat16), teacher_rows, proj_weight, vocab_size, 512 if student_hidden.shape[1] % 512 == 0 else student_hidden.shape[1])
         projected_own, line = reduce_blocks(parts)
-        hidden = spread(tie(turned(student_hidden), parts[-1]), line)
-        projected = spread(turned(projected_own.astype(jnp.bfloat16)), line)
+        hidden = spread(tie(turned(student_hidden), parts[-1]), line, True)
+        projected = spread(turned(projected_own.astype(jnp.bfloat16)), line, False)
 
         column = (in_order(targets) - me * vocab_dev)[:, None]
         logit_stud, scaled_stud, stats_stud, head = student_logits(as_pieces(hidden), heads, column, 256, chunk)
-        scaled_teach, stats = teacher_logits(as_pieces(projected), head, logit_stud, stats_stud, 512, chunk)
-        tables = [stats] + [
-            lax.ppermute(stats, "vocab", [(at, at ^ mask) for at in range(vocab_size)])
-            for mask in range(1, vocab_size)
-        ]
+        scaled_teach, stats = teacher_logits(as_pieces(projected), head, logit_stud, stats_stud, 1024, chunk)
+        tables = [stats]
+        for mask in range(1, vocab_size):
+            far, near = mask & ~3, mask & 3
+            tables.append(trade(tables[far], near) if near else trade(stats, far))
         loss, *terms = gradient(place, tables, scaled_teach, scaled_stud, column, head, bits, chunk)
         return (loss[0], turned(reduce_blocks(terms)[0].astype(jnp.bfloat16)))
 

time: 138 us -> 142 us (1.029)
  waiting for transfers between devices: 39 us -> 48.4 us
  starting transfers between devices: 55.3 us -> 49.5 us
    ppermute x35, waiting for transfers between devices: 39 us -> 48.4 us  [trade(): lax.ppermute(block, 'vocab', [(at, at ^ mask) for at in range(vocab_size)])]
    ppermute x35, starting transfers between devices: 54.8 us -> 49 us  [trade(): lax.ppermute(block, 'vocab', [(at, at ^ mask) for at in range(vocab_size)])]
  transfers between devices with their start and end apart: 36 -> 36, of which waited for: 17 -> 20; matrix products, arithmetic and copies ran while one was open for 4% -> 4% of each run, Pallas kernels for 12% -> 12%
where the time goes in v10:
time: 142 us; the launch traced here: 141 us
  starting transfers between devices  49.5 us (35%)
  waiting for transfers between devices  48.4 us (34%)
  Pallas kernels  32.3 us (23%)
  other arithmetic  5.19 us (4%)
  local copies, waits for them, and re-layouts  4.35 us (3%)
  between operations  1.51 us (1%)
    ppermute x35, starting transfers between devices, trade(): lax.ppermute(block, 'vocab', [(at, at ^ mask) for at in range(vocab_size)])  49 us
    ppermute x35, waiting for transfers between devices, trade(): lax.ppermute(block, 'vocab', [(at, at ^ mask) for at in range(vocab_size)])  48.4 us
    pallas_call x1, Pallas kernels, student_logits(): pl.pallas_call(functools.partial(student_kernel, len(pieces), step, chunk...  11.9 us
    pallas_call x1, Pallas kernels, gradient(): pl.pallas_call(functools.partial(gradient_kernel, bits, step, chunk), in_...  8.4 us
    pallas_call x1, Pallas kernels, teacher_logits(): pl.pallas_call(functools.partial(teacher_kernel, len(pieces), step, chunk...  7.15 us
    pallas_call x1, Pallas kernels, project(): pl.pallas_call(functools.partial(project_kernel, count, step), in_specs=[...  4.83 us
    unnamed x6, local copies, waits for them, and re-layouts  3.49 us
  transfers between devices with their start and end apart: 36, of which 20 were waited for; matrix products, arithmetic and copies ran while one was open for 4% of the time, Pallas kernels for 12%

profile of v10, /device:TPU:0, one launch (start us, length us, event | category | flops | bytes accessed | tf_op | source)
XLA Modules:
  0.0 141.3 jit_solution(1311039547571172483)
XLA Ops:
  0.6 0.5 collective-permute-start.21
  1.8 0.8 and_convert_fusion.member_ref
  2.7 4.8 %shard_map.86 = (f32[32,3584]{1,0:T(8,128)S(1)}, f32[32,3584]{1,0:T(8,128)S(1)}, f32[32,3584]{1,0:T(8,128)S(1)}, f32[32,3584]{1,0:T(8,128)S(1)}, f32[32,3584]{1,...) custom-call(bf16[256,512]{1,0:T(8,128)(2,1)S(1)} %and_convert_fusion.member_ref, ...), custom_call_target="tpu_custom_call" | custom-call | flops 2147483648 | bytes 12058624 | tf_op jit(solution)/shard_map/pallas_call | solution.py:54
  7.5 0.7 convert_element_type.94
  8.2 2.6 %collective-permute-start = (f16[32,3584]{1,0:T(8,128)(2,1)}, f16[32,3584]{1,0:T(8,128)(2,1)}, u32[]{:S(2)}, u32[]{:S(2)}) collective-permute-start(f16[32,3584]{1,0:T(8,128)(2,1)} %convert_element_type.94), channel_id=1, source_target_pairs={{0,1},{1,0},{2,3},{3,2},{4,5},{5,4},{6,7},{7,6},{8,9},{9,8},{10,11... | collective-permute-start | bytes 688136 | tf_op jit(solution)/shard_map/ppermute | solution.py:322
  10.8 1.0 maximum_select_fusion.1.refs_0_
  11.8 2.7 %collective-permute-start.14 = (bf16[32,3584]{1,0:T(8,128)(2,1)S(1)}, bf16[32,3584]{1,0:T(8,128)(2,1)}, u32[]{:S(2)}, u32[]{:S(2)}) collective-permute-start(bf16[32,3584]{1,0:T(8,128)(2,1)S(1)} %maximum_select_fusion.1.refs_0_), channel_id=1, source_target_pairs={{0,4},{1,5},{2,6},{3,7},{4,0},{5,1},{6,2},{7,3},{8,12},{9,13},{10,... | collective-permute-start | bytes 688136 | tf_op jit(solution)/shard_map/ppermute | solution.py:322
  14.5 1.6 %collective-permute-start.10 = (bf16[32,3584]{1,0:T(8,128)(2,1)S(1)}, bf16[32,3584]{1,0:T(8,128)(2,1)}, u32[]{:S(2)}, u32[]{:S(2)}) collective-permute-start(bf16[32,3584]{1,0:T(8,128)(2,1)S(1)} %maximum_select_fusion.1.refs_0_), channel_id=1, source_target_pairs={{0,2},{1,3},{2,0},{3,1},{4,6},{5,7},{6,4},{7,5},{8,10},{9,11},{10,... | collective-permute-start | bytes 688136 | tf_op jit(solution)/shard_map/ppermute | solution.py:322
  16.1 0.6 collective-permute-start.2
  16.7 0.6 collective-permute-done
  17.3 2.2 %collective-permute-start.4 = (f16[32,3584]{1,0:T(8,128)(2,1)S(1)}, f16[32,3584]{1,0:T(8,128)(2,1)S(1)}, u32[]{:S(2)}, u32[]{:S(2)}) collective-permute-start(f16[32,3584]{1,0:T(8,128)(2,1)S(1)} %convert_element_type.102), channel_id=1, source_target_pairs={{0,1},{1,0},{2,3},{3,2},{4,5},{5,4},{6,7},{7,6},{8,9},{9,8},{10,11... | collective-permute-start | bytes 688136 | tf_op jit(solution)/shard_map/ppermute | solution.py:322
  19.5 1.0 add_convert_fusion.7
  20.5 4.2 %collective-permute-done.2 = f16[32,3584]{1,0:T(8,128)(2,1)S(1)} collective-permute-done((f16[32,3584]{1,0:T(8,128)(2,1)S(1)}, f16[32,3584]{1,0:T(8,128)(2,1)S(1)}, u32[]{:S(2)}, u32[]{:S(2)}) %collective-permute-start.2) | collective-permute-done | bytes 229408 | tf_op jit(solution)/shard_map/ppermute | solution.py:322
  24.7 0.4 collective-permute-start.1
  25.1 2.1 %collective-permute-done.4 = f16[32,3584]{1,0:T(8,128)(2,1)S(1)} collective-permute-done((f16[32,3584]{1,0:T(8,128)(2,1)S(1)}, f16[32,3584]{1,0:T(8,128)(2,1)S(1)}, u32[]{:S(2)}, u32[]{:S(2)}) %collective-permute-start.4) | collective-permute-done | bytes 229408 | tf_op jit(solution)/shard_map/ppermute | solution.py:322
  27.3 1.5 %collective-permute-start.6 = (f16[32,3584]{1,0:T(8,128)(2,1)S(1)}, f16[32,3584]{1,0:T(8,128)(2,1)S(1)}, u32[]{:S(2)}, u32[]{:S(2)}) collective-permute-start(f16[32,3584]{1,0:T(8,128)(2,1)S(1)} %convert_element_type.106), channel_id=1, source_target_pairs={{0,1},{1,0},{2,3},{3,2},{4,5},{5,4},{6,7},{7,6},{8,9},{9,8},{10,11... | collective-permute-start | bytes 688136 | tf_op jit(solution)/shard_map/ppermute | solution.py:322
  28.9 1.9 %collective-permute-done.1 = f16[32,3584]{1,0:T(8,128)(2,1)S(1)} collective-permute-done((f16[32,3584]{1,0:T(8,128)(2,1)S(1)}, f16[32,3584]{1,0:T(8,128)(2,1)S(1)}, u32[]{:S(2)}, u32[]{:S(2)}) %collective-permute-start.1) | collective-permute-done | bytes 229408 | tf_op jit(solution)/shard_map/ppermute | solution.py:322
  30.7 0.4 collective-permute-start.5
  31.3 2.7 %collective-permute-start.3 = (f16[32,3584]{1,0:T(8,128)(2,1)S(1)}, f16[32,3584]{1,0:T(8,128)(2,1)S(1)}, u32[]{:S(2)}, u32[]{:S(2)}) collective-permute-start(f16[32,3584]{1,0:T(8,128)(2,1)S(1)} %add_convert_fusion.6), channel_id=1, source_target_pairs={{0,4},{1,5},{2,6},{3,7},{4,0},{5,1},{6,2},{7,3},{8,12},{9,13},{10,... | collective-permute-start | bytes 688136 | tf_op jit(solution)/shard_map/ppermute | solution.py:322
  34.0 1.5 %collective-permute-start.7 = (bf16[32,3584]{1,0:T(8,128)(2,1)S(1)}, bf16[32,3584]{1,0:T(8,128)(2,1)S(1)}, u32[]{:S(2)}, u32[]{:S(2)}) collective-permute-start(bf16[32,3584]{1,0:T(8,128)(2,1)S(1)} %maximum_select_fusion.1.refs_0_), channel_id=1, source_target_pairs={{0,1},{1,0},{2,3},{3,2},{4,5},{5,4},{6,7},{7,6},{8,9},{9,8},{10,11... | collective-permute-start | bytes 688136 | tf_op jit(solution)/shard_map/ppermute | solution.py:322
  35.5 0.5 collective-permute-start.15
  36.0 4.4 %collective-permute-done.5 = f16[32,3584]{1,0:T(8,128)(2,1)S(1)} collective-permute-done((f16[32,3584]{1,0:T(8,128)(2,1)S(1)}, f16[32,3584]{1,0:T(8,128)(2,1)S(1)}, u32[]{:S(2)}, u32[]{:S(2)}) %collective-permute-start.5) | collective-permute-done | bytes 229408 | tf_op jit(solution)/shard_map/ppermute | solution.py:322
  40.4 1.0 collective-permute-start.11
  41.4 1.9 %collective-permute-done.3 = f16[32,3584]{1,0:T(8,128)(2,1)S(1)} collective-permute-done((f16[32,3584]{1,0:T(8,128)(2,1)S(1)}, f16[32,3584]{1,0:T(8,128)(2,1)S(1)}, u32[]{:S(2)}, u32[]{:S(2)}) %collective-permute-start.3) | collective-permute-done | bytes 229408 | tf_op jit(solution)/shard_map/ppermute | solution.py:322
  43.6 2.9 %collective-permute-start.9 = (bf16[32,3584]{1,0:T(8,128)(2,1)S(1)}, bf16[32,3584]{1,0:T(8,128)(2,1)S(1)}, u32[]{:S(2)}, u32[]{:S(2)}) collective-permute-start(bf16[32,3584]{1,0:T(8,128)(2,1)S(1)} %maximum_select_fusion.refs_0_), channel_id=1, source_target_pairs={{0,2},{1,3},{2,0},{3,1},{4,6},{5,7},{6,4},{7,5},{8,10},{9,11},{10,... | collective-permute-start | bytes 688136 | tf_op jit(solution)/shard_map/ppermute | solution.py:322
  46.6 0.4 collective-permute-done.15.refs_5_
  47.0 2.3 %collective-permute-start.19 = (bf16[32,3584]{1,0:T(8,128)(2,1)}, bf16[32,3584]{1,0:T(8,128)(2,1)S(1)}, u32[]{:S(2)}, u32[]{:S(2)}) collective-permute-start(bf16[32,3584]{1,0:T(8,128)(2,1)} %collective-permute-done.14.refs_4_), channel_id=1, source_target_pairs={{0,2},{1,3},{2,0},{3,1},{4,6},{5,7},{6,4},{7,5},{8,10},{9,11},{10,... | collective-permute-start | bytes 688136 | tf_op jit(solution)/shard_map/ppermute | solution.py:322
  49.3 0.3 collective-permute-done.11.refs_3_
  49.6 1.5 %collective-permute-start.8 = (bf16[32,3584]{1,0:T(8,128)(2,1)S(1)}, bf16[32,3584]{1,0:T(8,128)(2,1)S(1)}, u32[]{:S(2)}, u32[]{:S(2)}) collective-permute-start(bf16[32,3584]{1,0:T(8,128)(2,1)S(1)} %maximum_select_fusion.refs_0_), channel_id=1, source_target_pairs={{0,1},{1,0},{2,3},{3,2},{4,5},{5,4},{6,7},{7,6},{8,9},{9,8},{10,11... | collective-permute-start | bytes 688136 | tf_op jit(solution)/shard_map/ppermute | solution.py:322
  51.1 1.9 %collective-permute-done.13.refs_4_ = bf16[32,3584]{1,0:T(8,128)(2,1)S(1)} collective-permute-done((bf16[32,3584]{1,0:T(8,128)(2,1)S(1)}, bf16[32,3584]{1,0:T(8,128)(2,1)S(1)}, u32[]{:S(2)}, u32[]{:S(2)}) %collective-permute-start.13) | collective-permute-done | bytes 229408 | tf_op jit(solution)/shard_map/ppermute | solution.py:322
  53.0 0.7 collective-permute-start.17
  53.7 2.0 %collective-permute-done.9.refs_2_ = bf16[32,3584]{1,0:T(8,128)(2,1)S(1)} collective-permute-done((bf16[32,3584]{1,0:T(8,128)(2,1)S(1)}, bf16[32,3584]{1,0:T(8,128)(2,1)S(1)}, u32[]{:S(2)}, u32[]{:S(2)}) %collective-permute-start.9) | collective-permute-done | bytes 229408 | tf_op jit(solution)/shard_map/ppermute | solution.py:322
  55.7 1.4 collective-permute-start.20
  57.1 2.1 %collective-permute-start.16 = (bf16[32,3584]{1,0:T(8,128)(2,1)S(1)}, bf16[32,3584]{1,0:T(8,128)(2,1)S(1)}, u32[]{:S(2)}, u32[]{:S(2)}) collective-permute-start(bf16[32,3584]{1,0:T(8,128)(2,1)S(1)} %collective-permute-done.13.refs_4_), channel_id=1, source_target_pairs={{0,1},{1,0},{2,3},{3,2},{4,5},{5,4},{6,7},{7,6},{8,9},{9,8},{10,11... | collective-permute-start | bytes 688136 | tf_op jit(solution)/shard_map/ppermute | solution.py:322
  59.1 6.1 %collective-permute-done.17.refs_6_ = bf16[32,3584]{1,0:T(8,128)(2,1)S(1)} collective-permute-done((bf16[32,3584]{1,0:T(8,128)(2,1)S(1)}, bf16[32,3584]{1,0:T(8,128)(2,1)S(1)}, u32[]{:S(2)}, u32[]{:S(2)}) %collective-permute-start.17) | collective-permute-done | bytes 229408 | tf_op jit(solution)/shard_map/ppermute | solution.py:322
  65.3 1.3 collective-permute-start.12
  66.6 0.7 collective-permute-start.18
  67.4 0.3 collective-permute-done.20.refs_7_
  67.7 3.5 %copy-done = bf16[1792,2432]{1,0:T(8,128)(2,1)S(1)} copy-done((bf16[1792,2432]{1,0:T(8,128)(2,1)S(1)}, bf16[1792,2432]{1,0:T(8,128)(2,1)}, u32[]{:S(2)}) %copy-start) | copy-done | bytes 8716312
  71.2 11.9 %shard_map.87 = (f32[256,2432]{1,0:T(8,128)S(1)}, f32[256,2432]{1,0:T(8,128)S(1)}, f32[8,256]{1,0:T(8,128)S(1)}, bf16[3584,2432]{1,0:T(8,128)(2,1)S(1)}) custom-call(bf16[32,3584]{1,0:T(8,128)(2,1)S(1)} %maximum_select_fusion.1.refs_0_, bf16[32,3584]{1,0:T(8,128)(2,1)S(1)} %collective-permute-done.7.refs_1_, ...), custom_call_target="tpu_custom_call" | custom-call | flops 2231369728 | bytes 16187392 | tf_op jit(solution)/shard_map/pallas_call | solution.py:192
  83.1 7.1 %shard_map.88 = (f32[256,2432]{1,0:T(8,128)S(1)}, f32[8,256]{1,0:T(8,128)S(1)}) custom-call(bf16[32,3584]{1,0:T(8,128)(2,1)S(1)} %maximum_select_fusion.refs_0_, bf16[32,3584]{1,0:T(8,128)(2,1)S(1)} %collective-permute-done.8.refs_1_, bf16[32,3584]{1,0:T(8,128)(2,1)S(1)} %collective-permute-done.9.refs_2_, ...), custom_call_target="tpu_custom_call" | custom-call | flops 4462739456 | bytes 24903680 | tf_op jit(solution)/shard_map/pallas_call | solution.py:215
  90.3 1.8 %collective-permute-start.25 = (f32[8,256]{1,0:T(8,128)S(1)}, f32[8,256]{1,0:T(8,128)S(1)}, u32[]{:S(2)}, u32[]{:S(2)}) collective-permute-start(f32[8,256]{1,0:T(8,128)S(1)} %get-tuple-element.58.refs_0_), channel_id=1, source_target_pairs={{0,4},{1,5},{2,6},{3,7},{4,0},{5,1},{6,2},{7,3},{8,12},{9,13},{10,... | collective-permute-start | bytes 24584 | tf_op jit(solution)/shard_map/ppermute | solution.py:322
  92.1 2.5 %collective-permute-start.24 = (f32[8,256]{1,0:T(8,128)S(1)}, f32[8,256]{1,0:T(8,128)S(1)}, u32[]{:S(2)}, u32[]{:S(2)}) collective-permute-start(f32[8,256]{1,0:T(8,128)S(1)} %get-tuple-element.58.refs_0_), channel_id=1, source_target_pairs={{0,3},{1,2},{2,1},{3,0},{4,7},{5,6},{6,5},{7,4},{8,11},{9,10},{10,... | collective-permute-start | bytes 24584 | tf_op jit(solution)/shard_map/ppermute | solution.py:322
  94.6 1.0 collective-permute-start.22
  95.6 2.5 %collective-permute-start.28 = (f32[8,256]{1,0:T(8,128)S(1)}, f32[8,256]{1,0:T(8,128)S(1)}, u32[]{:S(2)}, u32[]{:S(2)}) collective-permute-start(f32[8,256]{1,0:T(8,128)S(1)} %collective-permute-done.25.refs_4_), channel_id=1, source_target_pairs={{0,3},{1,2},{2,1},{3,0},{4,7},{5,6},{6,5},{7,4},{8,11},{9,10},{10,... | collective-permute-start | bytes 24584 | tf_op jit(solution)/shard_map/ppermute | solution.py:322
  98.1 1.0 collective-permute-start.26
  99.2 1.0 collective-permute-done.28.refs_7_
  100.1 1.6 %collective-permute-done.27.refs_6_ = f32[8,256]{1,0:T(8,128)S(1)} collective-permute-done((f32[8,256]{1,0:T(8,128)S(1)}, f32[8,256]{1,0:T(8,128)S(1)}, u32[]{:S(2)}, u32[]{:S(2)}) %collective-permute-start.27) | collective-permute-done | bytes 8224 | tf_op jit(solution)/shard_map/ppermute | solution.py:322
  101.8 8.4 %shard_map.89 = (f32[8,256]{1,0:T(8,128)S(1)}, f32[32,3584]{1,0:T(8,128)S(1)}, f32[32,3584]{1,0:T(8,128)S(1)}, f32[32,3584]{1,0:T(8,128)S(1)}, f32[32,3584]{1,0:...) custom-call(s32[2]{0:T(128)S(1)} %pad_add_fusion.place_ref, ...), custom_call_target="tpu_custom_call" | custom-call | flops 4462739456 | bytes 24903680 | tf_op jit(solution)/shard_map/pallas_call | solution.py:297
  110.2 1.0 collective-permute-start.31
  111.3 1.1 collective-permute-start.29
  112.5 6.4 %collective-permute-done.31 = f16[32,3584]{1,0:T(8,128)(2,1)S(1)} collective-permute-done((f16[32,3584]{1,0:T(8,128)(2,1)S(1)}, f16[32,3584]{1,0:T(8,128)(2,1)S(1)}, u32[]{:S(2)}, u32[]{:S(2)}) %collective-permute-start.31) | collective-permute-done | bytes 229408 | tf_op jit(solution)/shard_map/ppermute | solution.py:322
  118.8 1.0 collective-permute-start.35
  119.8 2.4 %collective-permute-done.29 = f16[32,3584]{1,0:T(8,128)(2,1)S(1)} collective-permute-done((f16[32,3584]{1,0:T(8,128)(2,1)S(1)}, f16[32,3584]{1,0:T(8,128)(2,1)S(1)}, u32[]{:S(2)}, u32[]{:S(2)}) %collective-permute-start.29) | collective-permute-done | bytes 229408 | tf_op jit(solution)/shard_map/ppermute | solution.py:322
  122.2 1.2 collective-permute-start.33
  123.5 2.1 %collective-permute-start.30 = (f16[32,3584]{1,0:T(8,128)(2,1)S(1)}, f16[32,3584]{1,0:T(8,128)(2,1)S(1)}, u32[]{:S(2)}, u32[]{:S(2)}) collective-permute-start(f16[32,3584]{1,0:T(8,128)(2,1)S(1)} %add_convert_fusion.3), channel_id=1, source_target_pairs={{0,2},{1,3},{2,0},{3,1},{4,6},{5,7},{6,4},{7,5},{8,10},{9,11},{10,... | collective-permute-start | bytes 688136 | tf_op jit(solution)/shard_map/ppermute | solution.py:322
  125.5 2.7 %collective-permute-done.33 = f16[32,3584]{1,0:T(8,128)(2,1)S(1)} collective-permute-done((f16[32,3584]{1,0:T(8,128)(2,1)S(1)}, f16[32,3584]{1,0:T(8,128)(2,1)S(1)}, u32[]{:S(2)}, u32[]{:S(2)}) %collective-permute-start.33) | collective-permute-done | bytes 229408 | tf_op jit(solution)/shard_map/ppermute | solution.py:322
  128.3 1.5 %collective-permute-start.34 = (f16[32,3584]{1,0:T(8,128)(2,1)S(1)}, f16[32,3584]{1,0:T(8,128)(2,1)S(1)}, u32[]{:S(2)}, u32[]{:S(2)}) collective-permute-start(f16[32,3584]{1,0:T(8,128)(2,1)S(1)} %add_convert_fusion.1), channel_id=1, source_target_pairs={{0,2},{1,3},{2,0},{3,1},{4,6},{5,7},{6,4},{7,5},{8,10},{9,11},{10,... | collective-permute-start | bytes 688136 | tf_op jit(solution)/shard_map/ppermute | solution.py:322
  129.8 1.0 collective-permute-done.30
  131.0 1.7 %collective-permute-start.32 = (f16[32,3584]{1,0:T(8,128)(2,1)S(1)}, f16[32,3584]{1,0:T(8,128)(2,1)S(1)}, u32[]{:S(2)}, u32[]{:S(2)}) collective-permute-start(f16[32,3584]{1,0:T(8,128)(2,1)S(1)} %add_convert_fusion.2), channel_id=1, source_target_pairs={{0,4},{1,5},{2,6},{3,7},{4,0},{5,1},{6,2},{7,3},{8,12},{9,13},{10,... | collective-permute-start | bytes 688136 | tf_op jit(solution)/shard_map/ppermute | solution.py:322
  132.6 0.6 slice.27
  133.2 1.2 collective-permute-done.34
  134.4 6.0 %collective-permute-done.32 = f16[32,3584]{1,0:T(8,128)(2,1)S(1)} collective-permute-done((f16[32,3584]{1,0:T(8,128)(2,1)S(1)}, f16[32,3584]{1,0:T(8,128)(2,1)S(1)}, u32[]{:S(2)}, u32[]{:S(2)}) %collective-permute-start.32) | collective-permute-done | bytes 229408 | tf_op jit(solution)/shard_map/ppermute | solution.py:322
  140.5 0.8 maximum_select_fusion.2
  (51 shorter events, 1.4 us)
Async XLA Ops:
  0.6 10.2 %copy-start.1 = (bf16[32,3584]{1,0:T(8,128)(2,1)S(1)}, bf16[32,3584]{1,0:T(8,128)(2,1)}, u32[]{:S(2)}) copy-start(bf16[32,3584]{1,0:T(8,128)(2,1)} %param.11) | copy-start | bytes 688132
  0.6 67.1 %collective-permute-start.21 = (bf16[1792,2432]{1,0:T(8,128)(2,1)}, bf16[1792,2432]{1,0:T(8,128)(2,1)}, u32[]{:S(2)}, u32[]{:S(2)}) collective-permute-start(bf16[1792,2432]{1,0:T(8,128)(2,1)} %refs_8_.1), channel_id=1, source_target_pairs={{0,8},{8,0},{1,9},{9,1},{2,10},{10,2},{3,11},{11,3},{4,12},{12,4},... | collective-permute-start | bytes 26148872 | tf_op jit(solution)/shard_map/ppermute | solution.py:377
  2.7 43.8 %copy-start.2 = (s32[256]{0:T(256)S(1)}, s32[256]{0:T(256)}, u32[]{:S(2)}) copy-start(s32[256]{0:T(256)} %param.13) | copy-start | bytes 3076
  8.2 9.1 %collective-permute-start = (f16[32,3584]{1,0:T(8,128)(2,1)}, f16[32,3584]{1,0:T(8,128)(2,1)}, u32[]{:S(2)}, u32[]{:S(2)}) collective-permute-start(f16[32,3584]{1,0:T(8,128)(2,1)} %convert_element_type.94), channel_id=1, source_target_pairs={{0,1},{1,0},{2,3},{3,2},{4,5},{5,4},{6,7},{7,6},{8,9},{9,8},{10,11... | collective-permute-start | bytes 688136 | tf_op jit(solution)/shard_map/ppermute | solution.py:322
  11.8 19.4 %collective-permute-start.14 = (bf16[32,3584]{1,0:T(8,128)(2,1)S(1)}, bf16[32,3584]{1,0:T(8,128)(2,1)}, u32[]{:S(2)}, u32[]{:S(2)}) collective-permute-start(bf16[32,3584]{1,0:T(8,128)(2,1)S(1)} %maximum_select_fusion.1.refs_0_), channel_id=1, source_target_pairs={{0,4},{1,5},{2,6},{3,7},{4,0},{5,1},{6,2},{7,3},{8,12},{9,13},{10,... | collective-permute-start | bytes 688136 | tf_op jit(solution)/shard_map/ppermute | solution.py:322
  14.5 21.0 %collective-permute-start.10 = (bf16[32,3584]{1,0:T(8,128)(2,1)S(1)}, bf16[32,3584]{1,0:T(8,128)(2,1)}, u32[]{:S(2)}, u32[]{:S(2)}) collective-permute-start(bf16[32,3584]{1,0:T(8,128)(2,1)S(1)} %maximum_select_fusion.1.refs_0_), channel_id=1, source_target_pairs={{0,2},{1,3},{2,0},{3,1},{4,6},{5,7},{6,4},{7,5},{8,10},{9,11},{10,... | collective-permute-start | bytes 688136 | tf_op jit(solution)/shard_map/ppermute | solution.py:322
  16.1 8.6 %collective-permute-start.2 = (f16[32,3584]{1,0:T(8,128)(2,1)S(1)}, f16[32,3584]{1,0:T(8,128)(2,1)S(1)}, u32[]{:S(2)}, u32[]{:S(2)}) collective-permute-start(f16[32,3584]{1,0:T(8,128)(2,1)S(1)} %convert_element_type.98), channel_id=1, source_target_pairs={{0,1},{1,0},{2,3},{3,2},{4,5},{5,4},{6,7},{7,6},{8,9},{9,8},{10,11... | collective-permute-start | bytes 688136 | tf_op jit(solution)/shard_map/ppermute | solution.py:322
  17.3 9.9 %collective-permute-start.4 = (f16[32,3584]{1,0:T(8,128)(2,1)S(1)}, f16[32,3584]{1,0:T(8,128)(2,1)S(1)}, u32[]{:S(2)}, u32[]{:S(2)}) collective-permute-start(f16[32,3584]{1,0:T(8,128)(2,1)S(1)} %convert_element_type.102), channel_id=1, source_target_pairs={{0,1},{1,0},{2,3},{3,2},{4,5},{5,4},{6,7},{7,6},{8,9},{9,8},{10,11... | collective-permute-start | bytes 688136 | tf_op jit(solution)/shard_map/ppermute | solution.py:322
  24.7 6.0 %collective-permute-start.1 = (f16[32,3584]{1,0:T(8,128)(2,1)S(1)}, f16[32,3584]{1,0:T(8,128)(2,1)S(1)}, u32[]{:S(2)}, u32[]{:S(2)}) collective-permute-start(f16[32,3584]{1,0:T(8,128)(2,1)S(1)} %add_convert_fusion.7), channel_id=1, source_target_pairs={{0,2},{1,3},{2,0},{3,1},{4,6},{5,7},{6,4},{7,5},{8,10},{9,11},{10,... | collective-permute-start | bytes 688136 | tf_op jit(solution)/shard_map/ppermute | solution.py:322
  27.3 6.7 %collective-permute-start.6 = (f16[32,3584]{1,0:T(8,128)(2,1)S(1)}, f16[32,3584]{1,0:T(8,128)(2,1)S(1)}, u32[]{:S(2)}, u32[]{:S(2)}) collective-permute-start(f16[32,3584]{1,0:T(8,128)(2,1)S(1)} %convert_element_type.106), channel_id=1, source_target_pairs={{0,1},{1,0},{2,3},{3,2},{4,5},{5,4},{6,7},{7,6},{8,9},{9,8},{10,11... | collective-permute-start | bytes 688136 | tf_op jit(solution)/shard_map/ppermute | solution.py:322
  30.7 9.7 %collective-permute-start.5 = (f16[32,3584]{1,0:T(8,128)(2,1)S(1)}, f16[32,3584]{1,0:T(8,128)(2,1)S(1)}, u32[]{:S(2)}, u32[]{:S(2)}) collective-permute-start(f16[32,3584]{1,0:T(8,128)(2,1)S(1)} %add_convert_fusion.5), channel_id=1, source_target_pairs={{0,2},{1,3},{2,0},{3,1},{4,6},{5,7},{6,4},{7,5},{8,10},{9,11},{10,... | collective-permute-start | bytes 688136 | tf_op jit(solution)/shard_map/ppermute | solution.py:322
  31.3 12.0 %collective-permute-start.3 = (f16[32,3584]{1,0:T(8,128)(2,1)S(1)}, f16[32,3584]{1,0:T(8,128)(2,1)S(1)}, u32[]{:S(2)}, u32[]{:S(2)}) collective-permute-start(f16[32,3584]{1,0:T(8,128)(2,1)S(1)} %add_convert_fusion.6), channel_id=1, source_target_pairs={{0,4},{1,5},{2,6},{3,7},{4,0},{5,1},{6,2},{7,3},{8,12},{9,13},{10,... | collective-permute-start | bytes 688136 | tf_op jit(solution)/shard_map/ppermute | solution.py:322
  34.0 9.6 %collective-permute-start.7 = (bf16[32,3584]{1,0:T(8,128)(2,1)S(1)}, bf16[32,3584]{1,0:T(8,128)(2,1)S(1)}, u32[]{:S(2)}, u32[]{:S(2)}) collective-permute-start(bf16[32,3584]{1,0:T(8,128)(2,1)S(1)} %maximum_select_fusion.1.refs_0_), channel_id=1, source_target_pairs={{0,1},{1,0},{2,3},{3,2},{4,5},{5,4},{6,7},{7,6},{8,9},{9,8},{10,11... | collective-permute-start | bytes 688136 | tf_op jit(solution)/shard_map/ppermute | solution.py:322
  35.5 11.5 %collective-permute-start.15 = (bf16[32,3584]{1,0:T(8,128)(2,1)}, bf16[32,3584]{1,0:T(8,128)(2,1)S(1)}, u32[]{:S(2)}, u32[]{:S(2)}) collective-permute-start(bf16[32,3584]{1,0:T(8,128)(2,1)} %collective-permute-done.14.refs_4_), channel_id=1, source_target_pairs={{0,1},{1,0},{2,3},{3,2},{4,5},{5,4},{6,7},{7,6},{8,9},{9,8},{10,11... | collective-permute-start | bytes 688136 | tf_op jit(solution)/shard_map/ppermute | solution.py:322
  40.4 9.2 %collective-permute-start.11 = (bf16[32,3584]{1,0:T(8,128)(2,1)}, bf16[32,3584]{1,0:T(8,128)(2,1)S(1)}, u32[]{:S(2)}, u32[]{:S(2)}) collective-permute-start(bf16[32,3584]{1,0:T(8,128)(2,1)} %collective-permute-done.10.refs_2_), channel_id=1, source_target_pairs={{0,1},{1,0},{2,3},{3,2},{4,5},{5,4},{6,7},{7,6},{8,9},{9,8},{10,11... | collective-permute-start | bytes 688136 | tf_op jit(solution)/shard_map/ppermute | solution.py:322
  43.5 9.5 %collective-permute-start.13 = (bf16[32,3584]{1,0:T(8,128)(2,1)S(1)}, bf16[32,3584]{1,0:T(8,128)(2,1)S(1)}, u32[]{:S(2)}, u32[]{:S(2)}) collective-permute-start(bf16[32,3584]{1,0:T(8,128)(2,1)S(1)} %maximum_select_fusion.refs_0_), channel_id=1, source_target_pairs={{0,4},{1,5},{2,6},{3,7},{4,0},{5,1},{6,2},{7,3},{8,12},{9,13},{10,... | collective-permute-start | bytes 688136 | tf_op jit(solution)/shard_map/ppermute | solution.py:322
  43.6 12.1 %collective-permute-start.9 = (bf16[32,3584]{1,0:T(8,128)(2,1)S(1)}, bf16[32,3584]{1,0:T(8,128)(2,1)S(1)}, u32[]{:S(2)}, u32[]{:S(2)}) collective-permute-start(bf16[32,3584]{1,0:T(8,128)(2,1)S(1)} %maximum_select_fusion.refs_0_), channel_id=1, source_target_pairs={{0,2},{1,3},{2,0},{3,1},{4,6},{5,7},{6,4},{7,5},{8,10},{9,11},{10,... | collective-permute-start | bytes 688136 | tf_op jit(solution)/shard_map/ppermute | solution.py:322
  47.0 19.6 %collective-permute-start.19 = (bf16[32,3584]{1,0:T(8,128)(2,1)}, bf16[32,3584]{1,0:T(8,128)(2,1)S(1)}, u32[]{:S(2)}, u32[]{:S(2)}) collective-permute-start(bf16[32,3584]{1,0:T(8,128)(2,1)} %collective-permute-done.14.refs_4_), channel_id=1, source_target_pairs={{0,2},{1,3},{2,0},{3,1},{4,6},{5,7},{6,4},{7,5},{8,10},{9,11},{10,... | collective-permute-start | bytes 688136 | tf_op jit(solution)/shard_map/ppermute | solution.py:322
  49.6 7.5 %collective-permute-start.8 = (bf16[32,3584]{1,0:T(8,128)(2,1)S(1)}, bf16[32,3584]{1,0:T(8,128)(2,1)S(1)}, u32[]{:S(2)}, u32[]{:S(2)}) collective-permute-start(bf16[32,3584]{1,0:T(8,128)(2,1)S(1)} %maximum_select_fusion.refs_0_), channel_id=1, source_target_pairs={{0,1},{1,0},{2,3},{3,2},{4,5},{5,4},{6,7},{7,6},{8,9},{9,8},{10,11... | collective-permute-start | bytes 688136 | tf_op jit(solution)/shard_map/ppermute | solution.py:322
  53.0 12.2 %collective-permute-start.17 = (bf16[32,3584]{1,0:T(8,128)(2,1)S(1)}, bf16[32,3584]{1,0:T(8,128)(2,1)S(1)}, u32[]{:S(2)}, u32[]{:S(2)}) collective-permute-start(bf16[32,3584]{1,0:T(8,128)(2,1)S(1)} %collective-permute-done.13.refs_4_), channel_id=1, source_target_pairs={{0,2},{1,3},{2,0},{3,1},{4,6},{5,7},{6,4},{7,5},{8,10},{9,11},{10,... | collective-permute-start | bytes 688136 | tf_op jit(solution)/shard_map/ppermute | solution.py:322
  55.7 12.1 %collective-permute-start.20 = (bf16[32,3584]{1,0:T(8,128)(2,1)S(1)}, bf16[32,3584]{1,0:T(8,128)(2,1)S(1)}, u32[]{:S(2)}, u32[]{:S(2)}) collective-permute-start(bf16[32,3584]{1,0:T(8,128)(2,1)S(1)} %collective-permute-done.15.refs_5_), channel_id=1, source_target_pairs={{0,2},{1,3},{2,0},{3,1},{4,6},{5,7},{6,4},{7,5},{8,10},{9,11},{10,... | collective-permute-start | bytes 688136 | tf_op jit(solution)/shard_map/ppermute | solution.py:322
  57.1 26.0 %collective-permute-start.16 = (bf16[32,3584]{1,0:T(8,128)(2,1)S(1)}, bf16[32,3584]{1,0:T(8,128)(2,1)S(1)}, u32[]{:S(2)}, u32[]{:S(2)}) collective-permute-start(bf16[32,3584]{1,0:T(8,128)(2,1)S(1)} %collective-permute-done.13.refs_4_), channel_id=1, source_target_pairs={{0,1},{1,0},{2,3},{3,2},{4,5},{5,4},{6,7},{7,6},{8,9},{9,8},{10,11... | collective-permute-start | bytes 688136 | tf_op jit(solution)/shard_map/ppermute | solution.py:322
  65.3 17.8 %collective-permute-start.12 = (bf16[32,3584]{1,0:T(8,128)(2,1)S(1)}, bf16[32,3584]{1,0:T(8,128)(2,1)S(1)}, u32[]{:S(2)}, u32[]{:S(2)}) collective-permute-start(bf16[32,3584]{1,0:T(8,128)(2,1)S(1)} %collective-permute-done.9.refs_2_), channel_id=1, source_target_pairs={{0,1},{1,0},{2,3},{3,2},{4,5},{5,4},{6,7},{7,6},{8,9},{9,8},{10,11... | collective-permute-start | bytes 688136 | tf_op jit(solution)/shard_map/ppermute | solution.py:322
  66.6 16.5 %collective-permute-start.18 = (bf16[32,3584]{1,0:T(8,128)(2,1)S(1)}, bf16[32,3584]{1,0:T(8,128)(2,1)S(1)}, u32[]{:S(2)}, u32[]{:S(2)}) collective-permute-start(bf16[32,3584]{1,0:T(8,128)(2,1)S(1)} %collective-permute-done.17.refs_6_), channel_id=1, source_target_pairs={{0,1},{1,0},{2,3},{3,2},{4,5},{5,4},{6,7},{7,6},{8,9},{9,8},{10,11... | collective-permute-start | bytes 688136 | tf_op jit(solution)/shard_map/ppermute | solution.py:322
  67.7 3.5 %copy-start = (bf16[1792,2432]{1,0:T(8,128)(2,1)S(1)}, bf16[1792,2432]{1,0:T(8,128)(2,1)}, u32[]{:S(2)}) copy-start(bf16[1792,2432]{1,0:T(8,128)(2,1)} %refs_8_.1) | copy-start | bytes 26148868
  90.3 5.3 %collective-permute-start.25 = (f32[8,256]{1,0:T(8,128)S(1)}, f32[8,256]{1,0:T(8,128)S(1)}, u32[]{:S(2)}, u32[]{:S(2)}) collective-permute-start(f32[8,256]{1,0:T(8,128)S(1)} %get-tuple-element.58.refs_0_), channel_id=1, source_target_pairs={{0,4},{1,5},{2,6},{3,7},{4,0},{5,1},{6,2},{7,3},{8,12},{9,13},{10,... | collective-permute-start | bytes 24584 | tf_op jit(solution)/shard_map/ppermute | solution.py:322
  92.1 6.0 %collective-permute-start.24 = (f32[8,256]{1,0:T(8,128)S(1)}, f32[8,256]{1,0:T(8,128)S(1)}, u32[]{:S(2)}, u32[]{:S(2)}) collective-permute-start(f32[8,256]{1,0:T(8,128)S(1)} %get-tuple-element.58.refs_0_), channel_id=1, source_target_pairs={{0,3},{1,2},{2,1},{3,0},{4,7},{5,6},{6,5},{7,4},{8,11},{9,10},{10,... | collective-permute-start | bytes 24584 | tf_op jit(solution)/shard_map/ppermute | solution.py:322
  94.6 4.5 %collective-permute-start.23 = (f32[8,256]{1,0:T(8,128)S(1)}, f32[8,256]{1,0:T(8,128)S(1)}, u32[]{:S(2)}, u32[]{:S(2)}) collective-permute-start(f32[8,256]{1,0:T(8,128)S(1)} %get-tuple-element.58.refs_0_), channel_id=1, source_target_pairs={{0,2},{1,3},{2,0},{3,1},{4,6},{5,7},{6,4},{7,5},{8,10},{9,11},{10,... | collective-permute-start | bytes 24584 | tf_op jit(solution)/shard_map/ppermute | solution.py:322
  94.6 4.5 %collective-permute-start.22 = (f32[8,256]{1,0:T(8,128)S(1)}, f32[8,256]{1,0:T(8,128)S(1)}, u32[]{:S(2)}, u32[]{:S(2)}) collective-permute-start(f32[8,256]{1,0:T(8,128)S(1)} %get-tuple-element.58.refs_0_), channel_id=1, source_target_pairs={{0,1},{1,0},{2,3},{3,2},{4,5},{5,4},{6,7},{7,6},{8,9},{9,8},{10,11... | collective-permute-start | bytes 24584 | tf_op jit(solution)/shard_map/ppermute | solution.py:322
  95.6 4.6 %collective-permute-start.28 = (f32[8,256]{1,0:T(8,128)S(1)}, f32[8,256]{1,0:T(8,128)S(1)}, u32[]{:S(2)}, u32[]{:S(2)}) collective-permute-start(f32[8,256]{1,0:T(8,128)S(1)} %collective-permute-done.25.refs_4_), channel_id=1, source_target_pairs={{0,3},{1,2},{2,1},{3,0},{4,7},{5,6},{6,5},{7,4},{8,11},{9,10},{10,... | collective-permute-start | bytes 24584 | tf_op jit(solution)/shard_map/ppermute | solution.py:322
  98.1 3.7 %collective-permute-start.27 = (f32[8,256]{1,0:T(8,128)S(1)}, f32[8,256]{1,0:T(8,128)S(1)}, u32[]{:S(2)}, u32[]{:S(2)}) collective-permute-start(f32[8,256]{1,0:T(8,128)S(1)} %collective-permute-done.25.refs_4_), channel_id=1, source_target_pairs={{0,2},{1,3},{2,0},{3,1},{4,6},{5,7},{6,4},{7,5},{8,10},{9,11},{10,... | collective-permute-start | bytes 24584 | tf_op jit(solution)/shard_map/ppermute | solution.py:322
  98.1 3.7 %collective-permute-start.26 = (f32[8,256]{1,0:T(8,128)S(1)}, f32[8,256]{1,0:T(8,128)S(1)}, u32[]{:S(2)}, u32[]{:S(2)}) collective-permute-start(f32[8,256]{1,0:T(8,128)S(1)} %collective-permute-done.25.refs_4_), channel_id=1, source_target_pairs={{0,1},{1,0},{2,3},{3,2},{4,5},{5,4},{6,7},{7,6},{8,9},{9,8},{10,11... | collective-permute-start | bytes 24584 | tf_op jit(solution)/shard_map/ppermute | solution.py:322
  110.2 8.6 %collective-permute-start.31 = (f16[32,3584]{1,0:T(8,128)(2,1)S(1)}, f16[32,3584]{1,0:T(8,128)(2,1)S(1)}, u32[]{:S(2)}, u32[]{:S(2)}) collective-permute-start(f16[32,3584]{1,0:T(8,128)(2,1)S(1)} %convert_element_type.113), channel_id=1, source_target_pairs={{0,1},{1,0},{2,3},{3,2},{4,5},{5,4},{6,7},{7,6},{8,9},{9,8},{10,11... | collective-permute-start | bytes 688136 | tf_op jit(solution)/shard_map/ppermute | solution.py:322
  111.3 10.9 %collective-permute-start.29 = (f16[32,3584]{1,0:T(8,128)(2,1)S(1)}, f16[32,3584]{1,0:T(8,128)(2,1)S(1)}, u32[]{:S(2)}, u32[]{:S(2)}) collective-permute-start(f16[32,3584]{1,0:T(8,128)(2,1)S(1)} %convert_element_type.109), channel_id=1, source_target_pairs={{0,1},{1,0},{2,3},{3,2},{4,5},{5,4},{6,7},{7,6},{8,9},{9,8},{10,11... | collective-permute-start | bytes 688136 | tf_op jit(solution)/shard_map/ppermute | solution.py:322
  118.8 14.3 %collective-permute-start.35 = (f16[32,3584]{1,0:T(8,128)(2,1)S(1)}, f16[32,3584]{1,0:T(8,128)(2,1)S(1)}, u32[]{:S(2)}, u32[]{:S(2)}) collective-permute-start(f16[32,3584]{1,0:T(8,128)(2,1)S(1)} %convert_element_type.121), channel_id=1, source_target_pairs={{0,1},{1,0},{2,3},{3,2},{4,5},{5,4},{6,7},{7,6},{8,9},{9,8},{10,11... | collective-permute-start | bytes 688136 | tf_op jit(solution)/shard_map/ppermute | solution.py:322
  122.2 6.0 %collective-permute-start.33 = (f16[32,3584]{1,0:T(8,128)(2,1)S(1)}, f16[32,3584]{1,0:T(8,128)(2,1)S(1)}, u32[]{:S(2)}, u32[]{:S(2)}) collective-permute-start(f16[32,3584]{1,0:T(8,128)(2,1)S(1)} %convert_element_type.117), channel_id=1, source_target_pairs={{0,1},{1,0},{2,3},{3,2},{4,5},{5,4},{6,7},{7,6},{8,9},{9,8},{10,11... | collective-permute-start | bytes 688136 | tf_op jit(solution)/shard_map/ppermute | solution.py:322
  123.5 7.4 %collective-permute-start.30 = (f16[32,3584]{1,0:T(8,128)(2,1)S(1)}, f16[32,3584]{1,0:T(8,128)(2,1)S(1)}, u32[]{:S(2)}, u32[]{:S(2)}) collective-permute-start(f16[32,3584]{1,0:T(8,128)(2,1)S(1)} %add_convert_fusion.3), channel_id=1, source_target_pairs={{0,2},{1,3},{2,0},{3,1},{4,6},{5,7},{6,4},{7,5},{8,10},{9,11},{10,... | collective-permute-start | bytes 688136 | tf_op jit(solution)/shard_map/ppermute | solution.py:322
  128.3 6.1 %collective-permute-start.34 = (f16[32,3584]{1,0:T(8,128)(2,1)S(1)}, f16[32,3584]{1,0:T(8,128)(2,1)S(1)}, u32[]{:S(2)}, u32[]{:S(2)}) collective-permute-start(f16[32,3584]{1,0:T(8,128)(2,1)S(1)} %add_convert_fusion.1), channel_id=1, source_target_pairs={{0,2},{1,3},{2,0},{3,1},{4,6},{5,7},{6,4},{7,5},{8,10},{9,11},{10,... | collective-permute-start | bytes 688136 | tf_op jit(solution)/shard_map/ppermute | solution.py:322
  131.0 9.4 %collective-permute-start.32 = (f16[32,3584]{1,0:T(8,128)(2,1)S(1)}, f16[32,3584]{1,0:T(8,128)(2,1)S(1)}, u32[]{:S(2)}, u32[]{:S(2)}) collective-permute-start(f16[32,3584]{1,0:T(8,128)(2,1)S(1)} %add_convert_fusion.2), channel_id=1, source_target_pairs={{0,4},{1,5},{2,6},{3,7},{4,0},{5,1},{6,2},{7,3},{8,12},{9,13},{10,... | collective-permute-start | bytes 688136 | tf_op jit(solution)/shard_map/ppermute | solution.py:322

commit v11 on v10

--- a/solution.py
+++ b/solution.py
@@ -293,7 +293,7 @@
 def gradient(place, tables, scaled_teach, scaled_stud, column, head, bits, chunk):
     rows, vocab_dev = scaled_teach.shape
     count, width = 1 << bits, head.shape[0]
-    step = 896 if width % 896 == 0 else width
+    step = 512 if width % 512 == 0 else width
     return pl.pallas_call(
         functools.partial(gradient_kernel, bits, step, chunk),
         in_specs=[in_smem] + [in_vmem] * (count + 4),
@@ -327,10 +327,10 @@
     def lowest(mask):
         return (mask & -mask).bit_length() - 1
 
-    def spread(own, line, around):
+    def spread(own, line):
         blocks = [own]
         for mask in range(1, vocab_size):
-            bit = 1 if around and mask & 3 == 3 and mask > 3 else lowest(mask)
+            bit = lowest(mask)
             block = blocks[mask ^ (1 << bit)]
             if bit == 0:
                 block = tie(block, line[-3])
@@ -382,11 +382,11 @@
         member = (owner[None, :] == row_id[:, None]) & alive[None, :]
         parts = project(member.astype(jnp.bfloat16), teacher_rows, proj_weight, vocab_size, 512 if student_hidden.shape[1] % 512 == 0 else student_hidden.shape[1])
         projected_own, line = reduce_blocks(parts)
-        hidden = spread(tie(turned(student_hidden), parts[-1]), line, True)
-        projected = spread(turned(projected_own.astype(jnp.bfloat16)), line, False)
+        hidden = spread(tie(turned(student_hidden), parts[-1]), line)
+        projected = spread(turned(projected_own.astype(jnp.bfloat16)), line)
 
         column = (in_order(targets) - me * vocab_dev)[:, None]
-        logit_stud, scaled_stud, stats_stud, head = student_logits(as_pieces(hidden), heads, column, 256, chunk)
+        logit_stud, scaled_stud, stats_stud, head = student_logits(as_pieces(hidden), heads, column, 512, chunk)
         scaled_teach, stats = teacher_logits(as_pieces(projected), head, logit_stud, stats_stud, 1024, chunk)
         tables = [stats]
         for mask in range(1, vocab_size):

time: 142 us -> 135 us (0.951)
  waiting for transfers between devices: 48.4 us -> 39.3 us
  starting transfers between devices: 49.5 us -> 52.9 us
    ppermute x35, waiting for transfers between devices: 48.4 us -> 39.3 us  [trade(): lax.ppermute(block, 'vocab', [(at, at ^ mask) for at in range(vocab_size)])]
    ppermute x35, starting transfers between devices: 49 us -> 52.4 us  [trade(): lax.ppermute(block, 'vocab', [(at, at ^ mask) for at in range(vocab_size)])]
  transfers between devices with their start and end apart: 36 -> 36, of which waited for: 20 -> 17; matrix products, arithmetic and copies ran while one was open for 4% -> 4% of each run, Pallas kernels for 12% -> 12%
where the time goes in v11:
time: 135 us
  starting transfers between devices  52.9 us (39%)
  waiting for transfers between devices  39.3 us (29%)
  Pallas kernels  31.6 us (23%)
  other arithmetic  5.18 us (4%)
  local copies, waits for them, and re-layouts  4.35 us (3%)
  between operations  1.53 us (1%)
    ppermute x35, starting transfers between devices, trade(): lax.ppermute(block, 'vocab', [(at, at ^ mask) for at in range(vocab_size)])  52.4 us
    ppermute x35, waiting for transfers between devices, trade(): lax.ppermute(block, 'vocab', [(at, at ^ mask) for at in range(vocab_size)])  39.3 us
    pallas_call x1, Pallas kernels, student_logits(): pl.pallas_call(functools.partial(student_kernel, len(pieces), step, chunk...  11.2 us
    pallas_call x1, Pallas kernels, gradient(): pl.pallas_call(functools.partial(gradient_kernel, bits, step, chunk), in_...  8.33 us
    pallas_call x1, Pallas kernels, teacher_logits(): pl.pallas_call(functools.partial(teacher_kernel, len(pieces), step, chunk...  7.15 us
    pallas_call x1, Pallas kernels, project(): pl.pallas_call(functools.partial(project_kernel, count, step), in_specs=[...  4.83 us
    unnamed x6, local copies, waits for them, and re-layouts  3.48 us
  transfers between devices with their start and end apart: 36, of which 17 were waited for; matrix products, arithmetic and copies ran while one was open for 4% of the time, Pallas kernels for 12%

profile of v11, /device:TPU:0, one launch (start us, length us, event | category | flops | bytes accessed | tf_op | source)
XLA Modules:
  0.0 134.8 jit_solution(9383580103165051692)
XLA Ops:
  0.6 0.5 collective-permute-start.21
  1.8 0.8 and_convert_fusion.member_ref
  2.7 4.8 %shard_map.86 = (f32[32,3584]{1,0:T(8,128)S(1)}, f32[32,3584]{1,0:T(8,128)S(1)}, f32[32,3584]{1,0:T(8,128)S(1)}, f32[32,3584]{1,0:T(8,128)S(1)}, f32[32,3584]{1,...) custom-call(bf16[256,512]{1,0:T(8,128)(2,1)S(1)} %and_convert_fusion.member_ref, ...), custom_call_target="tpu_custom_call" | custom-call | flops 2147483648 | bytes 12058624 | tf_op jit(solution)/shard_map/pallas_call | solution.py:54
  7.5 0.7 convert_element_type.94
  8.2 2.6 %collective-permute-start = (f16[32,3584]{1,0:T(8,128)(2,1)}, f16[32,3584]{1,0:T(8,128)(2,1)}, u32[]{:S(2)}, u32[]{:S(2)}) collective-permute-start(f16[32,3584]{1,0:T(8,128)(2,1)} %convert_element_type.94), channel_id=1, source_target_pairs={{0,1},{1,0},{2,3},{3,2},{4,5},{5,4},{6,7},{7,6},{8,9},{9,8},{10,11... | collective-permute-start | bytes 688136 | tf_op jit(solution)/shard_map/ppermute | solution.py:322
  10.8 1.0 maximum_select_fusion.1.refs_0_
  11.8 2.7 %collective-permute-start.11 = (bf16[32,3584]{1,0:T(8,128)(2,1)S(1)}, bf16[32,3584]{1,0:T(8,128)(2,1)}, u32[]{:S(2)}, u32[]{:S(2)}) collective-permute-start(bf16[32,3584]{1,0:T(8,128)(2,1)S(1)} %maximum_select_fusion.1.refs_0_), channel_id=1, source_target_pairs={{0,4},{1,5},{2,6},{3,7},{4,0},{5,1},{6,2},{7,3},{8,12},{9,13},{10,... | collective-permute-start | bytes 688136 | tf_op jit(solution)/shard_map/ppermute | solution.py:322
  14.5 1.6 %collective-permute-start.7 = (bf16[32,3584]{1,0:T(8,128)(2,1)S(1)}, bf16[32,3584]{1,0:T(8,128)(2,1)}, u32[]{:S(2)}, u32[]{:S(2)}) collective-permute-start(bf16[32,3584]{1,0:T(8,128)(2,1)S(1)} %maximum_select_fusion.1.refs_0_), channel_id=1, source_target_pairs={{0,2},{1,3},{2,0},{3,1},{4,6},{5,7},{6,4},{7,5},{8,10},{9,11},{10,... | collective-permute-start | bytes 688136 | tf_op jit(solution)/shard_map/ppermute | solution.py:322
  16.1 0.6 collective-permute-start.2
  16.7 0.6 collective-permute-done
  17.3 2.2 %collective-permute-start.4 = (f16[32,3584]{1,0:T(8,128)(2,1)S(1)}, f16[32,3584]{1,0:T(8,128)(2,1)S(1)}, u32[]{:S(2)}, u32[]{:S(2)}) collective-permute-start(f16[32,3584]{1,0:T(8,128)(2,1)S(1)} %convert_element_type.102), channel_id=1, source_target_pairs={{0,1},{1,0},{2,3},{3,2},{4,5},{5,4},{6,7},{7,6},{8,9},{9,8},{10,11... | collective-permute-start | bytes 688136 | tf_op jit(solution)/shard_map/ppermute | solution.py:322
  19.5 1.0 add_convert_fusion.7
  20.5 4.2 %collective-permute-done.2 = f16[32,3584]{1,0:T(8,128)(2,1)S(1)} collective-permute-done((f16[32,3584]{1,0:T(8,128)(2,1)S(1)}, f16[32,3584]{1,0:T(8,128)(2,1)S(1)}, u32[]{:S(2)}, u32[]{:S(2)}) %collective-permute-start.2) | collective-permute-done | bytes 229408 | tf_op jit(solution)/shard_map/ppermute | solution.py:322
  24.7 0.4 collective-permute-start.1
  25.1 2.1 %collective-permute-done.4 = f16[32,3584]{1,0:T(8,128)(2,1)S(1)} collective-permute-done((f16[32,3584]{1,0:T(8,128)(2,1)S(1)}, f16[32,3584]{1,0:T(8,128)(2,1)S(1)}, u32[]{:S(2)}, u32[]{:S(2)}) %collective-permute-start.4) | collective-permute-done | bytes 229408 | tf_op jit(solution)/shard_map/ppermute | solution.py:322
  27.3 1.5 %collective-permute-start.6 = (f16[32,3584]{1,0:T(8,128)(2,1)S(1)}, f16[32,3584]{1,0:T(8,128)(2,1)S(1)}, u32[]{:S(2)}, u32[]{:S(2)}) collective-permute-start(f16[32,3584]{1,0:T(8,128)(2,1)S(1)} %convert_element_type.106), channel_id=1, source_target_pairs={{0,1},{1,0},{2,3},{3,2},{4,5},{5,4},{6,7},{7,6},{8,9},{9,8},{10,11... | collective-permute-start | bytes 688136 | tf_op jit(solution)/shard_map/ppermute | solution.py:322
  28.9 1.9 %collective-permute-done.1 = f16[32,3584]{1,0:T(8,128)(2,1)S(1)} collective-permute-done((f16[32,3584]{1,0:T(8,128)(2,1)S(1)}, f16[32,3584]{1,0:T(8,128)(2,1)S(1)}, u32[]{:S(2)}, u32[]{:S(2)}) %collective-permute-start.1) | collective-permute-done | bytes 229408 | tf_op jit(solution)/shard_map/ppermute | solution.py:322
  30.7 0.4 collective-permute-start.5
  31.3 2.7 %collective-permute-start.3 = (f16[32,3584]{1,0:T(8,128)(2,1)S(1)}, f16[32,3584]{1,0:T(8,128)(2,1)S(1)}, u32[]{:S(2)}, u32[]{:S(2)}) collective-permute-start(f16[32,3584]{1,0:T(8,128)(2,1)S(1)} %add_convert_fusion.6), channel_id=1, source_target_pairs={{0,4},{1,5},{2,6},{3,7},{4,0},{5,1},{6,2},{7,3},{8,12},{9,13},{10,... | collective-permute-start | bytes 688136 | tf_op jit(solution)/shard_map/ppermute | solution.py:322
  34.0 1.5 %collective-permute-start.16 = (bf16[32,3584]{1,0:T(8,128)(2,1)S(1)}, bf16[32,3584]{1,0:T(8,128)(2,1)S(1)}, u32[]{:S(2)}, u32[]{:S(2)}) collective-permute-start(bf16[32,3584]{1,0:T(8,128)(2,1)S(1)} %maximum_select_fusion.1.refs_0_), channel_id=1, source_target_pairs={{0,1},{1,0},{2,3},{3,2},{4,5},{5,4},{6,7},{7,6},{8,9},{9,8},{10,11... | collective-permute-start | bytes 688136 | tf_op jit(solution)/shard_map/ppermute | solution.py:322
  35.5 2.1 %collective-permute-start.15 = (bf16[32,3584]{1,0:T(8,128)(2,1)}, bf16[32,3584]{1,0:T(8,128)(2,1)S(1)}, u32[]{:S(2)}, u32[]{:S(2)}) collective-permute-start(bf16[32,3584]{1,0:T(8,128)(2,1)} %collective-permute-done.11.refs_4_), channel_id=1, source_target_pairs={{0,2},{1,3},{2,0},{3,1},{4,6},{5,7},{6,4},{7,5},{8,10},{9,11},{10,... | collective-permute-start | bytes 688136 | tf_op jit(solution)/shard_map/ppermute | solution.py:322
  37.6 4.7 %collective-permute-done.5 = f16[32,3584]{1,0:T(8,128)(2,1)S(1)} collective-permute-done((f16[32,3584]{1,0:T(8,128)(2,1)S(1)}, f16[32,3584]{1,0:T(8,128)(2,1)S(1)}, u32[]{:S(2)}, u32[]{:S(2)}) %collective-permute-start.5) | collective-permute-done | bytes 229408 | tf_op jit(solution)/shard_map/ppermute | solution.py:322
  42.3 1.6 %collective-permute-start.12 = (bf16[32,3584]{1,0:T(8,128)(2,1)}, bf16[32,3584]{1,0:T(8,128)(2,1)S(1)}, u32[]{:S(2)}, u32[]{:S(2)}) collective-permute-start(bf16[32,3584]{1,0:T(8,128)(2,1)} %collective-permute-done.11.refs_4_), channel_id=1, source_target_pairs={{0,1},{1,0},{2,3},{3,2},{4,5},{5,4},{6,7},{7,6},{8,9},{9,8},{10,11... | collective-permute-start | bytes 688136 | tf_op jit(solution)/shard_map/ppermute | solution.py:322
  43.9 0.4 collective-permute-start.8
  44.5 2.9 %collective-permute-start.14 = (bf16[32,3584]{1,0:T(8,128)(2,1)S(1)}, bf16[32,3584]{1,0:T(8,128)(2,1)S(1)}, u32[]{:S(2)}, u32[]{:S(2)}) collective-permute-start(bf16[32,3584]{1,0:T(8,128)(2,1)S(1)} %maximum_select_fusion.refs_0_), channel_id=1, source_target_pairs={{0,4},{1,5},{2,6},{3,7},{4,0},{5,1},{6,2},{7,3},{8,12},{9,13},{10,... | collective-permute-start | bytes 688136 | tf_op jit(solution)/shard_map/ppermute | solution.py:322
  47.5 0.5 collective-permute-done.15.refs_6_
  48.0 1.3 collective-permute-start.17
  49.3 4.7 %collective-permute-done.8.refs_3_ = bf16[32,3584]{1,0:T(8,128)(2,1)S(1)} collective-permute-done((bf16[32,3584]{1,0:T(8,128)(2,1)}, bf16[32,3584]{1,0:T(8,128)(2,1)S(1)}, u32[]{:S(2)}, u32[]{:S(2)}) %collective-permute-start.8) | collective-permute-done | bytes 229408 | tf_op jit(solution)/shard_map/ppermute | solution.py:322
  54.1 1.4 %collective-permute-start.10 = (bf16[32,3584]{1,0:T(8,128)(2,1)S(1)}, bf16[32,3584]{1,0:T(8,128)(2,1)S(1)}, u32[]{:S(2)}, u32[]{:S(2)}) collective-permute-start(bf16[32,3584]{1,0:T(8,128)(2,1)S(1)} %maximum_select_fusion.refs_0_), channel_id=1, source_target_pairs={{0,2},{1,3},{2,0},{3,1},{4,6},{5,7},{6,4},{7,5},{8,10},{9,11},{10,... | collective-permute-start | bytes 688136 | tf_op jit(solution)/shard_map/ppermute | solution.py:322
  55.5 1.6 %collective-permute-start.9 = (bf16[32,3584]{1,0:T(8,128)(2,1)S(1)}, bf16[32,3584]{1,0:T(8,128)(2,1)S(1)}, u32[]{:S(2)}, u32[]{:S(2)}) collective-permute-start(bf16[32,3584]{1,0:T(8,128)(2,1)S(1)} %maximum_select_fusion.refs_0_), channel_id=1, source_target_pairs={{0,1},{1,0},{2,3},{3,2},{4,5},{5,4},{6,7},{7,6},{8,9},{9,8},{10,11... | collective-permute-start | bytes 688136 | tf_op jit(solution)/shard_map/ppermute | solution.py:322
  57.1 1.4 %collective-permute-start.19 = (bf16[32,3584]{1,0:T(8,128)(2,1)S(1)}, bf16[32,3584]{1,0:T(8,128)(2,1)S(1)}, u32[]{:S(2)}, u32[]{:S(2)}) collective-permute-start(bf16[32,3584]{1,0:T(8,128)(2,1)S(1)} %collective-permute-done.14.refs_4_), channel_id=1, source_target_pairs={{0,2},{1,3},{2,0},{3,1},{4,6},{5,7},{6,4},{7,5},{8,10},{9,11},{10,... | collective-permute-start | bytes 688136 | tf_op jit(solution)/shard_map/ppermute | solution.py:322
  58.5 1.6 %collective-permute-done.10.refs_2_ = bf16[32,3584]{1,0:T(8,128)(2,1)S(1)} collective-permute-done((bf16[32,3584]{1,0:T(8,128)(2,1)S(1)}, bf16[32,3584]{1,0:T(8,128)(2,1)S(1)}, u32[]{:S(2)}, u32[]{:S(2)}) %collective-permute-start.10) | collective-permute-done | bytes 229408 | tf_op jit(solution)/shard_map/ppermute | solution.py:322
  60.1 2.4 %collective-permute-start.13 = (bf16[32,3584]{1,0:T(8,128)(2,1)S(1)}, bf16[32,3584]{1,0:T(8,128)(2,1)S(1)}, u32[]{:S(2)}, u32[]{:S(2)}) collective-permute-start(bf16[32,3584]{1,0:T(8,128)(2,1)S(1)} %collective-permute-done.10.refs_2_), channel_id=1, source_target_pairs={{0,1},{1,0},{2,3},{3,2},{4,5},{5,4},{6,7},{7,6},{8,9},{9,8},{10,11... | collective-permute-start | bytes 688136 | tf_op jit(solution)/shard_map/ppermute | solution.py:322
  62.5 1.5 %collective-permute-done.9.refs_1_ = bf16[32,3584]{1,0:T(8,128)(2,1)S(1)} collective-permute-done((bf16[32,3584]{1,0:T(8,128)(2,1)S(1)}, bf16[32,3584]{1,0:T(8,128)(2,1)S(1)}, u32[]{:S(2)}, u32[]{:S(2)}) %collective-permute-start.9) | collective-permute-done | bytes 229408 | tf_op jit(solution)/shard_map/ppermute | solution.py:322
  64.0 2.1 %collective-permute-start.20 = (bf16[32,3584]{1,0:T(8,128)(2,1)S(1)}, bf16[32,3584]{1,0:T(8,128)(2,1)S(1)}, u32[]{:S(2)}, u32[]{:S(2)}) collective-permute-start(bf16[32,3584]{1,0:T(8,128)(2,1)S(1)} %collective-permute-done.19.refs_6_), channel_id=1, source_target_pairs={{0,1},{1,0},{2,3},{3,2},{4,5},{5,4},{6,7},{7,6},{8,9},{9,8},{10,11... | collective-permute-start | bytes 688136 | tf_op jit(solution)/shard_map/ppermute | solution.py:322
  66.1 0.1 sub.26.refs_10_
  66.3 3.5 %copy-done = bf16[1792,2432]{1,0:T(8,128)(2,1)S(1)} copy-done((bf16[1792,2432]{1,0:T(8,128)(2,1)S(1)}, bf16[1792,2432]{1,0:T(8,128)(2,1)}, u32[]{:S(2)}) %copy-start) | copy-done | bytes 8716312
  69.8 11.2 %shard_map.87 = (f32[256,2432]{1,0:T(8,128)S(1)}, f32[256,2432]{1,0:T(8,128)S(1)}, f32[8,256]{1,0:T(8,128)S(1)}, bf16[3584,2432]{1,0:T(8,128)(2,1)S(1)}) custom-call(bf16[32,3584]{1,0:T(8,128)(2,1)S(1)} %maximum_select_fusion.1.refs_0_, bf16[32,3584]{1,0:T(8,128)(2,1)S(1)} %collective-permute-done.16.refs_1_, ...), custom_call_target="tpu_custom_call" | custom-call | flops 2231369728 | bytes 16187392 | tf_op jit(solution)/shard_map/pallas_call | solution.py:192
  81.1 7.2 %shard_map.88 = (f32[256,2432]{1,0:T(8,128)S(1)}, f32[8,256]{1,0:T(8,128)S(1)}) custom-call(bf16[32,3584]{1,0:T(8,128)(2,1)S(1)} %maximum_select_fusion.refs_0_, bf16[32,3584]{1,0:T(8,128)(2,1)S(1)} %collective-permute-done.9.refs_1_, bf16[32,3584]{1,0:T(8,128)(2,1)S(1)} %collective-permute-done.10.refs_2_, ...), custom_call_target="tpu_custom_call" | custom-call | flops 4462739456 | bytes 24903680 | tf_op jit(solution)/shard_map/pallas_call | solution.py:215
  88.2 2.4 %collective-permute-start.25 = (f32[8,256]{1,0:T(8,128)S(1)}, f32[8,256]{1,0:T(8,128)S(1)}, u32[]{:S(2)}, u32[]{:S(2)}) collective-permute-start(f32[8,256]{1,0:T(8,128)S(1)} %get-tuple-element.60.refs_0_), channel_id=1, source_target_pairs={{0,4},{1,5},{2,6},{3,7},{4,0},{5,1},{6,2},{7,3},{8,12},{9,13},{10,... | collective-permute-start | bytes 24584 | tf_op jit(solution)/shard_map/ppermute | solution.py:322
  90.6 0.4 collective-permute-start.24
  91.1 1.2 collective-permute-start.23
  92.3 1.8 %collective-permute-start.22 = (f32[8,256]{1,0:T(8,128)S(1)}, f32[8,256]{1,0:T(8,128)S(1)}, u32[]{:S(2)}, u32[]{:S(2)}) collective-permute-start(f32[8,256]{1,0:T(8,128)S(1)} %get-tuple-element.60.refs_0_), channel_id=1, source_target_pairs={{0,1},{1,0},{2,3},{3,2},{4,5},{5,4},{6,7},{7,6},{8,9},{9,8},{10,11... | collective-permute-start | bytes 24584 | tf_op jit(solution)/shard_map/ppermute | solution.py:322
  94.1 0.4 collective-permute-start.28
  94.6 1.2 collective-permute-start.27
  95.8 1.8 %collective-permute-start.26 = (f32[8,256]{1,0:T(8,128)S(1)}, f32[8,256]{1,0:T(8,128)S(1)}, u32[]{:S(2)}, u32[]{:S(2)}) collective-permute-start(f32[8,256]{1,0:T(8,128)S(1)} %collective-permute-done.25.refs_4_), channel_id=1, source_target_pairs={{0,1},{1,0},{2,3},{3,2},{4,5},{5,4},{6,7},{7,6},{8,9},{9,8},{10,11... | collective-permute-start | bytes 24584 | tf_op jit(solution)/shard_map/ppermute | solution.py:322
  97.7 1.0 collective-permute-done.28.refs_7_
  98.7 0.8 collective-permute-done.26.refs_5_
  99.4 8.3 %shard_map.89 = (f32[8,256]{1,0:T(8,128)S(1)}, f32[32,3584]{1,0:T(8,128)S(1)}, f32[32,3584]{1,0:T(8,128)S(1)}, f32[32,3584]{1,0:T(8,128)S(1)}, f32[32,3584]{1,0:...) custom-call(s32[2]{0:T(128)S(1)} %pad_add_fusion.place_ref, ...), custom_call_target="tpu_custom_call" | custom-call | flops 4462739456 | bytes 24903680 | tf_op jit(solution)/shard_map/pallas_call | solution.py:297
  107.8 1.9 %collective-permute-start.31 = (f16[32,3584]{1,0:T(8,128)(2,1)S(1)}, f16[32,3584]{1,0:T(8,128)(2,1)S(1)}, u32[]{:S(2)}, u32[]{:S(2)}) collective-permute-start(f16[32,3584]{1,0:T(8,128)(2,1)S(1)} %convert_element_type.113), channel_id=1, source_target_pairs={{0,1},{1,0},{2,3},{3,2},{4,5},{5,4},{6,7},{7,6},{8,9},{9,8},{10,11... | collective-permute-start | bytes 688136 | tf_op jit(solution)/shard_map/ppermute | solution.py:322
  109.7 0.3 collective-permute-start.29
  110.0 3.8 %collective-permute-done.31 = f16[32,3584]{1,0:T(8,128)(2,1)S(1)} collective-permute-done((f16[32,3584]{1,0:T(8,128)(2,1)S(1)}, f16[32,3584]{1,0:T(8,128)(2,1)S(1)}, u32[]{:S(2)}, u32[]{:S(2)}) %collective-permute-start.31) | collective-permute-done | bytes 229408 | tf_op jit(solution)/shard_map/ppermute | solution.py:322
  113.9 1.8 %collective-permute-start.35 = (f16[32,3584]{1,0:T(8,128)(2,1)S(1)}, f16[32,3584]{1,0:T(8,128)(2,1)S(1)}, u32[]{:S(2)}, u32[]{:S(2)}) collective-permute-start(f16[32,3584]{1,0:T(8,128)(2,1)S(1)} %convert_element_type.121), channel_id=1, source_target_pairs={{0,1},{1,0},{2,3},{3,2},{4,5},{5,4},{6,7},{7,6},{8,9},{9,8},{10,11... | collective-permute-start | bytes 688136 | tf_op jit(solution)/shard_map/ppermute | solution.py:322
  115.7 0.6 collective-permute-done.29
  116.3 1.8 %collective-permute-start.33 = (f16[32,3584]{1,0:T(8,128)(2,1)S(1)}, f16[32,3584]{1,0:T(8,128)(2,1)S(1)}, u32[]{:S(2)}, u32[]{:S(2)}) collective-permute-start(f16[32,3584]{1,0:T(8,128)(2,1)S(1)} %convert_element_type.117), channel_id=1, source_target_pairs={{0,1},{1,0},{2,3},{3,2},{4,5},{5,4},{6,7},{7,6},{8,9},{9,8},{10,11... | collective-permute-start | bytes 688136 | tf_op jit(solution)/shard_map/ppermute | solution.py:322
  118.2 1.2 collective-permute-start.30
  119.4 2.9 %collective-permute-done.33 = f16[32,3584]{1,0:T(8,128)(2,1)S(1)} collective-permute-done((f16[32,3584]{1,0:T(8,128)(2,1)S(1)}, f16[32,3584]{1,0:T(8,128)(2,1)S(1)}, u32[]{:S(2)}, u32[]{:S(2)}) %collective-permute-start.33) | collective-permute-done | bytes 229408 | tf_op jit(solution)/shard_map/ppermute | solution.py:322
  122.4 1.5 %collective-permute-start.34 = (f16[32,3584]{1,0:T(8,128)(2,1)S(1)}, f16[32,3584]{1,0:T(8,128)(2,1)S(1)}, u32[]{:S(2)}, u32[]{:S(2)}) collective-permute-start(f16[32,3584]{1,0:T(8,128)(2,1)S(1)} %add_convert_fusion.1), channel_id=1, source_target_pairs={{0,2},{1,3},{2,0},{3,1},{4,6},{5,7},{6,4},{7,5},{8,10},{9,11},{10,... | collective-permute-start | bytes 688136 | tf_op jit(solution)/shard_map/ppermute | solution.py:322
  123.9 0.5 collective-permute-done.30
  124.5 1.1 collective-permute-start.32
  125.5 0.6 slice.27
  126.1 2.4 %collective-permute-done.34 = f16[32,3584]{1,0:T(8,128)(2,1)S(1)} collective-permute-done((f16[32,3584]{1,0:T(8,128)(2,1)S(1)}, f16[32,3584]{1,0:T(8,128)(2,1)S(1)}, u32[]{:S(2)}, u32[]{:S(2)}) %collective-permute-start.34) | collective-permute-done | bytes 229408 | tf_op jit(solution)/shard_map/ppermute | solution.py:322
  128.5 5.4 %collective-permute-done.32 = f16[32,3584]{1,0:T(8,128)(2,1)S(1)} collective-permute-done((f16[32,3584]{1,0:T(8,128)(2,1)S(1)}, f16[32,3584]{1,0:T(8,128)(2,1)S(1)}, u32[]{:S(2)}, u32[]{:S(2)}) %collective-permute-start.32) | collective-permute-done | bytes 229408 | tf_op jit(solution)/shard_map/ppermute | solution.py:322
  134.0 0.8 maximum_select_fusion.2
  (51 shorter events, 1.1 us)
Async XLA Ops:
  0.6 10.2 %copy-start.1 = (bf16[32,3584]{1,0:T(8,128)(2,1)S(1)}, bf16[32,3584]{1,0:T(8,128)(2,1)}, u32[]{:S(2)}) copy-start(bf16[32,3584]{1,0:T(8,128)(2,1)} %param.11) | copy-start | bytes 688132
  0.6 65.7 %collective-permute-start.21 = (bf16[1792,2432]{1,0:T(8,128)(2,1)}, bf16[1792,2432]{1,0:T(8,128)(2,1)}, u32[]{:S(2)}, u32[]{:S(2)}) collective-permute-start(bf16[1792,2432]{1,0:T(8,128)(2,1)} %refs_8_.1), channel_id=1, source_target_pairs={{0,8},{8,0},{1,9},{9,1},{2,10},{10,2},{3,11},{11,3},{4,12},{12,4},... | collective-permute-start | bytes 26148872 | tf_op jit(solution)/shard_map/ppermute | solution.py:377
  2.7 44.7 %copy-start.2 = (s32[256]{0:T(256)S(1)}, s32[256]{0:T(256)}, u32[]{:S(2)}) copy-start(s32[256]{0:T(256)} %param.13) | copy-start | bytes 3076
  8.2 9.1 %collective-permute-start = (f16[32,3584]{1,0:T(8,128)(2,1)}, f16[32,3584]{1,0:T(8,128)(2,1)}, u32[]{:S(2)}, u32[]{:S(2)}) collective-permute-start(f16[32,3584]{1,0:T(8,128)(2,1)} %convert_element_type.94), channel_id=1, source_target_pairs={{0,1},{1,0},{2,3},{3,2},{4,5},{5,4},{6,7},{7,6},{8,9},{9,8},{10,11... | collective-permute-start | bytes 688136 | tf_op jit(solution)/shard_map/ppermute | solution.py:322
  11.8 19.4 %collective-permute-start.11 = (bf16[32,3584]{1,0:T(8,128)(2,1)S(1)}, bf16[32,3584]{1,0:T(8,128)(2,1)}, u32[]{:S(2)}, u32[]{:S(2)}) collective-permute-start(bf16[32,3584]{1,0:T(8,128)(2,1)S(1)} %maximum_select_fusion.1.refs_0_), channel_id=1, source_target_pairs={{0,4},{1,5},{2,6},{3,7},{4,0},{5,1},{6,2},{7,3},{8,12},{9,13},{10,... | collective-permute-start | bytes 688136 | tf_op jit(solution)/shard_map/ppermute | solution.py:322
  14.5 21.0 %collective-permute-start.7 = (bf16[32,3584]{1,0:T(8,128)(2,1)S(1)}, bf16[32,3584]{1,0:T(8,128)(2,1)}, u32[]{:S(2)}, u32[]{:S(2)}) collective-permute-start(bf16[32,3584]{1,0:T(8,128)(2,1)S(1)} %maximum_select_fusion.1.refs_0_), channel_id=1, source_target_pairs={{0,2},{1,3},{2,0},{3,1},{4,6},{5,7},{6,4},{7,5},{8,10},{9,11},{10,... | collective-permute-start | bytes 688136 | tf_op jit(solution)/shard_map/ppermute | solution.py:322
  16.1 8.6 %collective-permute-start.2 = (f16[32,3584]{1,0:T(8,128)(2,1)S(1)}, f16[32,3584]{1,0:T(8,128)(2,1)S(1)}, u32[]{:S(2)}, u32[]{:S(2)}) collective-permute-start(f16[32,3584]{1,0:T(8,128)(2,1)S(1)} %convert_element_type.98), channel_id=1, source_target_pairs={{0,1},{1,0},{2,3},{3,2},{4,5},{5,4},{6,7},{7,6},{8,9},{9,8},{10,11... | collective-permute-start | bytes 688136 | tf_op jit(solution)/shard_map/ppermute | solution.py:322
  17.3 9.9 %collective-permute-start.4 = (f16[32,3584]{1,0:T(8,128)(2,1)S(1)}, f16[32,3584]{1,0:T(8,128)(2,1)S(1)}, u32[]{:S(2)}, u32[]{:S(2)}) collective-permute-start(f16[32,3584]{1,0:T(8,128)(2,1)S(1)} %convert_element_type.102), channel_id=1, source_target_pairs={{0,1},{1,0},{2,3},{3,2},{4,5},{5,4},{6,7},{7,6},{8,9},{9,8},{10,11... | collective-permute-start | bytes 688136 | tf_op jit(solution)/shard_map/ppermute | solution.py:322
  24.7 6.0 %collective-permute-start.1 = (f16[32,3584]{1,0:T(8,128)(2,1)S(1)}, f16[32,3584]{1,0:T(8,128)(2,1)S(1)}, u32[]{:S(2)}, u32[]{:S(2)}) collective-permute-start(f16[32,3584]{1,0:T(8,128)(2,1)S(1)} %add_convert_fusion.7), channel_id=1, source_target_pairs={{0,2},{1,3},{2,0},{3,1},{4,6},{5,7},{6,4},{7,5},{8,10},{9,11},{10,... | collective-permute-start | bytes 688136 | tf_op jit(solution)/shard_map/ppermute | solution.py:322
  27.3 6.7 %collective-permute-start.6 = (f16[32,3584]{1,0:T(8,128)(2,1)S(1)}, f16[32,3584]{1,0:T(8,128)(2,1)S(1)}, u32[]{:S(2)}, u32[]{:S(2)}) collective-permute-start(f16[32,3584]{1,0:T(8,128)(2,1)S(1)} %convert_element_type.106), channel_id=1, source_target_pairs={{0,1},{1,0},{2,3},{3,2},{4,5},{5,4},{6,7},{7,6},{8,9},{9,8},{10,11... | collective-permute-start | bytes 688136 | tf_op jit(solution)/shard_map/ppermute | solution.py:322
  30.7 11.5 %collective-permute-start.5 = (f16[32,3584]{1,0:T(8,128)(2,1)S(1)}, f16[32,3584]{1,0:T(8,128)(2,1)S(1)}, u32[]{:S(2)}, u32[]{:S(2)}) collective-permute-start(f16[32,3584]{1,0:T(8,128)(2,1)S(1)} %add_convert_fusion.5), channel_id=1, source_target_pairs={{0,2},{1,3},{2,0},{3,1},{4,6},{5,7},{6,4},{7,5},{8,10},{9,11},{10,... | collective-permute-start | bytes 688136 | tf_op jit(solution)/shard_map/ppermute | solution.py:322
  31.3 12.6 %collective-permute-start.3 = (f16[32,3584]{1,0:T(8,128)(2,1)S(1)}, f16[32,3584]{1,0:T(8,128)(2,1)S(1)}, u32[]{:S(2)}, u32[]{:S(2)}) collective-permute-start(f16[32,3584]{1,0:T(8,128)(2,1)S(1)} %add_convert_fusion.6), channel_id=1, source_target_pairs={{0,4},{1,5},{2,6},{3,7},{4,0},{5,1},{6,2},{7,3},{8,12},{9,13},{10,... | collective-permute-start | bytes 688136 | tf_op jit(solution)/shard_map/ppermute | solution.py:322
  34.0 10.5 %collective-permute-start.16 = (bf16[32,3584]{1,0:T(8,128)(2,1)S(1)}, bf16[32,3584]{1,0:T(8,128)(2,1)S(1)}, u32[]{:S(2)}, u32[]{:S(2)}) collective-permute-start(bf16[32,3584]{1,0:T(8,128)(2,1)S(1)} %maximum_select_fusion.1.refs_0_), channel_id=1, source_target_pairs={{0,1},{1,0},{2,3},{3,2},{4,5},{5,4},{6,7},{7,6},{8,9},{9,8},{10,11... | collective-permute-start | bytes 688136 | tf_op jit(solution)/shard_map/ppermute | solution.py:322
  35.5 12.5 %collective-permute-start.15 = (bf16[32,3584]{1,0:T(8,128)(2,1)}, bf16[32,3584]{1,0:T(8,128)(2,1)S(1)}, u32[]{:S(2)}, u32[]{:S(2)}) collective-permute-start(bf16[32,3584]{1,0:T(8,128)(2,1)} %collective-permute-done.11.refs_4_), channel_id=1, source_target_pairs={{0,2},{1,3},{2,0},{3,1},{4,6},{5,7},{6,4},{7,5},{8,10},{9,11},{10,... | collective-permute-start | bytes 688136 | tf_op jit(solution)/shard_map/ppermute | solution.py:322
  42.3 13.2 %collective-permute-start.12 = (bf16[32,3584]{1,0:T(8,128)(2,1)}, bf16[32,3584]{1,0:T(8,128)(2,1)S(1)}, u32[]{:S(2)}, u32[]{:S(2)}) collective-permute-start(bf16[32,3584]{1,0:T(8,128)(2,1)} %collective-permute-done.11.refs_4_), channel_id=1, source_target_pairs={{0,1},{1,0},{2,3},{3,2},{4,5},{5,4},{6,7},{7,6},{8,9},{9,8},{10,11... | collective-permute-start | bytes 688136 | tf_op jit(solution)/shard_map/ppermute | solution.py:322
  43.9 10.2 %collective-permute-start.8 = (bf16[32,3584]{1,0:T(8,128)(2,1)}, bf16[32,3584]{1,0:T(8,128)(2,1)S(1)}, u32[]{:S(2)}, u32[]{:S(2)}) collective-permute-start(bf16[32,3584]{1,0:T(8,128)(2,1)} %collective-permute-done.7.refs_2_), channel_id=1, source_target_pairs={{0,1},{1,0},{2,3},{3,2},{4,5},{5,4},{6,7},{7,6},{8,9},{9,8},{10,11... | collective-permute-start | bytes 688136 | tf_op jit(solution)/shard_map/ppermute | solution.py:322
  44.5 12.6 %collective-permute-start.14 = (bf16[32,3584]{1,0:T(8,128)(2,1)S(1)}, bf16[32,3584]{1,0:T(8,128)(2,1)S(1)}, u32[]{:S(2)}, u32[]{:S(2)}) collective-permute-start(bf16[32,3584]{1,0:T(8,128)(2,1)S(1)} %maximum_select_fusion.refs_0_), channel_id=1, source_target_pairs={{0,4},{1,5},{2,6},{3,7},{4,0},{5,1},{6,2},{7,3},{8,12},{9,13},{10,... | collective-permute-start | bytes 688136 | tf_op jit(solution)/shard_map/ppermute | solution.py:322
  48.0 14.4 %collective-permute-start.17 = (bf16[32,3584]{1,0:T(8,128)(2,1)S(1)}, bf16[32,3584]{1,0:T(8,128)(2,1)S(1)}, u32[]{:S(2)}, u32[]{:S(2)}) collective-permute-start(bf16[32,3584]{1,0:T(8,128)(2,1)S(1)} %collective-permute-done.15.refs_6_), channel_id=1, source_target_pairs={{0,1},{1,0},{2,3},{3,2},{4,5},{5,4},{6,7},{7,6},{8,9},{9,8},{10,11... | collective-permute-start | bytes 688136 | tf_op jit(solution)/shard_map/ppermute | solution.py:322
  54.1 6.0 %collective-permute-start.10 = (bf16[32,3584]{1,0:T(8,128)(2,1)S(1)}, bf16[32,3584]{1,0:T(8,128)(2,1)S(1)}, u32[]{:S(2)}, u32[]{:S(2)}) collective-permute-start(bf16[32,3584]{1,0:T(8,128)(2,1)S(1)} %maximum_select_fusion.refs_0_), channel_id=1, source_target_pairs={{0,2},{1,3},{2,0},{3,1},{4,6},{5,7},{6,4},{7,5},{8,10},{9,11},{10,... | collective-permute-start | bytes 688136 | tf_op jit(solution)/shard_map/ppermute | solution.py:322
  55.5 8.5 %collective-permute-start.9 = (bf16[32,3584]{1,0:T(8,128)(2,1)S(1)}, bf16[32,3584]{1,0:T(8,128)(2,1)S(1)}, u32[]{:S(2)}, u32[]{:S(2)}) collective-permute-start(bf16[32,3584]{1,0:T(8,128)(2,1)S(1)} %maximum_select_fusion.refs_0_), channel_id=1, source_target_pairs={{0,1},{1,0},{2,3},{3,2},{4,5},{5,4},{6,7},{7,6},{8,9},{9,8},{10,11... | collective-permute-start | bytes 688136 | tf_op jit(solution)/shard_map/ppermute | solution.py:322
  57.1 6.9 %collective-permute-start.19 = (bf16[32,3584]{1,0:T(8,128)(2,1)S(1)}, bf16[32,3584]{1,0:T(8,128)(2,1)S(1)}, u32[]{:S(2)}, u32[]{:S(2)}) collective-permute-start(bf16[32,3584]{1,0:T(8,128)(2,1)S(1)} %collective-permute-done.14.refs_4_), channel_id=1, source_target_pairs={{0,2},{1,3},{2,0},{3,1},{4,6},{5,7},{6,4},{7,5},{8,10},{9,11},{10,... | collective-permute-start | bytes 688136 | tf_op jit(solution)/shard_map/ppermute | solution.py:322
  60.1 20.9 %collective-permute-start.13 = (bf16[32,3584]{1,0:T(8,128)(2,1)S(1)}, bf16[32,3584]{1,0:T(8,128)(2,1)S(1)}, u32[]{:S(2)}, u32[]{:S(2)}) collective-permute-start(bf16[32,3584]{1,0:T(8,128)(2,1)S(1)} %collective-permute-done.10.refs_2_), channel_id=1, source_target_pairs={{0,1},{1,0},{2,3},{3,2},{4,5},{5,4},{6,7},{7,6},{8,9},{9,8},{10,11... | collective-permute-start | bytes 688136 | tf_op jit(solution)/shard_map/ppermute | solution.py:322
  62.5 18.6 %collective-permute-start.18 = (bf16[32,3584]{1,0:T(8,128)(2,1)S(1)}, bf16[32,3584]{1,0:T(8,128)(2,1)S(1)}, u32[]{:S(2)}, u32[]{:S(2)}) collective-permute-start(bf16[32,3584]{1,0:T(8,128)(2,1)S(1)} %collective-permute-done.14.refs_4_), channel_id=1, source_target_pairs={{0,1},{1,0},{2,3},{3,2},{4,5},{5,4},{6,7},{7,6},{8,9},{9,8},{10,11... | collective-permute-start | bytes 688136 | tf_op jit(solution)/shard_map/ppermute | solution.py:322
  64.0 17.0 %collective-permute-start.20 = (bf16[32,3584]{1,0:T(8,128)(2,1)S(1)}, bf16[32,3584]{1,0:T(8,128)(2,1)S(1)}, u32[]{:S(2)}, u32[]{:S(2)}) collective-permute-start(bf16[32,3584]{1,0:T(8,128)(2,1)S(1)} %collective-permute-done.19.refs_6_), channel_id=1, source_target_pairs={{0,1},{1,0},{2,3},{3,2},{4,5},{5,4},{6,7},{7,6},{8,9},{9,8},{10,11... | collective-permute-start | bytes 688136 | tf_op jit(solution)/shard_map/ppermute | solution.py:322
  66.3 3.5 %copy-start = (bf16[1792,2432]{1,0:T(8,128)(2,1)S(1)}, bf16[1792,2432]{1,0:T(8,128)(2,1)}, u32[]{:S(2)}) copy-start(bf16[1792,2432]{1,0:T(8,128)(2,1)} %refs_8_.1) | copy-start | bytes 26148868
  88.2 5.9 %collective-permute-start.25 = (f32[8,256]{1,0:T(8,128)S(1)}, f32[8,256]{1,0:T(8,128)S(1)}, u32[]{:S(2)}, u32[]{:S(2)}) collective-permute-start(f32[8,256]{1,0:T(8,128)S(1)} %get-tuple-element.60.refs_0_), channel_id=1, source_target_pairs={{0,4},{1,5},{2,6},{3,7},{4,0},{5,1},{6,2},{7,3},{8,12},{9,13},{10,... | collective-permute-start | bytes 24584 | tf_op jit(solution)/shard_map/ppermute | solution.py:322
  90.6 5.2 %collective-permute-start.24 = (f32[8,256]{1,0:T(8,128)S(1)}, f32[8,256]{1,0:T(8,128)S(1)}, u32[]{:S(2)}, u32[]{:S(2)}) collective-permute-start(f32[8,256]{1,0:T(8,128)S(1)} %get-tuple-element.60.refs_0_), channel_id=1, source_target_pairs={{0,3},{1,2},{2,1},{3,0},{4,7},{5,6},{6,5},{7,4},{8,11},{9,10},{10,... | collective-permute-start | bytes 24584 | tf_op jit(solution)/shard_map/ppermute | solution.py:322
  91.1 6.6 %collective-permute-start.23 = (f32[8,256]{1,0:T(8,128)S(1)}, f32[8,256]{1,0:T(8,128)S(1)}, u32[]{:S(2)}, u32[]{:S(2)}) collective-permute-start(f32[8,256]{1,0:T(8,128)S(1)} %get-tuple-element.60.refs_0_), channel_id=1, source_target_pairs={{0,2},{1,3},{2,0},{3,1},{4,6},{5,7},{6,4},{7,5},{8,10},{9,11},{10,... | collective-permute-start | bytes 24584 | tf_op jit(solution)/shard_map/ppermute | solution.py:322
  92.3 5.4 %collective-permute-start.22 = (f32[8,256]{1,0:T(8,128)S(1)}, f32[8,256]{1,0:T(8,128)S(1)}, u32[]{:S(2)}, u32[]{:S(2)}) collective-permute-start(f32[8,256]{1,0:T(8,128)S(1)} %get-tuple-element.60.refs_0_), channel_id=1, source_target_pairs={{0,1},{1,0},{2,3},{3,2},{4,5},{5,4},{6,7},{7,6},{8,9},{9,8},{10,11... | collective-permute-start | bytes 24584 | tf_op jit(solution)/shard_map/ppermute | solution.py:322
  94.1 4.6 %collective-permute-start.28 = (f32[8,256]{1,0:T(8,128)S(1)}, f32[8,256]{1,0:T(8,128)S(1)}, u32[]{:S(2)}, u32[]{:S(2)}) collective-permute-start(f32[8,256]{1,0:T(8,128)S(1)} %collective-permute-done.25.refs_4_), channel_id=1, source_target_pairs={{0,3},{1,2},{2,1},{3,0},{4,7},{5,6},{6,5},{7,4},{8,11},{9,10},{10,... | collective-permute-start | bytes 24584 | tf_op jit(solution)/shard_map/ppermute | solution.py:322
  94.6 4.1 %collective-permute-start.27 = (f32[8,256]{1,0:T(8,128)S(1)}, f32[8,256]{1,0:T(8,128)S(1)}, u32[]{:S(2)}, u32[]{:S(2)}) collective-permute-start(f32[8,256]{1,0:T(8,128)S(1)} %collective-permute-done.25.refs_4_), channel_id=1, source_target_pairs={{0,2},{1,3},{2,0},{3,1},{4,6},{5,7},{6,4},{7,5},{8,10},{9,11},{10,... | collective-permute-start | bytes 24584 | tf_op jit(solution)/shard_map/ppermute | solution.py:322
  95.8 3.7 %collective-permute-start.26 = (f32[8,256]{1,0:T(8,128)S(1)}, f32[8,256]{1,0:T(8,128)S(1)}, u32[]{:S(2)}, u32[]{:S(2)}) collective-permute-start(f32[8,256]{1,0:T(8,128)S(1)} %collective-permute-done.25.refs_4_), channel_id=1, source_target_pairs={{0,1},{1,0},{2,3},{3,2},{4,5},{5,4},{6,7},{7,6},{8,9},{9,8},{10,11... | collective-permute-start | bytes 24584 | tf_op jit(solution)/shard_map/ppermute | solution.py:322
  107.8 6.1 %collective-permute-start.31 = (f16[32,3584]{1,0:T(8,128)(2,1)S(1)}, f16[32,3584]{1,0:T(8,128)(2,1)S(1)}, u32[]{:S(2)}, u32[]{:S(2)}) collective-permute-start(f16[32,3584]{1,0:T(8,128)(2,1)S(1)} %convert_element_type.113), channel_id=1, source_target_pairs={{0,1},{1,0},{2,3},{3,2},{4,5},{5,4},{6,7},{7,6},{8,9},{9,8},{10,11... | collective-permute-start | bytes 688136 | tf_op jit(solution)/shard_map/ppermute | solution.py:322
  109.7 6.6 %collective-permute-start.29 = (f16[32,3584]{1,0:T(8,128)(2,1)S(1)}, f16[32,3584]{1,0:T(8,128)(2,1)S(1)}, u32[]{:S(2)}, u32[]{:S(2)}) collective-permute-start(f16[32,3584]{1,0:T(8,128)(2,1)S(1)} %convert_element_type.109), channel_id=1, source_target_pairs={{0,1},{1,0},{2,3},{3,2},{4,5},{5,4},{6,7},{7,6},{8,9},{9,8},{10,11... | collective-permute-start | bytes 688136 | tf_op jit(solution)/shard_map/ppermute | solution.py:322
  113.9 12.2 %collective-permute-start.35 = (f16[32,3584]{1,0:T(8,128)(2,1)S(1)}, f16[32,3584]{1,0:T(8,128)(2,1)S(1)}, u32[]{:S(2)}, u32[]{:S(2)}) collective-permute-start(f16[32,3584]{1,0:T(8,128)(2,1)S(1)} %convert_element_type.121), channel_id=1, source_target_pairs={{0,1},{1,0},{2,3},{3,2},{4,5},{5,4},{6,7},{7,6},{8,9},{9,8},{10,11... | collective-permute-start | bytes 688136 | tf_op jit(solution)/shard_map/ppermute | solution.py:322
  116.3 6.0 %collective-permute-start.33 = (f16[32,3584]{1,0:T(8,128)(2,1)S(1)}, f16[32,3584]{1,0:T(8,128)(2,1)S(1)}, u32[]{:S(2)}, u32[]{:S(2)}) collective-permute-start(f16[32,3584]{1,0:T(8,128)(2,1)S(1)} %convert_element_type.117), channel_id=1, source_target_pairs={{0,1},{1,0},{2,3},{3,2},{4,5},{5,4},{6,7},{7,6},{8,9},{9,8},{10,11... | collective-permute-start | bytes 688136 | tf_op jit(solution)/shard_map/ppermute | solution.py:322
  118.2 6.1 %collective-permute-start.30 = (f16[32,3584]{1,0:T(8,128)(2,1)S(1)}, f16[32,3584]{1,0:T(8,128)(2,1)S(1)}, u32[]{:S(2)}, u32[]{:S(2)}) collective-permute-start(f16[32,3584]{1,0:T(8,128)(2,1)S(1)} %add_convert_fusion.3), channel_id=1, source_target_pairs={{0,2},{1,3},{2,0},{3,1},{4,6},{5,7},{6,4},{7,5},{8,10},{9,11},{10,... | collective-permute-start | bytes 688136 | tf_op jit(solution)/shard_map/ppermute | solution.py:322
  122.4 6.1 %collective-permute-start.34 = (f16[32,3584]{1,0:T(8,128)(2,1)S(1)}, f16[32,3584]{1,0:T(8,128)(2,1)S(1)}, u32[]{:S(2)}, u32[]{:S(2)}) collective-permute-start(f16[32,3584]{1,0:T(8,128)(2,1)S(1)} %add_convert_fusion.1), channel_id=1, source_target_pairs={{0,2},{1,3},{2,0},{3,1},{4,6},{5,7},{6,4},{7,5},{8,10},{9,11},{10,... | collective-permute-start | bytes 688136 | tf_op jit(solution)/shard_map/ppermute | solution.py:322
  124.5 9.4 %collective-permute-start.32 = (f16[32,3584]{1,0:T(8,128)(2,1)S(1)}, f16[32,3584]{1,0:T(8,128)(2,1)S(1)}, u32[]{:S(2)}, u32[]{:S(2)}) collective-permute-start(f16[32,3584]{1,0:T(8,128)(2,1)S(1)} %add_convert_fusion.2), channel_id=1, source_target_pairs={{0,4},{1,5},{2,6},{3,7},{4,0},{5,1},{6,2},{7,3},{8,12},{9,13},{10,... | collective-permute-start | bytes 688136 | tf_op jit(solution)/shard_map/ppermute | solution.py:322

commit v12 on v11

--- a/solution.py
+++ b/solution.py
@@ -11,7 +11,7 @@
 wire = jnp.float16
 lanes = 128
 vmem_bytes = 12 * 1024 * 1024
-project_bytes = 50 * 1024 * 1024
+project_bytes = 49 * 1024 * 1024
 
 in_vmem = pl.BlockSpec(memory_space=pltpu.VMEM)
 in_smem = pl.BlockSpec(memory_space=pltpu.SMEM)
@@ -22,7 +22,7 @@
     return [(start, min(step, total - start)) for start in range(0, total, step)]
 
 
-def project_kernel(count, step, member_ref, teacher_ref, weight_ref, *rest):
+def project_kernel(count, step, place_ref, member_ref, student_ref, teacher_ref, weight_ref, turned_ref, *rest):
     outs, (teacher, weight, aligned, sems) = rest[:count], rest[count:]
     blk = outs[0].shape[0]
     parts = cuts(weight.shape[1], step)
@@ -31,6 +31,11 @@
     for index, (start, size) in enumerate(parts):
         at = pl.ds(start, size)
         pltpu.make_async_copy(weight_ref.at[:, at], weight.at[:, at], sems.at[index]).start()
+    half = student_ref.shape[1] // 2
+    odd = place_ref[1] == 1
+    low, high = student_ref[:, :half], student_ref[:, half:]
+    turned_ref[:, :half] = jnp.where(odd, high, low)
+    turned_ref[:, half:] = jnp.where(odd, low, high)
     member = member_ref[...]
     sizes = jnp.sum(member.astype(jnp.float32), axis=1, keepdims=True)
     first.wait()
@@ -48,14 +53,15 @@
     lax.fori_loop(0, len(parts), one, 0)
 
 
-def project(member, teacher_rows, proj_weight, count, step):
+def project(place, member, student, teacher_rows, proj_weight, count, step):
     slab_rows, (depth, width) = member.shape[0], proj_weight.shape
     blk = slab_rows // count
     return pl.pallas_call(
         functools.partial(project_kernel, count, step),
-        in_specs=[in_vmem, in_place, in_place],
-        out_specs=[in_vmem] * count,
-        out_shape=[jax.ShapeDtypeStruct((blk, width), jnp.float32)] * count,
+        in_specs=[in_smem, in_vmem, in_vmem, in_place, in_place],
+        out_specs=[in_vmem] * (count + 1),
+        out_shape=[jax.ShapeDtypeStruct(student.shape, jnp.bfloat16)]
+        + [jax.ShapeDtypeStruct((blk, width), jnp.float32)] * count,
         scratch_shapes=[
             pltpu.VMEM(teacher_rows.shape, jnp.bfloat16),
             pltpu.VMEM(proj_weight.shape, jnp.bfloat16),
@@ -68,7 +74,7 @@
             bytes_accessed=2 * depth * (width + teacher_rows.shape[0]) + 4 * slab_rows * width,
             transcendentals=0,
         ),
-    )(member, teacher_rows, proj_weight)
+    )(place, member, student, teacher_rows, proj_weight)
 
 
 class Fetch:
@@ -380,9 +386,12 @@
         row_id = ((spot // blk) ^ me) * blk + spot % blk
         alive = lax.iota(jnp.int32, teach_rows) < counts[0]
         member = (owner[None, :] == row_id[:, None]) & alive[None, :]
-        parts = project(member.astype(jnp.bfloat16), teacher_rows, proj_weight, vocab_size, 512 if student_hidden.shape[1] % 512 == 0 else student_hidden.shape[1])
+        own_rows, *parts = project(
+            place, member.astype(jnp.bfloat16), student_hidden, teacher_rows, proj_weight, vocab_size,
+            512 if student_hidden.shape[1] % 512 == 0 else student_hidden.shape[1],
+        )
         projected_own, line = reduce_blocks(parts)
-        hidden = spread(tie(turned(student_hidden), parts[-1]), line)
+        hidden = spread(own_rows, line)
         projected = spread(turned(projected_own.astype(jnp.bfloat16)), line)
 
         column = (in_order(targets) - me * vocab_dev)[:, None]

time: 135 us -> 148 us (1.096)
  waiting for transfers between devices: 39.3 us -> 52.5 us
  other arithmetic: 5.18 us -> 2.57 us
  Pallas kernels: 31.6 us -> 33.9 us
    ppermute x35, waiting for transfers between devices: 39.3 us -> 52.5 us  [trade(): lax.ppermute(block, 'vocab', [(at, at ^ mask) for at in range(vocab_size)])]
    convert_element_type x14, other arithmetic: 2.23 us -> 0.63 us  [reduce_blocks(): block = terms[mask].astype(wire)]
  transfers between devices with their start and end apart: 36 -> 36, of which waited for: 17 -> 18; matrix products, arithmetic and copies ran while one was open for 4% -> 2% of each run, Pallas kernels for 12% -> 12%
where the time goes in v12:
time: 148 us
  waiting for transfers between devices  52.5 us (35%)
  starting transfers between devices  52 us (35%)
  Pallas kernels  33.9 us (23%)
  local copies, waits for them, and re-layouts  5.26 us (4%)
  other arithmetic  2.57 us (2%)
  between operations  1.53 us (1%)
    ppermute x35, waiting for transfers between devices, trade(): lax.ppermute(block, 'vocab', [(at, at ^ mask) for at in range(vocab_size)])  52.5 us
    ppermute x35, starting transfers between devices, trade(): lax.ppermute(block, 'vocab', [(at, at ^ mask) for at in range(vocab_size)])  51.5 us
    pallas_call x1, Pallas kernels, student_logits(): pl.pallas_call(functools.partial(student_kernel, len(pieces), step, chunk...  11.9 us
    pallas_call x1, Pallas kernels, gradient(): pl.pallas_call(functools.partial(gradient_kernel, bits, step, chunk), in_...  8.37 us
    pallas_call x1, Pallas kernels, teacher_logits(): pl.pallas_call(functools.partial(teacher_kernel, len(pieces), step, chunk...  8.3 us
    pallas_call x1, Pallas kernels, project(): pl.pallas_call(functools.partial(project_kernel, count, step), in_specs=[...  5.34 us
    unnamed x6, local copies, waits for them, and re-layouts  4.41 us
  transfers between devices with their start and end apart: 36, of which 18 were waited for; matrix products, arithmetic and copies ran while one was open for 2% of the time, Pallas kernels for 12%

profile of v12, /device:TPU:0, one launch (start us, length us, event | category | flops | bytes accessed | tf_op | source)
XLA Modules:
  0.0 147.8 jit_solution(9101125736987143446)
XLA Ops:
  0.6 0.5 collective-permute-start.21
  1.9 0.8 and_convert_fusion.member_ref
  2.7 0.9 copy-done.1
  3.7 5.3 %shard_map.86 = (bf16[32,3584]{1,0:T(8,128)(2,1)S(1)}, f32[32,3584]{1,0:T(8,128)S(1)}, f32[32,3584]{1,0:T(8,128)S(1)}, f32[32,3584]{1,0:T(8,128)S(1)}, f32[32,35...) custom-call(s32[2]{0:T(128)S(1)} %pad_add_fusion.place_ref, ...), custom_call_target="tpu_custom_call" | custom-call | flops 2147483648 | bytes 12058624 | tf_op jit(solution)/shard_map/pallas_call | solution.py:59
  9.1 2.6 %collective-permute-start.2 = (f16[32,3584]{1,0:T(8,128)(2,1)S(1)}, f16[32,3584]{1,0:T(8,128)(2,1)S(1)}, u32[]{:S(2)}, u32[]{:S(2)}) collective-permute-start(f16[32,3584]{1,0:T(8,128)(2,1)S(1)} %convert_element_type.98), channel_id=1, source_target_pairs={{0,1},{1,0},{2,3},{3,2},{4,5},{5,4},{6,7},{7,6},{8,9},{9,8},{10,11... | collective-permute-start | bytes 688136 | tf_op jit(solution)/shard_map/ppermute | solution.py:328
  11.7 0.1 collective-permute-start
  11.8 3.1 %collective-permute-start.11 = (bf16[32,3584]{1,0:T(8,128)(2,1)S(1)}, bf16[32,3584]{1,0:T(8,128)(2,1)S(1)}, u32[]{:S(2)}, u32[]{:S(2)}) collective-permute-start(bf16[32,3584]{1,0:T(8,128)(2,1)S(1)} %get-tuple-element.53.refs_0_), channel_id=1, source_target_pairs={{0,4},{1,5},{2,6},{3,7},{4,0},{5,1},{6,2},{7,3},{8,12},{9,13},{10,... | collective-permute-start | bytes 688136 | tf_op jit(solution)/shard_map/ppermute | solution.py:328
  14.8 1.6 %collective-permute-start.7 = (bf16[32,3584]{1,0:T(8,128)(2,1)S(1)}, bf16[32,3584]{1,0:T(8,128)(2,1)S(1)}, u32[]{:S(2)}, u32[]{:S(2)}) collective-permute-start(bf16[32,3584]{1,0:T(8,128)(2,1)S(1)} %get-tuple-element.53.refs_0_), channel_id=1, source_target_pairs={{0,2},{1,3},{2,0},{3,1},{4,6},{5,7},{6,4},{7,5},{8,10},{9,11},{10,... | collective-permute-start | bytes 688136 | tf_op jit(solution)/shard_map/ppermute | solution.py:328
  16.5 1.6 %collective-permute-done.2 = f16[32,3584]{1,0:T(8,128)(2,1)S(1)} collective-permute-done((f16[32,3584]{1,0:T(8,128)(2,1)S(1)}, f16[32,3584]{1,0:T(8,128)(2,1)S(1)}, u32[]{:S(2)}, u32[]{:S(2)}) %collective-permute-start.2) | collective-permute-done | bytes 229408 | tf_op jit(solution)/shard_map/ppermute | solution.py:328
  18.1 1.9 %collective-permute-start.6 = (f16[32,3584]{1,0:T(8,128)(2,1)S(1)}, f16[32,3584]{1,0:T(8,128)(2,1)S(1)}, u32[]{:S(2)}, u32[]{:S(2)}) collective-permute-start(f16[32,3584]{1,0:T(8,128)(2,1)S(1)} %convert_element_type.106), channel_id=1, source_target_pairs={{0,1},{1,0},{2,3},{3,2},{4,5},{5,4},{6,7},{7,6},{8,9},{9,8},{10,11... | collective-permute-start | bytes 688136 | tf_op jit(solution)/shard_map/ppermute | solution.py:328
  20.0 3.0 %collective-permute-done = f16[32,3584]{1,0:T(8,128)(2,1)S(1)} collective-permute-done((f16[32,3584]{1,0:T(8,128)(2,1)S(1)}, f16[32,3584]{1,0:T(8,128)(2,1)S(1)}, u32[]{:S(2)}, u32[]{:S(2)}) %collective-permute-start) | collective-permute-done | bytes 229408 | tf_op jit(solution)/shard_map/ppermute | solution.py:328
  23.0 1.9 %collective-permute-start.4 = (f16[32,3584]{1,0:T(8,128)(2,1)S(1)}, f16[32,3584]{1,0:T(8,128)(2,1)S(1)}, u32[]{:S(2)}, u32[]{:S(2)}) collective-permute-start(f16[32,3584]{1,0:T(8,128)(2,1)S(1)} %convert_element_type.102), channel_id=1, source_target_pairs={{0,1},{1,0},{2,3},{3,2},{4,5},{5,4},{6,7},{7,6},{8,9},{9,8},{10,11... | collective-permute-start | bytes 688136 | tf_op jit(solution)/shard_map/ppermute | solution.py:328
  25.0 7.6 %collective-permute-done.4 = f16[32,3584]{1,0:T(8,128)(2,1)S(1)} collective-permute-done((f16[32,3584]{1,0:T(8,128)(2,1)S(1)}, f16[32,3584]{1,0:T(8,128)(2,1)S(1)}, u32[]{:S(2)}, u32[]{:S(2)}) %collective-permute-start.4) | collective-permute-done | bytes 229408 | tf_op jit(solution)/shard_map/ppermute | solution.py:328
  32.7 1.8 %collective-permute-start.1 = (f16[32,3584]{1,0:T(8,128)(2,1)S(1)}, f16[32,3584]{1,0:T(8,128)(2,1)S(1)}, u32[]{:S(2)}, u32[]{:S(2)}) collective-permute-start(f16[32,3584]{1,0:T(8,128)(2,1)S(1)} %add_convert_fusion.7), channel_id=1, source_target_pairs={{0,2},{1,3},{2,0},{3,1},{4,6},{5,7},{6,4},{7,5},{8,10},{9,11},{10,... | collective-permute-start | bytes 688136 | tf_op jit(solution)/shard_map/ppermute | solution.py:328
  34.5 5.6 %collective-permute-done.1 = f16[32,3584]{1,0:T(8,128)(2,1)S(1)} collective-permute-done((f16[32,3584]{1,0:T(8,128)(2,1)S(1)}, f16[32,3584]{1,0:T(8,128)(2,1)S(1)}, u32[]{:S(2)}, u32[]{:S(2)}) %collective-permute-start.1) | collective-permute-done | bytes 229408 | tf_op jit(solution)/shard_map/ppermute | solution.py:328
  40.1 1.6 %collective-permute-start.5 = (f16[32,3584]{1,0:T(8,128)(2,1)S(1)}, f16[32,3584]{1,0:T(8,128)(2,1)S(1)}, u32[]{:S(2)}, u32[]{:S(2)}) collective-permute-start(f16[32,3584]{1,0:T(8,128)(2,1)S(1)} %add_convert_fusion.5), channel_id=1, source_target_pairs={{0,2},{1,3},{2,0},{3,1},{4,6},{5,7},{6,4},{7,5},{8,10},{9,11},{10,... | collective-permute-start | bytes 688136 | tf_op jit(solution)/shard_map/ppermute | solution.py:328
  41.7 0.1 add_convert_fusion.6
  41.8 2.7 %collective-permute-start.3 = (f16[32,3584]{1,0:T(8,128)(2,1)S(1)}, f16[32,3584]{1,0:T(8,128)(2,1)S(1)}, u32[]{:S(2)}, u32[]{:S(2)}) collective-permute-start(f16[32,3584]{1,0:T(8,128)(2,1)S(1)} %add_convert_fusion.6), channel_id=1, source_target_pairs={{0,4},{1,5},{2,6},{3,7},{4,0},{5,1},{6,2},{7,3},{8,12},{9,13},{10,... | collective-permute-start | bytes 688136 | tf_op jit(solution)/shard_map/ppermute | solution.py:328
  44.4 1.5 %collective-permute-start.16 = (bf16[32,3584]{1,0:T(8,128)(2,1)S(1)}, bf16[32,3584]{1,0:T(8,128)(2,1)S(1)}, u32[]{:S(2)}, u32[]{:S(2)}) collective-permute-start(bf16[32,3584]{1,0:T(8,128)(2,1)S(1)} %get-tuple-element.53.refs_0_), channel_id=1, source_target_pairs={{0,1},{1,0},{2,3},{3,2},{4,5},{5,4},{6,7},{7,6},{8,9},{9,8},{10,11... | collective-permute-start | bytes 688136 | tf_op jit(solution)/shard_map/ppermute | solution.py:328
  46.0 0.5 collective-permute-start.15
  46.4 7.1 %collective-permute-done.5 = f16[32,3584]{1,0:T(8,128)(2,1)S(1)} collective-permute-done((f16[32,3584]{1,0:T(8,128)(2,1)S(1)}, f16[32,3584]{1,0:T(8,128)(2,1)S(1)}, u32[]{:S(2)}, u32[]{:S(2)}) %collective-permute-start.5) | collective-permute-done | bytes 229408 | tf_op jit(solution)/shard_map/ppermute | solution.py:328
  53.5 2.0 %collective-permute-start.12 = (bf16[32,3584]{1,0:T(8,128)(2,1)S(1)}, bf16[32,3584]{1,0:T(8,128)(2,1)S(1)}, u32[]{:S(2)}, u32[]{:S(2)}) collective-permute-start(bf16[32,3584]{1,0:T(8,128)(2,1)S(1)} %collective-permute-done.11.refs_4_), channel_id=1, source_target_pairs={{0,1},{1,0},{2,3},{3,2},{4,5},{5,4},{6,7},{7,6},{8,9},{9,8},{10,11... | collective-permute-start | bytes 688136 | tf_op jit(solution)/shard_map/ppermute | solution.py:328
  55.6 0.1 add_convert_fusion.4
  55.8 2.0 %collective-permute-start.14 = (bf16[32,3584]{1,0:T(8,128)(2,1)S(1)}, bf16[32,3584]{1,0:T(8,128)(2,1)S(1)}, u32[]{:S(2)}, u32[]{:S(2)}) collective-permute-start(bf16[32,3584]{1,0:T(8,128)(2,1)S(1)} %maximum_select_fusion.refs_0_), channel_id=1, source_target_pairs={{0,4},{1,5},{2,6},{3,7},{4,0},{5,1},{6,2},{7,3},{8,12},{9,13},{10,... | collective-permute-start | bytes 688136 | tf_op jit(solution)/shard_map/ppermute | solution.py:328
  57.9 1.0 collective-permute-done.15.refs_6_
  58.9 1.9 %collective-permute-start.17 = (bf16[32,3584]{1,0:T(8,128)(2,1)S(1)}, bf16[32,3584]{1,0:T(8,128)(2,1)S(1)}, u32[]{:S(2)}, u32[]{:S(2)}) collective-permute-start(bf16[32,3584]{1,0:T(8,128)(2,1)S(1)} %collective-permute-done.15.refs_6_), channel_id=1, source_target_pairs={{0,1},{1,0},{2,3},{3,2},{4,5},{5,4},{6,7},{7,6},{8,9},{9,8},{10,11... | collective-permute-start | bytes 688136 | tf_op jit(solution)/shard_map/ppermute | solution.py:328
  60.8 5.7 %collective-permute-done.8.refs_3_ = bf16[32,3584]{1,0:T(8,128)(2,1)S(1)} collective-permute-done((bf16[32,3584]{1,0:T(8,128)(2,1)S(1)}, bf16[32,3584]{1,0:T(8,128)(2,1)S(1)}, u32[]{:S(2)}, u32[]{:S(2)}) %collective-permute-start.8) | collective-permute-done | bytes 229408 | tf_op jit(solution)/shard_map/ppermute | solution.py:328
  66.5 2.3 %collective-permute-start.9 = (bf16[32,3584]{1,0:T(8,128)(2,1)S(1)}, bf16[32,3584]{1,0:T(8,128)(2,1)S(1)}, u32[]{:S(2)}, u32[]{:S(2)}) collective-permute-start(bf16[32,3584]{1,0:T(8,128)(2,1)S(1)} %maximum_select_fusion.refs_0_), channel_id=1, source_target_pairs={{0,1},{1,0},{2,3},{3,2},{4,5},{5,4},{6,7},{7,6},{8,9},{9,8},{10,11... | collective-permute-start | bytes 688136 | tf_op jit(solution)/shard_map/ppermute | solution.py:328
  68.8 2.0 %collective-permute-start.19 = (bf16[32,3584]{1,0:T(8,128)(2,1)S(1)}, bf16[32,3584]{1,0:T(8,128)(2,1)S(1)}, u32[]{:S(2)}, u32[]{:S(2)}) collective-permute-start(bf16[32,3584]{1,0:T(8,128)(2,1)S(1)} %collective-permute-done.14.refs_4_), channel_id=1, source_target_pairs={{0,2},{1,3},{2,0},{3,1},{4,6},{5,7},{6,4},{7,5},{8,10},{9,11},{10,... | collective-permute-start | bytes 688136 | tf_op jit(solution)/shard_map/ppermute | solution.py:328
  70.9 1.7 %collective-permute-done.10.refs_2_ = bf16[32,3584]{1,0:T(8,128)(2,1)S(1)} collective-permute-done((bf16[32,3584]{1,0:T(8,128)(2,1)S(1)}, bf16[32,3584]{1,0:T(8,128)(2,1)S(1)}, u32[]{:S(2)}, u32[]{:S(2)}) %collective-permute-start.10) | collective-permute-done | bytes 229408 | tf_op jit(solution)/shard_map/ppermute | solution.py:328
  72.5 2.3 %collective-permute-start.13 = (bf16[32,3584]{1,0:T(8,128)(2,1)S(1)}, bf16[32,3584]{1,0:T(8,128)(2,1)S(1)}, u32[]{:S(2)}, u32[]{:S(2)}) collective-permute-start(bf16[32,3584]{1,0:T(8,128)(2,1)S(1)} %collective-permute-done.10.refs_2_), channel_id=1, source_target_pairs={{0,1},{1,0},{2,3},{3,2},{4,5},{5,4},{6,7},{7,6},{8,9},{9,8},{10,11... | collective-permute-start | bytes 688136 | tf_op jit(solution)/shard_map/ppermute | solution.py:328
  74.9 1.5 %collective-permute-done.9.refs_1_ = bf16[32,3584]{1,0:T(8,128)(2,1)S(1)} collective-permute-done((bf16[32,3584]{1,0:T(8,128)(2,1)S(1)}, bf16[32,3584]{1,0:T(8,128)(2,1)S(1)}, u32[]{:S(2)}, u32[]{:S(2)}) %collective-permute-start.9) | collective-permute-done | bytes 229408 | tf_op jit(solution)/shard_map/ppermute | solution.py:328
  76.3 2.3 %collective-permute-start.20 = (bf16[32,3584]{1,0:T(8,128)(2,1)S(1)}, bf16[32,3584]{1,0:T(8,128)(2,1)}, u32[]{:S(2)}, u32[]{:S(2)}) collective-permute-start(bf16[32,3584]{1,0:T(8,128)(2,1)S(1)} %collective-permute-done.19.refs_6_), channel_id=1, source_target_pairs={{0,1},{1,0},{2,3},{3,2},{4,5},{5,4},{6,7},{7,6},{8,9},{9,8},{10,11... | collective-permute-start | bytes 688136 | tf_op jit(solution)/shard_map/ppermute | solution.py:328
  78.6 0.1 sub.26.refs_10_
  78.8 3.5 %copy-done = bf16[1792,2432]{1,0:T(8,128)(2,1)S(1)} copy-done((bf16[1792,2432]{1,0:T(8,128)(2,1)S(1)}, bf16[1792,2432]{1,0:T(8,128)(2,1)}, u32[]{:S(2)}) %copy-start) | copy-done | bytes 8716312
  82.3 11.9 %shard_map.87 = (f32[256,2432]{1,0:T(8,128)S(1)}, f32[256,2432]{1,0:T(8,128)S(1)}, f32[8,256]{1,0:T(8,128)S(1)}, bf16[3584,2432]{1,0:T(8,128)(2,1)S(1)}) custom-call(bf16[32,3584]{1,0:T(8,128)(2,1)S(1)} %get-tuple-element.53.refs_0_, bf16[32,3584]{1,0:T(8,128)(2,1)S(1)} %collective-permute-done.16.refs_1_, ...), custom_call_target="tpu_custom_call" | custom-call | flops 2231369728 | bytes 16187392 | tf_op jit(solution)/shard_map/pallas_call | solution.py:198
  94.2 8.3 %shard_map.88 = (f32[256,2432]{1,0:T(8,128)S(1)}, f32[8,256]{1,0:T(8,128)S(1)}) custom-call(bf16[32,3584]{1,0:T(8,128)(2,1)S(1)} %maximum_select_fusion.refs_0_, bf16[32,3584]{1,0:T(8,128)(2,1)S(1)} %collective-permute-done.9.refs_1_, bf16[32,3584]{1,0:T(8,128)(2,1)S(1)} %collective-permute-done.10.refs_2_, ...), custom_call_target="tpu_custom_call" | custom-call | flops 4462739456 | bytes 24903680 | tf_op jit(solution)/shard_map/pallas_call | solution.py:221
  102.6 0.2 collective-permute-start.24
  102.8 1.3 collective-permute-start.23
  104.1 2.0 %collective-permute-start.22 = (f32[8,256]{1,0:T(8,128)S(1)}, f32[8,256]{1,0:T(8,128)S(1)}, u32[]{:S(2)}, u32[]{:S(2)}) collective-permute-start(f32[8,256]{1,0:T(8,128)S(1)} %get-tuple-element.60.refs_0_), channel_id=1, source_target_pairs={{0,1},{1,0},{2,3},{3,2},{4,5},{5,4},{6,7},{7,6},{8,9},{9,8},{10,11... | collective-permute-start | bytes 24584 | tf_op jit(solution)/shard_map/ppermute | solution.py:328
  106.1 1.0 collective-permute-done.25.refs_4_
  107.1 0.2 collective-permute-start.28
  107.3 1.3 collective-permute-start.27
  108.6 2.0 %collective-permute-start.26 = (f32[8,256]{1,0:T(8,128)S(1)}, f32[8,256]{1,0:T(8,128)S(1)}, u32[]{:S(2)}, u32[]{:S(2)}) collective-permute-start(f32[8,256]{1,0:T(8,128)S(1)} %collective-permute-done.25.refs_4_), channel_id=1, source_target_pairs={{0,1},{1,0},{2,3},{3,2},{4,5},{5,4},{6,7},{7,6},{8,9},{9,8},{10,11... | collective-permute-start | bytes 24584 | tf_op jit(solution)/shard_map/ppermute | solution.py:328
  110.6 1.1 collective-permute-done.28.refs_7_
  111.7 0.6 collective-permute-done.26.refs_5_
  112.2 8.4 %shard_map.89 = (f32[8,256]{1,0:T(8,128)S(1)}, f32[32,3584]{1,0:T(8,128)S(1)}, f32[32,3584]{1,0:T(8,128)S(1)}, f32[32,3584]{1,0:T(8,128)S(1)}, f32[32,3584]{1,0:...) custom-call(s32[2]{0:T(128)S(1)} %pad_add_fusion.place_ref, ...), custom_call_target="tpu_custom_call" | custom-call | flops 4462739456 | bytes 24903680 | tf_op jit(solution)/shard_map/pallas_call | solution.py:303
  120.6 2.1 %collective-permute-start.31 = (f16[32,3584]{1,0:T(8,128)(2,1)S(1)}, f16[32,3584]{1,0:T(8,128)(2,1)S(1)}, u32[]{:S(2)}, u32[]{:S(2)}) collective-permute-start(f16[32,3584]{1,0:T(8,128)(2,1)S(1)} %convert_element_type.113), channel_id=1, source_target_pairs={{0,1},{1,0},{2,3},{3,2},{4,5},{5,4},{6,7},{7,6},{8,9},{9,8},{10,11... | collective-permute-start | bytes 688136 | tf_op jit(solution)/shard_map/ppermute | solution.py:328
  122.8 0.1 collective-permute-start.29
  122.9 3.8 %collective-permute-done.31 = f16[32,3584]{1,0:T(8,128)(2,1)S(1)} collective-permute-done((f16[32,3584]{1,0:T(8,128)(2,1)S(1)}, f16[32,3584]{1,0:T(8,128)(2,1)S(1)}, u32[]{:S(2)}, u32[]{:S(2)}) %collective-permute-start.31) | collective-permute-done | bytes 229408 | tf_op jit(solution)/shard_map/ppermute | solution.py:328
  126.7 2.0 %collective-permute-start.35 = (f16[32,3584]{1,0:T(8,128)(2,1)S(1)}, f16[32,3584]{1,0:T(8,128)(2,1)S(1)}, u32[]{:S(2)}, u32[]{:S(2)}) collective-permute-start(f16[32,3584]{1,0:T(8,128)(2,1)S(1)} %convert_element_type.121), channel_id=1, source_target_pairs={{0,1},{1,0},{2,3},{3,2},{4,5},{5,4},{6,7},{7,6},{8,9},{9,8},{10,11... | collective-permute-start | bytes 688136 | tf_op jit(solution)/shard_map/ppermute | solution.py:328
  128.8 0.4 collective-permute-done.29
  129.2 2.0 %collective-permute-start.33 = (f16[32,3584]{1,0:T(8,128)(2,1)S(1)}, f16[32,3584]{1,0:T(8,128)(2,1)S(1)}, u32[]{:S(2)}, u32[]{:S(2)}) collective-permute-start(f16[32,3584]{1,0:T(8,128)(2,1)S(1)} %convert_element_type.117), channel_id=1, source_target_pairs={{0,1},{1,0},{2,3},{3,2},{4,5},{5,4},{6,7},{7,6},{8,9},{9,8},{10,11... | collective-permute-start | bytes 688136 | tf_op jit(solution)/shard_map/ppermute | solution.py:328
  131.3 0.8 collective-permute-start.30
  132.1 3.1 %collective-permute-done.33 = f16[32,3584]{1,0:T(8,128)(2,1)S(1)} collective-permute-done((f16[32,3584]{1,0:T(8,128)(2,1)S(1)}, f16[32,3584]{1,0:T(8,128)(2,1)S(1)}, u32[]{:S(2)}, u32[]{:S(2)}) %collective-permute-start.33) | collective-permute-done | bytes 229408 | tf_op jit(solution)/shard_map/ppermute | solution.py:328
  135.3 1.3 collective-permute-start.34
  136.6 0.8 collective-permute-done.30
  137.4 0.1 add_convert_fusion.2
  137.5 2.0 %collective-permute-start.32 = (f16[32,3584]{1,0:T(8,128)(2,1)S(1)}, f16[32,3584]{1,0:T(8,128)(2,1)S(1)}, u32[]{:S(2)}, u32[]{:S(2)}) collective-permute-start(f16[32,3584]{1,0:T(8,128)(2,1)S(1)} %add_convert_fusion.2), channel_id=1, source_target_pairs={{0,4},{1,5},{2,6},{3,7},{4,0},{5,1},{6,2},{7,3},{8,12},{9,13},{10,... | collective-permute-start | bytes 688136 | tf_op jit(solution)/shard_map/ppermute | solution.py:328
  139.4 0.6 slice.19
  140.0 1.4 collective-permute-done.34
  141.4 5.5 %collective-permute-done.32 = f16[32,3584]{1,0:T(8,128)(2,1)S(1)} collective-permute-done((f16[32,3584]{1,0:T(8,128)(2,1)S(1)}, f16[32,3584]{1,0:T(8,128)(2,1)S(1)}, u32[]{:S(2)}, u32[]{:S(2)}) %collective-permute-start.32) | collective-permute-done | bytes 229408 | tf_op jit(solution)/shard_map/ppermute | solution.py:328
  146.9 0.1 add_convert_fusion
  147.0 0.8 maximum_select_fusion.1
  (49 shorter events, 0.9 us)
Async XLA Ops:
  0.6 78.2 %collective-permute-start.21 = (bf16[1792,2432]{1,0:T(8,128)(2,1)}, bf16[1792,2432]{1,0:T(8,128)(2,1)}, u32[]{:S(2)}, u32[]{:S(2)}) collective-permute-start(bf16[1792,2432]{1,0:T(8,128)(2,1)} %refs_8_.1), channel_id=1, source_target_pairs={{0,8},{8,0},{1,9},{9,1},{2,10},{10,2},{3,11},{11,3},{4,12},{12,4},... | collective-permute-start | bytes 26148872 | tf_op jit(solution)/shard_map/ppermute | solution.py:383
  2.7 0.9 copy-start.1
  3.7 54.2 %copy-start.2 = (s32[256]{0:T(256)S(1)}, s32[256]{0:T(256)}, u32[]{:S(2)}) copy-start(s32[256]{0:T(256)} %param.13) | copy-start | bytes 3076
  9.1 9.1 %collective-permute-start.2 = (f16[32,3584]{1,0:T(8,128)(2,1)S(1)}, f16[32,3584]{1,0:T(8,128)(2,1)S(1)}, u32[]{:S(2)}, u32[]{:S(2)}) collective-permute-start(f16[32,3584]{1,0:T(8,128)(2,1)S(1)} %convert_element_type.98), channel_id=1, source_target_pairs={{0,1},{1,0},{2,3},{3,2},{4,5},{5,4},{6,7},{7,6},{8,9},{9,8},{10,11... | collective-permute-start | bytes 688136 | tf_op jit(solution)/shard_map/ppermute | solution.py:328
  11.7 11.3 %collective-permute-start = (f16[32,3584]{1,0:T(8,128)(2,1)S(1)}, f16[32,3584]{1,0:T(8,128)(2,1)S(1)}, u32[]{:S(2)}, u32[]{:S(2)}) collective-permute-start(f16[32,3584]{1,0:T(8,128)(2,1)S(1)} %convert_element_type.94), channel_id=1, source_target_pairs={{0,1},{1,0},{2,3},{3,2},{4,5},{5,4},{6,7},{7,6},{8,9},{9,8},{10,11... | collective-permute-start | bytes 688136 | tf_op jit(solution)/shard_map/ppermute | solution.py:328
  11.8 30.0 %collective-permute-start.11 = (bf16[32,3584]{1,0:T(8,128)(2,1)S(1)}, bf16[32,3584]{1,0:T(8,128)(2,1)S(1)}, u32[]{:S(2)}, u32[]{:S(2)}) collective-permute-start(bf16[32,3584]{1,0:T(8,128)(2,1)S(1)} %get-tuple-element.53.refs_0_), channel_id=1, source_target_pairs={{0,4},{1,5},{2,6},{3,7},{4,0},{5,1},{6,2},{7,3},{8,12},{9,13},{10,... | collective-permute-start | bytes 688136 | tf_op jit(solution)/shard_map/ppermute | solution.py:328
  14.8 31.1 %collective-permute-start.7 = (bf16[32,3584]{1,0:T(8,128)(2,1)S(1)}, bf16[32,3584]{1,0:T(8,128)(2,1)S(1)}, u32[]{:S(2)}, u32[]{:S(2)}) collective-permute-start(bf16[32,3584]{1,0:T(8,128)(2,1)S(1)} %get-tuple-element.53.refs_0_), channel_id=1, source_target_pairs={{0,2},{1,3},{2,0},{3,1},{4,6},{5,7},{6,4},{7,5},{8,10},{9,11},{10,... | collective-permute-start | bytes 688136 | tf_op jit(solution)/shard_map/ppermute | solution.py:328
  18.1 26.3 %collective-permute-start.6 = (f16[32,3584]{1,0:T(8,128)(2,1)S(1)}, f16[32,3584]{1,0:T(8,128)(2,1)S(1)}, u32[]{:S(2)}, u32[]{:S(2)}) collective-permute-start(f16[32,3584]{1,0:T(8,128)(2,1)S(1)} %convert_element_type.106), channel_id=1, source_target_pairs={{0,1},{1,0},{2,3},{3,2},{4,5},{5,4},{6,7},{7,6},{8,9},{9,8},{10,11... | collective-permute-start | bytes 688136 | tf_op jit(solution)/shard_map/ppermute | solution.py:328
  23.0 9.6 %collective-permute-start.4 = (f16[32,3584]{1,0:T(8,128)(2,1)S(1)}, f16[32,3584]{1,0:T(8,128)(2,1)S(1)}, u32[]{:S(2)}, u32[]{:S(2)}) collective-permute-start(f16[32,3584]{1,0:T(8,128)(2,1)S(1)} %convert_element_type.102), channel_id=1, source_target_pairs={{0,1},{1,0},{2,3},{3,2},{4,5},{5,4},{6,7},{7,6},{8,9},{9,8},{10,11... | collective-permute-start | bytes 688136 | tf_op jit(solution)/shard_map/ppermute | solution.py:328
  32.7 7.4 %collective-permute-start.1 = (f16[32,3584]{1,0:T(8,128)(2,1)S(1)}, f16[32,3584]{1,0:T(8,128)(2,1)S(1)}, u32[]{:S(2)}, u32[]{:S(2)}) collective-permute-start(f16[32,3584]{1,0:T(8,128)(2,1)S(1)} %add_convert_fusion.7), channel_id=1, source_target_pairs={{0,2},{1,3},{2,0},{3,1},{4,6},{5,7},{6,4},{7,5},{8,10},{9,11},{10,... | collective-permute-start | bytes 688136 | tf_op jit(solution)/shard_map/ppermute | solution.py:328
  40.1 13.5 %collective-permute-start.5 = (f16[32,3584]{1,0:T(8,128)(2,1)S(1)}, f16[32,3584]{1,0:T(8,128)(2,1)S(1)}, u32[]{:S(2)}, u32[]{:S(2)}) collective-permute-start(f16[32,3584]{1,0:T(8,128)(2,1)S(1)} %add_convert_fusion.5), channel_id=1, source_target_pairs={{0,2},{1,3},{2,0},{3,1},{4,6},{5,7},{6,4},{7,5},{8,10},{9,11},{10,... | collective-permute-start | bytes 688136 | tf_op jit(solution)/shard_map/ppermute | solution.py:328
  41.8 13.8 %collective-permute-start.3 = (f16[32,3584]{1,0:T(8,128)(2,1)S(1)}, f16[32,3584]{1,0:T(8,128)(2,1)S(1)}, u32[]{:S(2)}, u32[]{:S(2)}) collective-permute-start(f16[32,3584]{1,0:T(8,128)(2,1)S(1)} %add_convert_fusion.6), channel_id=1, source_target_pairs={{0,4},{1,5},{2,6},{3,7},{4,0},{5,1},{6,2},{7,3},{8,12},{9,13},{10,... | collective-permute-start | bytes 688136 | tf_op jit(solution)/shard_map/ppermute | solution.py:328
  44.4 11.3 %collective-permute-start.16 = (bf16[32,3584]{1,0:T(8,128)(2,1)S(1)}, bf16[32,3584]{1,0:T(8,128)(2,1)S(1)}, u32[]{:S(2)}, u32[]{:S(2)}) collective-permute-start(bf16[32,3584]{1,0:T(8,128)(2,1)S(1)} %get-tuple-element.53.refs_0_), channel_id=1, source_target_pairs={{0,1},{1,0},{2,3},{3,2},{4,5},{5,4},{6,7},{7,6},{8,9},{9,8},{10,11... | collective-permute-start | bytes 688136 | tf_op jit(solution)/shard_map/ppermute | solution.py:328
  46.0 13.0 %collective-permute-start.15 = (bf16[32,3584]{1,0:T(8,128)(2,1)S(1)}, bf16[32,3584]{1,0:T(8,128)(2,1)S(1)}, u32[]{:S(2)}, u32[]{:S(2)}) collective-permute-start(bf16[32,3584]{1,0:T(8,128)(2,1)S(1)} %collective-permute-done.11.refs_4_), channel_id=1, source_target_pairs={{0,2},{1,3},{2,0},{3,1},{4,6},{5,7},{6,4},{7,5},{8,10},{9,11},{10,... | collective-permute-start | bytes 688136 | tf_op jit(solution)/shard_map/ppermute | solution.py:328
  53.5 13.0 %collective-permute-start.12 = (bf16[32,3584]{1,0:T(8,128)(2,1)S(1)}, bf16[32,3584]{1,0:T(8,128)(2,1)S(1)}, u32[]{:S(2)}, u32[]{:S(2)}) collective-permute-start(bf16[32,3584]{1,0:T(8,128)(2,1)S(1)} %collective-permute-done.11.refs_4_), channel_id=1, source_target_pairs={{0,1},{1,0},{2,3},{3,2},{4,5},{5,4},{6,7},{7,6},{8,9},{9,8},{10,11... | collective-permute-start | bytes 688136 | tf_op jit(solution)/shard_map/ppermute | solution.py:328
  55.6 11.0 %collective-permute-start.8 = (bf16[32,3584]{1,0:T(8,128)(2,1)S(1)}, bf16[32,3584]{1,0:T(8,128)(2,1)S(1)}, u32[]{:S(2)}, u32[]{:S(2)}) collective-permute-start(bf16[32,3584]{1,0:T(8,128)(2,1)S(1)} %collective-permute-done.7.refs_2_), channel_id=1, source_target_pairs={{0,1},{1,0},{2,3},{3,2},{4,5},{5,4},{6,7},{7,6},{8,9},{9,8},{10,11... | collective-permute-start | bytes 688136 | tf_op jit(solution)/shard_map/ppermute | solution.py:328
  55.8 13.0 %collective-permute-start.14 = (bf16[32,3584]{1,0:T(8,128)(2,1)S(1)}, bf16[32,3584]{1,0:T(8,128)(2,1)S(1)}, u32[]{:S(2)}, u32[]{:S(2)}) collective-permute-start(bf16[32,3584]{1,0:T(8,128)(2,1)S(1)} %maximum_select_fusion.refs_0_), channel_id=1, source_target_pairs={{0,4},{1,5},{2,6},{3,7},{4,0},{5,1},{6,2},{7,3},{8,12},{9,13},{10,... | collective-permute-start | bytes 688136 | tf_op jit(solution)/shard_map/ppermute | solution.py:328
  58.9 15.9 %collective-permute-start.17 = (bf16[32,3584]{1,0:T(8,128)(2,1)S(1)}, bf16[32,3584]{1,0:T(8,128)(2,1)S(1)}, u32[]{:S(2)}, u32[]{:S(2)}) collective-permute-start(bf16[32,3584]{1,0:T(8,128)(2,1)S(1)} %collective-permute-done.15.refs_6_), channel_id=1, source_target_pairs={{0,1},{1,0},{2,3},{3,2},{4,5},{5,4},{6,7},{7,6},{8,9},{9,8},{10,11... | collective-permute-start | bytes 688136 | tf_op jit(solution)/shard_map/ppermute | solution.py:328
  66.5 6.0 %collective-permute-start.10 = (bf16[32,3584]{1,0:T(8,128)(2,1)S(1)}, bf16[32,3584]{1,0:T(8,128)(2,1)S(1)}, u32[]{:S(2)}, u32[]{:S(2)}) collective-permute-start(bf16[32,3584]{1,0:T(8,128)(2,1)S(1)} %maximum_select_fusion.refs_0_), channel_id=1, source_target_pairs={{0,2},{1,3},{2,0},{3,1},{4,6},{5,7},{6,4},{7,5},{8,10},{9,11},{10,... | collective-permute-start | bytes 688136 | tf_op jit(solution)/shard_map/ppermute | solution.py:328
  66.5 9.8 %collective-permute-start.9 = (bf16[32,3584]{1,0:T(8,128)(2,1)S(1)}, bf16[32,3584]{1,0:T(8,128)(2,1)S(1)}, u32[]{:S(2)}, u32[]{:S(2)}) collective-permute-start(bf16[32,3584]{1,0:T(8,128)(2,1)S(1)} %maximum_select_fusion.refs_0_), channel_id=1, source_target_pairs={{0,1},{1,0},{2,3},{3,2},{4,5},{5,4},{6,7},{7,6},{8,9},{9,8},{10,11... | collective-permute-start | bytes 688136 | tf_op jit(solution)/shard_map/ppermute | solution.py:328
  68.8 7.5 %collective-permute-start.19 = (bf16[32,3584]{1,0:T(8,128)(2,1)S(1)}, bf16[32,3584]{1,0:T(8,128)(2,1)S(1)}, u32[]{:S(2)}, u32[]{:S(2)}) collective-permute-start(bf16[32,3584]{1,0:T(8,128)(2,1)S(1)} %collective-permute-done.14.refs_4_), channel_id=1, source_target_pairs={{0,2},{1,3},{2,0},{3,1},{4,6},{5,7},{6,4},{7,5},{8,10},{9,11},{10,... | collective-permute-start | bytes 688136 | tf_op jit(solution)/shard_map/ppermute | solution.py:328
  72.5 21.7 %collective-permute-start.13 = (bf16[32,3584]{1,0:T(8,128)(2,1)S(1)}, bf16[32,3584]{1,0:T(8,128)(2,1)S(1)}, u32[]{:S(2)}, u32[]{:S(2)}) collective-permute-start(bf16[32,3584]{1,0:T(8,128)(2,1)S(1)} %collective-permute-done.10.refs_2_), channel_id=1, source_target_pairs={{0,1},{1,0},{2,3},{3,2},{4,5},{5,4},{6,7},{7,6},{8,9},{9,8},{10,11... | collective-permute-start | bytes 688136 | tf_op jit(solution)/shard_map/ppermute | solution.py:328
  74.8 19.4 %collective-permute-start.18 = (bf16[32,3584]{1,0:T(8,128)(2,1)S(1)}, bf16[32,3584]{1,0:T(8,128)(2,1)}, u32[]{:S(2)}, u32[]{:S(2)}) collective-permute-start(bf16[32,3584]{1,0:T(8,128)(2,1)S(1)} %collective-permute-done.14.refs_4_), channel_id=1, source_target_pairs={{0,1},{1,0},{2,3},{3,2},{4,5},{5,4},{6,7},{7,6},{8,9},{9,8},{10,11... | collective-permute-start | bytes 688136 | tf_op jit(solution)/shard_map/ppermute | solution.py:328
  76.3 17.9 %collective-permute-start.20 = (bf16[32,3584]{1,0:T(8,128)(2,1)S(1)}, bf16[32,3584]{1,0:T(8,128)(2,1)}, u32[]{:S(2)}, u32[]{:S(2)}) collective-permute-start(bf16[32,3584]{1,0:T(8,128)(2,1)S(1)} %collective-permute-done.19.refs_6_), channel_id=1, source_target_pairs={{0,1},{1,0},{2,3},{3,2},{4,5},{5,4},{6,7},{7,6},{8,9},{9,8},{10,11... | collective-permute-start | bytes 688136 | tf_op jit(solution)/shard_map/ppermute | solution.py:328
  78.8 3.5 %copy-start = (bf16[1792,2432]{1,0:T(8,128)(2,1)S(1)}, bf16[1792,2432]{1,0:T(8,128)(2,1)}, u32[]{:S(2)}) copy-start(bf16[1792,2432]{1,0:T(8,128)(2,1)} %refs_8_.1) | copy-start | bytes 26148868
  102.5 4.6 %collective-permute-start.25 = (f32[8,256]{1,0:T(8,128)S(1)}, f32[8,256]{1,0:T(8,128)S(1)}, u32[]{:S(2)}, u32[]{:S(2)}) collective-permute-start(f32[8,256]{1,0:T(8,128)S(1)} %get-tuple-element.60.refs_0_), channel_id=1, source_target_pairs={{0,4},{1,5},{2,6},{3,7},{4,0},{5,1},{6,2},{7,3},{8,12},{9,13},{10,... | collective-permute-start | bytes 24584 | tf_op jit(solution)/shard_map/ppermute | solution.py:328
  102.6 6.0 %collective-permute-start.24 = (f32[8,256]{1,0:T(8,128)S(1)}, f32[8,256]{1,0:T(8,128)S(1)}, u32[]{:S(2)}, u32[]{:S(2)}) collective-permute-start(f32[8,256]{1,0:T(8,128)S(1)} %get-tuple-element.60.refs_0_), channel_id=1, source_target_pairs={{0,3},{1,2},{2,1},{3,0},{4,7},{5,6},{6,5},{7,4},{8,11},{9,10},{10,... | collective-permute-start | bytes 24584 | tf_op jit(solution)/shard_map/ppermute | solution.py:328
  102.8 7.8 %collective-permute-start.23 = (f32[8,256]{1,0:T(8,128)S(1)}, f32[8,256]{1,0:T(8,128)S(1)}, u32[]{:S(2)}, u32[]{:S(2)}) collective-permute-start(f32[8,256]{1,0:T(8,128)S(1)} %get-tuple-element.60.refs_0_), channel_id=1, source_target_pairs={{0,2},{1,3},{2,0},{3,1},{4,6},{5,7},{6,4},{7,5},{8,10},{9,11},{10,... | collective-permute-start | bytes 24584 | tf_op jit(solution)/shard_map/ppermute | solution.py:328
  104.1 6.5 %collective-permute-start.22 = (f32[8,256]{1,0:T(8,128)S(1)}, f32[8,256]{1,0:T(8,128)S(1)}, u32[]{:S(2)}, u32[]{:S(2)}) collective-permute-start(f32[8,256]{1,0:T(8,128)S(1)} %get-tuple-element.60.refs_0_), channel_id=1, source_target_pairs={{0,1},{1,0},{2,3},{3,2},{4,5},{5,4},{6,7},{7,6},{8,9},{9,8},{10,11... | collective-permute-start | bytes 24584 | tf_op jit(solution)/shard_map/ppermute | solution.py:328
  107.1 4.5 %collective-permute-start.28 = (f32[8,256]{1,0:T(8,128)S(1)}, f32[8,256]{1,0:T(8,128)S(1)}, u32[]{:S(2)}, u32[]{:S(2)}) collective-permute-start(f32[8,256]{1,0:T(8,128)S(1)} %collective-permute-done.25.refs_4_), channel_id=1, source_target_pairs={{0,3},{1,2},{2,1},{3,0},{4,7},{5,6},{6,5},{7,4},{8,11},{9,10},{10,... | collective-permute-start | bytes 24584 | tf_op jit(solution)/shard_map/ppermute | solution.py:328
  107.3 4.4 %collective-permute-start.27 = (f32[8,256]{1,0:T(8,128)S(1)}, f32[8,256]{1,0:T(8,128)S(1)}, u32[]{:S(2)}, u32[]{:S(2)}) collective-permute-start(f32[8,256]{1,0:T(8,128)S(1)} %collective-permute-done.25.refs_4_), channel_id=1, source_target_pairs={{0,2},{1,3},{2,0},{3,1},{4,6},{5,7},{6,4},{7,5},{8,10},{9,11},{10,... | collective-permute-start | bytes 24584 | tf_op jit(solution)/shard_map/ppermute | solution.py:328
  108.6 3.7 %collective-permute-start.26 = (f32[8,256]{1,0:T(8,128)S(1)}, f32[8,256]{1,0:T(8,128)S(1)}, u32[]{:S(2)}, u32[]{:S(2)}) collective-permute-start(f32[8,256]{1,0:T(8,128)S(1)} %collective-permute-done.25.refs_4_), channel_id=1, source_target_pairs={{0,1},{1,0},{2,3},{3,2},{4,5},{5,4},{6,7},{7,6},{8,9},{9,8},{10,11... | collective-permute-start | bytes 24584 | tf_op jit(solution)/shard_map/ppermute | solution.py:328
  120.6 6.1 %collective-permute-start.31 = (f16[32,3584]{1,0:T(8,128)(2,1)S(1)}, f16[32,3584]{1,0:T(8,128)(2,1)S(1)}, u32[]{:S(2)}, u32[]{:S(2)}) collective-permute-start(f16[32,3584]{1,0:T(8,128)(2,1)S(1)} %convert_element_type.113), channel_id=1, source_target_pairs={{0,1},{1,0},{2,3},{3,2},{4,5},{5,4},{6,7},{7,6},{8,9},{9,8},{10,11... | collective-permute-start | bytes 688136 | tf_op jit(solution)/shard_map/ppermute | solution.py:328
  122.8 6.4 %collective-permute-start.29 = (f16[32,3584]{1,0:T(8,128)(2,1)S(1)}, f16[32,3584]{1,0:T(8,128)(2,1)S(1)}, u32[]{:S(2)}, u32[]{:S(2)}) collective-permute-start(f16[32,3584]{1,0:T(8,128)(2,1)S(1)} %convert_element_type.109), channel_id=1, source_target_pairs={{0,1},{1,0},{2,3},{3,2},{4,5},{5,4},{6,7},{7,6},{8,9},{9,8},{10,11... | collective-permute-start | bytes 688136 | tf_op jit(solution)/shard_map/ppermute | solution.py:328
  126.7 13.3 %collective-permute-start.35 = (f16[32,3584]{1,0:T(8,128)(2,1)S(1)}, f16[32,3584]{1,0:T(8,128)(2,1)S(1)}, u32[]{:S(2)}, u32[]{:S(2)}) collective-permute-start(f16[32,3584]{1,0:T(8,128)(2,1)S(1)} %convert_element_type.121), channel_id=1, source_target_pairs={{0,1},{1,0},{2,3},{3,2},{4,5},{5,4},{6,7},{7,6},{8,9},{9,8},{10,11... | collective-permute-start | bytes 688136 | tf_op jit(solution)/shard_map/ppermute | solution.py:328
  129.2 6.0 %collective-permute-start.33 = (f16[32,3584]{1,0:T(8,128)(2,1)S(1)}, f16[32,3584]{1,0:T(8,128)(2,1)S(1)}, u32[]{:S(2)}, u32[]{:S(2)}) collective-permute-start(f16[32,3584]{1,0:T(8,128)(2,1)S(1)} %convert_element_type.117), channel_id=1, source_target_pairs={{0,1},{1,0},{2,3},{3,2},{4,5},{5,4},{6,7},{7,6},{8,9},{9,8},{10,11... | collective-permute-start | bytes 688136 | tf_op jit(solution)/shard_map/ppermute | solution.py:328
  131.3 6.1 %collective-permute-start.30 = (f16[32,3584]{1,0:T(8,128)(2,1)S(1)}, f16[32,3584]{1,0:T(8,128)(2,1)S(1)}, u32[]{:S(2)}, u32[]{:S(2)}) collective-permute-start(f16[32,3584]{1,0:T(8,128)(2,1)S(1)} %add_convert_fusion.3), channel_id=1, source_target_pairs={{0,2},{1,3},{2,0},{3,1},{4,6},{5,7},{6,4},{7,5},{8,10},{9,11},{10,... | collective-permute-start | bytes 688136 | tf_op jit(solution)/shard_map/ppermute | solution.py:328
  135.3 6.1 %collective-permute-start.34 = (f16[32,3584]{1,0:T(8,128)(2,1)S(1)}, f16[32,3584]{1,0:T(8,128)(2,1)S(1)}, u32[]{:S(2)}, u32[]{:S(2)}) collective-permute-start(f16[32,3584]{1,0:T(8,128)(2,1)S(1)} %add_convert_fusion.1), channel_id=1, source_target_pairs={{0,2},{1,3},{2,0},{3,1},{4,6},{5,7},{6,4},{7,5},{8,10},{9,11},{10,... | collective-permute-start | bytes 688136 | tf_op jit(solution)/shard_map/ppermute | solution.py:328
  137.5 9.4 %collective-permute-start.32 = (f16[32,3584]{1,0:T(8,128)(2,1)S(1)}, f16[32,3584]{1,0:T(8,128)(2,1)S(1)}, u32[]{:S(2)}, u32[]{:S(2)}) collective-permute-start(f16[32,3584]{1,0:T(8,128)(2,1)S(1)} %add_convert_fusion.2), channel_id=1, source_target_pairs={{0,4},{1,5},{2,6},{3,7},{4,0},{5,1},{6,2},{7,3},{8,12},{9,13},{10,... | collective-permute-start | bytes 688136 | tf_op jit(solution)/shard_map/ppermute | solution.py:328

commit v13 on v11

--- a/solution.py
+++ b/solution.py
@@ -11,7 +11,7 @@
 wire = jnp.float16
 lanes = 128
 vmem_bytes = 12 * 1024 * 1024
-project_bytes = 50 * 1024 * 1024
+project_bytes = 49 * 1024 * 1024
 
 in_vmem = pl.BlockSpec(memory_space=pltpu.VMEM)
 in_smem = pl.BlockSpec(memory_space=pltpu.SMEM)

time: 135 us -> 136 us (level)
    unnamed x6 -> x8, local copies, waits for them, and re-layouts: 3.48 us -> 4.7 us
where the time goes in v13:
time: 136 us
  starting transfers between devices  52.5 us (39%)
  waiting for transfers between devices  39.5 us (29%)
  Pallas kernels  31.2 us (23%)
  local copies, waits for them, and re-layouts  5.56 us (4%)
  other arithmetic  5.18 us (4%)
  between operations  1.54 us (1%)
    ppermute x35, starting transfers between devices, trade(): lax.ppermute(block, 'vocab', [(at, at ^ mask) for at in range(vocab_size)])  52 us
    ppermute x35, waiting for transfers between devices, trade(): lax.ppermute(block, 'vocab', [(at, at ^ mask) for at in range(vocab_size)])  39.5 us
    pallas_call x1, Pallas kernels, student_logits(): pl.pallas_call(functools.partial(student_kernel, len(pieces), step, chunk...  11.2 us
    pallas_call x1, Pallas kernels, gradient(): pl.pallas_call(functools.partial(gradient_kernel, bits, step, chunk), in_...  8.33 us
    pallas_call x1, Pallas kernels, teacher_logits(): pl.pallas_call(functools.partial(teacher_kernel, len(pieces), step, chunk...  7.15 us
    unnamed x8, local copies, waits for them, and re-layouts  4.7 us
    pallas_call x1, Pallas kernels, project(): pl.pallas_call(functools.partial(project_kernel, count, step), in_specs=[...  4.45 us
  transfers between devices with their start and end apart: 36, of which 17 were waited for; matrix products, arithmetic and copies ran while one was open for 4% of the time, Pallas kernels for 12%

profile of v13, /device:TPU:0, one launch (start us, length us, event | category | flops | bytes accessed | tf_op | source)
XLA Modules:
  0.0 135.5 jit_solution(16650548922308050820)
XLA Ops:
  0.6 0.5 collective-permute-start.21
  1.8 0.8 and_convert_fusion.member_ref
  2.7 1.2 copy-done.1
  3.9 4.4 %shard_map.86 = (f32[32,3584]{1,0:T(8,128)S(1)}, f32[32,3584]{1,0:T(8,128)S(1)}, f32[32,3584]{1,0:T(8,128)S(1)}, f32[32,3584]{1,0:T(8,128)S(1)}, f32[32,3584]{1,...) custom-call(bf16[256,512]{1,0:T(8,128)(2,1)S(1)} %and_convert_fusion.member_ref, ...), custom_call_target="tpu_custom_call" | custom-call | flops 2147483648 | bytes 12058624 | tf_op jit(solution)/shard_map/pallas_call | solution.py:54
  8.4 0.7 convert_element_type.94
  9.1 2.6 %collective-permute-start = (f16[32,3584]{1,0:T(8,128)(2,1)}, f16[32,3584]{1,0:T(8,128)(2,1)}, u32[]{:S(2)}, u32[]{:S(2)}) collective-permute-start(f16[32,3584]{1,0:T(8,128)(2,1)} %convert_element_type.94), channel_id=1, source_target_pairs={{0,1},{1,0},{2,3},{3,2},{4,5},{5,4},{6,7},{7,6},{8,9},{9,8},{10,11... | collective-permute-start | bytes 688136 | tf_op jit(solution)/shard_map/ppermute | solution.py:322
  11.7 1.0 maximum_select_fusion.1.refs_0_
  12.7 2.7 %collective-permute-start.11 = (bf16[32,3584]{1,0:T(8,128)(2,1)S(1)}, bf16[32,3584]{1,0:T(8,128)(2,1)}, u32[]{:S(2)}, u32[]{:S(2)}) collective-permute-start(bf16[32,3584]{1,0:T(8,128)(2,1)S(1)} %maximum_select_fusion.1.refs_0_), channel_id=1, source_target_pairs={{0,4},{1,5},{2,6},{3,7},{4,0},{5,1},{6,2},{7,3},{8,12},{9,13},{10,... | collective-permute-start | bytes 688136 | tf_op jit(solution)/shard_map/ppermute | solution.py:322
  15.3 1.6 %collective-permute-start.7 = (bf16[32,3584]{1,0:T(8,128)(2,1)S(1)}, bf16[32,3584]{1,0:T(8,128)(2,1)}, u32[]{:S(2)}, u32[]{:S(2)}) collective-permute-start(bf16[32,3584]{1,0:T(8,128)(2,1)S(1)} %maximum_select_fusion.1.refs_0_), channel_id=1, source_target_pairs={{0,2},{1,3},{2,0},{3,1},{4,6},{5,7},{6,4},{7,5},{8,10},{9,11},{10,... | collective-permute-start | bytes 688136 | tf_op jit(solution)/shard_map/ppermute | solution.py:322
  16.9 0.6 collective-permute-start.2
  17.6 0.6 collective-permute-done
  18.2 2.2 %collective-permute-start.4 = (f16[32,3584]{1,0:T(8,128)(2,1)S(1)}, f16[32,3584]{1,0:T(8,128)(2,1)S(1)}, u32[]{:S(2)}, u32[]{:S(2)}) collective-permute-start(f16[32,3584]{1,0:T(8,128)(2,1)S(1)} %convert_element_type.102), channel_id=1, source_target_pairs={{0,1},{1,0},{2,3},{3,2},{4,5},{5,4},{6,7},{7,6},{8,9},{9,8},{10,11... | collective-permute-start | bytes 688136 | tf_op jit(solution)/shard_map/ppermute | solution.py:322
  20.4 1.0 add_convert_fusion.7
  21.4 4.2 %collective-permute-done.2 = f16[32,3584]{1,0:T(8,128)(2,1)S(1)} collective-permute-done((f16[32,3584]{1,0:T(8,128)(2,1)S(1)}, f16[32,3584]{1,0:T(8,128)(2,1)S(1)}, u32[]{:S(2)}, u32[]{:S(2)}) %collective-permute-start.2) | collective-permute-done | bytes 229408 | tf_op jit(solution)/shard_map/ppermute | solution.py:322
  25.5 0.4 collective-permute-start.1
  26.0 2.1 %collective-permute-done.4 = f16[32,3584]{1,0:T(8,128)(2,1)S(1)} collective-permute-done((f16[32,3584]{1,0:T(8,128)(2,1)S(1)}, f16[32,3584]{1,0:T(8,128)(2,1)S(1)}, u32[]{:S(2)}, u32[]{:S(2)}) %collective-permute-start.4) | collective-permute-done | bytes 229408 | tf_op jit(solution)/shard_map/ppermute | solution.py:322
  28.1 1.5 %collective-permute-start.6 = (f16[32,3584]{1,0:T(8,128)(2,1)S(1)}, f16[32,3584]{1,0:T(8,128)(2,1)S(1)}, u32[]{:S(2)}, u32[]{:S(2)}) collective-permute-start(f16[32,3584]{1,0:T(8,128)(2,1)S(1)} %convert_element_type.106), channel_id=1, source_target_pairs={{0,1},{1,0},{2,3},{3,2},{4,5},{5,4},{6,7},{7,6},{8,9},{9,8},{10,11... | collective-permute-start | bytes 688136 | tf_op jit(solution)/shard_map/ppermute | solution.py:322
  29.7 1.9 %collective-permute-done.1 = f16[32,3584]{1,0:T(8,128)(2,1)S(1)} collective-permute-done((f16[32,3584]{1,0:T(8,128)(2,1)S(1)}, f16[32,3584]{1,0:T(8,128)(2,1)S(1)}, u32[]{:S(2)}, u32[]{:S(2)}) %collective-permute-start.1) | collective-permute-done | bytes 229408 | tf_op jit(solution)/shard_map/ppermute | solution.py:322
  31.6 0.4 collective-permute-start.5
  32.1 2.7 %collective-permute-start.3 = (f16[32,3584]{1,0:T(8,128)(2,1)S(1)}, f16[32,3584]{1,0:T(8,128)(2,1)S(1)}, u32[]{:S(2)}, u32[]{:S(2)}) collective-permute-start(f16[32,3584]{1,0:T(8,128)(2,1)S(1)} %add_convert_fusion.6), channel_id=1, source_target_pairs={{0,4},{1,5},{2,6},{3,7},{4,0},{5,1},{6,2},{7,3},{8,12},{9,13},{10,... | collective-permute-start | bytes 688136 | tf_op jit(solution)/shard_map/ppermute | solution.py:322
  34.8 1.5 %collective-permute-start.16 = (bf16[32,3584]{1,0:T(8,128)(2,1)S(1)}, bf16[32,3584]{1,0:T(8,128)(2,1)S(1)}, u32[]{:S(2)}, u32[]{:S(2)}) collective-permute-start(bf16[32,3584]{1,0:T(8,128)(2,1)S(1)} %maximum_select_fusion.1.refs_0_), channel_id=1, source_target_pairs={{0,1},{1,0},{2,3},{3,2},{4,5},{5,4},{6,7},{7,6},{8,9},{9,8},{10,11... | collective-permute-start | bytes 688136 | tf_op jit(solution)/shard_map/ppermute | solution.py:322
  36.4 2.1 %collective-permute-start.15 = (bf16[32,3584]{1,0:T(8,128)(2,1)}, bf16[32,3584]{1,0:T(8,128)(2,1)S(1)}, u32[]{:S(2)}, u32[]{:S(2)}) collective-permute-start(bf16[32,3584]{1,0:T(8,128)(2,1)} %collective-permute-done.11.refs_4_), channel_id=1, source_target_pairs={{0,2},{1,3},{2,0},{3,1},{4,6},{5,7},{6,4},{7,5},{8,10},{9,11},{10,... | collective-permute-start | bytes 688136 | tf_op jit(solution)/shard_map/ppermute | solution.py:322
  38.4 4.7 %collective-permute-done.5 = f16[32,3584]{1,0:T(8,128)(2,1)S(1)} collective-permute-done((f16[32,3584]{1,0:T(8,128)(2,1)S(1)}, f16[32,3584]{1,0:T(8,128)(2,1)S(1)}, u32[]{:S(2)}, u32[]{:S(2)}) %collective-permute-start.5) | collective-permute-done | bytes 229408 | tf_op jit(solution)/shard_map/ppermute | solution.py:322
  43.1 1.6 %collective-permute-start.12 = (bf16[32,3584]{1,0:T(8,128)(2,1)}, bf16[32,3584]{1,0:T(8,128)(2,1)S(1)}, u32[]{:S(2)}, u32[]{:S(2)}) collective-permute-start(bf16[32,3584]{1,0:T(8,128)(2,1)} %collective-permute-done.11.refs_4_), channel_id=1, source_target_pairs={{0,1},{1,0},{2,3},{3,2},{4,5},{5,4},{6,7},{7,6},{8,9},{9,8},{10,11... | collective-permute-start | bytes 688136 | tf_op jit(solution)/shard_map/ppermute | solution.py:322
  44.7 0.4 collective-permute-start.8
  45.3 2.8 %collective-permute-start.14 = (bf16[32,3584]{1,0:T(8,128)(2,1)S(1)}, bf16[32,3584]{1,0:T(8,128)(2,1)S(1)}, u32[]{:S(2)}, u32[]{:S(2)}) collective-permute-start(bf16[32,3584]{1,0:T(8,128)(2,1)S(1)} %maximum_select_fusion.refs_0_), channel_id=1, source_target_pairs={{0,4},{1,5},{2,6},{3,7},{4,0},{5,1},{6,2},{7,3},{8,12},{9,13},{10,... | collective-permute-start | bytes 688136 | tf_op jit(solution)/shard_map/ppermute | solution.py:322
  48.3 0.6 collective-permute-done.15.refs_6_
  48.9 1.3 collective-permute-start.17
  50.1 4.7 %collective-permute-done.8.refs_3_ = bf16[32,3584]{1,0:T(8,128)(2,1)S(1)} collective-permute-done((bf16[32,3584]{1,0:T(8,128)(2,1)}, bf16[32,3584]{1,0:T(8,128)(2,1)S(1)}, u32[]{:S(2)}, u32[]{:S(2)}) %collective-permute-start.8) | collective-permute-done | bytes 229408 | tf_op jit(solution)/shard_map/ppermute | solution.py:322
  54.9 1.4 %collective-permute-start.10 = (bf16[32,3584]{1,0:T(8,128)(2,1)S(1)}, bf16[32,3584]{1,0:T(8,128)(2,1)S(1)}, u32[]{:S(2)}, u32[]{:S(2)}) collective-permute-start(bf16[32,3584]{1,0:T(8,128)(2,1)S(1)} %maximum_select_fusion.refs_0_), channel_id=1, source_target_pairs={{0,2},{1,3},{2,0},{3,1},{4,6},{5,7},{6,4},{7,5},{8,10},{9,11},{10,... | collective-permute-start | bytes 688136 | tf_op jit(solution)/shard_map/ppermute | solution.py:322
  56.3 1.6 %collective-permute-start.9 = (bf16[32,3584]{1,0:T(8,128)(2,1)S(1)}, bf16[32,3584]{1,0:T(8,128)(2,1)S(1)}, u32[]{:S(2)}, u32[]{:S(2)}) collective-permute-start(bf16[32,3584]{1,0:T(8,128)(2,1)S(1)} %maximum_select_fusion.refs_0_), channel_id=1, source_target_pairs={{0,1},{1,0},{2,3},{3,2},{4,5},{5,4},{6,7},{7,6},{8,9},{9,8},{10,11... | collective-permute-start | bytes 688136 | tf_op jit(solution)/shard_map/ppermute | solution.py:322
  57.9 1.4 %collective-permute-start.19 = (bf16[32,3584]{1,0:T(8,128)(2,1)S(1)}, bf16[32,3584]{1,0:T(8,128)(2,1)S(1)}, u32[]{:S(2)}, u32[]{:S(2)}) collective-permute-start(bf16[32,3584]{1,0:T(8,128)(2,1)S(1)} %collective-permute-done.14.refs_4_), channel_id=1, source_target_pairs={{0,2},{1,3},{2,0},{3,1},{4,6},{5,7},{6,4},{7,5},{8,10},{9,11},{10,... | collective-permute-start | bytes 688136 | tf_op jit(solution)/shard_map/ppermute | solution.py:322
  59.3 1.6 %collective-permute-done.10.refs_2_ = bf16[32,3584]{1,0:T(8,128)(2,1)S(1)} collective-permute-done((bf16[32,3584]{1,0:T(8,128)(2,1)S(1)}, bf16[32,3584]{1,0:T(8,128)(2,1)S(1)}, u32[]{:S(2)}, u32[]{:S(2)}) %collective-permute-start.10) | collective-permute-done | bytes 229408 | tf_op jit(solution)/shard_map/ppermute | solution.py:322
  60.9 2.4 %collective-permute-start.13 = (bf16[32,3584]{1,0:T(8,128)(2,1)S(1)}, bf16[32,3584]{1,0:T(8,128)(2,1)S(1)}, u32[]{:S(2)}, u32[]{:S(2)}) collective-permute-start(bf16[32,3584]{1,0:T(8,128)(2,1)S(1)} %collective-permute-done.10.refs_2_), channel_id=1, source_target_pairs={{0,1},{1,0},{2,3},{3,2},{4,5},{5,4},{6,7},{7,6},{8,9},{9,8},{10,11... | collective-permute-start | bytes 688136 | tf_op jit(solution)/shard_map/ppermute | solution.py:322
  63.3 1.5 %collective-permute-done.9.refs_1_ = bf16[32,3584]{1,0:T(8,128)(2,1)S(1)} collective-permute-done((bf16[32,3584]{1,0:T(8,128)(2,1)S(1)}, bf16[32,3584]{1,0:T(8,128)(2,1)S(1)}, u32[]{:S(2)}, u32[]{:S(2)}) %collective-permute-start.9) | collective-permute-done | bytes 229408 | tf_op jit(solution)/shard_map/ppermute | solution.py:322
  64.8 2.1 %collective-permute-start.20 = (bf16[32,3584]{1,0:T(8,128)(2,1)S(1)}, bf16[32,3584]{1,0:T(8,128)(2,1)S(1)}, u32[]{:S(2)}, u32[]{:S(2)}) collective-permute-start(bf16[32,3584]{1,0:T(8,128)(2,1)S(1)} %collective-permute-done.19.refs_6_), channel_id=1, source_target_pairs={{0,1},{1,0},{2,3},{3,2},{4,5},{5,4},{6,7},{7,6},{8,9},{9,8},{10,11... | collective-permute-start | bytes 688136 | tf_op jit(solution)/shard_map/ppermute | solution.py:322
  67.1 3.5 %copy-done = bf16[1792,2432]{1,0:T(8,128)(2,1)S(1)} copy-done((bf16[1792,2432]{1,0:T(8,128)(2,1)S(1)}, bf16[1792,2432]{1,0:T(8,128)(2,1)}, u32[]{:S(2)}) %copy-start) | copy-done | bytes 8716312
  70.6 11.2 %shard_map.87 = (f32[256,2432]{1,0:T(8,128)S(1)}, f32[256,2432]{1,0:T(8,128)S(1)}, f32[8,256]{1,0:T(8,128)S(1)}, bf16[3584,2432]{1,0:T(8,128)(2,1)S(1)}) custom-call(bf16[32,3584]{1,0:T(8,128)(2,1)S(1)} %maximum_select_fusion.1.refs_0_, bf16[32,3584]{1,0:T(8,128)(2,1)S(1)} %collective-permute-done.16.refs_1_, ...), custom_call_target="tpu_custom_call" | custom-call | flops 2231369728 | bytes 16187392 | tf_op jit(solution)/shard_map/pallas_call | solution.py:192
  81.9 7.2 %shard_map.88 = (f32[256,2432]{1,0:T(8,128)S(1)}, f32[8,256]{1,0:T(8,128)S(1)}) custom-call(bf16[32,3584]{1,0:T(8,128)(2,1)S(1)} %maximum_select_fusion.refs_0_, bf16[32,3584]{1,0:T(8,128)(2,1)S(1)} %collective-permute-done.9.refs_1_, bf16[32,3584]{1,0:T(8,128)(2,1)S(1)} %collective-permute-done.10.refs_2_, ...), custom_call_target="tpu_custom_call" | custom-call | flops 4462739456 | bytes 24903680 | tf_op jit(solution)/shard_map/pallas_call | solution.py:215
  89.0 2.4 %collective-permute-start.25 = (f32[8,256]{1,0:T(8,128)S(1)}, f32[8,256]{1,0:T(8,128)S(1)}, u32[]{:S(2)}, u32[]{:S(2)}) collective-permute-start(f32[8,256]{1,0:T(8,128)S(1)} %get-tuple-element.60.refs_0_), channel_id=1, source_target_pairs={{0,4},{1,5},{2,6},{3,7},{4,0},{5,1},{6,2},{7,3},{8,12},{9,13},{10,... | collective-permute-start | bytes 24584 | tf_op jit(solution)/shard_map/ppermute | solution.py:322
  91.4 0.6 collective-permute-start.24
  91.9 1.2 collective-permute-start.23
  93.2 1.7 %collective-permute-start.22 = (f32[8,256]{1,0:T(8,128)S(1)}, f32[8,256]{1,0:T(8,128)S(1)}, u32[]{:S(2)}, u32[]{:S(2)}) collective-permute-start(f32[8,256]{1,0:T(8,128)S(1)} %get-tuple-element.60.refs_0_), channel_id=1, source_target_pairs={{0,1},{1,0},{2,3},{3,2},{4,5},{5,4},{6,7},{7,6},{8,9},{9,8},{10,11... | collective-permute-start | bytes 24584 | tf_op jit(solution)/shard_map/ppermute | solution.py:322
  94.9 0.6 collective-permute-start.28
  95.4 1.2 collective-permute-start.27
  96.7 1.7 %collective-permute-start.26 = (f32[8,256]{1,0:T(8,128)S(1)}, f32[8,256]{1,0:T(8,128)S(1)}, u32[]{:S(2)}, u32[]{:S(2)}) collective-permute-start(f32[8,256]{1,0:T(8,128)S(1)} %collective-permute-done.25.refs_4_), channel_id=1, source_target_pairs={{0,1},{1,0},{2,3},{3,2},{4,5},{5,4},{6,7},{7,6},{8,9},{9,8},{10,11... | collective-permute-start | bytes 24584 | tf_op jit(solution)/shard_map/ppermute | solution.py:322
  98.4 1.0 collective-permute-done.28.refs_7_
  99.4 0.9 collective-permute-done.26.refs_5_
  100.3 8.3 %shard_map.89 = (f32[8,256]{1,0:T(8,128)S(1)}, f32[32,3584]{1,0:T(8,128)S(1)}, f32[32,3584]{1,0:T(8,128)S(1)}, f32[32,3584]{1,0:T(8,128)S(1)}, f32[32,3584]{1,0:...) custom-call(s32[2]{0:T(128)S(1)} %pad_add_fusion.place_ref, ...), custom_call_target="tpu_custom_call" | custom-call | flops 4462739456 | bytes 24903680 | tf_op jit(solution)/shard_map/pallas_call | solution.py:297
  108.7 1.8 %collective-permute-start.31 = (f16[32,3584]{1,0:T(8,128)(2,1)S(1)}, f16[32,3584]{1,0:T(8,128)(2,1)S(1)}, u32[]{:S(2)}, u32[]{:S(2)}) collective-permute-start(f16[32,3584]{1,0:T(8,128)(2,1)S(1)} %convert_element_type.113), channel_id=1, source_target_pairs={{0,1},{1,0},{2,3},{3,2},{4,5},{5,4},{6,7},{7,6},{8,9},{9,8},{10,11... | collective-permute-start | bytes 688136 | tf_op jit(solution)/shard_map/ppermute | solution.py:322
  110.5 0.4 collective-permute-start.29
  110.9 3.8 %collective-permute-done.31 = f16[32,3584]{1,0:T(8,128)(2,1)S(1)} collective-permute-done((f16[32,3584]{1,0:T(8,128)(2,1)S(1)}, f16[32,3584]{1,0:T(8,128)(2,1)S(1)}, u32[]{:S(2)}, u32[]{:S(2)}) %collective-permute-start.31) | collective-permute-done | bytes 229408 | tf_op jit(solution)/shard_map/ppermute | solution.py:322
  114.8 1.7 %collective-permute-start.35 = (f16[32,3584]{1,0:T(8,128)(2,1)S(1)}, f16[32,3584]{1,0:T(8,128)(2,1)S(1)}, u32[]{:S(2)}, u32[]{:S(2)}) collective-permute-start(f16[32,3584]{1,0:T(8,128)(2,1)S(1)} %convert_element_type.121), channel_id=1, source_target_pairs={{0,1},{1,0},{2,3},{3,2},{4,5},{5,4},{6,7},{7,6},{8,9},{9,8},{10,11... | collective-permute-start | bytes 688136 | tf_op jit(solution)/shard_map/ppermute | solution.py:322
  116.5 0.8 collective-permute-done.29
  117.2 1.7 %collective-permute-start.33 = (f16[32,3584]{1,0:T(8,128)(2,1)S(1)}, f16[32,3584]{1,0:T(8,128)(2,1)S(1)}, u32[]{:S(2)}, u32[]{:S(2)}) collective-permute-start(f16[32,3584]{1,0:T(8,128)(2,1)S(1)} %convert_element_type.117), channel_id=1, source_target_pairs={{0,1},{1,0},{2,3},{3,2},{4,5},{5,4},{6,7},{7,6},{8,9},{9,8},{10,11... | collective-permute-start | bytes 688136 | tf_op jit(solution)/shard_map/ppermute | solution.py:322
  119.0 1.3 collective-permute-start.30
  120.3 2.9 %collective-permute-done.33 = f16[32,3584]{1,0:T(8,128)(2,1)S(1)} collective-permute-done((f16[32,3584]{1,0:T(8,128)(2,1)S(1)}, f16[32,3584]{1,0:T(8,128)(2,1)S(1)}, u32[]{:S(2)}, u32[]{:S(2)}) %collective-permute-start.33) | collective-permute-done | bytes 229408 | tf_op jit(solution)/shard_map/ppermute | solution.py:322
  123.3 1.4 %collective-permute-start.34 = (f16[32,3584]{1,0:T(8,128)(2,1)S(1)}, f16[32,3584]{1,0:T(8,128)(2,1)S(1)}, u32[]{:S(2)}, u32[]{:S(2)}) collective-permute-start(f16[32,3584]{1,0:T(8,128)(2,1)S(1)} %add_convert_fusion.1), channel_id=1, source_target_pairs={{0,2},{1,3},{2,0},{3,1},{4,6},{5,7},{6,4},{7,5},{8,10},{9,11},{10,... | collective-permute-start | bytes 688136 | tf_op jit(solution)/shard_map/ppermute | solution.py:322
  124.7 0.4 collective-permute-done.30
  125.2 1.1 collective-permute-start.32
  126.3 0.6 slice.27
  126.9 2.5 %collective-permute-done.34 = f16[32,3584]{1,0:T(8,128)(2,1)S(1)} collective-permute-done((f16[32,3584]{1,0:T(8,128)(2,1)S(1)}, f16[32,3584]{1,0:T(8,128)(2,1)S(1)}, u32[]{:S(2)}, u32[]{:S(2)}) %collective-permute-start.34) | collective-permute-done | bytes 229408 | tf_op jit(solution)/shard_map/ppermute | solution.py:322
  129.4 5.2 %collective-permute-done.32 = f16[32,3584]{1,0:T(8,128)(2,1)S(1)} collective-permute-done((f16[32,3584]{1,0:T(8,128)(2,1)S(1)}, f16[32,3584]{1,0:T(8,128)(2,1)S(1)}, u32[]{:S(2)}, u32[]{:S(2)}) %collective-permute-start.32) | collective-permute-done | bytes 229408 | tf_op jit(solution)/shard_map/ppermute | solution.py:322
  134.8 0.8 maximum_select_fusion.2
  (53 shorter events, 1.3 us)
Async XLA Ops:
  0.6 11.0 %copy-start.2 = (bf16[32,3584]{1,0:T(8,128)(2,1)S(1)}, bf16[32,3584]{1,0:T(8,128)(2,1)}, u32[]{:S(2)}) copy-start(bf16[32,3584]{1,0:T(8,128)(2,1)} %param.11) | copy-start | bytes 688132
  0.6 66.5 %collective-permute-start.21 = (bf16[1792,2432]{1,0:T(8,128)(2,1)}, bf16[1792,2432]{1,0:T(8,128)(2,1)}, u32[]{:S(2)}, u32[]{:S(2)}) collective-permute-start(bf16[1792,2432]{1,0:T(8,128)(2,1)} %refs_8_.1), channel_id=1, source_target_pairs={{0,8},{8,0},{1,9},{9,1},{2,10},{10,2},{3,11},{11,3},{4,12},{12,4},... | collective-permute-start | bytes 26148872 | tf_op jit(solution)/shard_map/ppermute | solution.py:377
  2.7 1.2 copy-start.1
  3.9 44.3 %copy-start.3 = (s32[256]{0:T(256)S(1)}, s32[256]{0:T(256)}, u32[]{:S(2)}) copy-start(s32[256]{0:T(256)} %param.13) | copy-start | bytes 3076
  9.1 9.1 %collective-permute-start = (f16[32,3584]{1,0:T(8,128)(2,1)}, f16[32,3584]{1,0:T(8,128)(2,1)}, u32[]{:S(2)}, u32[]{:S(2)}) collective-permute-start(f16[32,3584]{1,0:T(8,128)(2,1)} %convert_element_type.94), channel_id=1, source_target_pairs={{0,1},{1,0},{2,3},{3,2},{4,5},{5,4},{6,7},{7,6},{8,9},{9,8},{10,11... | collective-permute-start | bytes 688136 | tf_op jit(solution)/shard_map/ppermute | solution.py:322
  12.7 19.4 %collective-permute-start.11 = (bf16[32,3584]{1,0:T(8,128)(2,1)S(1)}, bf16[32,3584]{1,0:T(8,128)(2,1)}, u32[]{:S(2)}, u32[]{:S(2)}) collective-permute-start(bf16[32,3584]{1,0:T(8,128)(2,1)S(1)} %maximum_select_fusion.1.refs_0_), channel_id=1, source_target_pairs={{0,4},{1,5},{2,6},{3,7},{4,0},{5,1},{6,2},{7,3},{8,12},{9,13},{10,... | collective-permute-start | bytes 688136 | tf_op jit(solution)/shard_map/ppermute | solution.py:322
  15.3 21.0 %collective-permute-start.7 = (bf16[32,3584]{1,0:T(8,128)(2,1)S(1)}, bf16[32,3584]{1,0:T(8,128)(2,1)}, u32[]{:S(2)}, u32[]{:S(2)}) collective-permute-start(bf16[32,3584]{1,0:T(8,128)(2,1)S(1)} %maximum_select_fusion.1.refs_0_), channel_id=1, source_target_pairs={{0,2},{1,3},{2,0},{3,1},{4,6},{5,7},{6,4},{7,5},{8,10},{9,11},{10,... | collective-permute-start | bytes 688136 | tf_op jit(solution)/shard_map/ppermute | solution.py:322
  16.9 8.6 %collective-permute-start.2 = (f16[32,3584]{1,0:T(8,128)(2,1)S(1)}, f16[32,3584]{1,0:T(8,128)(2,1)S(1)}, u32[]{:S(2)}, u32[]{:S(2)}) collective-permute-start(f16[32,3584]{1,0:T(8,128)(2,1)S(1)} %convert_element_type.98), channel_id=1, source_target_pairs={{0,1},{1,0},{2,3},{3,2},{4,5},{5,4},{6,7},{7,6},{8,9},{9,8},{10,11... | collective-permute-start | bytes 688136 | tf_op jit(solution)/shard_map/ppermute | solution.py:322
  18.2 9.9 %collective-permute-start.4 = (f16[32,3584]{1,0:T(8,128)(2,1)S(1)}, f16[32,3584]{1,0:T(8,128)(2,1)S(1)}, u32[]{:S(2)}, u32[]{:S(2)}) collective-permute-start(f16[32,3584]{1,0:T(8,128)(2,1)S(1)} %convert_element_type.102), channel_id=1, source_target_pairs={{0,1},{1,0},{2,3},{3,2},{4,5},{5,4},{6,7},{7,6},{8,9},{9,8},{10,11... | collective-permute-start | bytes 688136 | tf_op jit(solution)/shard_map/ppermute | solution.py:322
  25.5 6.0 %collective-permute-start.1 = (f16[32,3584]{1,0:T(8,128)(2,1)S(1)}, f16[32,3584]{1,0:T(8,128)(2,1)S(1)}, u32[]{:S(2)}, u32[]{:S(2)}) collective-permute-start(f16[32,3584]{1,0:T(8,128)(2,1)S(1)} %add_convert_fusion.7), channel_id=1, source_target_pairs={{0,2},{1,3},{2,0},{3,1},{4,6},{5,7},{6,4},{7,5},{8,10},{9,11},{10,... | collective-permute-start | bytes 688136 | tf_op jit(solution)/shard_map/ppermute | solution.py:322
  28.1 6.7 %collective-permute-start.6 = (f16[32,3584]{1,0:T(8,128)(2,1)S(1)}, f16[32,3584]{1,0:T(8,128)(2,1)S(1)}, u32[]{:S(2)}, u32[]{:S(2)}) collective-permute-start(f16[32,3584]{1,0:T(8,128)(2,1)S(1)} %convert_element_type.106), channel_id=1, source_target_pairs={{0,1},{1,0},{2,3},{3,2},{4,5},{5,4},{6,7},{7,6},{8,9},{9,8},{10,11... | collective-permute-start | bytes 688136 | tf_op jit(solution)/shard_map/ppermute | solution.py:322
  31.6 11.5 %collective-permute-start.5 = (f16[32,3584]{1,0:T(8,128)(2,1)S(1)}, f16[32,3584]{1,0:T(8,128)(2,1)S(1)}, u32[]{:S(2)}, u32[]{:S(2)}) collective-permute-start(f16[32,3584]{1,0:T(8,128)(2,1)S(1)} %add_convert_fusion.5), channel_id=1, source_target_pairs={{0,2},{1,3},{2,0},{3,1},{4,6},{5,7},{6,4},{7,5},{8,10},{9,11},{10,... | collective-permute-start | bytes 688136 | tf_op jit(solution)/shard_map/ppermute | solution.py:322
  32.1 12.6 %collective-permute-start.3 = (f16[32,3584]{1,0:T(8,128)(2,1)S(1)}, f16[32,3584]{1,0:T(8,128)(2,1)S(1)}, u32[]{:S(2)}, u32[]{:S(2)}) collective-permute-start(f16[32,3584]{1,0:T(8,128)(2,1)S(1)} %add_convert_fusion.6), channel_id=1, source_target_pairs={{0,4},{1,5},{2,6},{3,7},{4,0},{5,1},{6,2},{7,3},{8,12},{9,13},{10,... | collective-permute-start | bytes 688136 | tf_op jit(solution)/shard_map/ppermute | solution.py:322
  34.8 10.5 %collective-permute-start.16 = (bf16[32,3584]{1,0:T(8,128)(2,1)S(1)}, bf16[32,3584]{1,0:T(8,128)(2,1)S(1)}, u32[]{:S(2)}, u32[]{:S(2)}) collective-permute-start(bf16[32,3584]{1,0:T(8,128)(2,1)S(1)} %maximum_select_fusion.1.refs_0_), channel_id=1, source_target_pairs={{0,1},{1,0},{2,3},{3,2},{4,5},{5,4},{6,7},{7,6},{8,9},{9,8},{10,11... | collective-permute-start | bytes 688136 | tf_op jit(solution)/shard_map/ppermute | solution.py:322
  36.4 12.5 %collective-permute-start.15 = (bf16[32,3584]{1,0:T(8,128)(2,1)}, bf16[32,3584]{1,0:T(8,128)(2,1)S(1)}, u32[]{:S(2)}, u32[]{:S(2)}) collective-permute-start(bf16[32,3584]{1,0:T(8,128)(2,1)} %collective-permute-done.11.refs_4_), channel_id=1, source_target_pairs={{0,2},{1,3},{2,0},{3,1},{4,6},{5,7},{6,4},{7,5},{8,10},{9,11},{10,... | collective-permute-start | bytes 688136 | tf_op jit(solution)/shard_map/ppermute | solution.py:322
  43.1 13.2 %collective-permute-start.12 = (bf16[32,3584]{1,0:T(8,128)(2,1)}, bf16[32,3584]{1,0:T(8,128)(2,1)S(1)}, u32[]{:S(2)}, u32[]{:S(2)}) collective-permute-start(bf16[32,3584]{1,0:T(8,128)(2,1)} %collective-permute-done.11.refs_4_), channel_id=1, source_target_pairs={{0,1},{1,0},{2,3},{3,2},{4,5},{5,4},{6,7},{7,6},{8,9},{9,8},{10,11... | collective-permute-start | bytes 688136 | tf_op jit(solution)/shard_map/ppermute | solution.py:322
  44.7 10.2 %collective-permute-start.8 = (bf16[32,3584]{1,0:T(8,128)(2,1)}, bf16[32,3584]{1,0:T(8,128)(2,1)S(1)}, u32[]{:S(2)}, u32[]{:S(2)}) collective-permute-start(bf16[32,3584]{1,0:T(8,128)(2,1)} %collective-permute-done.7.refs_2_), channel_id=1, source_target_pairs={{0,1},{1,0},{2,3},{3,2},{4,5},{5,4},{6,7},{7,6},{8,9},{9,8},{10,11... | collective-permute-start | bytes 688136 | tf_op jit(solution)/shard_map/ppermute | solution.py:322
  45.3 12.6 %collective-permute-start.14 = (bf16[32,3584]{1,0:T(8,128)(2,1)S(1)}, bf16[32,3584]{1,0:T(8,128)(2,1)S(1)}, u32[]{:S(2)}, u32[]{:S(2)}) collective-permute-start(bf16[32,3584]{1,0:T(8,128)(2,1)S(1)} %maximum_select_fusion.refs_0_), channel_id=1, source_target_pairs={{0,4},{1,5},{2,6},{3,7},{4,0},{5,1},{6,2},{7,3},{8,12},{9,13},{10,... | collective-permute-start | bytes 688136 | tf_op jit(solution)/shard_map/ppermute | solution.py:322
  48.9 14.4 %collective-permute-start.17 = (bf16[32,3584]{1,0:T(8,128)(2,1)S(1)}, bf16[32,3584]{1,0:T(8,128)(2,1)S(1)}, u32[]{:S(2)}, u32[]{:S(2)}) collective-permute-start(bf16[32,3584]{1,0:T(8,128)(2,1)S(1)} %collective-permute-done.15.refs_6_), channel_id=1, source_target_pairs={{0,1},{1,0},{2,3},{3,2},{4,5},{5,4},{6,7},{7,6},{8,9},{9,8},{10,11... | collective-permute-start | bytes 688136 | tf_op jit(solution)/shard_map/ppermute | solution.py:322
  54.9 6.0 %collective-permute-start.10 = (bf16[32,3584]{1,0:T(8,128)(2,1)S(1)}, bf16[32,3584]{1,0:T(8,128)(2,1)S(1)}, u32[]{:S(2)}, u32[]{:S(2)}) collective-permute-start(bf16[32,3584]{1,0:T(8,128)(2,1)S(1)} %maximum_select_fusion.refs_0_), channel_id=1, source_target_pairs={{0,2},{1,3},{2,0},{3,1},{4,6},{5,7},{6,4},{7,5},{8,10},{9,11},{10,... | collective-permute-start | bytes 688136 | tf_op jit(solution)/shard_map/ppermute | solution.py:322
  56.3 8.5 %collective-permute-start.9 = (bf16[32,3584]{1,0:T(8,128)(2,1)S(1)}, bf16[32,3584]{1,0:T(8,128)(2,1)S(1)}, u32[]{:S(2)}, u32[]{:S(2)}) collective-permute-start(bf16[32,3584]{1,0:T(8,128)(2,1)S(1)} %maximum_select_fusion.refs_0_), channel_id=1, source_target_pairs={{0,1},{1,0},{2,3},{3,2},{4,5},{5,4},{6,7},{7,6},{8,9},{9,8},{10,11... | collective-permute-start | bytes 688136 | tf_op jit(solution)/shard_map/ppermute | solution.py:322
  57.9 6.9 %collective-permute-start.19 = (bf16[32,3584]{1,0:T(8,128)(2,1)S(1)}, bf16[32,3584]{1,0:T(8,128)(2,1)S(1)}, u32[]{:S(2)}, u32[]{:S(2)}) collective-permute-start(bf16[32,3584]{1,0:T(8,128)(2,1)S(1)} %collective-permute-done.14.refs_4_), channel_id=1, source_target_pairs={{0,2},{1,3},{2,0},{3,1},{4,6},{5,7},{6,4},{7,5},{8,10},{9,11},{10,... | collective-permute-start | bytes 688136 | tf_op jit(solution)/shard_map/ppermute | solution.py:322
  60.9 20.9 %collective-permute-start.13 = (bf16[32,3584]{1,0:T(8,128)(2,1)S(1)}, bf16[32,3584]{1,0:T(8,128)(2,1)S(1)}, u32[]{:S(2)}, u32[]{:S(2)}) collective-permute-start(bf16[32,3584]{1,0:T(8,128)(2,1)S(1)} %collective-permute-done.10.refs_2_), channel_id=1, source_target_pairs={{0,1},{1,0},{2,3},{3,2},{4,5},{5,4},{6,7},{7,6},{8,9},{9,8},{10,11... | collective-permute-start | bytes 688136 | tf_op jit(solution)/shard_map/ppermute | solution.py:322
  63.3 18.6 %collective-permute-start.18 = (bf16[32,3584]{1,0:T(8,128)(2,1)S(1)}, bf16[32,3584]{1,0:T(8,128)(2,1)S(1)}, u32[]{:S(2)}, u32[]{:S(2)}) collective-permute-start(bf16[32,3584]{1,0:T(8,128)(2,1)S(1)} %collective-permute-done.14.refs_4_), channel_id=1, source_target_pairs={{0,1},{1,0},{2,3},{3,2},{4,5},{5,4},{6,7},{7,6},{8,9},{9,8},{10,11... | collective-permute-start | bytes 688136 | tf_op jit(solution)/shard_map/ppermute | solution.py:322
  64.8 17.0 %collective-permute-start.20 = (bf16[32,3584]{1,0:T(8,128)(2,1)S(1)}, bf16[32,3584]{1,0:T(8,128)(2,1)S(1)}, u32[]{:S(2)}, u32[]{:S(2)}) collective-permute-start(bf16[32,3584]{1,0:T(8,128)(2,1)S(1)} %collective-permute-done.19.refs_6_), channel_id=1, source_target_pairs={{0,1},{1,0},{2,3},{3,2},{4,5},{5,4},{6,7},{7,6},{8,9},{9,8},{10,11... | collective-permute-start | bytes 688136 | tf_op jit(solution)/shard_map/ppermute | solution.py:322
  67.1 3.5 %copy-start = (bf16[1792,2432]{1,0:T(8,128)(2,1)S(1)}, bf16[1792,2432]{1,0:T(8,128)(2,1)}, u32[]{:S(2)}) copy-start(bf16[1792,2432]{1,0:T(8,128)(2,1)} %refs_8_.1) | copy-start | bytes 26148868
  89.0 5.8 %collective-permute-start.25 = (f32[8,256]{1,0:T(8,128)S(1)}, f32[8,256]{1,0:T(8,128)S(1)}, u32[]{:S(2)}, u32[]{:S(2)}) collective-permute-start(f32[8,256]{1,0:T(8,128)S(1)} %get-tuple-element.60.refs_0_), channel_id=1, source_target_pairs={{0,4},{1,5},{2,6},{3,7},{4,0},{5,1},{6,2},{7,3},{8,12},{9,13},{10,... | collective-permute-start | bytes 24584 | tf_op jit(solution)/shard_map/ppermute | solution.py:322
  91.4 5.3 %collective-permute-start.24 = (f32[8,256]{1,0:T(8,128)S(1)}, f32[8,256]{1,0:T(8,128)S(1)}, u32[]{:S(2)}, u32[]{:S(2)}) collective-permute-start(f32[8,256]{1,0:T(8,128)S(1)} %get-tuple-element.60.refs_0_), channel_id=1, source_target_pairs={{0,3},{1,2},{2,1},{3,0},{4,7},{5,6},{6,5},{7,4},{8,11},{9,10},{10,... | collective-permute-start | bytes 24584 | tf_op jit(solution)/shard_map/ppermute | solution.py:322
  91.9 6.5 %collective-permute-start.23 = (f32[8,256]{1,0:T(8,128)S(1)}, f32[8,256]{1,0:T(8,128)S(1)}, u32[]{:S(2)}, u32[]{:S(2)}) collective-permute-start(f32[8,256]{1,0:T(8,128)S(1)} %get-tuple-element.60.refs_0_), channel_id=1, source_target_pairs={{0,2},{1,3},{2,0},{3,1},{4,6},{5,7},{6,4},{7,5},{8,10},{9,11},{10,... | collective-permute-start | bytes 24584 | tf_op jit(solution)/shard_map/ppermute | solution.py:322
  93.2 5.3 %collective-permute-start.22 = (f32[8,256]{1,0:T(8,128)S(1)}, f32[8,256]{1,0:T(8,128)S(1)}, u32[]{:S(2)}, u32[]{:S(2)}) collective-permute-start(f32[8,256]{1,0:T(8,128)S(1)} %get-tuple-element.60.refs_0_), channel_id=1, source_target_pairs={{0,1},{1,0},{2,3},{3,2},{4,5},{5,4},{6,7},{7,6},{8,9},{9,8},{10,11... | collective-permute-start | bytes 24584 | tf_op jit(solution)/shard_map/ppermute | solution.py:322
  94.9 4.6 %collective-permute-start.28 = (f32[8,256]{1,0:T(8,128)S(1)}, f32[8,256]{1,0:T(8,128)S(1)}, u32[]{:S(2)}, u32[]{:S(2)}) collective-permute-start(f32[8,256]{1,0:T(8,128)S(1)} %collective-permute-done.25.refs_4_), channel_id=1, source_target_pairs={{0,3},{1,2},{2,1},{3,0},{4,7},{5,6},{6,5},{7,4},{8,11},{9,10},{10,... | collective-permute-start | bytes 24584 | tf_op jit(solution)/shard_map/ppermute | solution.py:322
  95.4 4.0 %collective-permute-start.27 = (f32[8,256]{1,0:T(8,128)S(1)}, f32[8,256]{1,0:T(8,128)S(1)}, u32[]{:S(2)}, u32[]{:S(2)}) collective-permute-start(f32[8,256]{1,0:T(8,128)S(1)} %collective-permute-done.25.refs_4_), channel_id=1, source_target_pairs={{0,2},{1,3},{2,0},{3,1},{4,6},{5,7},{6,4},{7,5},{8,10},{9,11},{10,... | collective-permute-start | bytes 24584 | tf_op jit(solution)/shard_map/ppermute | solution.py:322
  96.7 3.7 %collective-permute-start.26 = (f32[8,256]{1,0:T(8,128)S(1)}, f32[8,256]{1,0:T(8,128)S(1)}, u32[]{:S(2)}, u32[]{:S(2)}) collective-permute-start(f32[8,256]{1,0:T(8,128)S(1)} %collective-permute-done.25.refs_4_), channel_id=1, source_target_pairs={{0,1},{1,0},{2,3},{3,2},{4,5},{5,4},{6,7},{7,6},{8,9},{9,8},{10,11... | collective-permute-start | bytes 24584 | tf_op jit(solution)/shard_map/ppermute | solution.py:322
  108.7 6.1 %collective-permute-start.31 = (f16[32,3584]{1,0:T(8,128)(2,1)S(1)}, f16[32,3584]{1,0:T(8,128)(2,1)S(1)}, u32[]{:S(2)}, u32[]{:S(2)}) collective-permute-start(f16[32,3584]{1,0:T(8,128)(2,1)S(1)} %convert_element_type.113), channel_id=1, source_target_pairs={{0,1},{1,0},{2,3},{3,2},{4,5},{5,4},{6,7},{7,6},{8,9},{9,8},{10,11... | collective-permute-start | bytes 688136 | tf_op jit(solution)/shard_map/ppermute | solution.py:322
  110.5 6.8 %collective-permute-start.29 = (f16[32,3584]{1,0:T(8,128)(2,1)S(1)}, f16[32,3584]{1,0:T(8,128)(2,1)S(1)}, u32[]{:S(2)}, u32[]{:S(2)}) collective-permute-start(f16[32,3584]{1,0:T(8,128)(2,1)S(1)} %convert_element_type.109), channel_id=1, source_target_pairs={{0,1},{1,0},{2,3},{3,2},{4,5},{5,4},{6,7},{7,6},{8,9},{9,8},{10,11... | collective-permute-start | bytes 688136 | tf_op jit(solution)/shard_map/ppermute | solution.py:322
  114.8 12.1 %collective-permute-start.35 = (f16[32,3584]{1,0:T(8,128)(2,1)S(1)}, f16[32,3584]{1,0:T(8,128)(2,1)S(1)}, u32[]{:S(2)}, u32[]{:S(2)}) collective-permute-start(f16[32,3584]{1,0:T(8,128)(2,1)S(1)} %convert_element_type.121), channel_id=1, source_target_pairs={{0,1},{1,0},{2,3},{3,2},{4,5},{5,4},{6,7},{7,6},{8,9},{9,8},{10,11... | collective-permute-start | bytes 688136 | tf_op jit(solution)/shard_map/ppermute | solution.py:322
  117.2 6.0 %collective-permute-start.33 = (f16[32,3584]{1,0:T(8,128)(2,1)S(1)}, f16[32,3584]{1,0:T(8,128)(2,1)S(1)}, u32[]{:S(2)}, u32[]{:S(2)}) collective-permute-start(f16[32,3584]{1,0:T(8,128)(2,1)S(1)} %convert_element_type.117), channel_id=1, source_target_pairs={{0,1},{1,0},{2,3},{3,2},{4,5},{5,4},{6,7},{7,6},{8,9},{9,8},{10,11... | collective-permute-start | bytes 688136 | tf_op jit(solution)/shard_map/ppermute | solution.py:322
  119.0 6.1 %collective-permute-start.30 = (f16[32,3584]{1,0:T(8,128)(2,1)S(1)}, f16[32,3584]{1,0:T(8,128)(2,1)S(1)}, u32[]{:S(2)}, u32[]{:S(2)}) collective-permute-start(f16[32,3584]{1,0:T(8,128)(2,1)S(1)} %add_convert_fusion.3), channel_id=1, source_target_pairs={{0,2},{1,3},{2,0},{3,1},{4,6},{5,7},{6,4},{7,5},{8,10},{9,11},{10,... | collective-permute-start | bytes 688136 | tf_op jit(solution)/shard_map/ppermute | solution.py:322
  123.3 6.1 %collective-permute-start.34 = (f16[32,3584]{1,0:T(8,128)(2,1)S(1)}, f16[32,3584]{1,0:T(8,128)(2,1)S(1)}, u32[]{:S(2)}, u32[]{:S(2)}) collective-permute-start(f16[32,3584]{1,0:T(8,128)(2,1)S(1)} %add_convert_fusion.1), channel_id=1, source_target_pairs={{0,2},{1,3},{2,0},{3,1},{4,6},{5,7},{6,4},{7,5},{8,10},{9,11},{10,... | collective-permute-start | bytes 688136 | tf_op jit(solution)/shard_map/ppermute | solution.py:322
  125.2 9.4 %collective-permute-start.32 = (f16[32,3584]{1,0:T(8,128)(2,1)S(1)}, f16[32,3584]{1,0:T(8,128)(2,1)S(1)}, u32[]{:S(2)}, u32[]{:S(2)}) collective-permute-start(f16[32,3584]{1,0:T(8,128)(2,1)S(1)} %add_convert_fusion.2), channel_id=1, source_target_pairs={{0,4},{1,5},{2,6},{3,7},{4,0},{5,1},{6,2},{7,3},{8,12},{9,13},{10,... | collective-permute-start | bytes 688136 | tf_op jit(solution)/shard_map/ppermute | solution.py:322

commit v14 on v11

--- a/solution.py
+++ b/solution.py
@@ -339,13 +339,13 @@
                 line.append(blocks[-1])
         return blocks
 
-    def reduce_blocks(parts):
+    def reduce_blocks(parts, single=False):
         terms, line = list(parts), []
         for mask in range(vocab_size - 1, 0, -1):
             bit = lowest(mask)
             block = terms[mask].astype(wire)
             if bit == 0 and len(line) > 1:
-                block = tie(block, line[-2])
+                block = tie(block, line[-1] if single and len(line) > 2 else line[-2])
             block = swap(block, bit)
             if bit == 0:
                 line.append(block)
@@ -393,7 +393,7 @@
             far, near = mask & ~3, mask & 3
             tables.append(trade(tables[far], near) if near else trade(stats, far))
         loss, *terms = gradient(place, tables, scaled_teach, scaled_stud, column, head, bits, chunk)
-        return (loss[0], turned(reduce_blocks(terms)[0].astype(jnp.bfloat16)))
+        return (loss[0], turned(reduce_blocks(terms, True)[0].astype(jnp.bfloat16)))
 
     return body
 

time: 135 us -> 135 us (level)
  transfers between devices with their start and end apart: 36 -> 36, of which waited for: 17 -> 16; matrix products, arithmetic and copies ran while one was open for 4% -> 4% of each run, Pallas kernels for 12% -> 12%
where the time goes in v14:
time: 135 us
  starting transfers between devices  52.2 us (39%)
  waiting for transfers between devices  40.3 us (30%)
  Pallas kernels  31.6 us (23%)
  other arithmetic  5.18 us (4%)
  local copies, waits for them, and re-layouts  4.35 us (3%)
  between operations  1.54 us (1%)
    ppermute x35, starting transfers between devices, trade(): lax.ppermute(block, 'vocab', [(at, at ^ mask) for at in range(vocab_size)])  51.7 us
    ppermute x35, waiting for transfers between devices, trade(): lax.ppermute(block, 'vocab', [(at, at ^ mask) for at in range(vocab_size)])  40.3 us
    pallas_call x1, Pallas kernels, student_logits(): pl.pallas_call(functools.partial(student_kernel, len(pieces), step, chunk...  11.2 us
    pallas_call x1, Pallas kernels, gradient(): pl.pallas_call(functools.partial(gradient_kernel, bits, step, chunk), in_...  8.33 us
    pallas_call x1, Pallas kernels, teacher_logits(): pl.pallas_call(functools.partial(teacher_kernel, len(pieces), step, chunk...  7.15 us
    pallas_call x1, Pallas kernels, project(): pl.pallas_call(functools.partial(project_kernel, count, step), in_specs=[...  4.83 us
    unnamed x6, local copies, waits for them, and re-layouts  3.48 us
  transfers between devices with their start and end apart: 36, of which 16 were waited for; matrix products, arithmetic and copies ran while one was open for 4% of the time, Pallas kernels for 12%

profile of v14, /device:TPU:0, one launch (start us, length us, event | category | flops | bytes accessed | tf_op | source)
XLA Modules:
  0.0 135.1 jit_solution(13838051163284011042)
XLA Ops:
  0.6 0.5 collective-permute-start.21
  1.8 0.8 and_convert_fusion.member_ref
  2.7 4.8 %shard_map.86 = (f32[32,3584]{1,0:T(8,128)S(1)}, f32[32,3584]{1,0:T(8,128)S(1)}, f32[32,3584]{1,0:T(8,128)S(1)}, f32[32,3584]{1,0:T(8,128)S(1)}, f32[32,3584]{1,...) custom-call(bf16[256,512]{1,0:T(8,128)(2,1)S(1)} %and_convert_fusion.member_ref, ...), custom_call_target="tpu_custom_call" | custom-call | flops 2147483648 | bytes 12058624 | tf_op jit(solution)/shard_map/pallas_call | solution.py:54
  7.5 0.7 convert_element_type.94
  8.2 2.6 %collective-permute-start = (f16[32,3584]{1,0:T(8,128)(2,1)}, f16[32,3584]{1,0:T(8,128)(2,1)}, u32[]{:S(2)}, u32[]{:S(2)}) collective-permute-start(f16[32,3584]{1,0:T(8,128)(2,1)} %convert_element_type.94), channel_id=1, source_target_pairs={{0,1},{1,0},{2,3},{3,2},{4,5},{5,4},{6,7},{7,6},{8,9},{9,8},{10,11... | collective-permute-start | bytes 688136 | tf_op jit(solution)/shard_map/ppermute | solution.py:322
  10.8 1.0 maximum_select_fusion.1.refs_0_
  11.8 2.7 %collective-permute-start.11 = (bf16[32,3584]{1,0:T(8,128)(2,1)S(1)}, bf16[32,3584]{1,0:T(8,128)(2,1)}, u32[]{:S(2)}, u32[]{:S(2)}) collective-permute-start(bf16[32,3584]{1,0:T(8,128)(2,1)S(1)} %maximum_select_fusion.1.refs_0_), channel_id=1, source_target_pairs={{0,4},{1,5},{2,6},{3,7},{4,0},{5,1},{6,2},{7,3},{8,12},{9,13},{10,... | collective-permute-start | bytes 688136 | tf_op jit(solution)/shard_map/ppermute | solution.py:322
  14.5 1.6 %collective-permute-start.7 = (bf16[32,3584]{1,0:T(8,128)(2,1)S(1)}, bf16[32,3584]{1,0:T(8,128)(2,1)}, u32[]{:S(2)}, u32[]{:S(2)}) collective-permute-start(bf16[32,3584]{1,0:T(8,128)(2,1)S(1)} %maximum_select_fusion.1.refs_0_), channel_id=1, source_target_pairs={{0,2},{1,3},{2,0},{3,1},{4,6},{5,7},{6,4},{7,5},{8,10},{9,11},{10,... | collective-permute-start | bytes 688136 | tf_op jit(solution)/shard_map/ppermute | solution.py:322
  16.1 0.6 collective-permute-start.2
  16.7 0.6 collective-permute-done
  17.3 2.2 %collective-permute-start.4 = (f16[32,3584]{1,0:T(8,128)(2,1)S(1)}, f16[32,3584]{1,0:T(8,128)(2,1)S(1)}, u32[]{:S(2)}, u32[]{:S(2)}) collective-permute-start(f16[32,3584]{1,0:T(8,128)(2,1)S(1)} %convert_element_type.102), channel_id=1, source_target_pairs={{0,1},{1,0},{2,3},{3,2},{4,5},{5,4},{6,7},{7,6},{8,9},{9,8},{10,11... | collective-permute-start | bytes 688136 | tf_op jit(solution)/shard_map/ppermute | solution.py:322
  19.5 1.0 add_convert_fusion.7
  20.5 4.2 %collective-permute-done.2 = f16[32,3584]{1,0:T(8,128)(2,1)S(1)} collective-permute-done((f16[32,3584]{1,0:T(8,128)(2,1)S(1)}, f16[32,3584]{1,0:T(8,128)(2,1)S(1)}, u32[]{:S(2)}, u32[]{:S(2)}) %collective-permute-start.2) | collective-permute-done | bytes 229408 | tf_op jit(solution)/shard_map/ppermute | solution.py:322
  24.7 0.4 collective-permute-start.1
  25.1 2.1 %collective-permute-done.4 = f16[32,3584]{1,0:T(8,128)(2,1)S(1)} collective-permute-done((f16[32,3584]{1,0:T(8,128)(2,1)S(1)}, f16[32,3584]{1,0:T(8,128)(2,1)S(1)}, u32[]{:S(2)}, u32[]{:S(2)}) %collective-permute-start.4) | collective-permute-done | bytes 229408 | tf_op jit(solution)/shard_map/ppermute | solution.py:322
  27.3 1.5 %collective-permute-start.6 = (f16[32,3584]{1,0:T(8,128)(2,1)S(1)}, f16[32,3584]{1,0:T(8,128)(2,1)S(1)}, u32[]{:S(2)}, u32[]{:S(2)}) collective-permute-start(f16[32,3584]{1,0:T(8,128)(2,1)S(1)} %convert_element_type.106), channel_id=1, source_target_pairs={{0,1},{1,0},{2,3},{3,2},{4,5},{5,4},{6,7},{7,6},{8,9},{9,8},{10,11... | collective-permute-start | bytes 688136 | tf_op jit(solution)/shard_map/ppermute | solution.py:322
  28.9 1.9 %collective-permute-done.1 = f16[32,3584]{1,0:T(8,128)(2,1)S(1)} collective-permute-done((f16[32,3584]{1,0:T(8,128)(2,1)S(1)}, f16[32,3584]{1,0:T(8,128)(2,1)S(1)}, u32[]{:S(2)}, u32[]{:S(2)}) %collective-permute-start.1) | collective-permute-done | bytes 229408 | tf_op jit(solution)/shard_map/ppermute | solution.py:322
  30.7 0.4 collective-permute-start.5
  31.3 2.7 %collective-permute-start.3 = (f16[32,3584]{1,0:T(8,128)(2,1)S(1)}, f16[32,3584]{1,0:T(8,128)(2,1)S(1)}, u32[]{:S(2)}, u32[]{:S(2)}) collective-permute-start(f16[32,3584]{1,0:T(8,128)(2,1)S(1)} %add_convert_fusion.6), channel_id=1, source_target_pairs={{0,4},{1,5},{2,6},{3,7},{4,0},{5,1},{6,2},{7,3},{8,12},{9,13},{10,... | collective-permute-start | bytes 688136 | tf_op jit(solution)/shard_map/ppermute | solution.py:322
  34.0 1.5 %collective-permute-start.16 = (bf16[32,3584]{1,0:T(8,128)(2,1)S(1)}, bf16[32,3584]{1,0:T(8,128)(2,1)S(1)}, u32[]{:S(2)}, u32[]{:S(2)}) collective-permute-start(bf16[32,3584]{1,0:T(8,128)(2,1)S(1)} %maximum_select_fusion.1.refs_0_), channel_id=1, source_target_pairs={{0,1},{1,0},{2,3},{3,2},{4,5},{5,4},{6,7},{7,6},{8,9},{9,8},{10,11... | collective-permute-start | bytes 688136 | tf_op jit(solution)/shard_map/ppermute | solution.py:322
  35.5 2.1 %collective-permute-start.15 = (bf16[32,3584]{1,0:T(8,128)(2,1)}, bf16[32,3584]{1,0:T(8,128)(2,1)S(1)}, u32[]{:S(2)}, u32[]{:S(2)}) collective-permute-start(bf16[32,3584]{1,0:T(8,128)(2,1)} %collective-permute-done.11.refs_4_), channel_id=1, source_target_pairs={{0,2},{1,3},{2,0},{3,1},{4,6},{5,7},{6,4},{7,5},{8,10},{9,11},{10,... | collective-permute-start | bytes 688136 | tf_op jit(solution)/shard_map/ppermute | solution.py:322
  37.6 4.7 %collective-permute-done.5 = f16[32,3584]{1,0:T(8,128)(2,1)S(1)} collective-permute-done((f16[32,3584]{1,0:T(8,128)(2,1)S(1)}, f16[32,3584]{1,0:T(8,128)(2,1)S(1)}, u32[]{:S(2)}, u32[]{:S(2)}) %collective-permute-start.5) | collective-permute-done | bytes 229408 | tf_op jit(solution)/shard_map/ppermute | solution.py:322
  42.3 1.6 %collective-permute-start.12 = (bf16[32,3584]{1,0:T(8,128)(2,1)}, bf16[32,3584]{1,0:T(8,128)(2,1)S(1)}, u32[]{:S(2)}, u32[]{:S(2)}) collective-permute-start(bf16[32,3584]{1,0:T(8,128)(2,1)} %collective-permute-done.11.refs_4_), channel_id=1, source_target_pairs={{0,1},{1,0},{2,3},{3,2},{4,5},{5,4},{6,7},{7,6},{8,9},{9,8},{10,11... | collective-permute-start | bytes 688136 | tf_op jit(solution)/shard_map/ppermute | solution.py:322
  43.9 0.4 collective-permute-start.8
  44.3 0.1 add_convert_fusion.4
  44.5 2.9 %collective-permute-start.14 = (bf16[32,3584]{1,0:T(8,128)(2,1)S(1)}, bf16[32,3584]{1,0:T(8,128)(2,1)S(1)}, u32[]{:S(2)}, u32[]{:S(2)}) collective-permute-start(bf16[32,3584]{1,0:T(8,128)(2,1)S(1)} %maximum_select_fusion.refs_0_), channel_id=1, source_target_pairs={{0,4},{1,5},{2,6},{3,7},{4,0},{5,1},{6,2},{7,3},{8,12},{9,13},{10,... | collective-permute-start | bytes 688136 | tf_op jit(solution)/shard_map/ppermute | solution.py:322
  47.5 0.5 collective-permute-done.15.refs_6_
  48.0 1.3 collective-permute-start.17
  49.3 4.7 %collective-permute-done.8.refs_3_ = bf16[32,3584]{1,0:T(8,128)(2,1)S(1)} collective-permute-done((bf16[32,3584]{1,0:T(8,128)(2,1)}, bf16[32,3584]{1,0:T(8,128)(2,1)S(1)}, u32[]{:S(2)}, u32[]{:S(2)}) %collective-permute-start.8) | collective-permute-done | bytes 229408 | tf_op jit(solution)/shard_map/ppermute | solution.py:322
  54.1 1.4 %collective-permute-start.10 = (bf16[32,3584]{1,0:T(8,128)(2,1)S(1)}, bf16[32,3584]{1,0:T(8,128)(2,1)S(1)}, u32[]{:S(2)}, u32[]{:S(2)}) collective-permute-start(bf16[32,3584]{1,0:T(8,128)(2,1)S(1)} %maximum_select_fusion.refs_0_), channel_id=1, source_target_pairs={{0,2},{1,3},{2,0},{3,1},{4,6},{5,7},{6,4},{7,5},{8,10},{9,11},{10,... | collective-permute-start | bytes 688136 | tf_op jit(solution)/shard_map/ppermute | solution.py:322
  55.5 1.6 %collective-permute-start.9 = (bf16[32,3584]{1,0:T(8,128)(2,1)S(1)}, bf16[32,3584]{1,0:T(8,128)(2,1)S(1)}, u32[]{:S(2)}, u32[]{:S(2)}) collective-permute-start(bf16[32,3584]{1,0:T(8,128)(2,1)S(1)} %maximum_select_fusion.refs_0_), channel_id=1, source_target_pairs={{0,1},{1,0},{2,3},{3,2},{4,5},{5,4},{6,7},{7,6},{8,9},{9,8},{10,11... | collective-permute-start | bytes 688136 | tf_op jit(solution)/shard_map/ppermute | solution.py:322
  57.1 1.4 %collective-permute-start.19 = (bf16[32,3584]{1,0:T(8,128)(2,1)S(1)}, bf16[32,3584]{1,0:T(8,128)(2,1)S(1)}, u32[]{:S(2)}, u32[]{:S(2)}) collective-permute-start(bf16[32,3584]{1,0:T(8,128)(2,1)S(1)} %collective-permute-done.14.refs_4_), channel_id=1, source_target_pairs={{0,2},{1,3},{2,0},{3,1},{4,6},{5,7},{6,4},{7,5},{8,10},{9,11},{10,... | collective-permute-start | bytes 688136 | tf_op jit(solution)/shard_map/ppermute | solution.py:322
  58.5 1.6 %collective-permute-done.10.refs_2_ = bf16[32,3584]{1,0:T(8,128)(2,1)S(1)} collective-permute-done((bf16[32,3584]{1,0:T(8,128)(2,1)S(1)}, bf16[32,3584]{1,0:T(8,128)(2,1)S(1)}, u32[]{:S(2)}, u32[]{:S(2)}) %collective-permute-start.10) | collective-permute-done | bytes 229408 | tf_op jit(solution)/shard_map/ppermute | solution.py:322
  60.1 2.4 %collective-permute-start.13 = (bf16[32,3584]{1,0:T(8,128)(2,1)S(1)}, bf16[32,3584]{1,0:T(8,128)(2,1)S(1)}, u32[]{:S(2)}, u32[]{:S(2)}) collective-permute-start(bf16[32,3584]{1,0:T(8,128)(2,1)S(1)} %collective-permute-done.10.refs_2_), channel_id=1, source_target_pairs={{0,1},{1,0},{2,3},{3,2},{4,5},{5,4},{6,7},{7,6},{8,9},{9,8},{10,11... | collective-permute-start | bytes 688136 | tf_op jit(solution)/shard_map/ppermute | solution.py:322
  62.5 1.5 %collective-permute-done.9.refs_1_ = bf16[32,3584]{1,0:T(8,128)(2,1)S(1)} collective-permute-done((bf16[32,3584]{1,0:T(8,128)(2,1)S(1)}, bf16[32,3584]{1,0:T(8,128)(2,1)S(1)}, u32[]{:S(2)}, u32[]{:S(2)}) %collective-permute-start.9) | collective-permute-done | bytes 229408 | tf_op jit(solution)/shard_map/ppermute | solution.py:322
  64.0 2.1 %collective-permute-start.20 = (bf16[32,3584]{1,0:T(8,128)(2,1)S(1)}, bf16[32,3584]{1,0:T(8,128)(2,1)S(1)}, u32[]{:S(2)}, u32[]{:S(2)}) collective-permute-start(bf16[32,3584]{1,0:T(8,128)(2,1)S(1)} %collective-permute-done.19.refs_6_), channel_id=1, source_target_pairs={{0,1},{1,0},{2,3},{3,2},{4,5},{5,4},{6,7},{7,6},{8,9},{9,8},{10,11... | collective-permute-start | bytes 688136 | tf_op jit(solution)/shard_map/ppermute | solution.py:322
  66.1 0.1 sub.26.refs_10_
  66.3 3.5 %copy-done = bf16[1792,2432]{1,0:T(8,128)(2,1)S(1)} copy-done((bf16[1792,2432]{1,0:T(8,128)(2,1)S(1)}, bf16[1792,2432]{1,0:T(8,128)(2,1)}, u32[]{:S(2)}) %copy-start) | copy-done | bytes 8716312
  69.8 11.2 %shard_map.87 = (f32[256,2432]{1,0:T(8,128)S(1)}, f32[256,2432]{1,0:T(8,128)S(1)}, f32[8,256]{1,0:T(8,128)S(1)}, bf16[3584,2432]{1,0:T(8,128)(2,1)S(1)}) custom-call(bf16[32,3584]{1,0:T(8,128)(2,1)S(1)} %maximum_select_fusion.1.refs_0_, bf16[32,3584]{1,0:T(8,128)(2,1)S(1)} %collective-permute-done.16.refs_1_, ...), custom_call_target="tpu_custom_call" | custom-call | flops 2231369728 | bytes 16187392 | tf_op jit(solution)/shard_map/pallas_call | solution.py:192
  81.1 7.2 %shard_map.88 = (f32[256,2432]{1,0:T(8,128)S(1)}, f32[8,256]{1,0:T(8,128)S(1)}) custom-call(bf16[32,3584]{1,0:T(8,128)(2,1)S(1)} %maximum_select_fusion.refs_0_, bf16[32,3584]{1,0:T(8,128)(2,1)S(1)} %collective-permute-done.9.refs_1_, bf16[32,3584]{1,0:T(8,128)(2,1)S(1)} %collective-permute-done.10.refs_2_, ...), custom_call_target="tpu_custom_call" | custom-call | flops 4462739456 | bytes 24903680 | tf_op jit(solution)/shard_map/pallas_call | solution.py:215
  88.2 2.4 %collective-permute-start.25 = (f32[8,256]{1,0:T(8,128)S(1)}, f32[8,256]{1,0:T(8,128)S(1)}, u32[]{:S(2)}, u32[]{:S(2)}) collective-permute-start(f32[8,256]{1,0:T(8,128)S(1)} %get-tuple-element.60.refs_0_), channel_id=1, source_target_pairs={{0,4},{1,5},{2,6},{3,7},{4,0},{5,1},{6,2},{7,3},{8,12},{9,13},{10,... | collective-permute-start | bytes 24584 | tf_op jit(solution)/shard_map/ppermute | solution.py:322
  90.6 0.4 collective-permute-start.24
  91.1 1.2 collective-permute-start.23
  92.3 1.8 %collective-permute-start.22 = (f32[8,256]{1,0:T(8,128)S(1)}, f32[8,256]{1,0:T(8,128)S(1)}, u32[]{:S(2)}, u32[]{:S(2)}) collective-permute-start(f32[8,256]{1,0:T(8,128)S(1)} %get-tuple-element.60.refs_0_), channel_id=1, source_target_pairs={{0,1},{1,0},{2,3},{3,2},{4,5},{5,4},{6,7},{7,6},{8,9},{9,8},{10,11... | collective-permute-start | bytes 24584 | tf_op jit(solution)/shard_map/ppermute | solution.py:322
  94.1 0.4 collective-permute-start.28
  94.6 1.2 collective-permute-start.27
  95.8 1.8 %collective-permute-start.26 = (f32[8,256]{1,0:T(8,128)S(1)}, f32[8,256]{1,0:T(8,128)S(1)}, u32[]{:S(2)}, u32[]{:S(2)}) collective-permute-start(f32[8,256]{1,0:T(8,128)S(1)} %collective-permute-done.25.refs_4_), channel_id=1, source_target_pairs={{0,1},{1,0},{2,3},{3,2},{4,5},{5,4},{6,7},{7,6},{8,9},{9,8},{10,11... | collective-permute-start | bytes 24584 | tf_op jit(solution)/shard_map/ppermute | solution.py:322
  97.7 1.0 collective-permute-done.28.refs_7_
  98.7 0.8 collective-permute-done.26.refs_5_
  99.4 8.3 %shard_map.89 = (f32[8,256]{1,0:T(8,128)S(1)}, f32[32,3584]{1,0:T(8,128)S(1)}, f32[32,3584]{1,0:T(8,128)S(1)}, f32[32,3584]{1,0:T(8,128)S(1)}, f32[32,3584]{1,0:...) custom-call(s32[2]{0:T(128)S(1)} %pad_add_fusion.place_ref, ...), custom_call_target="tpu_custom_call" | custom-call | flops 4462739456 | bytes 24903680 | tf_op jit(solution)/shard_map/pallas_call | solution.py:297
  107.8 1.9 %collective-permute-start.29 = (f16[32,3584]{1,0:T(8,128)(2,1)S(1)}, f16[32,3584]{1,0:T(8,128)(2,1)S(1)}, u32[]{:S(2)}, u32[]{:S(2)}) collective-permute-start(f16[32,3584]{1,0:T(8,128)(2,1)S(1)} %convert_element_type.109), channel_id=1, source_target_pairs={{0,1},{1,0},{2,3},{3,2},{4,5},{5,4},{6,7},{7,6},{8,9},{9,8},{10,11... | collective-permute-start | bytes 688136 | tf_op jit(solution)/shard_map/ppermute | solution.py:322
  109.8 0.3 collective-permute-start.31
  110.1 5.9 %collective-permute-done.29 = f16[32,3584]{1,0:T(8,128)(2,1)S(1)} collective-permute-done((f16[32,3584]{1,0:T(8,128)(2,1)S(1)}, f16[32,3584]{1,0:T(8,128)(2,1)S(1)}, u32[]{:S(2)}, u32[]{:S(2)}) %collective-permute-start.29) | collective-permute-done | bytes 229408 | tf_op jit(solution)/shard_map/ppermute | solution.py:322
  116.0 1.2 collective-permute-start.33
  117.3 1.4 %collective-permute-start.30 = (f16[32,3584]{1,0:T(8,128)(2,1)S(1)}, f16[32,3584]{1,0:T(8,128)(2,1)S(1)}, u32[]{:S(2)}, u32[]{:S(2)}) collective-permute-start(f16[32,3584]{1,0:T(8,128)(2,1)S(1)} %add_convert_fusion.3), channel_id=1, source_target_pairs={{0,2},{1,3},{2,0},{3,1},{4,6},{5,7},{6,4},{7,5},{8,10},{9,11},{10,... | collective-permute-start | bytes 688136 | tf_op jit(solution)/shard_map/ppermute | solution.py:322
  118.7 3.3 %collective-permute-done.33 = f16[32,3584]{1,0:T(8,128)(2,1)S(1)} collective-permute-done((f16[32,3584]{1,0:T(8,128)(2,1)S(1)}, f16[32,3584]{1,0:T(8,128)(2,1)S(1)}, u32[]{:S(2)}, u32[]{:S(2)}) %collective-permute-start.33) | collective-permute-done | bytes 229408 | tf_op jit(solution)/shard_map/ppermute | solution.py:322
  122.0 1.2 collective-permute-start.35
  123.3 1.4 %collective-permute-start.34 = (f16[32,3584]{1,0:T(8,128)(2,1)S(1)}, f16[32,3584]{1,0:T(8,128)(2,1)S(1)}, u32[]{:S(2)}, u32[]{:S(2)}) collective-permute-start(f16[32,3584]{1,0:T(8,128)(2,1)S(1)} %add_convert_fusion.1), channel_id=1, source_target_pairs={{0,2},{1,3},{2,0},{3,1},{4,6},{5,7},{6,4},{7,5},{8,10},{9,11},{10,... | collective-permute-start | bytes 688136 | tf_op jit(solution)/shard_map/ppermute | solution.py:322
  124.8 1.4 %collective-permute-start.32 = (f16[32,3584]{1,0:T(8,128)(2,1)S(1)}, f16[32,3584]{1,0:T(8,128)(2,1)S(1)}, u32[]{:S(2)}, u32[]{:S(2)}) collective-permute-start(f16[32,3584]{1,0:T(8,128)(2,1)S(1)} %add_convert_fusion.2), channel_id=1, source_target_pairs={{0,4},{1,5},{2,6},{3,7},{4,0},{5,1},{6,2},{7,3},{8,12},{9,13},{10,... | collective-permute-start | bytes 688136 | tf_op jit(solution)/shard_map/ppermute | solution.py:322
  126.3 0.6 slice.27
  126.8 1.2 collective-permute-done.35
  128.0 1.4 %collective-permute-done.34 = f16[32,3584]{1,0:T(8,128)(2,1)S(1)} collective-permute-done((f16[32,3584]{1,0:T(8,128)(2,1)S(1)}, f16[32,3584]{1,0:T(8,128)(2,1)S(1)}, u32[]{:S(2)}, u32[]{:S(2)}) %collective-permute-start.34) | collective-permute-done | bytes 229408 | tf_op jit(solution)/shard_map/ppermute | solution.py:322
  129.4 4.9 %collective-permute-done.32 = f16[32,3584]{1,0:T(8,128)(2,1)S(1)} collective-permute-done((f16[32,3584]{1,0:T(8,128)(2,1)S(1)}, f16[32,3584]{1,0:T(8,128)(2,1)S(1)}, u32[]{:S(2)}, u32[]{:S(2)}) %collective-permute-start.32) | collective-permute-done | bytes 229408 | tf_op jit(solution)/shard_map/ppermute | solution.py:322
  134.4 0.8 maximum_select_fusion.2
  (51 shorter events, 1.0 us)
Async XLA Ops:
  0.6 10.2 %copy-start.1 = (bf16[32,3584]{1,0:T(8,128)(2,1)S(1)}, bf16[32,3584]{1,0:T(8,128)(2,1)}, u32[]{:S(2)}) copy-start(bf16[32,3584]{1,0:T(8,128)(2,1)} %param.11) | copy-start | bytes 688132
  0.6 65.7 %collective-permute-start.21 = (bf16[1792,2432]{1,0:T(8,128)(2,1)}, bf16[1792,2432]{1,0:T(8,128)(2,1)}, u32[]{:S(2)}, u32[]{:S(2)}) collective-permute-start(bf16[1792,2432]{1,0:T(8,128)(2,1)} %refs_8_.1), channel_id=1, source_target_pairs={{0,8},{8,0},{1,9},{9,1},{2,10},{10,2},{3,11},{11,3},{4,12},{12,4},... | collective-permute-start | bytes 26148872 | tf_op jit(solution)/shard_map/ppermute | solution.py:377
  2.7 44.7 %copy-start.2 = (s32[256]{0:T(256)S(1)}, s32[256]{0:T(256)}, u32[]{:S(2)}) copy-start(s32[256]{0:T(256)} %param.13) | copy-start | bytes 3076
  8.2 9.1 %collective-permute-start = (f16[32,3584]{1,0:T(8,128)(2,1)}, f16[32,3584]{1,0:T(8,128)(2,1)}, u32[]{:S(2)}, u32[]{:S(2)}) collective-permute-start(f16[32,3584]{1,0:T(8,128)(2,1)} %convert_element_type.94), channel_id=1, source_target_pairs={{0,1},{1,0},{2,3},{3,2},{4,5},{5,4},{6,7},{7,6},{8,9},{9,8},{10,11... | collective-permute-start | bytes 688136 | tf_op jit(solution)/shard_map/ppermute | solution.py:322
  11.8 19.4 %collective-permute-start.11 = (bf16[32,3584]{1,0:T(8,128)(2,1)S(1)}, bf16[32,3584]{1,0:T(8,128)(2,1)}, u32[]{:S(2)}, u32[]{:S(2)}) collective-permute-start(bf16[32,3584]{1,0:T(8,128)(2,1)S(1)} %maximum_select_fusion.1.refs_0_), channel_id=1, source_target_pairs={{0,4},{1,5},{2,6},{3,7},{4,0},{5,1},{6,2},{7,3},{8,12},{9,13},{10,... | collective-permute-start | bytes 688136 | tf_op jit(solution)/shard_map/ppermute | solution.py:322
  14.5 21.0 %collective-permute-start.7 = (bf16[32,3584]{1,0:T(8,128)(2,1)S(1)}, bf16[32,3584]{1,0:T(8,128)(2,1)}, u32[]{:S(2)}, u32[]{:S(2)}) collective-permute-start(bf16[32,3584]{1,0:T(8,128)(2,1)S(1)} %maximum_select_fusion.1.refs_0_), channel_id=1, source_target_pairs={{0,2},{1,3},{2,0},{3,1},{4,6},{5,7},{6,4},{7,5},{8,10},{9,11},{10,... | collective-permute-start | bytes 688136 | tf_op jit(solution)/shard_map/ppermute | solution.py:322
  16.1 8.6 %collective-permute-start.2 = (f16[32,3584]{1,0:T(8,128)(2,1)S(1)}, f16[32,3584]{1,0:T(8,128)(2,1)S(1)}, u32[]{:S(2)}, u32[]{:S(2)}) collective-permute-start(f16[32,3584]{1,0:T(8,128)(2,1)S(1)} %convert_element_type.98), channel_id=1, source_target_pairs={{0,1},{1,0},{2,3},{3,2},{4,5},{5,4},{6,7},{7,6},{8,9},{9,8},{10,11... | collective-permute-start | bytes 688136 | tf_op jit(solution)/shard_map/ppermute | solution.py:322
  17.3 9.9 %collective-permute-start.4 = (f16[32,3584]{1,0:T(8,128)(2,1)S(1)}, f16[32,3584]{1,0:T(8,128)(2,1)S(1)}, u32[]{:S(2)}, u32[]{:S(2)}) collective-permute-start(f16[32,3584]{1,0:T(8,128)(2,1)S(1)} %convert_element_type.102), channel_id=1, source_target_pairs={{0,1},{1,0},{2,3},{3,2},{4,5},{5,4},{6,7},{7,6},{8,9},{9,8},{10,11... | collective-permute-start | bytes 688136 | tf_op jit(solution)/shard_map/ppermute | solution.py:322
  24.7 6.0 %collective-permute-start.1 = (f16[32,3584]{1,0:T(8,128)(2,1)S(1)}, f16[32,3584]{1,0:T(8,128)(2,1)S(1)}, u32[]{:S(2)}, u32[]{:S(2)}) collective-permute-start(f16[32,3584]{1,0:T(8,128)(2,1)S(1)} %add_convert_fusion.7), channel_id=1, source_target_pairs={{0,2},{1,3},{2,0},{3,1},{4,6},{5,7},{6,4},{7,5},{8,10},{9,11},{10,... | collective-permute-start | bytes 688136 | tf_op jit(solution)/shard_map/ppermute | solution.py:322
  27.3 6.7 %collective-permute-start.6 = (f16[32,3584]{1,0:T(8,128)(2,1)S(1)}, f16[32,3584]{1,0:T(8,128)(2,1)S(1)}, u32[]{:S(2)}, u32[]{:S(2)}) collective-permute-start(f16[32,3584]{1,0:T(8,128)(2,1)S(1)} %convert_element_type.106), channel_id=1, source_target_pairs={{0,1},{1,0},{2,3},{3,2},{4,5},{5,4},{6,7},{7,6},{8,9},{9,8},{10,11... | collective-permute-start | bytes 688136 | tf_op jit(solution)/shard_map/ppermute | solution.py:322
  30.7 11.5 %collective-permute-start.5 = (f16[32,3584]{1,0:T(8,128)(2,1)S(1)}, f16[32,3584]{1,0:T(8,128)(2,1)S(1)}, u32[]{:S(2)}, u32[]{:S(2)}) collective-permute-start(f16[32,3584]{1,0:T(8,128)(2,1)S(1)} %add_convert_fusion.5), channel_id=1, source_target_pairs={{0,2},{1,3},{2,0},{3,1},{4,6},{5,7},{6,4},{7,5},{8,10},{9,11},{10,... | collective-permute-start | bytes 688136 | tf_op jit(solution)/shard_map/ppermute | solution.py:322
  31.3 12.6 %collective-permute-start.3 = (f16[32,3584]{1,0:T(8,128)(2,1)S(1)}, f16[32,3584]{1,0:T(8,128)(2,1)S(1)}, u32[]{:S(2)}, u32[]{:S(2)}) collective-permute-start(f16[32,3584]{1,0:T(8,128)(2,1)S(1)} %add_convert_fusion.6), channel_id=1, source_target_pairs={{0,4},{1,5},{2,6},{3,7},{4,0},{5,1},{6,2},{7,3},{8,12},{9,13},{10,... | collective-permute-start | bytes 688136 | tf_op jit(solution)/shard_map/ppermute | solution.py:322
  34.0 10.5 %collective-permute-start.16 = (bf16[32,3584]{1,0:T(8,128)(2,1)S(1)}, bf16[32,3584]{1,0:T(8,128)(2,1)S(1)}, u32[]{:S(2)}, u32[]{:S(2)}) collective-permute-start(bf16[32,3584]{1,0:T(8,128)(2,1)S(1)} %maximum_select_fusion.1.refs_0_), channel_id=1, source_target_pairs={{0,1},{1,0},{2,3},{3,2},{4,5},{5,4},{6,7},{7,6},{8,9},{9,8},{10,11... | collective-permute-start | bytes 688136 | tf_op jit(solution)/shard_map/ppermute | solution.py:322
  35.5 12.5 %collective-permute-start.15 = (bf16[32,3584]{1,0:T(8,128)(2,1)}, bf16[32,3584]{1,0:T(8,128)(2,1)S(1)}, u32[]{:S(2)}, u32[]{:S(2)}) collective-permute-start(bf16[32,3584]{1,0:T(8,128)(2,1)} %collective-permute-done.11.refs_4_), channel_id=1, source_target_pairs={{0,2},{1,3},{2,0},{3,1},{4,6},{5,7},{6,4},{7,5},{8,10},{9,11},{10,... | collective-permute-start | bytes 688136 | tf_op jit(solution)/shard_map/ppermute | solution.py:322
  42.3 13.2 %collective-permute-start.12 = (bf16[32,3584]{1,0:T(8,128)(2,1)}, bf16[32,3584]{1,0:T(8,128)(2,1)S(1)}, u32[]{:S(2)}, u32[]{:S(2)}) collective-permute-start(bf16[32,3584]{1,0:T(8,128)(2,1)} %collective-permute-done.11.refs_4_), channel_id=1, source_target_pairs={{0,1},{1,0},{2,3},{3,2},{4,5},{5,4},{6,7},{7,6},{8,9},{9,8},{10,11... | collective-permute-start | bytes 688136 | tf_op jit(solution)/shard_map/ppermute | solution.py:322
  43.9 10.2 %collective-permute-start.8 = (bf16[32,3584]{1,0:T(8,128)(2,1)}, bf16[32,3584]{1,0:T(8,128)(2,1)S(1)}, u32[]{:S(2)}, u32[]{:S(2)}) collective-permute-start(bf16[32,3584]{1,0:T(8,128)(2,1)} %collective-permute-done.7.refs_2_), channel_id=1, source_target_pairs={{0,1},{1,0},{2,3},{3,2},{4,5},{5,4},{6,7},{7,6},{8,9},{9,8},{10,11... | collective-permute-start | bytes 688136 | tf_op jit(solution)/shard_map/ppermute | solution.py:322
  44.5 12.6 %collective-permute-start.14 = (bf16[32,3584]{1,0:T(8,128)(2,1)S(1)}, bf16[32,3584]{1,0:T(8,128)(2,1)S(1)}, u32[]{:S(2)}, u32[]{:S(2)}) collective-permute-start(bf16[32,3584]{1,0:T(8,128)(2,1)S(1)} %maximum_select_fusion.refs_0_), channel_id=1, source_target_pairs={{0,4},{1,5},{2,6},{3,7},{4,0},{5,1},{6,2},{7,3},{8,12},{9,13},{10,... | collective-permute-start | bytes 688136 | tf_op jit(solution)/shard_map/ppermute | solution.py:322
  48.0 14.4 %collective-permute-start.17 = (bf16[32,3584]{1,0:T(8,128)(2,1)S(1)}, bf16[32,3584]{1,0:T(8,128)(2,1)S(1)}, u32[]{:S(2)}, u32[]{:S(2)}) collective-permute-start(bf16[32,3584]{1,0:T(8,128)(2,1)S(1)} %collective-permute-done.15.refs_6_), channel_id=1, source_target_pairs={{0,1},{1,0},{2,3},{3,2},{4,5},{5,4},{6,7},{7,6},{8,9},{9,8},{10,11... | collective-permute-start | bytes 688136 | tf_op jit(solution)/shard_map/ppermute | solution.py:322
  54.1 6.0 %collective-permute-start.10 = (bf16[32,3584]{1,0:T(8,128)(2,1)S(1)}, bf16[32,3584]{1,0:T(8,128)(2,1)S(1)}, u32[]{:S(2)}, u32[]{:S(2)}) collective-permute-start(bf16[32,3584]{1,0:T(8,128)(2,1)S(1)} %maximum_select_fusion.refs_0_), channel_id=1, source_target_pairs={{0,2},{1,3},{2,0},{3,1},{4,6},{5,7},{6,4},{7,5},{8,10},{9,11},{10,... | collective-permute-start | bytes 688136 | tf_op jit(solution)/shard_map/ppermute | solution.py:322
  55.5 8.5 %collective-permute-start.9 = (bf16[32,3584]{1,0:T(8,128)(2,1)S(1)}, bf16[32,3584]{1,0:T(8,128)(2,1)S(1)}, u32[]{:S(2)}, u32[]{:S(2)}) collective-permute-start(bf16[32,3584]{1,0:T(8,128)(2,1)S(1)} %maximum_select_fusion.refs_0_), channel_id=1, source_target_pairs={{0,1},{1,0},{2,3},{3,2},{4,5},{5,4},{6,7},{7,6},{8,9},{9,8},{10,11... | collective-permute-start | bytes 688136 | tf_op jit(solution)/shard_map/ppermute | solution.py:322
  57.1 6.9 %collective-permute-start.19 = (bf16[32,3584]{1,0:T(8,128)(2,1)S(1)}, bf16[32,3584]{1,0:T(8,128)(2,1)S(1)}, u32[]{:S(2)}, u32[]{:S(2)}) collective-permute-start(bf16[32,3584]{1,0:T(8,128)(2,1)S(1)} %collective-permute-done.14.refs_4_), channel_id=1, source_target_pairs={{0,2},{1,3},{2,0},{3,1},{4,6},{5,7},{6,4},{7,5},{8,10},{9,11},{10,... | collective-permute-start | bytes 688136 | tf_op jit(solution)/shard_map/ppermute | solution.py:322
  60.1 20.9 %collective-permute-start.13 = (bf16[32,3584]{1,0:T(8,128)(2,1)S(1)}, bf16[32,3584]{1,0:T(8,128)(2,1)S(1)}, u32[]{:S(2)}, u32[]{:S(2)}) collective-permute-start(bf16[32,3584]{1,0:T(8,128)(2,1)S(1)} %collective-permute-done.10.refs_2_), channel_id=1, source_target_pairs={{0,1},{1,0},{2,3},{3,2},{4,5},{5,4},{6,7},{7,6},{8,9},{9,8},{10,11... | collective-permute-start | bytes 688136 | tf_op jit(solution)/shard_map/ppermute | solution.py:322
  62.5 18.6 %collective-permute-start.18 = (bf16[32,3584]{1,0:T(8,128)(2,1)S(1)}, bf16[32,3584]{1,0:T(8,128)(2,1)S(1)}, u32[]{:S(2)}, u32[]{:S(2)}) collective-permute-start(bf16[32,3584]{1,0:T(8,128)(2,1)S(1)} %collective-permute-done.14.refs_4_), channel_id=1, source_target_pairs={{0,1},{1,0},{2,3},{3,2},{4,5},{5,4},{6,7},{7,6},{8,9},{9,8},{10,11... | collective-permute-start | bytes 688136 | tf_op jit(solution)/shard_map/ppermute | solution.py:322
  64.0 17.0 %collective-permute-start.20 = (bf16[32,3584]{1,0:T(8,128)(2,1)S(1)}, bf16[32,3584]{1,0:T(8,128)(2,1)S(1)}, u32[]{:S(2)}, u32[]{:S(2)}) collective-permute-start(bf16[32,3584]{1,0:T(8,128)(2,1)S(1)} %collective-permute-done.19.refs_6_), channel_id=1, source_target_pairs={{0,1},{1,0},{2,3},{3,2},{4,5},{5,4},{6,7},{7,6},{8,9},{9,8},{10,11... | collective-permute-start | bytes 688136 | tf_op jit(solution)/shard_map/ppermute | solution.py:322
  66.3 3.5 %copy-start = (bf16[1792,2432]{1,0:T(8,128)(2,1)S(1)}, bf16[1792,2432]{1,0:T(8,128)(2,1)}, u32[]{:S(2)}) copy-start(bf16[1792,2432]{1,0:T(8,128)(2,1)} %refs_8_.1) | copy-start | bytes 26148868
  88.2 5.9 %collective-permute-start.25 = (f32[8,256]{1,0:T(8,128)S(1)}, f32[8,256]{1,0:T(8,128)S(1)}, u32[]{:S(2)}, u32[]{:S(2)}) collective-permute-start(f32[8,256]{1,0:T(8,128)S(1)} %get-tuple-element.60.refs_0_), channel_id=1, source_target_pairs={{0,4},{1,5},{2,6},{3,7},{4,0},{5,1},{6,2},{7,3},{8,12},{9,13},{10,... | collective-permute-start | bytes 24584 | tf_op jit(solution)/shard_map/ppermute | solution.py:322
  90.6 5.2 %collective-permute-start.24 = (f32[8,256]{1,0:T(8,128)S(1)}, f32[8,256]{1,0:T(8,128)S(1)}, u32[]{:S(2)}, u32[]{:S(2)}) collective-permute-start(f32[8,256]{1,0:T(8,128)S(1)} %get-tuple-element.60.refs_0_), channel_id=1, source_target_pairs={{0,3},{1,2},{2,1},{3,0},{4,7},{5,6},{6,5},{7,4},{8,11},{9,10},{10,... | collective-permute-start | bytes 24584 | tf_op jit(solution)/shard_map/ppermute | solution.py:322
  91.1 6.6 %collective-permute-start.23 = (f32[8,256]{1,0:T(8,128)S(1)}, f32[8,256]{1,0:T(8,128)S(1)}, u32[]{:S(2)}, u32[]{:S(2)}) collective-permute-start(f32[8,256]{1,0:T(8,128)S(1)} %get-tuple-element.60.refs_0_), channel_id=1, source_target_pairs={{0,2},{1,3},{2,0},{3,1},{4,6},{5,7},{6,4},{7,5},{8,10},{9,11},{10,... | collective-permute-start | bytes 24584 | tf_op jit(solution)/shard_map/ppermute | solution.py:322
  92.3 5.4 %collective-permute-start.22 = (f32[8,256]{1,0:T(8,128)S(1)}, f32[8,256]{1,0:T(8,128)S(1)}, u32[]{:S(2)}, u32[]{:S(2)}) collective-permute-start(f32[8,256]{1,0:T(8,128)S(1)} %get-tuple-element.60.refs_0_), channel_id=1, source_target_pairs={{0,1},{1,0},{2,3},{3,2},{4,5},{5,4},{6,7},{7,6},{8,9},{9,8},{10,11... | collective-permute-start | bytes 24584 | tf_op jit(solution)/shard_map/ppermute | solution.py:322
  94.1 4.6 %collective-permute-start.28 = (f32[8,256]{1,0:T(8,128)S(1)}, f32[8,256]{1,0:T(8,128)S(1)}, u32[]{:S(2)}, u32[]{:S(2)}) collective-permute-start(f32[8,256]{1,0:T(8,128)S(1)} %collective-permute-done.25.refs_4_), channel_id=1, source_target_pairs={{0,3},{1,2},{2,1},{3,0},{4,7},{5,6},{6,5},{7,4},{8,11},{9,10},{10,... | collective-permute-start | bytes 24584 | tf_op jit(solution)/shard_map/ppermute | solution.py:322
  94.6 4.1 %collective-permute-start.27 = (f32[8,256]{1,0:T(8,128)S(1)}, f32[8,256]{1,0:T(8,128)S(1)}, u32[]{:S(2)}, u32[]{:S(2)}) collective-permute-start(f32[8,256]{1,0:T(8,128)S(1)} %collective-permute-done.25.refs_4_), channel_id=1, source_target_pairs={{0,2},{1,3},{2,0},{3,1},{4,6},{5,7},{6,4},{7,5},{8,10},{9,11},{10,... | collective-permute-start | bytes 24584 | tf_op jit(solution)/shard_map/ppermute | solution.py:322
  95.8 3.7 %collective-permute-start.26 = (f32[8,256]{1,0:T(8,128)S(1)}, f32[8,256]{1,0:T(8,128)S(1)}, u32[]{:S(2)}, u32[]{:S(2)}) collective-permute-start(f32[8,256]{1,0:T(8,128)S(1)} %collective-permute-done.25.refs_4_), channel_id=1, source_target_pairs={{0,1},{1,0},{2,3},{3,2},{4,5},{5,4},{6,7},{7,6},{8,9},{9,8},{10,11... | collective-permute-start | bytes 24584 | tf_op jit(solution)/shard_map/ppermute | solution.py:322
  107.8 8.2 %collective-permute-start.29 = (f16[32,3584]{1,0:T(8,128)(2,1)S(1)}, f16[32,3584]{1,0:T(8,128)(2,1)S(1)}, u32[]{:S(2)}, u32[]{:S(2)}) collective-permute-start(f16[32,3584]{1,0:T(8,128)(2,1)S(1)} %convert_element_type.109), channel_id=1, source_target_pairs={{0,1},{1,0},{2,3},{3,2},{4,5},{5,4},{6,7},{7,6},{8,9},{9,8},{10,11... | collective-permute-start | bytes 688136 | tf_op jit(solution)/shard_map/ppermute | solution.py:322
  109.8 14.9 %collective-permute-start.31 = (f16[32,3584]{1,0:T(8,128)(2,1)S(1)}, f16[32,3584]{1,0:T(8,128)(2,1)S(1)}, u32[]{:S(2)}, u32[]{:S(2)}) collective-permute-start(f16[32,3584]{1,0:T(8,128)(2,1)S(1)} %convert_element_type.113), channel_id=1, source_target_pairs={{0,1},{1,0},{2,3},{3,2},{4,5},{5,4},{6,7},{7,6},{8,9},{9,8},{10,11... | collective-permute-start | bytes 688136 | tf_op jit(solution)/shard_map/ppermute | solution.py:322
  116.0 6.0 %collective-permute-start.33 = (f16[32,3584]{1,0:T(8,128)(2,1)S(1)}, f16[32,3584]{1,0:T(8,128)(2,1)S(1)}, u32[]{:S(2)}, u32[]{:S(2)}) collective-permute-start(f16[32,3584]{1,0:T(8,128)(2,1)S(1)} %convert_element_type.117), channel_id=1, source_target_pairs={{0,1},{1,0},{2,3},{3,2},{4,5},{5,4},{6,7},{7,6},{8,9},{9,8},{10,11... | collective-permute-start | bytes 688136 | tf_op jit(solution)/shard_map/ppermute | solution.py:322
  117.3 7.4 %collective-permute-start.30 = (f16[32,3584]{1,0:T(8,128)(2,1)S(1)}, f16[32,3584]{1,0:T(8,128)(2,1)S(1)}, u32[]{:S(2)}, u32[]{:S(2)}) collective-permute-start(f16[32,3584]{1,0:T(8,128)(2,1)S(1)} %add_convert_fusion.3), channel_id=1, source_target_pairs={{0,2},{1,3},{2,0},{3,1},{4,6},{5,7},{6,4},{7,5},{8,10},{9,11},{10,... | collective-permute-start | bytes 688136 | tf_op jit(solution)/shard_map/ppermute | solution.py:322
  122.0 6.0 %collective-permute-start.35 = (f16[32,3584]{1,0:T(8,128)(2,1)S(1)}, f16[32,3584]{1,0:T(8,128)(2,1)S(1)}, u32[]{:S(2)}, u32[]{:S(2)}) collective-permute-start(f16[32,3584]{1,0:T(8,128)(2,1)S(1)} %convert_element_type.121), channel_id=1, source_target_pairs={{0,1},{1,0},{2,3},{3,2},{4,5},{5,4},{6,7},{7,6},{8,9},{9,8},{10,11... | collective-permute-start | bytes 688136 | tf_op jit(solution)/shard_map/ppermute | solution.py:322
  123.3 6.1 %collective-permute-start.34 = (f16[32,3584]{1,0:T(8,128)(2,1)S(1)}, f16[32,3584]{1,0:T(8,128)(2,1)S(1)}, u32[]{:S(2)}, u32[]{:S(2)}) collective-permute-start(f16[32,3584]{1,0:T(8,128)(2,1)S(1)} %add_convert_fusion.1), channel_id=1, source_target_pairs={{0,2},{1,3},{2,0},{3,1},{4,6},{5,7},{6,4},{7,5},{8,10},{9,11},{10,... | collective-permute-start | bytes 688136 | tf_op jit(solution)/shard_map/ppermute | solution.py:322
  124.8 9.4 %collective-permute-start.32 = (f16[32,3584]{1,0:T(8,128)(2,1)S(1)}, f16[32,3584]{1,0:T(8,128)(2,1)S(1)}, u32[]{:S(2)}, u32[]{:S(2)}) collective-permute-start(f16[32,3584]{1,0:T(8,128)(2,1)S(1)} %add_convert_fusion.2), channel_id=1, source_target_pairs={{0,4},{1,5},{2,6},{3,7},{4,0},{5,1},{6,2},{7,3},{8,12},{9,13},{10,... | collective-permute-start | bytes 688136 | tf_op jit(solution)/shard_map/ppermute | solution.py:322
